TPU v7x, 32 devices: a whole 2x2x4 slice. The times are simulated.
32 devices in a mesh: vel: 2 (over x), cx: 4 (over y, core), cy: 4 (over z).
Axes of the slice: x: 2, y: 2, z: 4, core: 2. Of those that a mesh axis runs over, the one named last changes fastest.
Arguments:
- distribution: float32 [64, 16, 4, 13824], P('cx', 'cy', None, 'vel'), may hold values from 0.1 to 2
- refine_level: int32 [64, 16, 4], P('cx', 'cy'), may hold values from 0 to 2, as said below
- gain_one: float32 [24, 24, 24], replicated, may hold values from 0 to 2
- gain_two: float32 [24, 24, 24], replicated, may hold values from 0 to 2
- loss_kernel: float32 [24, 24, 24], replicated, may hold values from 0 to 2
Outputs:
- evolved: float32 [64, 16, 4, 13824], P('cx', 'cy', None, 'vel')
Inputs may be any that keep to these rules, and one draw needn't show every extreme that they name: `refine_level`: in each block of 256 cells (the 16 x 4 x 4 cells of one index of cx and cy) at most 128 cells have a level above 0, and some block has exactly 128.
All inputs are finite; a program needn't handle non-finite values.
Results may differ from a plain program's by a relative error of at most 0.0022.
Values may be sent and summed in bfloat16 or wider, within the bound.
No kernel may reach another device: no remote copies, remote signals or barrier semaphores. Data moves between devices by JAX's collectives and lax.ppermute only.
A program may use at most 128 MiB of HBM per device.

v0:
```python
import math

import jax
import jax.numpy as jnp
from jax import lax
from jax.sharding import PartitionSpec as P


def extended(array, sides, width):
    for axis, dim in sides:
        count, length = (lax.axis_size(axis), array.shape[dim])
        up = [(i, (i + 1) % count) for i in range(count)]
        down = [(j, i) for i, j in up]
        last = lax.slice_in_dim(array, length - width, length, axis=dim)
        leading = lax.slice_in_dim(array, 0, width, axis=dim)
        before = lax.ppermute(last, axis, up)
        after = lax.ppermute(leading, axis, down)
        array = jnp.concatenate([before, array, after], axis=dim)
    return array


def dft_tables(points):
    indices = jnp.arange(points, dtype=jnp.int32)
    products = indices[:, None] * indices[None, :] % points
    angles = products.astype(jnp.float32) * (2.0 * math.pi / points)
    cosine = jnp.cos(angles)
    sine_table = jnp.sin(angles)
    forward = jnp.stack([jnp.stack([cosine, sine_table]), jnp.stack([-sine_table, cosine])])
    inverse = jnp.stack([jnp.stack([cosine, -sine_table]), jnp.stack([sine_table, cosine])])
    return (forward.astype(jnp.bfloat16), inverse.astype(jnp.bfloat16))


def contract(pattern, left_side, right_side):
    return jnp.einsum(pattern, left_side, right_side, preferred_element_type=jnp.float32)


def collide(cells, forward, inverse, gain_one, gain_two, loss_kernel):
    points = forward.shape[-1]
    cell_count = cells.shape[0]
    field = cells.reshape(cell_count, points, points, points)
    section_z = contract("nabz,qzw->qnabw", field, forward[:, 0]).astype(jnp.bfloat16)
    section_y = contract("pnayc,qpyw->qnawc", section_z, forward).astype(jnp.bfloat16)
    spectrum = contract("pnxbc,qpxw->qnwbc", section_y, forward)
    scale_factor = 1.0 / float(points**3)

    def filtered(kernel):
        weighted = (spectrum * (kernel * scale_factor)[None, None]).astype(jnp.bfloat16)
        back_x = contract("pnxbc,qpxw->qnwbc", weighted, inverse).astype(jnp.bfloat16)
        back_y = contract("pnayc,qpyw->qnawc", back_x, inverse).astype(jnp.bfloat16)
        return contract("pnabz,pzw->nabw", back_y, inverse[0])

    gain_term = filtered(gain_one) * filtered(gain_two)
    result = gain_term - field.astype(jnp.float32) * filtered(loss_kernel)
    return result.reshape(cell_count, points**3)


def courants(points, first_vel, local_count):
    vel_index = first_vel + jnp.arange(local_count, dtype=jnp.int32)
    index_x = vel_index // (points * points)
    index_y = vel_index // points % points
    index_z = vel_index % points

    def speed(index_part):
        return 0.3 * (2.0 * index_part.astype(jnp.float32) - (points - 1)) / (points - 1)

    return (speed(index_x), speed(index_y), speed(index_z))


def upwind_flux(courant, center, lower_side, upper_side):
    return jnp.maximum(courant, 0.0) * (center - lower_side) + jnp.minimum(courant, 0.0) * (
        upper_side - center
    )


def per_device(distribution, refine_level, gain_one, gain_two, loss_kernel):
    points = gain_one.shape[0]
    width_x, width_y, width_z, local_vel = distribution.shape
    first_vel = lax.axis_index("vel") * local_vel
    courant_x, courant_y, courant_z = courants(points, first_vel, local_vel)
    padded = extended(distribution, (("cx", 0), ("cy", 1)), 1)
    fluxes = upwind_flux(courant_x, distribution, padded[:-2, 1:-1], padded[2:, 1:-1])
    fluxes = fluxes + upwind_flux(courant_y, distribution, padded[1:-1, :-2], padded[1:-1, 2:])
    fluxes = fluxes + upwind_flux(
        courant_z, distribution, jnp.roll(distribution, 1, 2), jnp.roll(distribution, -1, 2)
    )
    read = distribution - fluxes
    block_cells = width_x * width_y * width_z
    groups = lax.axis_size("vel")
    flattened = read.reshape(block_cells, local_vel).astype(jnp.bfloat16)
    forward, inverse = dft_tables(points)
    active = refine_level.reshape(block_cells) > 0
    slot_index = jnp.cumsum(active.astype(jnp.int32)) - 1
    capacity = block_cells // 2
    picker = (
        (slot_index[None, :] == jnp.arange(capacity, dtype=jnp.int32)[:, None]) & active[None, :]
    ).astype(jnp.bfloat16)
    chosen = jnp.dot(picker, flattened, preferred_element_type=jnp.float32).astype(jnp.bfloat16)
    terms = collide(
        lax.all_to_all(
            chosen.reshape(groups, capacity // groups, local_vel),
            "vel",
            split_axis=0,
            concat_axis=2,
            tiled=True,
        )[0],
        forward,
        inverse,
        gain_one,
        gain_two,
        loss_kernel,
    )[None]
    packed = lax.all_to_all(
        terms.astype(jnp.bfloat16), "vel", split_axis=2, concat_axis=0, tiled=True
    ).astype(terms.dtype)
    packed_rows = packed.reshape(capacity, local_vel)
    safe_slot = jnp.clip(slot_index, 0, capacity - 1)
    rates = jnp.where(active[:, None], packed_rows[safe_slot], 0.0)
    weight = 0.25 * refine_level.astype(jnp.float32)
    return read + weight[..., None] * rates.reshape(width_x, width_y, width_z, local_vel)


def solution(mesh):
    placed = (P("cx", "cy", None, "vel"), P("cx", "cy", None), P(), P(), P())
    return jax.shard_map(
        per_device,
        mesh=mesh,
        in_specs=placed,
        out_specs=P("cx", "cy", None, "vel"),
        check_vma=False,
    )
```

profile of v0, /device:TPU:0, one launch (start us, length us, event | category | flops | bytes accessed | tf_op | source)
XLA Modules:
  0.0 495.1 jit_solution(5454138850626341600)
XLA Ops:
  5.1 10.5 %fusion.129 = (f32[16,4,1,6912]{3,2,1,0:T(1,128)}, f32[16,4,1,6912]{3,2,1,0:T(1,128)}) fusion(f32[16,4,4,6912]{3,2,1,0:T(4,128)} %param.5), kind=kLoop, calls=%fused_computation.168 | loop fusion | bytes 7077888 | tf_op jit(solution)/shard_map/jit(_roll_static)/slice | solution.py:84
  17.5 7.0 %constant_dynamic-update-slice_fusion.1 = f32[18,4,4,6912]{3,2,1,0:T(4,128)} fusion(f32[18,4,4,6912]{3,2,1,0:T(4,128)} %constant_dynamic-update-slice_fusion.2, f32[16,4,4,6912]{3,2,1,0:T(4,128)} %param.5), kind=kLoop, calls=%fused_computation.153 | loop fusion | bytes 14155776
  32.4 3.8 fusion.130
  36.2 40.3 %collective-permute-done.2 = f32[18,1,4,6912]{3,2,1,0:T(4,128)S(1)} collective-permute-done((f32[18,1,4,6912]{3,2,1,0:T(4,128)S(1)}, f32[18,1,4,6912]{3,2,1,0:T(4,128)S(1)}, u32[]{:S(2)}, u32[]{:S(2)}) %collective-permute-start.2) | collective-permute-done | bytes 1990688 | tf_op jit(solution)/shard_map/ppermute | solution.py:16
  76.5 41.4 %collective-permute-done.3 = f32[18,1,4,6912]{3,2,1,0:T(4,128)S(1)} collective-permute-done((f32[18,1,4,6912]{3,2,1,0:T(4,128)S(1)}, f32[18,1,4,6912]{3,2,1,0:T(4,128)S(1)}, u32[]{:S(2)}, u32[]{:S(2)}) %collective-permute-start.3) | collective-permute-done | bytes 1990688 | tf_op jit(solution)/shard_map/ppermute | solution.py:17
  119.3 29.2 %fusion.125 = (bf16[16,4,4,6912]{3,2,1,0:T(4,128)(2,1)S(1)}, f32[16,4,4,6912]{3,2,1,0:T(4,128)}) fusion(f32[16,4,4,6912]{3,2,1,0:T(4,128)S(1)} %bitcast.197, f32[16,4,1,6912]{3,2,1,0:T(1,128)S(1)} %copy-done.1, f32[16,4,3,6912]{3,2,1,0:T(4,128)S(1)} %get-tuple-element.19, f32[6912]{0:T(1024)S(1)} %copy-done.19, ...), kind=kLoop, calls=%fused_computation.165 | loop fusion | flops 44236800 | bytes 44845056 | tf_op jit(solution)/shard_map/convert_element_type | solution.py:89
  151.0 4.0 convolution_convert_fusion
  155.0 3.9 all-to-all-start
  162.4 17.7 %all-to-all-done = bf16[2,64,6912]{2,1,0:T(8,128)(2,1)S(1)} async-done(((bf16[2,64,6912]{2,1,0:T(8,128)(2,1)}), bf16[2,64,6912]{2,1,0:T(8,128)(2,1)S(1)}, u32[]{:S(2)}, u32[]{:S(2)}) %all-to-all-start) | async-done | bytes 1769504 | tf_op jit(solution)/shard_map/all_to_all | solution.py:99
  181.3 3.4 copy.27
  184.7 2.8 convert_bitcast_fusion
  187.5 4.9 fusion.3
  192.4 15.4 %fusion.6 = (bf16[2,64,24,24,24]{1,2,4,3,0:T(8,128)(2,1)}, bf16[2,64,24,24,24]{1,2,4,3,0:T(8,128)(2,1)S(1)}, bf16[2,64,24,24,24]{1,2,4,3,0:T(8,128)(2,1)}) fusion(f32[24,24,24]{0,2,1:T(8,128)S(1)} %copy-done.11, f32[24,24,24]{0,2,1:T(8,128)S(1)} %copy-done.12, f32[24,24,24]{0,2,1:T(8,128)S(1)} %copy-done.13, bf16[2,64,24,24,24]{1,3,4,2,0:T(8,128)(2,1)} %fusion.3, ...), kind=kOutput, calls=%fused_computation.18 | convolution fusion | flops 180488448 | bytes 14326272 | tf_op jit(solution)/shard_map/pnxbc,qpxw->qnwbc/dot_general | solution.py:34
  209.9 12.9 %fusion.10 = bf16[2,64,24,24,24]{1,3,4,2,0:T(8,128)(2,1)} fusion(bf16[2,64,24,24,24]{1,2,4,3,0:T(8,128)(2,1)S(1)} %fusion.9, bf16[1,2,24,24]{2,3,1,0:T(8,128)(2,1)S(1)} %copy-done.7, bf16[1,2,24,24]{2,3,1,0:T(8,128)(2,1)S(1)} %get-tuple-element.20), kind=kOutput, calls=%fused_computation.22 | convolution fusion | flops 171648000 | bytes 7082496 | tf_op jit(solution)/shard_map/pnayc,qpyw->qnawc/dot_general | solution.py:34
  222.9 4.1 fusion.51
  227.0 8.8 %fusion.11 = bf16[2,64,24,24,24]{1,2,4,3,0:T(8,128)(2,1)} fusion(bf16[2,64,24,24,24]{1,2,4,3,0:T(8,128)(2,1)} %get-tuple-element.11, bf16[1,2,24,24]{2,3,1,0:T(8,128)(2,1)S(1)} %copy-done.7, bf16[1,2,24,24]{2,3,1,0:T(8,128)(2,1)S(1)} %get-tuple-element.20), kind=kOutput, calls=%fused_computation.23 | convolution fusion | flops 171648000 | bytes 7082496 | tf_op jit(solution)/shard_map/pnxbc,qpxw->qnwbc/dot_general | solution.py:34
  235.9 16.0 %fusion.12 = bf16[2,64,24,24,24]{1,3,4,2,0:T(8,128)(2,1)} fusion(bf16[2,64,24,24,24]{1,2,4,3,0:T(8,128)(2,1)} %fusion.11, bf16[1,2,24,24]{2,3,1,0:T(8,128)(2,1)S(1)} %copy-done.7, bf16[1,2,24,24]{2,3,1,0:T(8,128)(2,1)S(1)} %get-tuple-element.20), kind=kOutput, calls=%fused_computation.24 | convolution fusion | flops 171648000 | bytes 7082496 | tf_op jit(solution)/shard_map/pnayc,qpyw->qnawc/dot_general | solution.py:34
  251.8 7.1 %fusion.47 = f32[64,24,24,24,1]{0,3,4,2,1:T(8,128)} fusion(bf16[2,64,24,24,24]{1,3,4,2,0:T(8,128)(2,1)} %fusion.12, bf16[1,24,24]{1,2,0:T(8,128)(2,1)S(1)} %copy-done.15, bf16[1,24,24]{1,2,0:T(8,128)(2,1)S(1)} %copy-done.17), kind=kOutput, calls=%fused_computation.67 | convolution fusion | flops 84935808 | bytes 7080192 | tf_op jit(solution)/shard_map/pnabz,pzw->nabw/dot_general | solution.py:34
  258.9 8.5 %fusion.7 = bf16[2,64,24,24,24]{1,2,4,3,0:T(8,128)(2,1)} fusion(bf16[2,64,24,24,24]{1,2,4,3,0:T(8,128)(2,1)} %get-tuple-element.9, bf16[1,2,24,24]{2,3,1,0:T(8,128)(2,1)S(1)} %copy-done.7, bf16[1,2,24,24]{2,3,1,0:T(8,128)(2,1)S(1)} %get-tuple-element.20), kind=kOutput, calls=%fused_computation.19 | convolution fusion | flops 171648000 | bytes 7082496 | tf_op jit(solution)/shard_map/pnxbc,qpxw->qnwbc/dot_general | solution.py:34
  267.4 16.0 %fusion.8 = bf16[2,64,24,24,24]{1,3,4,2,0:T(8,128)(2,1)} fusion(bf16[2,64,24,24,24]{1,2,4,3,0:T(8,128)(2,1)} %fusion.7, bf16[1,2,24,24]{2,3,1,0:T(8,128)(2,1)S(1)} %copy-done.7, bf16[1,2,24,24]{2,3,1,0:T(8,128)(2,1)S(1)} %get-tuple-element.20), kind=kOutput, calls=%fused_computation.20 | convolution fusion | flops 171648000 | bytes 7082496 | tf_op jit(solution)/shard_map/pnayc,qpyw->qnawc/dot_general | solution.py:34
  283.4 7.2 %fusion.30 = bf16[64,24,24,24]{0,3,2,1:T(8,128)(2,1)S(1)} fusion(f32[64,24,24,24,1]{0,3,4,2,1:T(8,128)} %fusion.47, f32[64,24,24,24,1]{0,3,4,2,1:T(8,128)S(1)} %fusion.51, bf16[64,24,24,24]{0,3,2,1:T(8,128)(2,1)S(1)} %bitcast.199, bf16[2,64,24,24,24]{1,3,4,2,0:T(8,128)(2,1)} %fusion.8, bf16[1,24,24]{1,2,0:T(8,128)(2,1)S(1)} %copy-done.15, ...), kind=kOutput, calls=%fused_computation.49 | convolution fusion | flops 89359488 | bytes 14158080 | tf_op jit(solution)/shard_map/pnabz,pzw->nabw/dot_general | solution.py:34
  290.6 55.8 %copy.129 = bf16[1,64,13824]{1,0,2:T(2,128)(2,1)} copy(bf16[1,64,13824]{1,2,0:T(8,128)(2,1)S(1)} %bitcast.202) | data formatting | bytes 3538944 | tf_op jit(solution)/shard_map/convert_element_type | solution.py:113
  347.0 75.3 %reduce.2 = bf16[13824,64]{1,0:T(8,128)(2,1)S(1)} reduce(bf16[13824,1,64]{2,1,0:T(2,128)(2,1)} %bitcast.201, bf16[]{:T(256)} %broadcast.500), dimensions={1}, to_apply=%bitcast.194.reduce_sub_computation | reduce | bytes 3538946
  422.3 3.9 reshape.275
  426.2 3.7 all-to-all-start.1
  430.6 19.6 %all-to-all-done.1 = bf16[2,2,221184]{2,1,0:T(2,128)(2,1)S(1)} async-done(((bf16[2,2,221184]{2,1,0:T(2,128)(2,1)}), bf16[2,2,221184]{2,1,0:T(2,128)(2,1)S(1)}, u32[]{:S(2)}, u32[]{:S(2)}) %all-to-all-start.1) | async-done | bytes 1769504 | tf_op jit(solution)/shard_map/all_to_all | solution.py:112
  450.2 4.2 reshape.276
  454.5 9.5 %bitcast_convert_fusion.7 = f32[1,64,13824]{1,0,2:T(1,128)} fusion(bf16[13824,1,64]{2,1,0:T(2,128)(2,1)} %reshape.276), kind=kLoop, calls=%fused_computation.170 | loop fusion | flops 884736 | bytes 5308416 | tf_op jit(solution)/shard_map/convert_element_type | solution.py:114
  464.0 4.7 copy.45
  468.6 5.7 %gather_fusion = f32[256,6912]{1,0:T(8,128)} fusion(f32[128,6912]{1,0:T(8,128)S(1)} %bitcast.195, s32[1024]{0:T(1024)S(1)} %pad_clamp_fusion), kind=kCustom, calls=%fused_computation | custom fusion | bytes 14156800 | tf_op jit(solution)/shard_map/gather | solution.py:117
  474.3 8.7 %gather.6 = f32[16,4,4,6912]{3,2,1,0:T(4,128)} reshape(f32[256,6912]{1,0:T(8,128)} %gather_fusion) | data formatting | bytes 14155776 | tf_op jit(solution)/shard_map/gather | solution.py:117
  483.0 11.6 %multiply_add_fusion = f32[16,4,4,6912]{3,2,1,0:T(4,128)} fusion(f32[16,4,4,6912]{3,2,1,0:T(4,128)} %get-tuple-element.8, f32[16,4,4,6912]{3,2,1,0:T(4,128)} %gather.6, f32[16,4,4]{2,1,0:T(4,128)S(1)} %copy-done.18, pred[16,4,4]{2,1,0:T(4,128)(4,1)S(1)} %copy-done.26), kind=kLoop, calls=%fused_computation.81 | loop fusion | flops 5308416 | bytes 21234944 | tf_op jit(solution)/shard_map/add | solution.py:119
  (102 shorter events, 26.9 us)
Async XLA Ops:
  0.0 15.6 %copy-start.27 = (s32[16,4,4]{0,2,1:T(4,128)S(1)}, s32[16,4,4]{0,2,1:T(4,128)}, u32[]{:S(2)}) copy-start(s32[16,4,4]{0,2,1:T(4,128)} %param.6) | copy-start | bytes 3076
  1.2 15.5 %collective-permute-start = (f32[1,4,4,6912]{3,2,1,0:T(4,128)S(1)}, f32[1,4,4,6912]{3,2,1,0:T(4,128)S(1)}, u32[]{:S(2)}, u32[]{:S(2)}) collective-permute-start(f32[1,4,4,6912]{3,2,1,0:T(4,128)S(1)} %get-tuple-element.15), channel_id=1, source_target_pairs={{0,4},{4,8},{8,12},{12,0},{1,5},{5,9},{9,13},{13,1},{2,6},{6,10},{... | collective-permute-start | bytes 1327112 | tf_op jit(solution)/shard_map/ppermute | solution.py:16
  1.7 22.8 %collective-permute-start.1 = (f32[1,4,4,6912]{3,2,1,0:T(4,128)S(1)}, f32[1,4,4,6912]{3,2,1,0:T(4,128)S(1)}, u32[]{:S(2)}, u32[]{:S(2)}) collective-permute-start(f32[1,4,4,6912]{3,2,1,0:T(4,128)S(1)} %get-tuple-element.14), channel_id=1, source_target_pairs={{4,0},{8,4},{12,8},{0,12},{5,1},{9,5},{13,9},{1,13},{6,2},{10,6},{... | collective-permute-start | bytes 1327112 | tf_op jit(solution)/shard_map/ppermute | solution.py:17
  16.4 8.2 %copy-start.25 = (pred[16,4,4]{2,1,0:T(4,128)(4,1)}, pred[16,4,4]{2,1,0:T(4,128)(4,1)S(1)}, u32[]{:S(2)}) copy-start(pred[16,4,4]{2,1,0:T(4,128)(4,1)S(1)} %copy.23) | copy-start | bytes 772
  16.7 7.8 %copy-start.4 = (f32[1,4,4,6912]{3,2,1,0:T(4,128)}, f32[1,4,4,6912]{3,2,1,0:T(4,128)S(1)}, u32[]{:S(2)}) copy-start(f32[1,4,4,6912]{3,2,1,0:T(4,128)S(1)} %collective-permute-done) | copy-start | bytes 1327108
  16.7 15.7 %slice-start = ((s8[7077888]{0:T(1024)(128)(4,1)}), s8[4194304]{0:T(1024)(128)(4,1)S(1)}, s32[]{:S(2)}) async-start(s8[7077888]{0:T(1024)(128)(4,1)} %bitcast.196), calls=%async_computation.2 | async-start | bytes 8388608
  17.5 14.9 %slice-start.1 = ((s8[7077888]{0:T(1024)(128)(4,1)}), s8[2883584]{0:T(1024)(128)(4,1)S(1)}, s32[]{:S(2)}) async-start(s8[7077888]{0:T(1024)(128)(4,1)} %bitcast.196), calls=%async_computation.3 | async-start | bytes 5767168
  24.6 11.6 %copy-start.6 = (f32[1,4,4,6912]{3,2,1,0:T(4,128)}, f32[1,4,4,6912]{3,2,1,0:T(4,128)S(1)}, u32[]{:S(2)}) copy-start(f32[1,4,4,6912]{3,2,1,0:T(4,128)S(1)} %collective-permute-done.1) | copy-start | bytes 1327108
  27.9 48.6 %collective-permute-start.2 = (f32[18,1,4,6912]{3,2,1,0:T(4,128)S(1)}, f32[18,1,4,6912]{3,2,1,0:T(4,128)S(1)}, u32[]{:S(2)}, u32[]{:S(2)}) collective-permute-start(f32[18,1,4,6912]{3,2,1,0:T(4,128)S(1)} %get-tuple-element.12), channel_id=1, source_target_pairs={{0,1},{1,2},{2,3},{3,0},{4,5},{5,6},{6,7},{7,4},{8,9},{9,10},{10,1... | collective-permute-start | bytes 5971976 | tf_op jit(solution)/shard_map/ppermute | solution.py:16
  30.3 89.0 %copy-start = (f32[16,4,1,6912]{3,2,1,0:T(1,128)S(1)}, f32[16,4,1,6912]{3,2,1,0:T(1,128)}, u32[]{:S(2)}) copy-start(f32[16,4,1,6912]{3,2,1,0:T(1,128)} %get-tuple-element.16) | copy-start | bytes 5308420
  30.3 89.0 %copy-start.1 = (f32[16,4,1,6912]{3,2,1,0:T(1,128)S(1)}, f32[16,4,1,6912]{3,2,1,0:T(1,128)}, u32[]{:S(2)}) copy-start(f32[16,4,1,6912]{3,2,1,0:T(1,128)} %get-tuple-element.17) | copy-start | bytes 5308420
  30.3 89.0 %copy-start.5 = (f32[1,4,4,6912]{3,2,1,0:T(4,128)S(1)}, f32[1,4,4,6912]{3,2,1,0:T(4,128)}, u32[]{:S(2)}) copy-start(f32[1,4,4,6912]{3,2,1,0:T(4,128)} %copy-done.4) | copy-start | bytes 1327108
  30.3 89.0 %copy-start.19 = (f32[6912]{0:T(1024)S(1)}, f32[6912]{0:T(1024)}, u32[]{:S(2)}) copy-start(f32[6912]{0:T(1024)} %get-tuple-element.28) | copy-start | bytes 82948
  30.3 89.0 %copy-start.20 = (f32[6912]{0:T(1024)S(1)}, f32[6912]{0:T(1024)}, u32[]{:S(2)}) copy-start(f32[6912]{0:T(1024)} %get-tuple-element.29) | copy-start | bytes 82948
  30.3 89.0 %copy-start.21 = (f32[6912]{0:T(1024)S(1)}, f32[6912]{0:T(1024)}, u32[]{:S(2)}) copy-start(f32[6912]{0:T(1024)} %get-tuple-element.30) | copy-start | bytes 82948
  30.3 89.0 %copy-start.22 = (f32[6912]{0:T(1024)S(1)}, f32[6912]{0:T(1024)}, u32[]{:S(2)}) copy-start(f32[6912]{0:T(1024)} %get-tuple-element.31) | copy-start | bytes 82948
  30.3 87.6 %collective-permute-start.3 = (f32[18,1,4,6912]{3,2,1,0:T(4,128)S(1)}, f32[18,1,4,6912]{3,2,1,0:T(4,128)S(1)}, u32[]{:S(2)}, u32[]{:S(2)}) collective-permute-start(f32[18,1,4,6912]{3,2,1,0:T(4,128)S(1)} %get-tuple-element.13), channel_id=1, source_target_pairs={{1,0},{2,1},{3,2},{0,3},{5,4},{6,5},{7,6},{4,7},{9,8},{10,9},{11,1... | collective-permute-start | bytes 5971976 | tf_op jit(solution)/shard_map/ppermute | solution.py:17
  151.0 7.9 %copy-start.8 = (f32[24,24,24]{2,1,0:T(8,128)S(1)}, f32[24,24,24]{2,1,0:T(8,128)}, u32[]{:S(2)}) copy-start(f32[24,24,24]{2,1,0:T(8,128)} %param.7) | copy-start | bytes 165892
  151.0 8.8 %copy-start.9 = (f32[24,24,24]{2,1,0:T(8,128)S(1)}, f32[24,24,24]{2,1,0:T(8,128)}, u32[]{:S(2)}) copy-start(f32[24,24,24]{2,1,0:T(8,128)} %param.8) | copy-start | bytes 165892
  151.0 9.7 %copy-start.10 = (f32[24,24,24]{2,1,0:T(8,128)S(1)}, f32[24,24,24]{2,1,0:T(8,128)}, u32[]{:S(2)}) copy-start(f32[24,24,24]{2,1,0:T(8,128)} %param.9) | copy-start | bytes 165892
  155.0 25.1 %all-to-all-start = ((bf16[2,64,6912]{2,1,0:T(8,128)(2,1)}), bf16[2,64,6912]{2,1,0:T(8,128)(2,1)S(1)}, u32[]{:S(2)}, u32[]{:S(2)}) async-start(bf16[2,64,6912]{2,1,0:T(8,128)(2,1)} %bitcast.14), calls=%async_computation | async-start | bytes 3538944 | tf_op jit(solution)/shard_map/all_to_all | solution.py:99
  161.7 18.4 %copy-start.14 = (bf16[1,24,24]{1,2,0:T(8,128)(2,1)}, bf16[1,24,24]{1,2,0:T(8,128)(2,1)S(1)}, u32[]{:S(2)}) copy-start(bf16[1,24,24]{1,2,0:T(8,128)(2,1)S(1)} %cosine_convert_fusion) | copy-start | bytes 3460
  161.8 18.3 %copy-start.16 = (bf16[1,24,24]{1,2,0:T(8,128)(2,1)}, bf16[1,24,24]{1,2,0:T(8,128)(2,1)S(1)}, u32[]{:S(2)}) copy-start(bf16[1,24,24]{1,2,0:T(8,128)(2,1)S(1)} %get-tuple-element.34) | copy-start | bytes 3460
  187.5 4.9 copy-start.11
  187.5 4.9 copy-start.12
  192.4 15.4 %copy-start.7 = (bf16[1,2,24,24]{2,3,1,0:T(8,128)(2,1)S(1)}, bf16[1,2,24,24]{2,3,1,0:T(8,128)(2,1)}, u32[]{:S(2)}) copy-start(bf16[1,2,24,24]{2,3,1,0:T(8,128)(2,1)} %get-tuple-element.25) | copy-start | bytes 6916
  209.9 13.0 %copy-start.15 = (bf16[1,24,24]{1,2,0:T(8,128)(2,1)S(1)}, bf16[1,24,24]{1,2,0:T(8,128)(2,1)}, u32[]{:S(2)}) copy-start(bf16[1,24,24]{1,2,0:T(8,128)(2,1)} %copy-done.14) | copy-start | bytes 3460
  209.9 13.0 %copy-start.17 = (bf16[1,24,24]{1,2,0:T(8,128)(2,1)S(1)}, bf16[1,24,24]{1,2,0:T(8,128)(2,1)}, u32[]{:S(2)}) copy-start(bf16[1,24,24]{1,2,0:T(8,128)(2,1)} %copy-done.16) | copy-start | bytes 3460
  422.2 7.6 %copy-start.28 = (s32[16,4,4]{0,2,1:T(4,128)S(1)}, s32[16,4,4]{0,2,1:T(4,128)}, u32[]{:S(2)}) copy-start(s32[16,4,4]{0,2,1:T(4,128)} %param.6) | copy-start | bytes 3076
  426.2 24.1 %all-to-all-start.1 = ((bf16[2,2,221184]{2,1,0:T(2,128)(2,1)}), bf16[2,2,221184]{2,1,0:T(2,128)(2,1)S(1)}, u32[]{:S(2)}, u32[]{:S(2)}) async-start(bf16[2,2,221184]{2,1,0:T(2,128)(2,1)} %reshape.275), calls=%async_computation.1 | async-start | bytes 3538944 | tf_op jit(solution)/shard_map/all_to_all | solution.py:112
  474.3 8.7 %copy-start.18 = (f32[16,4,4]{2,1,0:T(4,128)S(1)}, f32[16,4,4]{2,1,0:T(4,128)}, u32[]{:S(2)}) copy-start(f32[16,4,4]{2,1,0:T(4,128)} %copy.22) | copy-start | bytes 3076
  474.3 8.7 %copy-start.26 = (pred[16,4,4]{2,1,0:T(4,128)(4,1)S(1)}, pred[16,4,4]{2,1,0:T(4,128)(4,1)}, u32[]{:S(2)}) copy-start(pred[16,4,4]{2,1,0:T(4,128)(4,1)} %copy-done.25) | copy-start | bytes 772
  (5 other events, 13.0 us)
where the time goes:
time: 503 us; the launch traced here: 495 us
  other arithmetic  128 us (25%)
  local copies, waits for them, and re-layouts  123 us (24%)
  waiting for transfers between devices  119 us (24%)
  matrix products  110 us (22%)
  starting transfers between devices  14.6 us (3%)
    dot_general x12, matrix products, contract(): jnp.einsum(pattern, left_side, right_side, preferred_element_type=jnp.flo...  106 us
    unnamed x2, other arithmetic  75.3 us
    convert_element_type x1, local copies, waits for them, and re-layouts, per_device(): terms.astype(jnp.bfloat16)  55.8 us
    ppermute x2, waiting for transfers between devices, extended(): after = lax.ppermute(leading, axis, down)  41.4 us
    ppermute x2, waiting for transfers between devices, extended(): before = lax.ppermute(last, axis, up)  40.3 us
    convert_element_type x1, other arithmetic, per_device(): flattened = read.reshape(block_cells, local_vel).astype(jnp.bfloat16)  29.2 us
    all_to_all x1, waiting for transfers between devices, per_device(): lax.all_to_all(terms.astype(jnp.bfloat16), 'vel', split_axis=2, concat_ax...  19.6 us
    unnamed x67, local copies, waits for them, and re-layouts  19.2 us
  transfers between devices with their start and end apart: 6, of which 4 were waited for; matrix products, arithmetic and copies ran while one was open for 6% of the time, Pallas kernels for 0%

commit v1 on v0

--- a/solution.py
+++ b/solution.py
@@ -1,8 +1,13 @@
+import functools
 import math
 
 import jax
 import jax.numpy as jnp
+import ml_dtypes
+import numpy as np
 from jax import lax
+from jax.experimental import pallas as pl
+from jax.experimental.pallas import tpu as pltpu
 from jax.sharding import PartitionSpec as P
 
 
@@ -72,7 +77,7 @@
     )
 
 
-def per_device(distribution, refine_level, gain_one, gain_two, loss_kernel):
+def plain_device(distribution, refine_level, gain_one, gain_two, loss_kernel):
     points = gain_one.shape[0]
     width_x, width_y, width_z, local_vel = distribution.shape
     first_vel = lax.axis_index("vel") * local_vel
@@ -118,6 +123,509 @@
     weight = 0.25 * refine_level.astype(jnp.float32)
     return read + weight[..., None] * rates.reshape(width_x, width_y, width_z, local_vel)
 
+LANES = 128
+PLANES = 4
+
+
+def half_set(points):
+    middle = points // 2
+    pairs = [(b, c) for c in range(1, middle) for b in range(points)]
+    pairs += [(b, c) for c in (0, middle) for b in range(middle + 1)]
+    weights = [1.0 if b % middle == 0 and c % middle == 0 else 2.0 for b, c in pairs]
+    return np.array(pairs), np.array(weights)
+
+
+def plane_table(points, padded, margin):
+    pairs, _ = half_set(points)
+    first, second = np.divmod(np.arange(points * points), points)
+    products = (first[:, None] * pairs[None, :, 0] + second[:, None] * pairs[None, :, 1]) % points
+    angles = 2.0 * np.pi * products / points
+    table = np.zeros((points * points + 2 * margin, 2 * padded), np.float32)
+    rows = slice(margin, margin + points * points)
+    table[rows, : len(pairs)] = np.cos(angles)
+    table[rows, padded : padded + len(pairs)] = -np.sin(angles)
+    return table.astype(ml_dtypes.bfloat16)
+
+
+def frequency_weights(kernels, padded):
+    points = kernels[0].shape[0]
+    pairs, weights = half_set(points)
+    plus = np.zeros((points * points, padded), np.float32)
+    minus = np.zeros((points * points, padded), np.float32)
+    column = np.arange(len(pairs))
+    plus[pairs[:, 0] * points + pairs[:, 1], column] = 1.0
+    minus[(-pairs[:, 0]) % points * points + (-pairs[:, 1]) % points, column] = 1.0
+    scale = np.zeros((padded,), np.float32)
+    scale[: len(pairs)] = 0.5 * weights / points**3
+    stacked = jnp.stack(kernels).reshape(3, points, points * points)
+    mirrored = jnp.concatenate([stacked[:, :1], jnp.flip(stacked[:, 1:], 1)], axis=1)
+    both = jnp.concatenate([stacked, mirrored], axis=2).reshape(3 * points, -1)
+    select = jnp.asarray(np.concatenate([plus, minus]))
+    picked = jnp.dot(both, select, precision=lax.Precision.HIGHEST)
+    return (picked * scale).reshape(3, points, padded)
+
+
+def transform_3(x, sign, wanted=(0, 1, 2)):
+    (ar, ai), (br, bi), (cr, ci) = x
+    sr, si = br + cr, bi + ci
+    out = {}
+    if 0 in wanted:
+        out[0] = (ar + sr, ai + si)
+    if 1 in wanted or 2 in wanted:
+        height = sign * math.sqrt(0.75)
+        mr, mi = ar - 0.5 * sr, ai - 0.5 * si
+        er, ei = height * (br - cr), height * (bi - ci)
+        if 1 in wanted:
+            out[1] = (mr - ei, mi + er)
+        if 2 in wanted:
+            out[2] = (mr + ei, mi - er)
+    return out
+
+
+def transform_4(x, sign):
+    (ar, ai), (br, bi), (cr, ci), (dr, di) = x
+    pr, pi, qr, qi = ar + cr, ai + ci, ar - cr, ai - ci
+    sr, si, tr, ti = br + dr, bi + di, br - dr, bi - di
+    if sign < 0:
+        tr, ti = -tr, -ti
+    return [(pr + sr, pi + si), (qr - ti, qi + tr), (pr - sr, pi - si), (qr + ti, qi - tr)]
+
+
+def transform_8(x, sign):
+    even = transform_4(x[0::2], sign)
+    odd = transform_4(x[1::2], sign)
+    root = math.sqrt(0.5)
+    (r0, i0), (r1, i1), (r2, i2), (r3, i3) = odd
+    if sign > 0:
+        turned = [(r0, i0), (root * (r1 - i1), root * (i1 + r1)), (-i2, r2)]
+        turned.append((-root * (r3 + i3), root * (r3 - i3)))
+    else:
+        turned = [(r0, i0), (root * (r1 + i1), root * (i1 - r1)), (i2, -r2)]
+        turned.append((root * (i3 - r3), -root * (i3 + r3)))
+    low = [(e[0] + t[0], e[1] + t[1]) for e, t in zip(even, turned)]
+    high = [(e[0] - t[0], e[1] - t[1]) for e, t in zip(even, turned)]
+    return low + high
+
+
+def spectrum_of(load):
+    stage = {}
+    for n2 in range(8):
+        part = transform_3([load((8 * n1 + 3 * n2) % 24) for n1 in range(3)], -1)
+        for k1 in range(3):
+            stage[k1, n2] = part[k1]
+    result = {}
+    for k1 in range(3):
+        part = transform_8([stage[k1, n2] for n2 in range(8)], -1)
+        for k2 in range(8):
+            result[(16 * k1 + 9 * k2) % 24] = part[k2]
+    return result
+
+
+def first_half_of(spectrum):
+    stage = {}
+    for k1 in range(3):
+        part = transform_8([spectrum[(16 * k1 + 9 * k2) % 24] for k2 in range(8)], 1)
+        for n2 in range(8):
+            stage[k1, n2] = part[n2]
+    result = {}
+    for n2 in range(8):
+        wanted = {n1: (8 * n1 + 3 * n2) % 24 for n1 in range(3) if (8 * n1 + 3 * n2) % 24 < 12}
+        part = transform_3([stage[k1, n2] for k1 in range(3)], 1, tuple(wanted))
+        for n1, index in wanted.items():
+            result[index] = part[n1]
+    return result
+
+
+def tile_pair(ref, step, rows):
+    parts = []
+    for parity in range(2):
+        at = (2 * step + parity) * LANES
+        part = ref[:, :, :, at : at + LANES]
+        parts.append(part.reshape(rows, part.shape[2], LANES))
+    return jnp.concatenate(parts, axis=1)
+
+
+def edges_kernel(edge_ref, speed_ref, low_ref, high_ref, plane_ref, down_ref, up_ref, across_ref):
+    steps = speed_ref.shape[1] // 8
+    width = low_ref.shape[0]
+    below = [speed_ref[1, 8 * s : 8 * s + 8, :][None] < 0.0 for s in range(steps)]
+
+    def put(ref, at, value):
+        ref[at] = value.reshape(-1, LANES).astype(jnp.bfloat16)
+
+    first = [tile_pair(low_ref, s, width) for s in range(steps)]
+    put(down_ref, 0, first[0])
+    for m in range(1, steps // 2 + 1):
+        put(down_ref, m, jnp.where(below[2 * m - 1], first[2 * m - 1], first[2 * m]))
+    last = [tile_pair(high_ref, s, width) for s in range(steps)]
+    for m in range(steps // 2):
+        put(up_ref, m, jnp.where(below[2 * m], last[2 * m + 1], last[2 * m]))
+    put(up_ref, steps // 2, last[steps - 1])
+    for s in range(steps):
+        put(across_ref, s, tile_pair(plane_ref, s, plane_ref.shape[1]))
+
+
+def upwind_kernel(
+    side_ref, speed_ref, picker_ref, block_ref, down_ref, up_ref, across_ref, read_ref, *chosen_refs
+):
+    width_x, width_y, width_z, lanes = block_ref.shape
+    rows = width_x * width_y
+    steps = lanes // (2 * LANES)
+    ahead = side_ref[0] == 0
+    place = lax.broadcasted_iota(jnp.int32, (1, 8, LANES), 1) % width_z
+    cells = []
+    for u in range(steps):
+        step = pl.program_id(0) * steps + u
+        speed = [speed_ref[d, 8 * u : 8 * u + 8, :] for d in range(3)]
+        flat = tile_pair(block_ref, u, rows)
+        field = flat.reshape(width_x, width_y, 8, LANES)
+        falls = speed[1] < 0.0
+        above = down_ref[(step + 1) // 2].astype(jnp.float32).reshape(width_x, 1, 8, LANES)
+        under = up_ref[step // 2].astype(jnp.float32).reshape(width_x, 1, 8, LANES)
+        border = jnp.where(falls[None, None], above, under)
+        beside_y = jnp.where(
+            falls[None, None],
+            jnp.concatenate([field[:, 1:], border], axis=1),
+            jnp.concatenate([border, field[:, :-1]], axis=1),
+        )
+        outer = across_ref[step].astype(jnp.float32).reshape(1, width_y, 8, LANES)
+        beside_x = jnp.where(
+            ahead,
+            jnp.concatenate([field[1:], outer], axis=0),
+            jnp.concatenate([outer, field[:-1]], axis=0),
+        )
+        upper = jnp.where(place == width_z - 1, pltpu.roll(flat, 3, 1), pltpu.roll(flat, 7, 1))
+        lower = jnp.where(place == 0, pltpu.roll(flat, 5, 1), pltpu.roll(flat, 1, 1))
+        beside_z = jnp.where((speed[2] < 0.0)[None], upper, lower)
+        fluxes = jnp.abs(speed[0])[None, None] * (field - beside_x)
+        fluxes = fluxes + jnp.abs(speed[1])[None, None] * (field - beside_y)
+        fluxes = fluxes.reshape(rows, 8, LANES) + jnp.abs(speed[2])[None] * (flat - beside_z)
+        read = flat - fluxes
+        read_ref[:, 8 * u : 8 * u + 8, :] = read
+        cells.append(read.reshape(rows * 8, LANES).astype(jnp.bfloat16))
+    picked = jnp.dot(
+        picker_ref[...], jnp.concatenate(cells, axis=1), preferred_element_type=jnp.float32
+    ).astype(jnp.bfloat16)
+    slots = chosen_refs[0].shape[0]
+    for parity in range(2):
+        for which, ref in enumerate(chosen_refs):
+            first = (parity * len(chosen_refs) + which) * slots
+            for u in range(steps):
+                at = (2 * u + parity) * LANES
+                ref[:, at : at + LANES] = picked[first : first + slots, u * LANES : (u + 1) * LANES]
+
+
+def collide_kernel(parts, weight_ref, table_ref, *refs):
+    own_refs, other_refs = refs[:parts], refs[parts : 2 * parts]
+    terms_ref, section, back = refs[2 * parts :]
+    slots = own_refs[0].shape[0]
+    padded = weight_ref.shape[2]
+    height = table_ref.shape[0]
+    window = height - 64
+    pair_lanes = 2 * (height - 128)
+    pairs = own_refs[0].shape[1] // pair_lanes
+    half = 2 * pairs * parts
+    for parity in range(2):
+        rows = []
+        for ref in own_refs + other_refs:
+            for p in range(pairs):
+                at = p * pair_lanes + parity * (pair_lanes - window)
+                rows.append(ref[:, at : at + window])
+        start = 64 * (1 - parity)
+        out = jnp.dot(
+            jnp.concatenate(rows, axis=0),
+            table_ref[start : start + window, :],
+            preferred_element_type=jnp.float32,
+        )
+        for at in range(half):
+            section[2 * at + parity] = out[at * slots : (at + 1) * slots]
+
+    lane_tiles = padded // LANES
+
+    def transform(index, carry):
+        row = pl.multiple_of(index // lane_tiles * 16, 16)
+        lane = pl.multiple_of(index % lane_tiles * LANES, LANES)
+        results = []
+        for octet in range(2):
+            here = pl.ds(row + 8 * octet, 8)
+
+            def load(i):
+                real = section[i, here, pl.ds(lane, LANES)]
+                return real, section[i, here, pl.ds(padded + lane, LANES)]
+
+            spectrum = spectrum_of(load)
+            per_kernel = []
+            for which in range(3):
+                weighted = {}
+                for a, (real, imag) in spectrum.items():
+                    weight = weight_ref[which, pl.ds(a, 1), pl.ds(lane, LANES)]
+                    weighted[a] = (real * weight, imag * weight)
+                per_kernel.append(first_half_of(weighted))
+            results.append(per_kernel)
+        for which in range(3):
+            for i in range(half):
+                for q in range(2):
+                    value = jnp.concatenate([results[o][which][i][q] for o in range(2)], axis=0)
+                    back[i % 2, which, i // 2, pl.ds(row, 16), pl.ds(q * padded + lane, LANES)] = (
+                        value.astype(jnp.bfloat16)
+                    )
+        return carry
+
+    lax.fori_loop(0, slots // 16 * lane_tiles, transform, 0)
+
+    outs = []
+    for parity in range(2):
+        start = 64 * (1 - parity)
+        outs.append(
+            lax.dot_general(
+                back[parity].reshape(3 * (half // 2) * slots, 2 * padded),
+                table_ref[start : start + window, :],
+                (((1,), (1,)), ((), ())),
+                preferred_element_type=jnp.float32,
+            ).reshape(3, half // 2, slots, window)
+        )
+    tiles = pair_lanes // LANES
+    near = lax.broadcasted_iota(jnp.int32, (slots, LANES), 1) < 64
+    for at in range(half // 2):
+        own = own_refs[at // pairs]
+        for tile in range(tiles):
+            lane = tile * LANES
+            odd_lane = lane - (pair_lanes - window)
+            values = []
+            for which in range(3):
+                if tile < tiles // 2:
+                    value = outs[0][which, at, :, lane : lane + LANES]
+                elif tile > tiles // 2:
+                    value = outs[1][which, at, :, odd_lane : odd_lane + LANES]
+                else:
+                    value = jnp.where(
+                        near,
+                        outs[0][which, at, :, lane : lane + LANES],
+                        outs[1][which, at, :, odd_lane : odd_lane + LANES],
+                    )
+                values.append(value)
+            from_lane = at % pairs * pair_lanes + lane
+            cells = own[:, from_lane : from_lane + LANES].astype(jnp.float32)
+            term = values[0] * values[1] - cells * values[2]
+            to_lane = at * pair_lanes + lane
+            terms_ref[:, to_lane : to_lane + LANES] = term.astype(jnp.bfloat16)
+
+
+def evolve_kernel(parts, spread_ref, *refs):
+    read_refs, term_refs, out_ref = refs[:parts], refs[parts:-1], refs[-1]
+    width_x, width_y, width_z, lanes = out_ref.shape
+    steps = lanes // (2 * LANES)
+    rows = width_x * width_y
+    per_part = pl.num_programs(0) // parts
+    columns = []
+    for u in range(steps):
+        stacked = []
+        for parity in range(2):
+            at = (2 * u + parity) * LANES
+            stacked += [ref[:, at : at + LANES] for ref in term_refs]
+        columns.append(jnp.concatenate(stacked, axis=0))
+    added = jnp.dot(
+        spread_ref[...], jnp.concatenate(columns, axis=1), preferred_element_type=jnp.float32
+    )
+    for part in range(parts):
+
+        @pl.when(pl.program_id(0) // per_part == part)
+        def _():
+            for u in range(steps):
+                here = added[:, u * LANES : (u + 1) * LANES].reshape(rows, 8, LANES)
+                value = read_refs[part][:, 8 * u : 8 * u + 8, :] + here
+                for parity in range(2):
+                    at = (2 * u + parity) * LANES
+                    piece = value[:, parity * width_z : (parity + 1) * width_z, :]
+                    out_ref[:, :, :, at : at + LANES] = piece.reshape(
+                        width_x, width_y, width_z, LANES
+                    )
+
+
+def params(mib):
+    return pltpu.CompilerParams(vmem_limit_bytes=mib * 2**20)
+
+
+def fast_fits(distribution, points):
+    width_x, width_y, width_z, local_vel = distribution.shape
+    group = PLANES * points * points
+    return (
+        points == 24
+        and lax.axis_size("vel") == 2
+        and width_z == 4
+        and local_vel * 2 == points**3
+        and local_vel % group == 0
+        and width_x * width_y * width_z % 128 == 0
+    )
+
+
+def fast_device(distribution, refine_level, gain_one, gain_two, loss_kernel):
+    points = gain_one.shape[0]
+    width_x, width_y, width_z, local_vel = distribution.shape
+    block_rows = width_x * width_y
+    block_cells = block_rows * width_z
+    group = PLANES * points * points
+    parts = local_vel // group
+    group_rows = group // LANES * width_z
+    steps = group_rows // 8
+    capacity = block_cells // 2
+    batches = 2
+    slots = capacity // batches
+    vel_at = lax.axis_index("vel")
+    count_x, count_y = lax.axis_size("cx"), lax.axis_size("cy")
+
+    speeds = jnp.stack(courants(points, vel_at * local_vel, local_vel))
+    speeds = jnp.broadcast_to(
+        speeds.reshape(3, local_vel // LANES, 1, LANES), (3, local_vel // LANES, width_z, LANES)
+    ).reshape(3, local_vel // LANES * width_z, LANES)
+    side = vel_at.reshape(1).astype(jnp.int32)
+    edge = jnp.where(vel_at == 0, 0, width_x - 1).reshape(1).astype(jnp.int32)
+
+    level = refine_level.reshape(block_cells)
+    active = level > 0
+    cell_at = jnp.arange(block_cells, dtype=jnp.int32)
+    before = (cell_at[:, None] < cell_at[None, :]) & active[:, None]
+    slot_index = jnp.where(active, jnp.sum(before.astype(jnp.int32), axis=0), -1)
+    spot = slot_index.reshape(block_rows, 1, width_z)
+    parity = jnp.arange(2, dtype=jnp.int32)[None, :, None]
+    shape = (block_rows, 2, width_z)
+    wanted = jnp.where(spot >= 0, spot + capacity * parity, -1)
+    wanted = jnp.broadcast_to(wanted, shape).reshape(-1)
+    numbers = jnp.arange(2 * capacity, dtype=jnp.int32)
+    picker = (numbers[:, None] == wanted[None, :]).astype(jnp.bfloat16)
+    strength = jnp.broadcast_to(
+        (0.25 * level.astype(jnp.float32)).reshape(block_rows, 1, width_z), shape
+    ).reshape(-1)
+    spread = jnp.where(wanted[:, None] == numbers[None, :], strength[:, None], 0.0)
+    spread = spread.astype(jnp.bfloat16)
+
+    padded = -(-len(half_set(points)[1]) // LANES) * LANES
+    weights = frequency_weights((gain_one, gain_two, loss_kernel), padded)
+    table = jnp.asarray(plane_table(points, padded, 64))
+
+    towards_lower = [(j, (j - 1) % count_y) for j in range(count_y)]
+    towards_upper = [(j, (j + 1) % count_y) for j in range(count_y)]
+    across_pairs = [(i, (i - 1) % count_x) for i in range(count_x)]
+    across_pairs += [(count_x + i, count_x + (i + 1) % count_x) for i in range(count_x)]
+    swap = [(0, 1), (1, 0)]
+    bf16 = jnp.bfloat16
+
+    halos = []
+    for g in range(parts):
+        half_steps = steps // 2 + 1
+        down, up, across = pl.pallas_call(
+            edges_kernel,
+            grid_spec=pltpu.PrefetchScalarGridSpec(
+                num_scalar_prefetch=1,
+                grid=(1,),
+                in_specs=[
+                    pl.BlockSpec((3, group_rows, LANES), lambda i, e, g=g: (0, g, 0)),
+                    pl.BlockSpec((width_x, 1, width_z, group), lambda i, e, g=g: (0, 0, 0, g)),
+                    pl.BlockSpec(
+                        (width_x, 1, width_z, group), lambda i, e, g=g: (0, width_y - 1, 0, g)
+                    ),
+                    pl.BlockSpec((1, width_y, width_z, group), lambda i, e, g=g: (e[0], 0, 0, g)),
+                ],
+                out_specs=[
+                    pl.BlockSpec((half_steps, width_x * 8, LANES), lambda i, e: (0, 0, 0)),
+                    pl.BlockSpec((half_steps, width_x * 8, LANES), lambda i, e: (0, 0, 0)),
+                    pl.BlockSpec((steps, width_y * 8, LANES), lambda i, e: (0, 0, 0)),
+                ],
+            ),
+            out_shape=[
+                jax.ShapeDtypeStruct((half_steps, width_x * 8, LANES), bf16),
+                jax.ShapeDtypeStruct((half_steps, width_x * 8, LANES), bf16),
+                jax.ShapeDtypeStruct((steps, width_y * 8, LANES), bf16),
+            ],
+            compiler_params=params(56),
+            name="edges",
+        )(edge, speeds, distribution, distribution, distribution)
+        halos.append(
+            (
+                lax.ppermute(down, "cy", towards_lower),
+                lax.ppermute(up, "cy", towards_upper),
+                lax.ppermute(across, ("vel", "cx"), across_pairs),
+            )
+        )
+
+    reads, own, other = [], [], []
+    wide = 3
+    for g in range(parts):
+        whole = [pl.BlockSpec(h.shape, lambda i: (0, 0, 0)) for h in halos[g]]
+        at = steps // wide * g
+        read, *chosen = pl.pallas_call(
+            upwind_kernel,
+            grid=(steps // wide,),
+            in_specs=[
+                pl.BlockSpec(memory_space=pltpu.SMEM),
+                pl.BlockSpec((3, 8 * wide, LANES), lambda i, at=at: (0, at + i, 0)),
+                pl.BlockSpec(picker.shape, lambda i: (0, 0)),
+                pl.BlockSpec(
+                    (width_x, width_y, width_z, 2 * wide * LANES),
+                    lambda i, at=at: (0, 0, 0, at + i),
+                ),
+                *whole,
+            ],
+            out_specs=[pl.BlockSpec((block_rows, 8 * wide, LANES), lambda i: (0, i, 0))]
+            + [pl.BlockSpec((slots, 2 * wide * LANES), lambda i: (0, i))] * batches,
+            out_shape=[jax.ShapeDtypeStruct((block_rows, group_rows, LANES), jnp.float32)]
+            + [jax.ShapeDtypeStruct((slots, group), bf16)] * batches,
+            compiler_params=params(56),
+            name="upwind",
+        )(side, speeds, picker, distribution, *halos[g])
+        reads.append(read)
+        own.append(chosen)
+        other.append([lax.ppermute(c, "vel", swap) for c in chosen])
+
+    terms = []
+    half = points // 2
+    for batch in range(batches):
+        terms.append(
+            pl.pallas_call(
+                functools.partial(collide_kernel, parts),
+                out_shape=jax.ShapeDtypeStruct((slots, local_vel), bf16),
+                scratch_shapes=[
+                    pltpu.VMEM((points, slots, 2 * padded), jnp.float32),
+                    pltpu.VMEM((2, 3, half // 2, slots, 2 * padded), bf16),
+                ],
+                compiler_params=params(56),
+                name="collide",
+            )(
+                weights,
+                table,
+                *[own[g][batch] for g in range(parts)],
+                *[other[g][batch] for g in range(parts)],
+            )
+        )
+
+    per_part = steps // wide
+
+    def read_spec(g):
+        return pl.BlockSpec(
+            (block_rows, 8 * wide, LANES),
+            lambda i: (0, jnp.clip(i - g * per_part, 0, per_part - 1), 0),
+        )
+
+    return pl.pallas_call(
+        functools.partial(evolve_kernel, parts),
+        grid=(parts * per_part,),
+        in_specs=[pl.BlockSpec(spread.shape, lambda i: (0, 0))]
+        + [read_spec(g) for g in range(parts)]
+        + [pl.BlockSpec((slots, 2 * wide * LANES), lambda i: (0, i))] * batches,
+        out_specs=pl.BlockSpec(
+            (width_x, width_y, width_z, 2 * wide * LANES), lambda i: (0, 0, 0, i)
+        ),
+        out_shape=jax.ShapeDtypeStruct(distribution.shape, jnp.float32),
+        compiler_params=params(56),
+        name="evolve",
+    )(spread, *reads, *terms)
+
+
+def per_device(distribution, refine_level, gain_one, gain_two, loss_kernel):
+    if fast_fits(distribution, gain_one.shape[0]):
+        return fast_device(distribution, refine_level, gain_one, gain_two, loss_kernel)
+    return plain_device(distribution, refine_level, gain_one, gain_two, loss_kernel)
+
 
 def solution(mesh):
     placed = (P("cx", "cy", None, "vel"), P("cx", "cy", None), P(), P(), P())

time: 503 us -> 108 us (0.21); the launches traced: 495 us -> 108 us
  other arithmetic: 128 us -> 2.18 us
  local copies, waits for them, and re-layouts: 123 us -> 6.61 us
  matrix products: 110 us -> 1.74 us
  waiting for transfers between devices: 119 us -> 21 us
  Pallas kernels: 0 us -> 58.9 us
    dot_general x13 -> x1, matrix products: 110 us -> 1.74 us  [frequency_weights(): picked = jnp.dot(both, select, precision=lax.Precision.HIGHEST)]
    unnamed x2 -> x0, other arithmetic: 75.3 us -> none
    convert_element_type x5 -> x0, local copies, waits for them, and re-layouts: 63.2 us -> none  [the longest x1 55.8 us: per_device(): terms.astype(jnp.bfloat16)]
    ppermute x4 -> x15, waiting for transfers between devices: 81.7 us -> 21 us  [the longest x6 9.96 us: fast_device(): other.append([lax.ppermute(c, 'vel', swap) for c in chosen])]
    pallas_call x0 -> x9, Pallas kernels: none -> 58.9 us  [the longest x2 25.3 us: fast_device(): pl.pallas_call(functools.partial(collide_kernel, parts), out_shape=jax.Sh...]
    all_to_all x2 -> x0, waiting for transfers between devices: 37.3 us -> none  [the longest x1 19.6 us: per_device(): lax.all_to_all(terms.astype(jnp.bfloat16), 'vel', split_axis=2, concat_ax...]
    convert_element_type x3 -> x2, other arithmetic: 38.7 us -> 1.68 us  [the longest x1 0.92 us: fast_device(): spread = spread.astype(jnp.bfloat16)]
    slice x4 -> x2, local copies, waits for them, and re-layouts: 17.9 us -> 0.02 us  [the longest x1 0.02 us: frequency_weights(): stacked[:, 1:]]
  transfers between devices with their start and end apart: 6 -> 15, of which waited for: 4 -> 3; matrix products, arithmetic and copies ran while one was open for 6% -> 5% of each run, Pallas kernels for 0% -> 31%
where the time goes in v1:
time: 108 us
  Pallas kernels  58.9 us (55%)
  waiting for transfers between devices  21 us (19%)
  starting transfers between devices  17.1 us (16%)
  local copies, waits for them, and re-layouts  6.61 us (6%)
  other arithmetic  2.18 us (2%)
  matrix products  1.74 us (2%)
    pallas_call x2, Pallas kernels, fast_device(): pl.pallas_call(functools.partial(collide_kernel, parts), out_shape=jax.Sh...  25.3 us
    pallas_call x3, Pallas kernels, fast_device(): pl.pallas_call(upwind_kernel, grid=(steps // wide,), in_specs=[pl.BlockSp...  16.1 us
    pallas_call x1, Pallas kernels, fast_device(): pl.pallas_call(functools.partial(evolve_kernel, parts), grid=(parts * per...  10.8 us
    ppermute x6, waiting for transfers between devices, fast_device(): other.append([lax.ppermute(c, 'vel', swap) for c in chosen])  9.96 us
    ppermute x3, waiting for transfers between devices, fast_device(): lax.ppermute(up, 'cy', towards_upper)  8.12 us
    pallas_call x3, Pallas kernels, fast_device(): pl.pallas_call(edges_kernel, grid_spec=pltpu.PrefetchScalarGridSpec(num_s...  6.73 us
    ppermute x6, starting transfers between devices, fast_device(): other.append([lax.ppermute(c, 'vel', swap) for c in chosen])  6.27 us
    ppermute x3, starting transfers between devices, fast_device(): lax.ppermute(down, 'cy', towards_lower)  4.15 us
  transfers between devices with their start and end apart: 15, of which 3 were waited for; matrix products, arithmetic and copies ran while one was open for 5% of the time, Pallas kernels for 31%

profile of v1, /device:TPU:0, one launch (start us, length us, event | category | flops | bytes accessed | tf_op | source)
XLA Modules:
  0.0 107.8 jit_solution(8280432539663901966)
XLA Ops:
  0.1 0.8 broadcast_in_dim.57
  0.9 2.2 %edges.5 = (bf16[5,128,128]{2,1,0:T(8,128)(2,1)}, bf16[5,128,128]{2,1,0:T(8,128)(2,1)}, bf16[9,32,128]{2,1,0:T(8,128)(2,1)}) custom-call(s32[1]{0:T(128)} %bitcast.4.edge_ref, f32[3,216,128]{2,1,0:T(8,128)} %bitcast.12, f32[16,4,4,6912]{3,2,1,0:T(4,128)} %block_ref.5, f32[16,4,4,6912]{3,2,1,0:T(4,128)} %block_ref.5, f32[16,4,4,6912]{3,2,1,0:T(4,128)} %block_ref.5), custom_call_target="tpu_custom_call" | custom-call | tf_op jit(solution)/shard_map/edges/pallas_call | solution.py:516
  3.2 2.4 %collective-permute-start.8 = (bf16[9,32,128]{2,1,0:T(8,128)(2,1)}, bf16[9,32,128]{2,1,0:T(8,128)(2,1)S(1)}, u32[]{:S(2)}, u32[]{:S(2)}) collective-permute-start(bf16[9,32,128]{2,1,0:T(8,128)(2,1)} %get-tuple-element.33), channel_id=1, source_target_pairs={{0,12},{4,0},{8,4},{12,8},{16,20},{20,24},{24,28},{28,16},{1,13},{... | collective-permute-start | bytes 221192 | tf_op jit(solution)/shard_map/ppermute | solution.py:547
  5.6 3.7 %collective-permute-start.6 = (bf16[5,128,128]{2,1,0:T(8,128)(2,1)}, bf16[5,128,128]{2,1,0:T(8,128)(2,1)S(1)}, u32[]{:S(2)}, u32[]{:S(2)}) collective-permute-start(bf16[5,128,128]{2,1,0:T(8,128)(2,1)} %get-tuple-element.31), channel_id=1, source_target_pairs={{0,3},{1,0},{2,1},{3,2},{4,7},{5,4},{6,5},{7,6},{8,11},{9,8},{10,9... | collective-permute-start | bytes 491528 | tf_op jit(solution)/shard_map/ppermute | solution.py:545
  9.2 2.2 %edges.3 = (bf16[5,128,128]{2,1,0:T(8,128)(2,1)}, bf16[5,128,128]{2,1,0:T(8,128)(2,1)}, bf16[9,32,128]{2,1,0:T(8,128)(2,1)}) custom-call(s32[1]{0:T(128)} %bitcast.4.edge_ref, f32[3,216,128]{2,1,0:T(8,128)} %bitcast.13, f32[16,4,4,6912]{3,2,1,0:T(4,128)} %block_ref.5, f32[16,4,4,6912]{3,2,1,0:T(4,128)} %block_ref.5, f32[16,4,4,6912]{3,2,1,0:T(4,128)} %block_ref.5), custom_call_target="tpu_custom_call" | custom-call | tf_op jit(solution)/shard_map/edges/pallas_call | solution.py:516
  11.9 0.5 collective-permute-start
  12.4 1.5 %collective-permute-start.1 = (bf16[5,128,128]{2,1,0:T(8,128)(2,1)}, bf16[5,128,128]{2,1,0:T(8,128)(2,1)S(1)}, u32[]{:S(2)}, u32[]{:S(2)}) collective-permute-start(bf16[5,128,128]{2,1,0:T(8,128)(2,1)} %get-tuple-element.24), channel_id=1, source_target_pairs={{0,1},{1,2},{2,3},{3,0},{4,5},{5,6},{6,7},{7,4},{8,9},{9,10},{10,1... | collective-permute-start | bytes 491528 | tf_op jit(solution)/shard_map/ppermute | solution.py:546
  15.5 0.8 fusion.picker_ref
  16.4 2.2 %edges.4 = (bf16[5,128,128]{2,1,0:T(8,128)(2,1)}, bf16[5,128,128]{2,1,0:T(8,128)(2,1)}, bf16[9,32,128]{2,1,0:T(8,128)(2,1)}) custom-call(s32[1]{0:T(128)} %bitcast.4.edge_ref, f32[3,216,128]{2,1,0:T(8,128)} %bitcast.14, f32[16,4,4,6912]{3,2,1,0:T(4,128)} %block_ref.5, f32[16,4,4,6912]{3,2,1,0:T(4,128)} %block_ref.5, f32[16,4,4,6912]{3,2,1,0:T(4,128)} %block_ref.5), custom_call_target="tpu_custom_call" | custom-call | tf_op jit(solution)/shard_map/edges/pallas_call | solution.py:516
  18.9 2.9 %collective-permute-done.down_ref = bf16[5,128,128]{2,1,0:T(8,128)(2,1)S(1)} collective-permute-done((bf16[5,128,128]{2,1,0:T(8,128)(2,1)}, bf16[5,128,128]{2,1,0:T(8,128)(2,1)S(1)}, u32[]{:S(2)}, u32[]{:S(2)}) %collective-permute-start) | collective-permute-done | bytes 163872 | tf_op jit(solution)/shard_map/ppermute | solution.py:545
  21.9 0.6 copy-done.11
  22.6 5.4 %upwind.3 = (f32[64,72,128]{2,1,0:T(8,128)}, bf16[64,2304]{1,0:T(8,128)(2,1)}, bf16[64,2304]{1,0:T(8,128)(2,1)}) custom-call(s32[1]{0:T(128)} %bitcast.1.side_ref, f32[3,216,128]{2,1,0:T(8,128)} %bitcast.15, bf16[256,512]{1,0:T(8,128)(2,1)} %fusion.picker_ref, f32[16,4,4,6912]{3,2,1,0:T(4,128)} %block_ref.5, bf16[5,128,128]{2,1,0:T(8,128)(2,1)} %copy-done.11, ...), custom_call_target="tpu_custom_call" | custom-call | tf_op jit(solution)/shard_map/upwind/pallas_call | solution.py:556
  28.0 1.7 %collective-permute-start.9 = (bf16[64,2304]{1,0:T(8,128)(2,1)}, bf16[64,2304]{1,0:T(8,128)(2,1)S(1)}, u32[]{:S(2)}, u32[]{:S(2)}) collective-permute-start(bf16[64,2304]{1,0:T(8,128)(2,1)} %get-tuple-element.35.refs_0_), channel_id=1, source_target_pairs={{0,16},{16,0},{1,17},{17,1},{2,18},{18,2},{3,19},{19,3},{4,20},{20... | collective-permute-start | bytes 884744 | tf_op jit(solution)/shard_map/ppermute | solution.py:578
  29.8 2.0 %collective-permute-start.7 = (bf16[5,128,128]{2,1,0:T(8,128)(2,1)S(1)}, bf16[5,128,128]{2,1,0:T(8,128)(2,1)S(1)}, u32[]{:S(2)}, u32[]{:S(2)}) collective-permute-start(bf16[5,128,128]{2,1,0:T(8,128)(2,1)S(1)} %copy-done.21), channel_id=1, source_target_pairs={{0,1},{1,2},{2,3},{3,0},{4,5},{5,6},{6,7},{7,4},{8,9},{9,10},{10,1... | collective-permute-start | bytes 491528 | tf_op jit(solution)/shard_map/ppermute | solution.py:546
  32.4 8.1 %collective-permute-done.4.up_ref = bf16[5,128,128]{2,1,0:T(8,128)(2,1)S(1)} collective-permute-done((bf16[5,128,128]{2,1,0:T(8,128)(2,1)S(1)}, bf16[5,128,128]{2,1,0:T(8,128)(2,1)S(1)}, u32[]{:S(2)}, u32[]{:S(2)}) %collective-permute-start.4) | collective-permute-done | bytes 163872 | tf_op jit(solution)/shard_map/ppermute | solution.py:546
  40.5 0.4 collective-permute-start.12
  41.2 5.3 %upwind.4 = (f32[64,72,128]{2,1,0:T(8,128)}, bf16[64,2304]{1,0:T(8,128)(2,1)}, bf16[64,2304]{1,0:T(8,128)(2,1)}) custom-call(s32[1]{0:T(128)} %bitcast.1.side_ref, f32[3,216,128]{2,1,0:T(8,128)} %bitcast.16, bf16[256,512]{1,0:T(8,128)(2,1)} %fusion.picker_ref, f32[16,4,4,6912]{3,2,1,0:T(4,128)} %block_ref.5, bf16[5,128,128]{2,1,0:T(8,128)(2,1)} %copy-done.14, ...), custom_call_target="tpu_custom_call" | custom-call | tf_op jit(solution)/shard_map/upwind/pallas_call | solution.py:556
  46.5 1.5 %collective-permute-start.10 = (bf16[64,2304]{1,0:T(8,128)(2,1)}, bf16[64,2304]{1,0:T(8,128)(2,1)S(1)}, u32[]{:S(2)}, u32[]{:S(2)}) collective-permute-start(bf16[64,2304]{1,0:T(8,128)(2,1)} %get-tuple-element.36.refs_1_), channel_id=1, source_target_pairs={{0,16},{16,0},{1,17},{17,1},{2,18},{18,2},{3,19},{19,3},{4,20},{20... | collective-permute-start | bytes 884744 | tf_op jit(solution)/shard_map/ppermute | solution.py:578
  48.0 0.7 collective-permute-start.13
  48.7 0.7 copy-done.13
  49.4 5.3 %upwind.5 = (f32[64,72,128]{2,1,0:T(8,128)}, bf16[64,2304]{1,0:T(8,128)(2,1)}, bf16[64,2304]{1,0:T(8,128)(2,1)}) custom-call(s32[1]{0:T(128)} %bitcast.1.side_ref, f32[3,216,128]{2,1,0:T(8,128)} %bitcast.17, bf16[256,512]{1,0:T(8,128)(2,1)} %fusion.picker_ref, f32[16,4,4,6912]{3,2,1,0:T(4,128)} %block_ref.5, bf16[5,128,128]{2,1,0:T(8,128)(2,1)} %copy-done.10, ...), custom_call_target="tpu_custom_call" | custom-call | tf_op jit(solution)/shard_map/upwind/pallas_call | solution.py:556
  54.8 1.4 %collective-permute-start.11 = (bf16[64,2304]{1,0:T(8,128)(2,1)}, bf16[64,2304]{1,0:T(8,128)(2,1)S(1)}, u32[]{:S(2)}, u32[]{:S(2)}) collective-permute-start(bf16[64,2304]{1,0:T(8,128)(2,1)} %get-tuple-element.37.refs_2_), channel_id=1, source_target_pairs={{0,16},{16,0},{1,17},{17,1},{2,18},{18,2},{3,19},{19,3},{4,20},{20... | collective-permute-start | bytes 884744 | tf_op jit(solution)/shard_map/ppermute | solution.py:578
  56.2 0.6 collective-permute-start.14
  56.8 0.9 select_convert_fusion.spread_ref
  57.7 1.7 %convolution_multiply_fusion = f32[72,384]{1,0:T(8,128)} fusion(f32[72,1152]{1,0:T(8,128)S(1)} %bitcast.18, f32[1152,384]{1,0:T(8,128)S(1)} %copy-done, f32[384]{0:T(512)S(1)} %copy-done.20), kind=kOutput, calls=%fused_computation | convolution fusion | flops 382233600 | bytes 2213376 | tf_op jit(solution)/shard_map/dot_general | solution.py:164
  59.5 10.0 %collective-permute-done.11.refs_5_ = bf16[64,2304]{1,0:T(8,128)(2,1)S(1)} collective-permute-done((bf16[64,2304]{1,0:T(8,128)(2,1)}, bf16[64,2304]{1,0:T(8,128)(2,1)S(1)}, u32[]{:S(2)}, u32[]{:S(2)}) %collective-permute-start.11) | collective-permute-done | bytes 294944 | tf_op jit(solution)/shard_map/ppermute | solution.py:578
  69.4 0.7 copy-done.6
  70.1 12.6 %collide.2.refs_3_ = bf16[64,6912]{1,0:T(8,128)(2,1)} custom-call(f32[3,24,384]{2,1,0:T(8,128)} %bitcast.19, bf16[704,768]{1,0:T(8,128)(2,1)} %constant.81.clone.table_ref, bf16[64,2304]{1,0:T(8,128)(2,1)} %get-tuple-element.35.refs_0_, bf16[64,2304]{1,0:T(8,128)(2,1)} %get-tuple-element.36.refs_1_, bf16[64,2304]{1,0:T(8,128)(2,1)} %get-tuple-element.37.refs_2_, ...), custom_call_target="tpu_custom_call" | custom-call | tf_op jit(solution)/shard_map/collide/pallas_call | solution.py:584
  82.8 0.7 copy-done.2
  83.6 0.7 copy-done.5
  84.4 12.7 %collide.3.refs_4_ = bf16[64,6912]{1,0:T(8,128)(2,1)} custom-call(f32[3,24,384]{2,1,0:T(8,128)} %bitcast.20, bf16[704,768]{1,0:T(8,128)(2,1)} %constant.81.clone.table_ref, bf16[64,2304]{1,0:T(8,128)(2,1)} %get-tuple-element.38.refs_0_, bf16[64,2304]{1,0:T(8,128)(2,1)} %get-tuple-element.39.refs_1_, bf16[64,2304]{1,0:T(8,128)(2,1)} %get-tuple-element.40.refs_2_, ...), custom_call_target="tpu_custom_call" | custom-call | tf_op jit(solution)/shard_map/collide/pallas_call | solution.py:584
  97.0 10.8 %evolve.1 = f32[16,4,4,6912]{3,2,1,0:T(4,128)} custom-call(bf16[512,256]{1,0:T(8,128)(2,1)} %select_convert_fusion.spread_ref, f32[64,72,128]{2,1,0:T(8,128)} %get-tuple-element.26.refs_0_, f32[64,72,128]{2,1,0:T(8,128)} %get-tuple-element.30.refs_1_, f32[64,72,128]{2,1,0:T(8,128)} %get-tuple-element.34.refs_2_, bf16[64,6912]{1,0:T(8,128)(2,1)} %collide.2.refs_3_, ...), custom_call_target="tpu_custom_call" | custom-call | tf_op jit(solution)/shard_map/evolve/pallas_call | solution.py:609
  (88 shorter events, 3.6 us)
Async XLA Ops:
  3.2 43.4 %collective-permute-start.8 = (bf16[9,32,128]{2,1,0:T(8,128)(2,1)}, bf16[9,32,128]{2,1,0:T(8,128)(2,1)S(1)}, u32[]{:S(2)}, u32[]{:S(2)}) collective-permute-start(bf16[9,32,128]{2,1,0:T(8,128)(2,1)} %get-tuple-element.33), channel_id=1, source_target_pairs={{0,12},{4,0},{8,4},{12,8},{16,20},{20,24},{24,28},{28,16},{1,13},{... | collective-permute-start | bytes 221192 | tf_op jit(solution)/shard_map/ppermute | solution.py:547
  5.6 8.3 %copy-start.19 = (s32[16,4,4]{0,2,1:T(4,128)S(1)}, s32[16,4,4]{0,2,1:T(4,128)}, u32[]{:S(2)}) copy-start(s32[16,4,4]{0,2,1:T(4,128)} %param.9) | copy-start | bytes 3076
  5.6 9.6 %copy-start.7 = (f32[24,24,24]{2,1,0:T(8,128)S(1)}, f32[24,24,24]{2,1,0:T(8,128)}, u32[]{:S(2)}) copy-start(f32[24,24,24]{2,1,0:T(8,128)} %param.10) | copy-start | bytes 165892
  5.6 9.7 %copy-start.8 = (f32[24,24,24]{2,1,0:T(8,128)S(1)}, f32[24,24,24]{2,1,0:T(8,128)}, u32[]{:S(2)}) copy-start(f32[24,24,24]{2,1,0:T(8,128)} %param.11) | copy-start | bytes 165892
  5.6 10.7 %copy-start.9 = (f32[24,24,24]{2,1,0:T(8,128)S(1)}, f32[24,24,24]{2,1,0:T(8,128)}, u32[]{:S(2)}) copy-start(f32[24,24,24]{2,1,0:T(8,128)} %param.12) | copy-start | bytes 165892
  5.6 42.4 %collective-permute-start.6 = (bf16[5,128,128]{2,1,0:T(8,128)(2,1)}, bf16[5,128,128]{2,1,0:T(8,128)(2,1)S(1)}, u32[]{:S(2)}, u32[]{:S(2)}) collective-permute-start(bf16[5,128,128]{2,1,0:T(8,128)(2,1)} %get-tuple-element.31), channel_id=1, source_target_pairs={{0,3},{1,0},{2,1},{3,2},{4,7},{5,4},{6,5},{7,6},{8,11},{9,8},{10,9... | collective-permute-start | bytes 491528 | tf_op jit(solution)/shard_map/ppermute | solution.py:545
  11.5 7.4 %collective-permute-start.2 = (bf16[9,32,128]{2,1,0:T(8,128)(2,1)}, bf16[9,32,128]{2,1,0:T(8,128)(2,1)S(1)}, u32[]{:S(2)}, u32[]{:S(2)}) collective-permute-start(bf16[9,32,128]{2,1,0:T(8,128)(2,1)} %get-tuple-element.25), channel_id=1, source_target_pairs={{0,12},{4,0},{8,4},{12,8},{16,20},{20,24},{24,28},{28,16},{1,13},{... | collective-permute-start | bytes 221192 | tf_op jit(solution)/shard_map/ppermute | solution.py:547
  11.9 9.9 %collective-permute-start = (bf16[5,128,128]{2,1,0:T(8,128)(2,1)}, bf16[5,128,128]{2,1,0:T(8,128)(2,1)S(1)}, u32[]{:S(2)}, u32[]{:S(2)}) collective-permute-start(bf16[5,128,128]{2,1,0:T(8,128)(2,1)} %get-tuple-element.23), channel_id=1, source_target_pairs={{0,3},{1,0},{2,1},{3,2},{4,7},{5,4},{6,5},{7,6},{8,11},{9,8},{10,9... | collective-permute-start | bytes 491528 | tf_op jit(solution)/shard_map/ppermute | solution.py:545
  12.4 9.5 %collective-permute-start.1 = (bf16[5,128,128]{2,1,0:T(8,128)(2,1)}, bf16[5,128,128]{2,1,0:T(8,128)(2,1)S(1)}, u32[]{:S(2)}, u32[]{:S(2)}) collective-permute-start(bf16[5,128,128]{2,1,0:T(8,128)(2,1)} %get-tuple-element.24), channel_id=1, source_target_pairs={{0,1},{1,2},{2,3},{3,0},{4,5},{5,6},{6,7},{7,4},{8,9},{9,10},{10,1... | collective-permute-start | bytes 491528 | tf_op jit(solution)/shard_map/ppermute | solution.py:546
  18.9 3.0 %copy-start.17 = (bf16[9,32,128]{2,1,0:T(8,128)(2,1)}, bf16[9,32,128]{2,1,0:T(8,128)(2,1)S(1)}, u32[]{:S(2)}) copy-start(bf16[9,32,128]{2,1,0:T(8,128)(2,1)S(1)} %collective-permute-done.2.across_ref) | copy-start | bytes 221188
  18.9 10.9 %collective-permute-start.5 = (bf16[9,32,128]{2,1,0:T(8,128)(2,1)}, bf16[9,32,128]{2,1,0:T(8,128)(2,1)S(1)}, u32[]{:S(2)}, u32[]{:S(2)}) collective-permute-start(bf16[9,32,128]{2,1,0:T(8,128)(2,1)} %get-tuple-element.29), channel_id=1, source_target_pairs={{0,12},{4,0},{8,4},{12,8},{16,20},{20,24},{24,28},{28,16},{1,13},{... | collective-permute-start | bytes 221192 | tf_op jit(solution)/shard_map/ppermute | solution.py:547
  21.8 10.0 %collective-permute-start.3 = (bf16[5,128,128]{2,1,0:T(8,128)(2,1)}, bf16[5,128,128]{2,1,0:T(8,128)(2,1)S(1)}, u32[]{:S(2)}, u32[]{:S(2)}) collective-permute-start(bf16[5,128,128]{2,1,0:T(8,128)(2,1)} %get-tuple-element.27), channel_id=1, source_target_pairs={{0,3},{1,0},{2,1},{3,2},{4,7},{5,4},{6,5},{7,6},{8,11},{9,8},{10,9... | collective-permute-start | bytes 491528 | tf_op jit(solution)/shard_map/ppermute | solution.py:545
  21.8 0.7 copy-start.12
  22.6 7.3 %copy-start.21 = (bf16[5,128,128]{2,1,0:T(8,128)(2,1)S(1)}, bf16[5,128,128]{2,1,0:T(8,128)(2,1)}, u32[]{:S(2)}) copy-start(bf16[5,128,128]{2,1,0:T(8,128)(2,1)} %get-tuple-element.32) | copy-start | bytes 491524
  22.6 9.3 %copy-start.22 = (bf16[5,128,128]{2,1,0:T(8,128)(2,1)S(1)}, bf16[5,128,128]{2,1,0:T(8,128)(2,1)}, u32[]{:S(2)}) copy-start(bf16[5,128,128]{2,1,0:T(8,128)(2,1)} %get-tuple-element.28) | copy-start | bytes 491524
  28.0 28.2 %collective-permute-start.9 = (bf16[64,2304]{1,0:T(8,128)(2,1)}, bf16[64,2304]{1,0:T(8,128)(2,1)S(1)}, u32[]{:S(2)}, u32[]{:S(2)}) collective-permute-start(bf16[64,2304]{1,0:T(8,128)(2,1)} %get-tuple-element.35.refs_0_), channel_id=1, source_target_pairs={{0,16},{16,0},{1,17},{17,1},{2,18},{18,2},{3,19},{19,3},{4,20},{20... | collective-permute-start | bytes 884744 | tf_op jit(solution)/shard_map/ppermute | solution.py:578
  29.8 11.1 %copy-start.18 = (bf16[9,32,128]{2,1,0:T(8,128)(2,1)}, bf16[9,32,128]{2,1,0:T(8,128)(2,1)S(1)}, u32[]{:S(2)}) copy-start(bf16[9,32,128]{2,1,0:T(8,128)(2,1)S(1)} %collective-permute-done.5.across_ref) | copy-start | bytes 221188
  29.8 18.9 %collective-permute-start.7 = (bf16[5,128,128]{2,1,0:T(8,128)(2,1)S(1)}, bf16[5,128,128]{2,1,0:T(8,128)(2,1)S(1)}, u32[]{:S(2)}, u32[]{:S(2)}) collective-permute-start(bf16[5,128,128]{2,1,0:T(8,128)(2,1)S(1)} %copy-done.21), channel_id=1, source_target_pairs={{0,1},{1,2},{2,3},{3,0},{4,5},{5,6},{6,7},{7,4},{8,9},{9,10},{10,1... | collective-permute-start | bytes 491528 | tf_op jit(solution)/shard_map/ppermute | solution.py:546
  31.9 9.1 %copy-start.14 = (bf16[5,128,128]{2,1,0:T(8,128)(2,1)}, bf16[5,128,128]{2,1,0:T(8,128)(2,1)S(1)}, u32[]{:S(2)}) copy-start(bf16[5,128,128]{2,1,0:T(8,128)(2,1)S(1)} %collective-permute-done.3.down_ref) | copy-start | bytes 491524
  31.9 8.7 %collective-permute-start.4 = (bf16[5,128,128]{2,1,0:T(8,128)(2,1)S(1)}, bf16[5,128,128]{2,1,0:T(8,128)(2,1)S(1)}, u32[]{:S(2)}, u32[]{:S(2)}) collective-permute-start(bf16[5,128,128]{2,1,0:T(8,128)(2,1)S(1)} %copy-done.22), channel_id=1, source_target_pairs={{0,1},{1,2},{2,3},{3,0},{4,5},{5,6},{6,7},{7,4},{8,9},{9,10},{10,1... | collective-permute-start | bytes 491528 | tf_op jit(solution)/shard_map/ppermute | solution.py:546
  40.5 42.3 %collective-permute-start.12 = (bf16[64,2304]{1,0:T(8,128)(2,1)}, bf16[64,2304]{1,0:T(8,128)(2,1)S(1)}, u32[]{:S(2)}, u32[]{:S(2)}) collective-permute-start(bf16[64,2304]{1,0:T(8,128)(2,1)} %get-tuple-element.38.refs_0_), channel_id=1, source_target_pairs={{0,16},{16,0},{1,17},{17,1},{2,18},{18,2},{3,19},{19,3},{4,20},{20... | collective-permute-start | bytes 884744 | tf_op jit(solution)/shard_map/ppermute | solution.py:578
  46.5 2.2 %copy-start.16 = (bf16[9,32,128]{2,1,0:T(8,128)(2,1)}, bf16[9,32,128]{2,1,0:T(8,128)(2,1)S(1)}, u32[]{:S(2)}) copy-start(bf16[9,32,128]{2,1,0:T(8,128)(2,1)S(1)} %collective-permute-done.8.across_ref) | copy-start | bytes 221188
  46.5 12.9 %collective-permute-start.10 = (bf16[64,2304]{1,0:T(8,128)(2,1)}, bf16[64,2304]{1,0:T(8,128)(2,1)S(1)}, u32[]{:S(2)}, u32[]{:S(2)}) collective-permute-start(bf16[64,2304]{1,0:T(8,128)(2,1)} %get-tuple-element.36.refs_1_), channel_id=1, source_target_pairs={{0,16},{16,0},{1,17},{17,1},{2,18},{18,2},{3,19},{19,3},{4,20},{20... | collective-permute-start | bytes 884744 | tf_op jit(solution)/shard_map/ppermute | solution.py:578
  48.0 9.7 %copy-start = (f32[1152,384]{1,0:T(8,128)S(1)}, f32[1152,384]{1,0:T(8,128)}, u32[]{:S(2)}) copy-start(f32[1152,384]{1,0:T(8,128)} %constant.79.clone) | copy-start | bytes 5308420
  48.0 9.7 %copy-start.20 = (f32[384]{0:T(512)S(1)}, f32[384]{0:T(512)}, u32[]{:S(2)}) copy-start(f32[384]{0:T(512)} %constant.80.clone) | copy-start | bytes 4612
  48.0 34.8 %collective-permute-start.13 = (bf16[64,2304]{1,0:T(8,128)(2,1)}, bf16[64,2304]{1,0:T(8,128)(2,1)S(1)}, u32[]{:S(2)}, u32[]{:S(2)}) collective-permute-start(bf16[64,2304]{1,0:T(8,128)(2,1)} %get-tuple-element.39.refs_1_), channel_id=1, source_target_pairs={{0,16},{16,0},{1,17},{17,1},{2,18},{18,2},{3,19},{19,3},{4,20},{20... | collective-permute-start | bytes 884744 | tf_op jit(solution)/shard_map/ppermute | solution.py:578
  54.8 14.7 %collective-permute-start.11 = (bf16[64,2304]{1,0:T(8,128)(2,1)}, bf16[64,2304]{1,0:T(8,128)(2,1)S(1)}, u32[]{:S(2)}, u32[]{:S(2)}) collective-permute-start(bf16[64,2304]{1,0:T(8,128)(2,1)} %get-tuple-element.37.refs_2_), channel_id=1, source_target_pairs={{0,16},{16,0},{1,17},{17,1},{2,18},{18,2},{3,19},{19,3},{4,20},{20... | collective-permute-start | bytes 884744 | tf_op jit(solution)/shard_map/ppermute | solution.py:578
  56.2 13.3 %copy-start.1 = (bf16[64,2304]{1,0:T(8,128)(2,1)}, bf16[64,2304]{1,0:T(8,128)(2,1)S(1)}, u32[]{:S(2)}) copy-start(bf16[64,2304]{1,0:T(8,128)(2,1)S(1)} %collective-permute-done.9.refs_3_) | copy-start | bytes 884740
  56.2 26.7 %collective-permute-start.14 = (bf16[64,2304]{1,0:T(8,128)(2,1)}, bf16[64,2304]{1,0:T(8,128)(2,1)S(1)}, u32[]{:S(2)}, u32[]{:S(2)}) collective-permute-start(bf16[64,2304]{1,0:T(8,128)(2,1)} %get-tuple-element.40.refs_2_), channel_id=1, source_target_pairs={{0,16},{16,0},{1,17},{17,1},{2,18},{18,2},{3,19},{19,3},{4,20},{20... | collective-permute-start | bytes 884744 | tf_op jit(solution)/shard_map/ppermute | solution.py:578
  59.5 10.0 %copy-start.4 = (bf16[64,2304]{1,0:T(8,128)(2,1)}, bf16[64,2304]{1,0:T(8,128)(2,1)S(1)}, u32[]{:S(2)}) copy-start(bf16[64,2304]{1,0:T(8,128)(2,1)S(1)} %collective-permute-done.10.refs_4_) | copy-start | bytes 884740
  69.4 0.7 copy-start.6
  82.8 0.8 copy-start.3
  (6 other events, 4.2 us)

commit v2 on v1

--- a/solution.py
+++ b/solution.py
@@ -266,58 +266,82 @@
 
 
 def upwind_kernel(
-    side_ref, speed_ref, picker_ref, block_ref, down_ref, up_ref, across_ref, read_ref, *chosen_refs
+    side_ref,
+    speed_ref,
+    picker_ref,
+    block_ref,
+    down_ref,
+    up_ref,
+    across_ref,
+    read_ref,
+    *refs,
 ):
+    *chosen_refs, wide, border, cells = refs
     width_x, width_y, width_z, lanes = block_ref.shape
-    rows = width_x * width_y
     steps = lanes // (2 * LANES)
-    ahead = side_ref[0] == 0
+    beside = jnp.where(side_ref[0] == 0, 2, 0)
     place = lax.broadcasted_iota(jnp.int32, (1, 8, LANES), 1) % width_z
-    cells = []
     for u in range(steps):
         step = pl.program_id(0) * steps + u
-        speed = [speed_ref[d, 8 * u : 8 * u + 8, :] for d in range(3)]
-        flat = tile_pair(block_ref, u, rows)
-        field = flat.reshape(width_x, width_y, 8, LANES)
+        speed = [speed_ref[d, 8 * u : 8 * u + 8, :][None] for d in range(3)]
+        size = [jnp.abs(c) for c in speed]
         falls = speed[1] < 0.0
-        above = down_ref[(step + 1) // 2].astype(jnp.float32).reshape(width_x, 1, 8, LANES)
-        under = up_ref[step // 2].astype(jnp.float32).reshape(width_x, 1, 8, LANES)
-        border = jnp.where(falls[None, None], above, under)
-        beside_y = jnp.where(
-            falls[None, None],
-            jnp.concatenate([field[:, 1:], border], axis=1),
-            jnp.concatenate([border, field[:, :-1]], axis=1),
-        )
-        outer = across_ref[step].astype(jnp.float32).reshape(1, width_y, 8, LANES)
-        beside_x = jnp.where(
-            ahead,
-            jnp.concatenate([field[1:], outer], axis=0),
-            jnp.concatenate([outer, field[:-1]], axis=0),
-        )
-        upper = jnp.where(place == width_z - 1, pltpu.roll(flat, 3, 1), pltpu.roll(flat, 7, 1))
-        lower = jnp.where(place == 0, pltpu.roll(flat, 5, 1), pltpu.roll(flat, 1, 1))
-        beside_z = jnp.where((speed[2] < 0.0)[None], upper, lower)
-        fluxes = jnp.abs(speed[0])[None, None] * (field - beside_x)
-        fluxes = fluxes + jnp.abs(speed[1])[None, None] * (field - beside_y)
-        fluxes = fluxes.reshape(rows, 8, LANES) + jnp.abs(speed[2])[None] * (flat - beside_z)
-        read = flat - fluxes
-        read_ref[:, 8 * u : 8 * u + 8, :] = read
-        cells.append(read.reshape(rows * 8, LANES).astype(jnp.bfloat16))
+        sinks = speed[2] < 0.0
+        outer = across_ref[step].astype(jnp.float32).reshape(width_y, 8, LANES)
+        wide[0] = outer
+        wide[width_x + 1] = outer
+        above = down_ref[(step + 1) // 2].astype(jnp.float32).reshape(width_x, 8, LANES)
+        under = up_ref[step // 2].astype(jnp.float32).reshape(width_x, 8, LANES)
+        border[...] = jnp.where(falls, above, under)
+
+        def spread_out(x, carry):
+            at = 2 * u * LANES
+            parts = [block_ref[x, :, :, at + p * LANES : at + (p + 1) * LANES] for p in range(2)]
+            wide[x + 1] = jnp.concatenate(parts, axis=1)
+            return carry
+
+        lax.fori_loop(0, width_x, spread_out, 0, unroll=2)
+
+        def advance(x, carry):
+            field = wide[x + 1]
+            edge = border[pl.ds(x, 1)]
+            fluxes = size[0] * (field - wide[x + beside])
+            beside_y = jnp.where(
+                falls,
+                jnp.concatenate([field[1:], edge], axis=0),
+                jnp.concatenate([edge, field[:-1]], axis=0),
+            )
+            fluxes = fluxes + size[1] * (field - beside_y)
+            upper = jnp.where(
+                place == width_z - 1, pltpu.roll(field, 3, 1), pltpu.roll(field, 7, 1)
+            )
+            lower = jnp.where(place == 0, pltpu.roll(field, 5, 1), pltpu.roll(field, 1, 1))
+            fluxes = fluxes + size[2] * (field - jnp.where(sinks, upper, lower))
+            read = field - fluxes
+            read_ref[pl.ds(x * width_y, width_y), 8 * u : 8 * u + 8, :] = read
+            rows = width_y * 8
+            at = pl.multiple_of(x * rows, rows)
+            cells[pl.ds(at, rows), u * LANES : (u + 1) * LANES] = read.reshape(
+                rows, LANES
+            ).astype(jnp.bfloat16)
+            return carry
+
+        lax.fori_loop(0, width_x, advance, 0, unroll=2)
     picked = jnp.dot(
-        picker_ref[...], jnp.concatenate(cells, axis=1), preferred_element_type=jnp.float32
+        picker_ref[...], cells[...], preferred_element_type=jnp.float32
     ).astype(jnp.bfloat16)
-    slots = chosen_refs[0].shape[0]
+    capacity = picked.shape[0] // 2
     for parity in range(2):
-        for which, ref in enumerate(chosen_refs):
-            first = (parity * len(chosen_refs) + which) * slots
+        first = parity * capacity
+        for ref in chosen_refs:
+            slots = ref.shape[0]
             for u in range(steps):
                 at = (2 * u + parity) * LANES
                 ref[:, at : at + LANES] = picked[first : first + slots, u * LANES : (u + 1) * LANES]
-
-
-def collide_kernel(parts, weight_ref, table_ref, *refs):
-    own_refs, other_refs = refs[:parts], refs[parts : 2 * parts]
-    terms_ref, section, back = refs[2 * parts :]
+            first += slots
+
+
+def filter_parts(parts, weight_ref, table_ref, own_refs, other_refs, section, back):
     slots = own_refs[0].shape[0]
     padded = weight_ref.shape[2]
     height = table_ref.shape[0]
@@ -373,21 +397,29 @@
 
     lax.fori_loop(0, slots // 16 * lane_tiles, transform, 0)
 
+
+def terms_of(part, table_ref, own_ref, back, put):
+    slots, lanes = own_ref.shape
+    height = table_ref.shape[0]
+    window = height - 64
+    pair_lanes = 2 * (height - 128)
+    pairs = lanes // pair_lanes
     outs = []
     for parity in range(2):
         start = 64 * (1 - parity)
         outs.append(
             lax.dot_general(
-                back[parity].reshape(3 * (half // 2) * slots, 2 * padded),
+                back[parity, :, part * pairs : (part + 1) * pairs].reshape(
+                    3 * pairs * slots, back.shape[-1]
+                ),
                 table_ref[start : start + window, :],
                 (((1,), (1,)), ((), ())),
                 preferred_element_type=jnp.float32,
-            ).reshape(3, half // 2, slots, window)
+            ).reshape(3, pairs, slots, window)
         )
     tiles = pair_lanes // LANES
     near = lax.broadcasted_iota(jnp.int32, (slots, LANES), 1) < 64
-    for at in range(half // 2):
-        own = own_refs[at // pairs]
+    for at in range(pairs):
         for tile in range(tiles):
             lane = tile * LANES
             odd_lane = lane - (pair_lanes - window)
@@ -404,42 +436,81 @@
                         outs[1][which, at, :, odd_lane : odd_lane + LANES],
                     )
                 values.append(value)
-            from_lane = at % pairs * pair_lanes + lane
-            cells = own[:, from_lane : from_lane + LANES].astype(jnp.float32)
-            term = values[0] * values[1] - cells * values[2]
-            to_lane = at * pair_lanes + lane
-            terms_ref[:, to_lane : to_lane + LANES] = term.astype(jnp.bfloat16)
-
-
-def evolve_kernel(parts, spread_ref, *refs):
-    read_refs, term_refs, out_ref = refs[:parts], refs[parts:-1], refs[-1]
-    width_x, width_y, width_z, lanes = out_ref.shape
-    steps = lanes // (2 * LANES)
-    rows = width_x * width_y
-    per_part = pl.num_programs(0) // parts
-    columns = []
-    for u in range(steps):
-        stacked = []
-        for parity in range(2):
-            at = (2 * u + parity) * LANES
-            stacked += [ref[:, at : at + LANES] for ref in term_refs]
-        columns.append(jnp.concatenate(stacked, axis=0))
-    added = jnp.dot(
-        spread_ref[...], jnp.concatenate(columns, axis=1), preferred_element_type=jnp.float32
-    )
+            lane = at * pair_lanes + lane
+            cells = own_ref[:, lane : lane + LANES].astype(jnp.float32)
+            put(at * tiles + tile, (values[0] * values[1] - cells * values[2]).astype(jnp.bfloat16))
+
+
+def collide_kernel(parts, weight_ref, table_ref, *refs):
+    own_refs, other_refs = refs[:parts], refs[parts : 2 * parts]
+    terms_ref, section, back = refs[2 * parts :]
+    filter_parts(parts, weight_ref, table_ref, own_refs, other_refs, section, back)
     for part in range(parts):
-
-        @pl.when(pl.program_id(0) // per_part == part)
-        def _():
-            for u in range(steps):
-                here = added[:, u * LANES : (u + 1) * LANES].reshape(rows, 8, LANES)
-                value = read_refs[part][:, 8 * u : 8 * u + 8, :] + here
-                for parity in range(2):
-                    at = (2 * u + parity) * LANES
-                    piece = value[:, parity * width_z : (parity + 1) * width_z, :]
-                    out_ref[:, :, :, at : at + LANES] = piece.reshape(
-                        width_x, width_y, width_z, LANES
+        first = part * own_refs[0].shape[1]
+
+        def put(tile, value):
+            terms_ref[:, first + tile * LANES : first + (tile + 1) * LANES] = value
+
+        terms_of(part, table_ref, own_refs[part], back, put)
+
+
+def finish_kernel(parts, weight_ref, table_ref, spread_ref, early_ref, *refs):
+    own_refs, other_refs = refs[:parts], refs[parts : 2 * parts]
+    read_refs = refs[2 * parts : 3 * parts]
+    out_ref, section, back, reads, spots, added, staged, read_sems, out_sems = refs[3 * parts :]
+    width_x, width_y, width_z, lanes = staged.shape[1:]
+    tiles = lanes // LANES
+    loads = [
+        pltpu.make_async_copy(read_refs[part], reads.at[part], read_sems.at[part])
+        for part in range(parts)
+    ]
+    for load in loads:
+        load.start()
+    filter_parts(parts, weight_ref, table_ref, own_refs, other_refs, section, back)
+    early = early_ref.shape[0]
+    capacity = early + own_refs[0].shape[0]
+    stores = []
+    for part in range(parts):
+
+        def put(tile, value):
+            first = tile % 2 * capacity
+            columns = slice(tile // 2 * LANES, (tile // 2 + 1) * LANES)
+            lane = part * lanes + tile * LANES
+            spots[first : first + early, columns] = early_ref[:, lane : lane + LANES]
+            spots[first + early : first + capacity, columns] = value
+
+        terms_of(part, table_ref, own_refs[part], back, put)
+        added[...] = jnp.dot(spread_ref[...], spots[...], preferred_element_type=jnp.float32)
+        loads[part].wait()
+        slot = part % 2
+        if part >= 2:
+            stores[part - 2].wait()
+
+        def add(x, carry):
+            for y in range(width_y):
+                row = x * width_y + y
+                at = pl.multiple_of(row * 8, 8)
+                for u in range(tiles // 2):
+                    value = (
+                        reads[part, row, 8 * u : 8 * u + 8, :]
+                        + added[pl.ds(at, 8), u * LANES : (u + 1) * LANES]
                     )
+                    for parity in range(2):
+                        lane = (2 * u + parity) * LANES
+                        piece = value[parity * width_z : (parity + 1) * width_z]
+                        staged[slot, x, y, :, lane : lane + LANES] = piece
+            return carry
+
+        lax.fori_loop(0, width_x, add, 0)
+        store = pltpu.make_async_copy(
+            staged.at[slot],
+            out_ref.at[:, :, :, part * lanes : (part + 1) * lanes],
+            out_sems.at[part],
+        )
+        store.start()
+        stores.append(store)
+    for store in stores[-2:]:
+        store.wait()
 
 
 def params(mib):
@@ -469,8 +540,8 @@
     group_rows = group // LANES * width_z
     steps = group_rows // 8
     capacity = block_cells // 2
-    batches = 2
-    slots = capacity // batches
+    late = capacity * 3 // 8 // 16 * 16
+    counts = (capacity - late, late)
     vel_at = lax.axis_index("vel")
     count_x, count_y = lax.axis_size("cx"), lax.axis_size("cy")
 
@@ -510,115 +581,121 @@
     swap = [(0, 1), (1, 0)]
     bf16 = jnp.bfloat16
 
-    halos = []
+    half_steps = steps // 2 + 1
+    edges = []
     for g in range(parts):
-        half_steps = steps // 2 + 1
-        down, up, across = pl.pallas_call(
-            edges_kernel,
-            grid_spec=pltpu.PrefetchScalarGridSpec(
-                num_scalar_prefetch=1,
-                grid=(1,),
-                in_specs=[
-                    pl.BlockSpec((3, group_rows, LANES), lambda i, e, g=g: (0, g, 0)),
-                    pl.BlockSpec((width_x, 1, width_z, group), lambda i, e, g=g: (0, 0, 0, g)),
-                    pl.BlockSpec(
-                        (width_x, 1, width_z, group), lambda i, e, g=g: (0, width_y - 1, 0, g)
-                    ),
-                    pl.BlockSpec((1, width_y, width_z, group), lambda i, e, g=g: (e[0], 0, 0, g)),
+        edges.append(
+            pl.pallas_call(
+                edges_kernel,
+                grid_spec=pltpu.PrefetchScalarGridSpec(
+                    num_scalar_prefetch=1,
+                    grid=(1,),
+                    in_specs=[
+                        pl.BlockSpec((3, group_rows, LANES), lambda i, e, g=g: (0, g, 0)),
+                        pl.BlockSpec((width_x, 1, width_z, group), lambda i, e, g=g: (0, 0, 0, g)),
+                        pl.BlockSpec(
+                            (width_x, 1, width_z, group), lambda i, e, g=g: (0, width_y - 1, 0, g)
+                        ),
+                        pl.BlockSpec(
+                            (1, width_y, width_z, group), lambda i, e, g=g: (e[0], 0, 0, g)
+                        ),
+                    ],
+                    out_specs=[
+                        pl.BlockSpec((half_steps, width_x * 8, LANES), lambda i, e: (0, 0, 0)),
+                        pl.BlockSpec((half_steps, width_x * 8, LANES), lambda i, e: (0, 0, 0)),
+                        pl.BlockSpec((steps, width_y * 8, LANES), lambda i, e: (0, 0, 0)),
+                    ],
+                ),
+                out_shape=[
+                    jax.ShapeDtypeStruct((half_steps, width_x * 8, LANES), bf16),
+                    jax.ShapeDtypeStruct((half_steps, width_x * 8, LANES), bf16),
+                    jax.ShapeDtypeStruct((steps, width_y * 8, LANES), bf16),
                 ],
-                out_specs=[
-                    pl.BlockSpec((half_steps, width_x * 8, LANES), lambda i, e: (0, 0, 0)),
-                    pl.BlockSpec((half_steps, width_x * 8, LANES), lambda i, e: (0, 0, 0)),
-                    pl.BlockSpec((steps, width_y * 8, LANES), lambda i, e: (0, 0, 0)),
-                ],
-            ),
-            out_shape=[
-                jax.ShapeDtypeStruct((half_steps, width_x * 8, LANES), bf16),
-                jax.ShapeDtypeStruct((half_steps, width_x * 8, LANES), bf16),
-                jax.ShapeDtypeStruct((steps, width_y * 8, LANES), bf16),
-            ],
-            compiler_params=params(56),
-            name="edges",
-        )(edge, speeds, distribution, distribution, distribution)
-        halos.append(
-            (
-                lax.ppermute(down, "cy", towards_lower),
-                lax.ppermute(up, "cy", towards_upper),
-                lax.ppermute(across, ("vel", "cx"), across_pairs),
-            )
+                compiler_params=params(60 if g == 0 else 16),
+                name="edges",
+            )(edge, speeds, distribution, distribution, distribution)
         )
 
-    reads, own, other = [], [], []
     wide = 3
-    for g in range(parts):
-        whole = [pl.BlockSpec(h.shape, lambda i: (0, 0, 0)) for h in halos[g]]
+
+    def upwind(g, halo):
         at = steps // wide * g
-        read, *chosen = pl.pallas_call(
+        return pl.pallas_call(
             upwind_kernel,
             grid=(steps // wide,),
             in_specs=[
                 pl.BlockSpec(memory_space=pltpu.SMEM),
-                pl.BlockSpec((3, 8 * wide, LANES), lambda i, at=at: (0, at + i, 0)),
+                pl.BlockSpec((3, 8 * wide, LANES), lambda i: (0, at + i, 0)),
                 pl.BlockSpec(picker.shape, lambda i: (0, 0)),
                 pl.BlockSpec(
-                    (width_x, width_y, width_z, 2 * wide * LANES),
-                    lambda i, at=at: (0, 0, 0, at + i),
+                    (width_x, width_y, width_z, 2 * wide * LANES), lambda i: (0, 0, 0, at + i)
                 ),
-                *whole,
+                *[pl.BlockSpec(h.shape, lambda i: (0, 0, 0)) for h in halo],
             ],
             out_specs=[pl.BlockSpec((block_rows, 8 * wide, LANES), lambda i: (0, i, 0))]
-            + [pl.BlockSpec((slots, 2 * wide * LANES), lambda i: (0, i))] * batches,
+            + [pl.BlockSpec((count, 2 * wide * LANES), lambda i: (0, i)) for count in counts],
             out_shape=[jax.ShapeDtypeStruct((block_rows, group_rows, LANES), jnp.float32)]
-            + [jax.ShapeDtypeStruct((slots, group), bf16)] * batches,
-            compiler_params=params(56),
+            + [jax.ShapeDtypeStruct((count, group), bf16) for count in counts],
+            scratch_shapes=[
+                pltpu.VMEM((width_x + 2, width_y, 8, LANES), jnp.float32),
+                pltpu.VMEM((width_x, 8, LANES), jnp.float32),
+                pltpu.VMEM((block_rows * 8, wide * LANES), bf16),
+            ],
+            compiler_params=params(20),
             name="upwind",
-        )(side, speeds, picker, distribution, *halos[g])
+        )(side, speeds, picker, distribution, *halo)
+
+    reads, own, other = [], [], []
+    for g in range(parts):
+        down, up, across = edges[g]
+        if own:
+            down, up, across, own[-1] = lax.optimization_barrier((down, up, across, own[-1]))
+        halo = (
+            lax.ppermute(down, "cy", towards_lower),
+            lax.ppermute(up, "cy", towards_upper),
+            lax.ppermute(across, ("vel", "cx"), across_pairs),
+        )
+        read, *chosen = upwind(g, halo)
         reads.append(read)
         own.append(chosen)
-        other.append([lax.ppermute(c, "vel", swap) for c in chosen])
-
-    terms = []
-    half = points // 2
-    for batch in range(batches):
-        terms.append(
-            pl.pallas_call(
-                functools.partial(collide_kernel, parts),
-                out_shape=jax.ShapeDtypeStruct((slots, local_vel), bf16),
-                scratch_shapes=[
-                    pltpu.VMEM((points, slots, 2 * padded), jnp.float32),
-                    pltpu.VMEM((2, 3, half // 2, slots, 2 * padded), bf16),
-                ],
-                compiler_params=params(56),
-                name="collide",
-            )(
-                weights,
-                table,
-                *[own[g][batch] for g in range(parts)],
-                *[other[g][batch] for g in range(parts)],
-            )
-        )
-
-    per_part = steps // wide
-
-    def read_spec(g):
-        return pl.BlockSpec(
-            (block_rows, 8 * wide, LANES),
-            lambda i: (0, jnp.clip(i - g * per_part, 0, per_part - 1), 0),
-        )
-
+    early = [lax.ppermute(own[g][0], "vel", swap) for g in range(parts)]
+    first_late = lax.ppermute(own[0][1], "vel", swap)
+    *later, _ = lax.optimization_barrier((*[own[g][1] for g in range(1, parts)], early[-1]))
+    lates = [first_late] + [lax.ppermute(x, "vel", swap) for x in later]
+
+    def scratch(count):
+        return [
+            pltpu.VMEM((points, count, 2 * padded), jnp.float32),
+            pltpu.VMEM((2, 3, points // 4, count, 2 * padded), bf16),
+        ]
+
+    terms = pl.pallas_call(
+        functools.partial(collide_kernel, parts),
+        out_shape=jax.ShapeDtypeStruct((counts[0], local_vel), bf16),
+        scratch_shapes=scratch(counts[0]),
+        compiler_params=params(36),
+        name="collide",
+    )(weights, table, *[chosen[0] for chosen in own], *early)
+
+    local = pl.BlockSpec(memory_space=pltpu.VMEM)
+    anywhere = pl.BlockSpec(memory_space=pl.ANY)
     return pl.pallas_call(
-        functools.partial(evolve_kernel, parts),
-        grid=(parts * per_part,),
-        in_specs=[pl.BlockSpec(spread.shape, lambda i: (0, 0))]
-        + [read_spec(g) for g in range(parts)]
-        + [pl.BlockSpec((slots, 2 * wide * LANES), lambda i: (0, i))] * batches,
-        out_specs=pl.BlockSpec(
-            (width_x, width_y, width_z, 2 * wide * LANES), lambda i: (0, 0, 0, i)
-        ),
+        functools.partial(finish_kernel, parts),
+        in_specs=[local] * (4 + 2 * parts) + [anywhere] * parts,
+        out_specs=anywhere,
         out_shape=jax.ShapeDtypeStruct(distribution.shape, jnp.float32),
-        compiler_params=params(56),
-        name="evolve",
-    )(spread, *reads, *terms)
+        scratch_shapes=scratch(counts[1])
+        + [
+            pltpu.VMEM((parts, block_rows, group_rows, LANES), jnp.float32),
+            pltpu.VMEM((2 * capacity, group // 2), bf16),
+            pltpu.VMEM((block_rows * 8, group // 2), jnp.float32),
+            pltpu.VMEM((2, width_x, width_y, width_z, group), jnp.float32),
+            pltpu.SemaphoreType.DMA((parts,)),
+            pltpu.SemaphoreType.DMA((parts,)),
+        ],
+        compiler_params=params(44),
+        name="finish",
+    )(weights, table, spread, terms, *[chosen[1] for chosen in own], *lates, *reads)
 
 
 def per_device(distribution, refine_level, gain_one, gain_two, loss_kernel):

time: 108 us -> 122 us (1.13)
  local copies, waits for them, and re-layouts: 6.61 us -> 31.6 us
  Pallas kernels: 58.9 us -> 43.4 us
  starting transfers between devices: 17.1 us -> 19.7 us
  waiting for transfers between devices: 21 us -> 22.4 us
    unnamed x48 -> x54, local copies, waits for them, and re-layouts: 3.99 us -> 18.2 us
    pallas_call x2 -> x1, Pallas kernels: 25.3 us -> 13.9 us  [fast_device(): pl.pallas_call(functools.partial(collide_kernel, parts), out_shape=jax.Sh...]
    ppermute x3, starting transfers between devices: 4.15 us -> 9.4 us  [fast_device(): lax.ppermute(down, 'cy', towards_lower)]
    ppermute x6, waiting for transfers between devices: 9.96 us -> 14.6 us  [the longest x3 14.6 us: fast_device(): early = [lax.ppermute(own[g][0], 'vel', swap) for g in range(parts)]]
    ppermute x3, waiting for transfers between devices: 8.12 us -> 4.2 us  [fast_device(): lax.ppermute(up, 'cy', towards_upper)]
    ppermute x3, starting transfers between devices: 3.82 us -> 0.01 us  [fast_device(): lax.ppermute(up, 'cy', towards_upper)]
    pallas_call x3, Pallas kernels: 6.73 us -> 3.39 us  [fast_device(): pl.pallas_call(edges_kernel, grid_spec=pltpu.PrefetchScalarGridSpec(num_s...]
    rev x1, local copies, waits for them, and re-layouts: 0.17 us -> 3.01 us  [frequency_weights(): jnp.flip(stacked[:, 1:], 1)]
  transfers between devices with their start and end apart: 15 -> 15, of which waited for: 3 -> 6; matrix products, arithmetic and copies ran while one was open for 5% -> 15% of each run, Pallas kernels for 31% -> 12%
where the time goes in v2:
time: 122 us
  Pallas kernels  43.4 us (36%)
  local copies, waits for them, and re-layouts  31.6 us (26%)
  waiting for transfers between devices  22.4 us (18%)
  starting transfers between devices  19.7 us (16%)
  other arithmetic  2.91 us (2%)
    unnamed x54, local copies, waits for them, and re-layouts  18.2 us
    ppermute x3, waiting for transfers between devices, fast_device(): early = [lax.ppermute(own[g][0], 'vel', swap) for g in range(parts)]  14.6 us
    pallas_call x1, Pallas kernels, fast_device(): pl.pallas_call(functools.partial(collide_kernel, parts), out_shape=jax.Sh...  13.9 us
    pallas_call x3, Pallas kernels, upwind(): pl.pallas_call(upwind_kernel, grid=(steps // wide,), in_specs=[pl.BlockSp...  13.7 us
    pallas_call x1, Pallas kernels, fast_device(): pl.pallas_call(functools.partial(finish_kernel, parts), in_specs=[local]...  12.3 us
    ppermute x3, starting transfers between devices, fast_device(): lax.ppermute(down, 'cy', towards_lower)  9.4 us
    ppermute x3, starting transfers between devices, fast_device(): early = [lax.ppermute(own[g][0], 'vel', swap) for g in range(parts)]  4.31 us
    ppermute x3, waiting for transfers between devices, fast_device(): lax.ppermute(up, 'cy', towards_upper)  4.2 us
  transfers between devices with their start and end apart: 15, of which 6 were waited for; matrix products, arithmetic and copies ran while one was open for 15% of the time, Pallas kernels for 12%

profile of v2, /device:TPU:0, one launch (start us, length us, event | category | flops | bytes accessed | tf_op | source)
XLA Modules:
  0.0 121.6 jit_solution(11608241848769794306)
XLA Ops:
  0.9 2.2 %edges.4 = (bf16[5,128,128]{2,1,0:T(8,128)(2,1)}, bf16[5,128,128]{2,1,0:T(8,128)(2,1)}, bf16[9,32,128]{2,1,0:T(8,128)(2,1)}) custom-call(s32[1]{0:T(128)} %bitcast.3.edge_ref, f32[3,216,128]{2,1,0:T(8,128)} %bitcast.12, f32[16,4,4,6912]{3,2,1,0:T(4,128)} %block_ref.5, f32[16,4,4,6912]{3,2,1,0:T(4,128)} %block_ref.5, f32[16,4,4,6912]{3,2,1,0:T(4,128)} %block_ref.5), custom_call_target="tpu_custom_call" | custom-call | tf_op jit(solution)/shard_map/edges/pallas_call | solution.py:588
  3.2 2.4 %collective-permute-start.2 = (bf16[9,32,128]{2,1,0:T(8,128)(2,1)}, bf16[9,32,128]{2,1,0:T(8,128)(2,1)S(1)}, u32[]{:S(2)}, u32[]{:S(2)}) collective-permute-start(bf16[9,32,128]{2,1,0:T(8,128)(2,1)} %get-tuple-element.40), channel_id=1, source_target_pairs={{0,12},{4,0},{8,4},{12,8},{16,20},{20,24},{24,28},{28,16},{1,13},{... | collective-permute-start | bytes 221192 | tf_op jit(solution)/shard_map/ppermute | solution.py:656
  5.6 3.6 %collective-permute-start = (bf16[5,128,128]{2,1,0:T(8,128)(2,1)}, bf16[5,128,128]{2,1,0:T(8,128)(2,1)S(1)}, u32[]{:S(2)}, u32[]{:S(2)}) collective-permute-start(bf16[5,128,128]{2,1,0:T(8,128)(2,1)} %get-tuple-element.38), channel_id=1, source_target_pairs={{0,3},{1,0},{2,1},{3,2},{4,7},{5,4},{6,5},{7,6},{8,11},{9,8},{10,9... | collective-permute-start | bytes 491528 | tf_op jit(solution)/shard_map/ppermute | solution.py:654
  10.5 3.0 %copy-done = f32[16,4,4,6912]{3,2,1,0:T(4,128)S(1)} copy-done((f32[16,4,4,6912]{3,2,1,0:T(4,128)S(1)}, f32[16,4,4,6912]{3,2,1,0:T(4,128)}, u32[]{:S(2)}) %copy-start) | copy-done | bytes 7077912
  15.4 1.6 %collective-permute-done.1.up_ref = bf16[5,128,128]{2,1,0:T(8,128)(2,1)S(1)} collective-permute-done((bf16[5,128,128]{2,1,0:T(8,128)(2,1)}, bf16[5,128,128]{2,1,0:T(8,128)(2,1)S(1)}, u32[]{:S(2)}, u32[]{:S(2)}) %collective-permute-start.1) | collective-permute-done | bytes 163872 | tf_op jit(solution)/shard_map/ppermute | solution.py:655
  17.0 3.0 %copy-done.1 = f32[16,4,4,6912]{3,2,1,0:T(4,128)S(1)} copy-done((f32[16,4,4,6912]{3,2,1,0:T(4,128)S(1)}, f32[16,4,4,6912]{3,2,1,0:T(4,128)}, u32[]{:S(2)}) %copy-start.1) | copy-done | bytes 7077912
  20.0 4.6 %upwind.3 = (f32[64,72,128]{2,1,0:T(8,128)S(1)}, bf16[80,2304]{1,0:T(8,128)(2,1)}, bf16[48,2304]{1,0:T(8,128)(2,1)S(1)}) custom-call(s32[1]{0:T(128)} %bitcast.6.side_ref, f32[3,216,128]{2,1,0:T(8,128)S(1)} %bitcast.14, bf16[256,512]{1,0:T(8,128)(2,1)S(1)} %fusion.picker_ref, f32[16,4,4,6912]{3,2,1,0:T(4,128)S(1)} %copy-done.1, ...), custom_call_target="tpu_custom_call" | custom-call | tf_op jit(solution)/shard_map/upwind/pallas_call | solution.py:623
  25.3 2.3 %collective-permute-start.3 = (bf16[5,128,128]{2,1,0:T(8,128)(2,1)}, bf16[5,128,128]{2,1,0:T(8,128)(2,1)S(1)}, u32[]{:S(2)}, u32[]{:S(2)}) collective-permute-start(bf16[5,128,128]{2,1,0:T(8,128)(2,1)} %get-tuple-element.47), channel_id=1, source_target_pairs={{0,3},{1,0},{2,1},{3,2},{4,7},{5,4},{6,5},{7,6},{8,11},{9,8},{10,9... | collective-permute-start | bytes 491528 | tf_op jit(solution)/shard_map/ppermute | solution.py:654
  30.8 1.6 %slice.9 = f32[3,23,576]{2,1,0:T(8,128)} slice(f32[3,24,576]{2,1,0:T(8,128)} %constant_dynamic-update-slice_fusion), slice={[0:3], [1:24], [0:576]} | slice | bytes 317952 | tf_op jit(solution)/shard_map/slice | solution.py:161
  32.4 3.0 %copy-done.2 = f32[16,4,4,6912]{3,2,1,0:T(4,128)S(1)} copy-done((f32[16,4,4,6912]{3,2,1,0:T(4,128)S(1)}, f32[16,4,4,6912]{3,2,1,0:T(4,128)}, u32[]{:S(2)}) %copy-start.2) | copy-done | bytes 7077912
  37.0 3.0 %rev.4 = f32[3,23,576]{2,1,0:T(8,128)} reverse(f32[3,23,576]{2,1,0:T(8,128)} %slice.9), dimensions={1} | reverse | bytes 317952 | tf_op jit(solution)/shard_map/jit(_flip)/rev | solution.py:161
  40.0 3.0 %copy-done.3 = f32[16,4,4,6912]{3,2,1,0:T(4,128)S(1)} copy-done((f32[16,4,4,6912]{3,2,1,0:T(4,128)S(1)}, f32[16,4,4,6912]{3,2,1,0:T(4,128)}, u32[]{:S(2)}) %copy-start.3) | copy-done | bytes 7077912
  43.0 4.6 %upwind.4 = (f32[64,72,128]{2,1,0:T(8,128)S(1)}, bf16[80,2304]{1,0:T(8,128)(2,1)}, bf16[48,2304]{1,0:T(8,128)(2,1)S(1)}) custom-call(s32[1]{0:T(128)} %bitcast.6.side_ref, f32[3,216,128]{2,1,0:T(8,128)S(1)} %bitcast.16, bf16[256,512]{1,0:T(8,128)(2,1)S(1)} %fusion.picker_ref, f32[16,4,4,6912]{3,2,1,0:T(4,128)S(1)} %copy-done.3, ...), custom_call_target="tpu_custom_call" | custom-call | tf_op jit(solution)/shard_map/upwind/pallas_call | solution.py:623
  47.6 1.4 %copy-done.6 = f32[64,72,128]{2,1,0:T(8,128)} copy-done((f32[64,72,128]{2,1,0:T(8,128)}, f32[64,72,128]{2,1,0:T(8,128)S(1)}, u32[]{:S(2)}) %copy-start.6) | copy-done | bytes 2359320
  49.0 1.3 %collective-permute-start.8 = (bf16[9,32,128]{2,1,0:T(8,128)(2,1)S(1)}, bf16[9,32,128]{2,1,0:T(8,128)(2,1)S(1)}, u32[]{:S(2)}, u32[]{:S(2)}) collective-permute-start(bf16[9,32,128]{2,1,0:T(8,128)(2,1)S(1)} %get-tuple-element.55), channel_id=1, source_target_pairs={{0,12},{4,0},{8,4},{12,8},{16,20},{20,24},{24,28},{28,16},{1,13},{... | collective-permute-start | bytes 221192 | tf_op jit(solution)/shard_map/ppermute | solution.py:656
  50.4 3.5 %collective-permute-start.6 = (bf16[5,128,128]{2,1,0:T(8,128)(2,1)S(1)}, bf16[5,128,128]{2,1,0:T(8,128)(2,1)S(1)}, u32[]{:S(2)}, u32[]{:S(2)}) collective-permute-start(bf16[5,128,128]{2,1,0:T(8,128)(2,1)S(1)} %copy-done.18), channel_id=1, source_target_pairs={{0,3},{1,0},{2,1},{3,2},{4,7},{5,4},{6,5},{7,6},{8,11},{9,8},{10,9... | collective-permute-start | bytes 491528 | tf_op jit(solution)/shard_map/ppermute | solution.py:654
  55.0 3.6 %collective-permute-done.6.down_ref = bf16[5,128,128]{2,1,0:T(8,128)(2,1)S(1)} collective-permute-done((bf16[5,128,128]{2,1,0:T(8,128)(2,1)S(1)}, bf16[5,128,128]{2,1,0:T(8,128)(2,1)S(1)}, u32[]{:S(2)}, u32[]{:S(2)}) %collective-permute-start.6) | collective-permute-done | bytes 163872 | tf_op jit(solution)/shard_map/ppermute | solution.py:654
  58.6 2.6 %collective-permute-done.7.up_ref = bf16[5,128,128]{2,1,0:T(8,128)(2,1)S(1)} collective-permute-done((bf16[5,128,128]{2,1,0:T(8,128)(2,1)S(1)}, bf16[5,128,128]{2,1,0:T(8,128)(2,1)S(1)}, u32[]{:S(2)}, u32[]{:S(2)}) %collective-permute-start.7) | collective-permute-done | bytes 163872 | tf_op jit(solution)/shard_map/ppermute | solution.py:655
  61.2 4.6 %upwind.5 = (f32[64,72,128]{2,1,0:T(8,128)S(1)}, bf16[80,2304]{1,0:T(8,128)(2,1)}, bf16[48,2304]{1,0:T(8,128)(2,1)S(1)}) custom-call(s32[1]{0:T(128)} %bitcast.6.side_ref, f32[3,216,128]{2,1,0:T(8,128)S(1)} %bitcast.17, bf16[256,512]{1,0:T(8,128)(2,1)S(1)} %fusion.picker_ref, f32[16,4,4,6912]{3,2,1,0:T(4,128)S(1)} %copy-done.3, ...), custom_call_target="tpu_custom_call" | custom-call | tf_op jit(solution)/shard_map/upwind/pallas_call | solution.py:623
  65.8 1.4 %copy-done.8 = f32[64,72,128]{2,1,0:T(8,128)} copy-done((f32[64,72,128]{2,1,0:T(8,128)}, f32[64,72,128]{2,1,0:T(8,128)S(1)}, u32[]{:S(2)}) %copy-start.8) | copy-done | bytes 2359320
  67.3 2.2 %collective-permute-start.11 = (bf16[80,2304]{1,0:T(8,128)(2,1)}, bf16[80,2304]{1,0:T(8,128)(2,1)}, u32[]{:S(2)}, u32[]{:S(2)}) collective-permute-start(bf16[80,2304]{1,0:T(8,128)(2,1)} %get-tuple-element.56.refs_2_), channel_id=1, source_target_pairs={{0,16},{16,0},{1,17},{17,1},{2,18},{18,2},{3,19},{19,3},{4,20},{20... | collective-permute-start | bytes 1105928 | tf_op jit(solution)/shard_map/ppermute | solution.py:661
  69.5 1.1 convolution_multiply_fusion
  70.7 2.0 %collective-permute-start.10 = (bf16[80,2304]{1,0:T(8,128)(2,1)}, bf16[80,2304]{1,0:T(8,128)(2,1)}, u32[]{:S(2)}, u32[]{:S(2)}) collective-permute-start(bf16[80,2304]{1,0:T(8,128)(2,1)} %get-tuple-element.52.refs_1_), channel_id=1, source_target_pairs={{0,16},{16,0},{1,17},{17,1},{2,18},{18,2},{3,19},{19,3},{4,20},{20... | collective-permute-start | bytes 1105928 | tf_op jit(solution)/shard_map/ppermute | solution.py:661
  73.3 1.4 %copy.23 = bf16[16,4,4]{2,1,0:T(4,128)(2,1)} copy(bf16[16,4,4]{0,2,1:T(4,128)(2,1)} %convert_multiply_fusion) | data formatting | bytes 1024 | tf_op jit(solution)/shard_map/mul | solution.py:568
  74.7 1.4 %broadcast_in_dim.52 = bf16[64,2,4]{2,1,0:T(2,128)(2,1)} broadcast(bf16[64,4]{1,0:T(8,128)(2,1)} %bitcast.21), dimensions={0,2} | broadcast | bytes 1536 | tf_op jit(solution)/shard_map/broadcast_in_dim | solution.py:567
  76.1 1.4 %broadcast_in_dim.53 = bf16[512]{0:T(512)(128)(2,1)} reshape(bf16[64,2,4]{2,1,0:T(2,128)(2,1)} %broadcast_in_dim.52) | data formatting | bytes 2048 | tf_op jit(solution)/shard_map/jit(_where)/broadcast_in_dim | solution.py:570
  77.6 1.7 %collective-permute-done.11.refs_5_ = bf16[80,2304]{1,0:T(8,128)(2,1)} collective-permute-done((bf16[80,2304]{1,0:T(8,128)(2,1)}, bf16[80,2304]{1,0:T(8,128)(2,1)}, u32[]{:S(2)}, u32[]{:S(2)}) %collective-permute-start.11) | collective-permute-done | bytes 368672 | tf_op jit(solution)/shard_map/ppermute | solution.py:661
  79.3 2.0 %collective-permute-start.13 = (bf16[48,2304]{1,0:T(8,128)(2,1)}, bf16[48,2304]{1,0:T(8,128)(2,1)S(1)}, u32[]{:S(2)}, u32[]{:S(2)}) collective-permute-start(bf16[48,2304]{1,0:T(8,128)(2,1)} %copy-done.11), channel_id=1, source_target_pairs={{0,16},{16,0},{1,17},{17,1},{2,18},{18,2},{3,19},{19,3},{4,20},{20... | collective-permute-start | bytes 663560 | tf_op jit(solution)/shard_map/ppermute | solution.py:664
  82.2 5.0 %collective-permute-done.9.refs_3_ = bf16[80,2304]{1,0:T(8,128)(2,1)} collective-permute-done((bf16[80,2304]{1,0:T(8,128)(2,1)}, bf16[80,2304]{1,0:T(8,128)(2,1)}, u32[]{:S(2)}, u32[]{:S(2)}) %collective-permute-start.9) | collective-permute-done | bytes 368672 | tf_op jit(solution)/shard_map/ppermute | solution.py:661
  87.2 7.9 %collective-permute-done.10.refs_4_ = bf16[80,2304]{1,0:T(8,128)(2,1)} collective-permute-done((bf16[80,2304]{1,0:T(8,128)(2,1)}, bf16[80,2304]{1,0:T(8,128)(2,1)}, u32[]{:S(2)}, u32[]{:S(2)}) %collective-permute-start.10) | collective-permute-done | bytes 368672 | tf_op jit(solution)/shard_map/ppermute | solution.py:661
  95.1 13.9 %collide.1.early_ref = bf16[80,6912]{1,0:T(8,128)(2,1)S(1)} custom-call(f32[3,24,384]{2,1,0:T(8,128)S(1)} %bitcast.18, bf16[704,768]{1,0:T(8,128)(2,1)S(1)} %copy-done.5, bf16[80,2304]{1,0:T(8,128)(2,1)} %get-tuple-element.43.refs_0_, bf16[80,2304]{1,0:T(8,128)(2,1)} %get-tuple-element.52.refs_1_, bf16[80,2304]{1,0:T(8,128)(2,1)} %get-tuple-element.56.refs_2_, ...), custom_call_target="tpu_custom_call" | custom-call | tf_op jit(solution)/shard_map/collide/pallas_call | solution.py:672
  109.1 12.3 %finish.1 = f32[16,4,4,6912]{3,2,1,0:T(4,128)} custom-call(f32[3,24,384]{2,1,0:T(8,128)S(1)} %bitcast.19, bf16[704,768]{1,0:T(8,128)(2,1)S(1)} %copy-done.5, bf16[512,256]{1,0:T(8,128)(2,1)S(1)} %select_convert_fusion.spread_ref, bf16[80,6912]{1,0:T(8,128)(2,1)S(1)} %collide.1.early_ref, bf16[48,2304]{1,0:T(8,128)(2,1)S(1)} %copy-done.10, ...), custom_call_target="tpu_custom_call" | custom-call | tf_op jit(solution)/shard_map/finish/pallas_call | solution.py:682
  (93 shorter events, 12.4 us)
Async XLA Ops:
  0.9 8.3 %copy-start.23 = (s32[16,4,4]{0,2,1:T(4,128)S(1)}, s32[16,4,4]{0,2,1:T(4,128)}, u32[]{:S(2)}) copy-start(s32[16,4,4]{0,2,1:T(4,128)} %param.9) | copy-start | bytes 3076
  0.9 9.6 %copy-start.4 = (f32[3,54,4,128]{3,2,1,0:T(4,128)S(1)}, f32[3,54,4,128]{3,2,1,0:T(4,128)}, u32[]{:S(2)}) copy-start(f32[3,54,4,128]{3,2,1,0:T(4,128)} %broadcast_in_dim.57) | copy-start | bytes 995332
  3.2 12.2 %collective-permute-start.2 = (bf16[9,32,128]{2,1,0:T(8,128)(2,1)}, bf16[9,32,128]{2,1,0:T(8,128)(2,1)S(1)}, u32[]{:S(2)}, u32[]{:S(2)}) collective-permute-start(bf16[9,32,128]{2,1,0:T(8,128)(2,1)} %get-tuple-element.40), channel_id=1, source_target_pairs={{0,12},{4,0},{8,4},{12,8},{16,20},{20,24},{24,28},{28,16},{1,13},{... | collective-permute-start | bytes 221192 | tf_op jit(solution)/shard_map/ppermute | solution.py:656
  5.6 9.8 %collective-permute-start = (bf16[5,128,128]{2,1,0:T(8,128)(2,1)}, bf16[5,128,128]{2,1,0:T(8,128)(2,1)S(1)}, u32[]{:S(2)}, u32[]{:S(2)}) collective-permute-start(bf16[5,128,128]{2,1,0:T(8,128)(2,1)} %get-tuple-element.38), channel_id=1, source_target_pairs={{0,3},{1,0},{2,1},{3,2},{4,7},{5,4},{6,5},{7,6},{8,11},{9,8},{10,9... | collective-permute-start | bytes 491528 | tf_op jit(solution)/shard_map/ppermute | solution.py:654
  9.2 7.8 %collective-permute-start.1 = (bf16[5,128,128]{2,1,0:T(8,128)(2,1)}, bf16[5,128,128]{2,1,0:T(8,128)(2,1)S(1)}, u32[]{:S(2)}, u32[]{:S(2)}) collective-permute-start(bf16[5,128,128]{2,1,0:T(8,128)(2,1)} %get-tuple-element.39), channel_id=1, source_target_pairs={{0,1},{1,2},{2,3},{3,0},{4,5},{5,6},{6,7},{7,4},{8,9},{9,10},{10,1... | collective-permute-start | bytes 491528 | tf_op jit(solution)/shard_map/ppermute | solution.py:655
  10.5 3.0 %copy-start = (f32[16,4,4,6912]{3,2,1,0:T(4,128)S(1)}, f32[16,4,4,6912]{3,2,1,0:T(4,128)}, u32[]{:S(2)}) copy-start(f32[16,4,4,6912]{3,2,1,0:T(4,128)} %block_ref.5) | copy-start | bytes 21233668
  25.3 14.7 %collective-permute-start.3 = (bf16[5,128,128]{2,1,0:T(8,128)(2,1)}, bf16[5,128,128]{2,1,0:T(8,128)(2,1)S(1)}, u32[]{:S(2)}, u32[]{:S(2)}) collective-permute-start(bf16[5,128,128]{2,1,0:T(8,128)(2,1)} %get-tuple-element.47), channel_id=1, source_target_pairs={{0,3},{1,0},{2,1},{3,2},{4,7},{5,4},{6,5},{7,6},{8,11},{9,8},{10,9... | collective-permute-start | bytes 491528 | tf_op jit(solution)/shard_map/ppermute | solution.py:654
  27.5 12.5 %collective-permute-start.4 = (bf16[5,128,128]{2,1,0:T(8,128)(2,1)}, bf16[5,128,128]{2,1,0:T(8,128)(2,1)S(1)}, u32[]{:S(2)}, u32[]{:S(2)}) collective-permute-start(bf16[5,128,128]{2,1,0:T(8,128)(2,1)} %get-tuple-element.48), channel_id=1, source_target_pairs={{0,1},{1,2},{2,3},{3,0},{4,5},{5,6},{6,7},{7,4},{8,9},{9,10},{10,1... | collective-permute-start | bytes 491528 | tf_op jit(solution)/shard_map/ppermute | solution.py:655
  29.3 10.8 %collective-permute-start.5 = (bf16[9,32,128]{2,1,0:T(8,128)(2,1)S(1)}, bf16[9,32,128]{2,1,0:T(8,128)(2,1)S(1)}, u32[]{:S(2)}, u32[]{:S(2)}) collective-permute-start(bf16[9,32,128]{2,1,0:T(8,128)(2,1)S(1)} %get-tuple-element.49), channel_id=1, source_target_pairs={{0,12},{4,0},{8,4},{12,8},{16,20},{20,24},{24,28},{28,16},{1,13},{... | collective-permute-start | bytes 221192 | tf_op jit(solution)/shard_map/ppermute | solution.py:656
  40.0 3.0 %copy-start.3 = (f32[16,4,4,6912]{3,2,1,0:T(4,128)S(1)}, f32[16,4,4,6912]{3,2,1,0:T(4,128)}, u32[]{:S(2)}) copy-start(f32[16,4,4,6912]{3,2,1,0:T(4,128)} %block_ref.5) | copy-start | bytes 21233668
  43.0 7.3 %copy-start.18 = (bf16[5,128,128]{2,1,0:T(8,128)(2,1)S(1)}, bf16[5,128,128]{2,1,0:T(8,128)(2,1)}, u32[]{:S(2)}) copy-start(bf16[5,128,128]{2,1,0:T(8,128)(2,1)} %copy-done.17) | copy-start | bytes 491524
  43.0 10.9 %copy-start.16 = (bf16[5,128,128]{2,1,0:T(8,128)(2,1)S(1)}, bf16[5,128,128]{2,1,0:T(8,128)(2,1)}, u32[]{:S(2)}) copy-start(bf16[5,128,128]{2,1,0:T(8,128)(2,1)} %copy-done.15) | copy-start | bytes 491524
  43.0 10.9 %copy-start.20 = (f32[3,23,576]{2,1,0:T(8,128)S(1)}, f32[3,23,576]{2,1,0:T(8,128)}, u32[]{:S(2)}) copy-start(f32[3,23,576]{2,1,0:T(8,128)} %rev.4) | copy-start | bytes 476932
  49.0 21.6 %copy-start.11 = (bf16[48,2304]{1,0:T(8,128)(2,1)}, bf16[48,2304]{1,0:T(8,128)(2,1)S(1)}, u32[]{:S(2)}) copy-start(bf16[48,2304]{1,0:T(8,128)(2,1)S(1)} %get-tuple-element.60.refs_1_) | copy-start | bytes 663556
  49.0 6.0 %collective-permute-start.8 = (bf16[9,32,128]{2,1,0:T(8,128)(2,1)S(1)}, bf16[9,32,128]{2,1,0:T(8,128)(2,1)S(1)}, u32[]{:S(2)}, u32[]{:S(2)}) collective-permute-start(bf16[9,32,128]{2,1,0:T(8,128)(2,1)S(1)} %get-tuple-element.55), channel_id=1, source_target_pairs={{0,12},{4,0},{8,4},{12,8},{16,20},{20,24},{24,28},{28,16},{1,13},{... | collective-permute-start | bytes 221192 | tf_op jit(solution)/shard_map/ppermute | solution.py:656
  50.4 8.2 %collective-permute-start.6 = (bf16[5,128,128]{2,1,0:T(8,128)(2,1)S(1)}, bf16[5,128,128]{2,1,0:T(8,128)(2,1)S(1)}, u32[]{:S(2)}, u32[]{:S(2)}) collective-permute-start(bf16[5,128,128]{2,1,0:T(8,128)(2,1)S(1)} %copy-done.18), channel_id=1, source_target_pairs={{0,3},{1,0},{2,1},{3,2},{4,7},{5,4},{6,5},{7,6},{8,11},{9,8},{10,9... | collective-permute-start | bytes 491528 | tf_op jit(solution)/shard_map/ppermute | solution.py:654
  53.9 7.3 %collective-permute-start.7 = (bf16[5,128,128]{2,1,0:T(8,128)(2,1)S(1)}, bf16[5,128,128]{2,1,0:T(8,128)(2,1)S(1)}, u32[]{:S(2)}, u32[]{:S(2)}) collective-permute-start(bf16[5,128,128]{2,1,0:T(8,128)(2,1)S(1)} %copy-done.16), channel_id=1, source_target_pairs={{0,1},{1,2},{2,3},{3,0},{4,5},{5,6},{6,7},{7,4},{8,9},{9,10},{10,1... | collective-permute-start | bytes 491528 | tf_op jit(solution)/shard_map/ppermute | solution.py:655
  55.0 14.5 %copy-start.19 = (f32[1152,384]{1,0:T(8,128)S(1)}, f32[1152,384]{1,0:T(8,128)}, u32[]{:S(2)}) copy-start(f32[1152,384]{1,0:T(8,128)} %constant.79.clone) | copy-start | bytes 5308420
  55.0 14.5 %copy-start.25 = (f32[384]{0:T(512)S(1)}, f32[384]{0:T(512)}, u32[]{:S(2)}) copy-start(f32[384]{0:T(512)} %constant.80.clone) | copy-start | bytes 4612
  67.3 3.4 %copy-start.13 = (bf16[48,2304]{1,0:T(8,128)(2,1)}, bf16[48,2304]{1,0:T(8,128)(2,1)S(1)}, u32[]{:S(2)}) copy-start(bf16[48,2304]{1,0:T(8,128)(2,1)S(1)} %get-tuple-element.61.refs_2_) | copy-start | bytes 663556
  67.3 5.5 %copy-start.24 = (s32[16,4,4]{0,2,1:T(4,128)S(1)}, s32[16,4,4]{0,2,1:T(4,128)}, u32[]{:S(2)}) copy-start(s32[16,4,4]{0,2,1:T(4,128)} %param.9) | copy-start | bytes 3076
  67.3 27.8 %copy-start.5 = (bf16[704,768]{1,0:T(8,128)(2,1)S(1)}, bf16[704,768]{1,0:T(8,128)(2,1)}, u32[]{:S(2)}) copy-start(bf16[704,768]{1,0:T(8,128)(2,1)} %constant.81.clone.table_ref) | copy-start | bytes 3244036
  67.3 12.0 %collective-permute-start.11 = (bf16[80,2304]{1,0:T(8,128)(2,1)}, bf16[80,2304]{1,0:T(8,128)(2,1)}, u32[]{:S(2)}, u32[]{:S(2)}) collective-permute-start(bf16[80,2304]{1,0:T(8,128)(2,1)} %get-tuple-element.56.refs_2_), channel_id=1, source_target_pairs={{0,16},{16,0},{1,17},{17,1},{2,18},{18,2},{3,19},{19,3},{4,20},{20... | collective-permute-start | bytes 1105928 | tf_op jit(solution)/shard_map/ppermute | solution.py:661
  70.6 16.6 %collective-permute-start.9 = (bf16[80,2304]{1,0:T(8,128)(2,1)}, bf16[80,2304]{1,0:T(8,128)(2,1)}, u32[]{:S(2)}, u32[]{:S(2)}) collective-permute-start(bf16[80,2304]{1,0:T(8,128)(2,1)} %get-tuple-element.43.refs_0_), channel_id=1, source_target_pairs={{0,16},{16,0},{1,17},{17,1},{2,18},{18,2},{3,19},{19,3},{4,20},{20... | collective-permute-start | bytes 1105928 | tf_op jit(solution)/shard_map/ppermute | solution.py:661
  70.7 24.4 %collective-permute-start.10 = (bf16[80,2304]{1,0:T(8,128)(2,1)}, bf16[80,2304]{1,0:T(8,128)(2,1)}, u32[]{:S(2)}, u32[]{:S(2)}) collective-permute-start(bf16[80,2304]{1,0:T(8,128)(2,1)} %get-tuple-element.52.refs_1_), channel_id=1, source_target_pairs={{0,16},{16,0},{1,17},{17,1},{2,18},{18,2},{3,19},{19,3},{4,20},{20... | collective-permute-start | bytes 1105928 | tf_op jit(solution)/shard_map/ppermute | solution.py:661
  77.5 31.6 %collective-permute-start.12 = (bf16[48,2304]{1,0:T(8,128)(2,1)}, bf16[48,2304]{1,0:T(8,128)(2,1)S(1)}, u32[]{:S(2)}, u32[]{:S(2)}) collective-permute-start(bf16[48,2304]{1,0:T(8,128)(2,1)} %copy-done.9), channel_id=1, source_target_pairs={{0,16},{16,0},{1,17},{17,1},{2,18},{18,2},{3,19},{19,3},{4,20},{20... | collective-permute-start | bytes 663560 | tf_op jit(solution)/shard_map/ppermute | solution.py:662
  79.3 29.8 %collective-permute-start.13 = (bf16[48,2304]{1,0:T(8,128)(2,1)}, bf16[48,2304]{1,0:T(8,128)(2,1)S(1)}, u32[]{:S(2)}, u32[]{:S(2)}) collective-permute-start(bf16[48,2304]{1,0:T(8,128)(2,1)} %copy-done.11), channel_id=1, source_target_pairs={{0,16},{16,0},{1,17},{17,1},{2,18},{18,2},{3,19},{19,3},{4,20},{20... | collective-permute-start | bytes 663560 | tf_op jit(solution)/shard_map/ppermute | solution.py:664
  81.3 27.7 %collective-permute-start.14 = (bf16[48,2304]{1,0:T(8,128)(2,1)}, bf16[48,2304]{1,0:T(8,128)(2,1)S(1)}, u32[]{:S(2)}, u32[]{:S(2)}) collective-permute-start(bf16[48,2304]{1,0:T(8,128)(2,1)} %copy-done.13), channel_id=1, source_target_pairs={{0,16},{16,0},{1,17},{17,1},{2,18},{18,2},{3,19},{19,3},{4,20},{20... | collective-permute-start | bytes 663560 | tf_op jit(solution)/shard_map/ppermute | solution.py:664
  95.1 14.0 %copy-start.7 = (f32[64,72,128]{2,1,0:T(8,128)S(1)}, f32[64,72,128]{2,1,0:T(8,128)}, u32[]{:S(2)}) copy-start(f32[64,72,128]{2,1,0:T(8,128)} %copy-done.6) | copy-start | bytes 7077892
  95.1 14.0 %copy-start.10 = (bf16[48,2304]{1,0:T(8,128)(2,1)S(1)}, bf16[48,2304]{1,0:T(8,128)(2,1)}, u32[]{:S(2)}) copy-start(bf16[48,2304]{1,0:T(8,128)(2,1)} %copy-done.9) | copy-start | bytes 663556
  95.1 14.0 %copy-start.12 = (bf16[48,2304]{1,0:T(8,128)(2,1)S(1)}, bf16[48,2304]{1,0:T(8,128)(2,1)}, u32[]{:S(2)}) copy-start(bf16[48,2304]{1,0:T(8,128)(2,1)} %copy-done.11) | copy-start | bytes 663556
  95.1 14.0 %copy-start.14 = (bf16[48,2304]{1,0:T(8,128)(2,1)S(1)}, bf16[48,2304]{1,0:T(8,128)(2,1)}, u32[]{:S(2)}) copy-start(bf16[48,2304]{1,0:T(8,128)(2,1)} %copy-done.13) | copy-start | bytes 663556
  (9 other events, 13.0 us)

commit v3 on v2

--- a/solution.py
+++ b/solution.py
@@ -147,22 +147,32 @@
     return table.astype(ml_dtypes.bfloat16)
 
 
-def frequency_weights(kernels, padded):
-    points = kernels[0].shape[0]
+def frequency_select(points, padded):
     pairs, weights = half_set(points)
-    plus = np.zeros((points * points, padded), np.float32)
-    minus = np.zeros((points * points, padded), np.float32)
+    select = np.zeros((points * points, 2 * padded), np.float32)
     column = np.arange(len(pairs))
-    plus[pairs[:, 0] * points + pairs[:, 1], column] = 1.0
-    minus[(-pairs[:, 0]) % points * points + (-pairs[:, 1]) % points, column] = 1.0
-    scale = np.zeros((padded,), np.float32)
-    scale[: len(pairs)] = 0.5 * weights / points**3
-    stacked = jnp.stack(kernels).reshape(3, points, points * points)
-    mirrored = jnp.concatenate([stacked[:, :1], jnp.flip(stacked[:, 1:], 1)], axis=1)
-    both = jnp.concatenate([stacked, mirrored], axis=2).reshape(3 * points, -1)
-    select = jnp.asarray(np.concatenate([plus, minus]))
-    picked = jnp.dot(both, select, precision=lax.Precision.HIGHEST)
-    return (picked * scale).reshape(3, points, padded)
+    select[pairs[:, 0] * points + pairs[:, 1], column] = 1.0
+    mirror = (-pairs[:, 0]) % points * points + (-pairs[:, 1]) % points
+    select[mirror, padded + column] = 1.0
+    scale = np.zeros((1, padded), np.float32)
+    scale[0, : len(pairs)] = 0.5 * weights / points**3
+    return select.astype(ml_dtypes.bfloat16), scale
+
+
+def weights_kernel(stacked_ref, select_ref, scale_ref, out_ref):
+    kernels, points, padded = out_ref.shape
+    rest = stacked_ref[...]
+    picked = None
+    for _ in range(3):
+        piece = rest.astype(jnp.bfloat16)
+        rest = rest - piece.astype(jnp.float32)
+        part = jnp.dot(piece, select_ref[...], preferred_element_type=jnp.float32)
+        picked = part if picked is None else picked + part
+    for which in range(kernels):
+        for a in range(points):
+            row, mirror = which * points + a, which * points + (-a) % points
+            both = picked[row : row + 1, :padded] + picked[mirror : mirror + 1, padded:]
+            out_ref[which, a : a + 1, :] = both * scale_ref[...]
 
 
 def transform_3(x, sign, wanted=(0, 1, 2)):
@@ -245,116 +255,152 @@
     return jnp.concatenate(parts, axis=1)
 
 
-def edges_kernel(edge_ref, speed_ref, low_ref, high_ref, plane_ref, down_ref, up_ref, across_ref):
-    steps = speed_ref.shape[1] // 8
+def edges_kernel(
+    first, edge_ref, falls_ref, field_ref, down_ref, up_ref, across_ref, low_ref, high_ref, plane_ref, sems
+):
+    steps = falls_ref.shape[0] // 8
+    here = pl.ds(first, low_ref.shape[3])
+    last_y = field_ref.shape[1] - 1
+    sources = [
+        field_ref.at[:, pl.ds(0, 1), :, here],
+        field_ref.at[:, pl.ds(last_y, 1), :, here],
+        field_ref.at[pl.ds(edge_ref[0], 1), :, :, here],
+    ]
+    loads = [
+        pltpu.make_async_copy(source, ref, sems.at[at])
+        for at, (source, ref) in enumerate(zip(sources, (low_ref, high_ref, plane_ref)))
+    ]
+    for load in loads:
+        load.start()
     width = low_ref.shape[0]
-    below = [speed_ref[1, 8 * s : 8 * s + 8, :][None] < 0.0 for s in range(steps)]
+    below = [falls_ref[8 * s : 8 * s + 8, :][None] > 0.0 for s in range(steps)]
 
     def put(ref, at, value):
         ref[at] = value.reshape(-1, LANES).astype(jnp.bfloat16)
 
-    first = [tile_pair(low_ref, s, width) for s in range(steps)]
-    put(down_ref, 0, first[0])
+    loads[0].wait()
+    lowest = [tile_pair(low_ref, s, width) for s in range(steps)]
+    put(down_ref, 0, lowest[0])
     for m in range(1, steps // 2 + 1):
-        put(down_ref, m, jnp.where(below[2 * m - 1], first[2 * m - 1], first[2 * m]))
+        put(down_ref, m, jnp.where(below[2 * m - 1], lowest[2 * m - 1], lowest[2 * m]))
+    loads[1].wait()
     last = [tile_pair(high_ref, s, width) for s in range(steps)]
     for m in range(steps // 2):
         put(up_ref, m, jnp.where(below[2 * m], last[2 * m + 1], last[2 * m]))
     put(up_ref, steps // 2, last[steps - 1])
+    loads[2].wait()
     for s in range(steps):
         put(across_ref, s, tile_pair(plane_ref, s, plane_ref.shape[1]))
 
 
 def upwind_kernel(
+    base,
     side_ref,
     speed_ref,
     picker_ref,
-    block_ref,
+    field_ref,
     down_ref,
     up_ref,
     across_ref,
-    read_ref,
     *refs,
 ):
-    *chosen_refs, wide, border, cells = refs
-    width_x, width_y, width_z, lanes = block_ref.shape
+    carried_refs, (read_ref, early_ref, late_ref), scratch = refs[:-8], refs[-8:-5], refs[-5:]
+    blocks, wide, border, cells, sems = scratch
+    chunks, width_x, width_y, width_z, lanes = blocks.shape
     steps = lanes // (2 * LANES)
+    loads = []
+    for t in range(chunks):
+        source = field_ref.at[:, :, :, pl.ds(base + t * lanes, lanes)]
+        loads.append(pltpu.make_async_copy(source, blocks.at[t], sems.at[t]))
+        loads[-1].start()
     beside = jnp.where(side_ref[0] == 0, 2, 0)
     place = lax.broadcasted_iota(jnp.int32, (1, 8, LANES), 1) % width_z
-    for u in range(steps):
-        step = pl.program_id(0) * steps + u
-        speed = [speed_ref[d, 8 * u : 8 * u + 8, :][None] for d in range(3)]
-        size = [jnp.abs(c) for c in speed]
-        falls = speed[1] < 0.0
-        sinks = speed[2] < 0.0
-        outer = across_ref[step].astype(jnp.float32).reshape(width_y, 8, LANES)
-        wide[0] = outer
-        wide[width_x + 1] = outer
-        above = down_ref[(step + 1) // 2].astype(jnp.float32).reshape(width_x, 8, LANES)
-        under = up_ref[step // 2].astype(jnp.float32).reshape(width_x, 8, LANES)
-        border[...] = jnp.where(falls, above, under)
+    capacity = picker_ref.shape[0] // 2
+    late = late_ref.shape[0]
+    early = capacity - late
+    for ref in carried_refs:
+        early_ref[early:, :] = ref[...]
+    for t in range(chunks):
+        sizes, falls, sinks = [], [], []
+        for u in range(steps):
+            step = t * steps + u
+            speed = [speed_ref[d, 8 * step : 8 * step + 8, :][None] for d in range(3)]
+            sizes.append([jnp.abs(c) for c in speed])
+            falls.append(speed[1] < 0.0)
+            sinks.append(speed[2] < 0.0)
+            outer = across_ref[step].astype(jnp.float32).reshape(width_y, 8, LANES)
+            wide[u, 0] = outer
+            wide[u, width_x + 1] = outer
+            above = down_ref[(step + 1) // 2].astype(jnp.float32).reshape(width_x, 8, LANES)
+            under = up_ref[step // 2].astype(jnp.float32).reshape(width_x, 8, LANES)
+            border[u] = jnp.where(falls[u], above, under)
+        loads[t].wait()
 
         def spread_out(x, carry):
-            at = 2 * u * LANES
-            parts = [block_ref[x, :, :, at + p * LANES : at + (p + 1) * LANES] for p in range(2)]
-            wide[x + 1] = jnp.concatenate(parts, axis=1)
+            for u in range(steps):
+                at = 2 * u * LANES
+                parts = [
+                    blocks[t, x, :, :, at + p * LANES : at + (p + 1) * LANES] for p in range(2)
+                ]
+                wide[u, x + 1] = jnp.concatenate(parts, axis=1)
             return carry
 
-        lax.fori_loop(0, width_x, spread_out, 0, unroll=2)
+        lax.fori_loop(0, width_x, spread_out, 0, unroll=4)
 
         def advance(x, carry):
-            field = wide[x + 1]
-            edge = border[pl.ds(x, 1)]
-            fluxes = size[0] * (field - wide[x + beside])
-            beside_y = jnp.where(
-                falls,
-                jnp.concatenate([field[1:], edge], axis=0),
-                jnp.concatenate([edge, field[:-1]], axis=0),
-            )
-            fluxes = fluxes + size[1] * (field - beside_y)
-            upper = jnp.where(
-                place == width_z - 1, pltpu.roll(field, 3, 1), pltpu.roll(field, 7, 1)
-            )
-            lower = jnp.where(place == 0, pltpu.roll(field, 5, 1), pltpu.roll(field, 1, 1))
-            fluxes = fluxes + size[2] * (field - jnp.where(sinks, upper, lower))
-            read = field - fluxes
-            read_ref[pl.ds(x * width_y, width_y), 8 * u : 8 * u + 8, :] = read
-            rows = width_y * 8
-            at = pl.multiple_of(x * rows, rows)
-            cells[pl.ds(at, rows), u * LANES : (u + 1) * LANES] = read.reshape(
-                rows, LANES
-            ).astype(jnp.bfloat16)
+            for u in range(steps):
+                field = wide[u, x + 1]
+                edge = border[u, pl.ds(x, 1)]
+                fluxes = sizes[u][0] * (field - wide[u, x + beside])
+                beside_y = jnp.where(
+                    falls[u],
+                    jnp.concatenate([field[1:], edge], axis=0),
+                    jnp.concatenate([edge, field[:-1]], axis=0),
+                )
+                fluxes = fluxes + sizes[u][1] * (field - beside_y)
+                upper = jnp.where(
+                    place == width_z - 1, pltpu.roll(field, 3, 1), pltpu.roll(field, 7, 1)
+                )
+                lower = jnp.where(place == 0, pltpu.roll(field, 5, 1), pltpu.roll(field, 1, 1))
+                fluxes = fluxes + sizes[u][2] * (field - jnp.where(sinks[u], upper, lower))
+                read = field - fluxes
+                row = 8 * (t * steps + u)
+                read_ref[pl.ds(x * width_y, width_y), row : row + 8, :] = read
+                rows = width_y * 8
+                at = pl.multiple_of(x * rows, rows)
+                cells[pl.ds(at, rows), u * LANES : (u + 1) * LANES] = read.reshape(
+                    rows, LANES
+                ).astype(jnp.bfloat16)
             return carry
 
         lax.fori_loop(0, width_x, advance, 0, unroll=2)
-    picked = jnp.dot(
-        picker_ref[...], cells[...], preferred_element_type=jnp.float32
-    ).astype(jnp.bfloat16)
-    capacity = picked.shape[0] // 2
-    for parity in range(2):
-        first = parity * capacity
-        for ref in chosen_refs:
-            slots = ref.shape[0]
+        picked = jnp.dot(
+            picker_ref[...], cells[...], preferred_element_type=jnp.float32
+        ).astype(jnp.bfloat16)
+        for parity in range(2):
+            first = parity * capacity
             for u in range(steps):
-                at = (2 * u + parity) * LANES
-                ref[:, at : at + LANES] = picked[first : first + slots, u * LANES : (u + 1) * LANES]
-            first += slots
+                tile = 2 * (t * steps + u) + parity
+                here = slice(tile * LANES, (tile + 1) * LANES)
+                values = picked[first : first + capacity, u * LANES : (u + 1) * LANES]
+                early_ref[:early, here] = values[:early]
+                late_ref[:, here] = values[early:]
 
 
 def filter_parts(parts, weight_ref, table_ref, own_refs, other_refs, section, back):
-    slots = own_refs[0].shape[0]
+    slots = section.shape[1]
     padded = weight_ref.shape[2]
     height = table_ref.shape[0]
     window = height - 64
     pair_lanes = 2 * (height - 128)
-    pairs = own_refs[0].shape[1] // pair_lanes
+    pairs = own_refs[0][0].shape[1] // pair_lanes
     half = 2 * pairs * parts
     for parity in range(2):
         rows = []
-        for ref in own_refs + other_refs:
+        for ref, first in own_refs + other_refs:
             for p in range(pairs):
                 at = p * pair_lanes + parity * (pair_lanes - window)
-                rows.append(ref[:, at : at + window])
+                rows.append(ref[first : first + slots, at : at + window])
         start = 64 * (1 - parity)
         out = jnp.dot(
             jnp.concatenate(rows, axis=0),
@@ -398,8 +444,9 @@
     lax.fori_loop(0, slots // 16 * lane_tiles, transform, 0)
 
 
-def terms_of(part, table_ref, own_ref, back, put):
-    slots, lanes = own_ref.shape
+def terms_of(part, table_ref, own, back, put):
+    own_ref, first = own
+    slots, lanes = back.shape[3], own_ref.shape[1]
     height = table_ref.shape[0]
     window = height - 64
     pair_lanes = 2 * (height - 128)
@@ -437,16 +484,18 @@
                     )
                 values.append(value)
             lane = at * pair_lanes + lane
-            cells = own_ref[:, lane : lane + LANES].astype(jnp.float32)
+            cells = own_ref[first : first + slots, lane : lane + LANES].astype(jnp.float32)
             put(at * tiles + tile, (values[0] * values[1] - cells * values[2]).astype(jnp.bfloat16))
 
 
-def collide_kernel(parts, weight_ref, table_ref, *refs):
-    own_refs, other_refs = refs[:parts], refs[parts : 2 * parts]
+def collide_kernel(firsts, weight_ref, table_ref, *refs):
+    parts = len(firsts) // 2
+    windows = list(zip(refs, firsts))
+    own_refs, other_refs = windows[:parts], windows[parts:]
     terms_ref, section, back = refs[2 * parts :]
     filter_parts(parts, weight_ref, table_ref, own_refs, other_refs, section, back)
     for part in range(parts):
-        first = part * own_refs[0].shape[1]
+        first = part * own_refs[0][0].shape[1]
 
         def put(tile, value):
             terms_ref[:, first + tile * LANES : first + (tile + 1) * LANES] = value
@@ -454,8 +503,10 @@
         terms_of(part, table_ref, own_refs[part], back, put)
 
 
-def finish_kernel(parts, weight_ref, table_ref, spread_ref, early_ref, *refs):
-    own_refs, other_refs = refs[:parts], refs[parts : 2 * parts]
+def finish_kernel(firsts, weight_ref, table_ref, spread_ref, early_ref, *refs):
+    parts = len(firsts) // 2
+    windows = list(zip(refs, firsts))
+    own_refs, other_refs = windows[:parts], windows[parts:]
     read_refs = refs[2 * parts : 3 * parts]
     out_ref, section, back, reads, spots, added, staged, read_sems, out_sems = refs[3 * parts :]
     width_x, width_y, width_z, lanes = staged.shape[1:]
@@ -468,7 +519,7 @@
         load.start()
     filter_parts(parts, weight_ref, table_ref, own_refs, other_refs, section, back)
     early = early_ref.shape[0]
-    capacity = early + own_refs[0].shape[0]
+    capacity = early + section.shape[1]
     stores = []
     for part in range(parts):
 
@@ -517,6 +568,10 @@
     return pltpu.CompilerParams(vmem_limit_bytes=mib * 2**20)
 
 
+def cost(flops, size):
+    return pl.CostEstimate(flops=flops, bytes_accessed=size, transcendentals=0)
+
+
 def fast_fits(distribution, points):
     width_x, width_y, width_z, local_vel = distribution.shape
     group = PLANES * points * points
@@ -545,10 +600,15 @@
     vel_at = lax.axis_index("vel")
     count_x, count_y = lax.axis_size("cx"), lax.axis_size("cy")
 
+    tiles = local_vel // LANES
     speeds = jnp.stack(courants(points, vel_at * local_vel, local_vel))
     speeds = jnp.broadcast_to(
-        speeds.reshape(3, local_vel // LANES, 1, LANES), (3, local_vel // LANES, width_z, LANES)
-    ).reshape(3, local_vel // LANES * width_z, LANES)
+        speeds.reshape(3, tiles, 1, LANES), (3, tiles, width_z, LANES)
+    ).reshape(3, parts, tiles * width_z // parts, LANES)
+    speeds = [speeds[:, g] for g in range(parts)]
+    falls = np.arange(group) // points % points < points // 2
+    falls = np.repeat(falls.reshape(-1, 1, LANES), width_z, axis=1).reshape(-1, LANES)
+    falls = jnp.asarray(falls.astype(np.float32))
     side = vel_at.reshape(1).astype(jnp.int32)
     edge = jnp.where(vel_at == 0, 0, width_x - 1).reshape(1).astype(jnp.int32)
 
@@ -571,7 +631,7 @@
     spread = spread.astype(jnp.bfloat16)
 
     padded = -(-len(half_set(points)[1]) // LANES) * LANES
-    weights = frequency_weights((gain_one, gain_two, loss_kernel), padded)
+    select, scale = frequency_select(points, padded)
     table = jnp.asarray(plane_table(points, padded, 64))
 
     towards_lower = [(j, (j - 1) % count_y) for j in range(count_y)]
@@ -582,86 +642,96 @@
     bf16 = jnp.bfloat16
 
     half_steps = steps // 2 + 1
-    edges = []
-    for g in range(parts):
-        edges.append(
-            pl.pallas_call(
-                edges_kernel,
-                grid_spec=pltpu.PrefetchScalarGridSpec(
-                    num_scalar_prefetch=1,
-                    grid=(1,),
-                    in_specs=[
-                        pl.BlockSpec((3, group_rows, LANES), lambda i, e, g=g: (0, g, 0)),
-                        pl.BlockSpec((width_x, 1, width_z, group), lambda i, e, g=g: (0, 0, 0, g)),
-                        pl.BlockSpec(
-                            (width_x, 1, width_z, group), lambda i, e, g=g: (0, width_y - 1, 0, g)
-                        ),
-                        pl.BlockSpec(
-                            (1, width_y, width_z, group), lambda i, e, g=g: (e[0], 0, 0, g)
-                        ),
-                    ],
-                    out_specs=[
-                        pl.BlockSpec((half_steps, width_x * 8, LANES), lambda i, e: (0, 0, 0)),
-                        pl.BlockSpec((half_steps, width_x * 8, LANES), lambda i, e: (0, 0, 0)),
-                        pl.BlockSpec((steps, width_y * 8, LANES), lambda i, e: (0, 0, 0)),
-                    ],
-                ),
-                out_shape=[
-                    jax.ShapeDtypeStruct((half_steps, width_x * 8, LANES), bf16),
-                    jax.ShapeDtypeStruct((half_steps, width_x * 8, LANES), bf16),
-                    jax.ShapeDtypeStruct((steps, width_y * 8, LANES), bf16),
-                ],
-                compiler_params=params(60 if g == 0 else 16),
-                name="edges",
-            )(edge, speeds, distribution, distribution, distribution)
-        )
-
+    local = pl.BlockSpec(memory_space=pltpu.VMEM)
+    scalar = pl.BlockSpec(memory_space=pltpu.SMEM)
+    remote = pl.BlockSpec(memory_space=pltpu.HBM)
+
+    def edges_of(g):
+        return pl.pallas_call(
+            functools.partial(edges_kernel, g * group),
+            in_specs=[scalar, local, remote],
+            out_specs=[local] * 3,
+            out_shape=[
+                jax.ShapeDtypeStruct((half_steps, width_x * 8, LANES), bf16),
+                jax.ShapeDtypeStruct((half_steps, width_x * 8, LANES), bf16),
+                jax.ShapeDtypeStruct((steps, width_y * 8, LANES), bf16),
+            ],
+            scratch_shapes=[
+                pltpu.VMEM((width_x, 1, width_z, group), jnp.float32),
+                pltpu.VMEM((width_x, 1, width_z, group), jnp.float32),
+                pltpu.VMEM((1, width_y, width_z, group), jnp.float32),
+                pltpu.SemaphoreType.DMA((3,)),
+            ],
+            compiler_params=params(58 if g == 0 else 16),
+            cost_estimate=cost(1, 1),
+            name="edges",
+        )(edge, falls, distribution)
+
+    edges = [edges_of(g) for g in range(parts)]
     wide = 3
-
-    def upwind(g, halo):
-        at = steps // wide * g
+    chunks = steps // wide
+
+    def upwind(g, halo, carried):
+        heights = (capacity if carried else counts[0], counts[1])
         return pl.pallas_call(
-            upwind_kernel,
-            grid=(steps // wide,),
-            in_specs=[
-                pl.BlockSpec(memory_space=pltpu.SMEM),
-                pl.BlockSpec((3, 8 * wide, LANES), lambda i: (0, at + i, 0)),
-                pl.BlockSpec(picker.shape, lambda i: (0, 0)),
-                pl.BlockSpec(
-                    (width_x, width_y, width_z, 2 * wide * LANES), lambda i: (0, 0, 0, at + i)
-                ),
-                *[pl.BlockSpec(h.shape, lambda i: (0, 0, 0)) for h in halo],
-            ],
-            out_specs=[pl.BlockSpec((block_rows, 8 * wide, LANES), lambda i: (0, i, 0))]
-            + [pl.BlockSpec((count, 2 * wide * LANES), lambda i: (0, i)) for count in counts],
+            functools.partial(upwind_kernel, g * group),
+            in_specs=[scalar, local, local, remote] + [local] * (len(halo) + len(carried)),
+            out_specs=[local] * 3,
             out_shape=[jax.ShapeDtypeStruct((block_rows, group_rows, LANES), jnp.float32)]
-            + [jax.ShapeDtypeStruct((count, group), bf16) for count in counts],
+            + [jax.ShapeDtypeStruct((height, group), bf16) for height in heights],
             scratch_shapes=[
-                pltpu.VMEM((width_x + 2, width_y, 8, LANES), jnp.float32),
-                pltpu.VMEM((width_x, 8, LANES), jnp.float32),
+                pltpu.VMEM((chunks, width_x, width_y, width_z, group // chunks), jnp.float32),
+                pltpu.VMEM((wide, width_x + 2, width_y, 8, LANES), jnp.float32),
+                pltpu.VMEM((wide, width_x, 8, LANES), jnp.float32),
                 pltpu.VMEM((block_rows * 8, wide * LANES), bf16),
+                pltpu.SemaphoreType.DMA((chunks,)),
             ],
             compiler_params=params(20),
+            cost_estimate=cost(1, 1),
             name="upwind",
-        )(side, speeds, picker, distribution, *halo)
-
-    reads, own, other = [], [], []
+        )(side, speeds[g], picker, distribution, *halo, *carried)
+
+    def turn(value, *earlier):
+        return lax.optimization_barrier((value, *earlier))[0]
+
+    def swapped(value):
+        return lax.ppermute(value, "vel", swap)
+
+    reads, firsts, lasts, halos, early = [], [], [], [], []
     for g in range(parts):
-        down, up, across = edges[g]
-        if own:
-            down, up, across, own[-1] = lax.optimization_barrier((down, up, across, own[-1]))
-        halo = (
-            lax.ppermute(down, "cy", towards_lower),
-            lax.ppermute(up, "cy", towards_upper),
-            lax.ppermute(across, ("vel", "cx"), across_pairs),
+        operands = edges[g] if g == 0 else turn(edges[g], halos[-1])
+        down, up, across = operands
+        halos.append(
+            (
+                lax.ppermute(down, "cy", towards_lower),
+                lax.ppermute(up, "cy", towards_upper),
+                lax.ppermute(across, ("vel", "cx"), across_pairs),
+            )
         )
-        read, *chosen = upwind(g, halo)
+    for g in range(parts):
+        halo = halos[g] if g == 0 else turn(halos[g], firsts[-1])
+        if g > 1:
+            halo = turn(halo, early[g - 2])
+        read, first, last = upwind(g, halo, lasts[:1] if g == 1 else [])
         reads.append(read)
-        own.append(chosen)
-    early = [lax.ppermute(own[g][0], "vel", swap) for g in range(parts)]
-    first_late = lax.ppermute(own[0][1], "vel", swap)
-    *later, _ = lax.optimization_barrier((*[own[g][1] for g in range(1, parts)], early[-1]))
-    lates = [first_late] + [lax.ppermute(x, "vel", swap) for x in later]
+        firsts.append(first)
+        lasts.append(last)
+        early.append(swapped(first))
+    later = turn(jnp.concatenate(lasts[1:], axis=0), *early[1:])
+    late = swapped(later)
+
+    kernels = turn((gain_one, gain_two, loss_kernel), firsts[-1])
+    weights = pl.pallas_call(
+        weights_kernel,
+        out_shape=jax.ShapeDtypeStruct((3, points, padded), jnp.float32),
+        compiler_params=params(12),
+        cost_estimate=cost(1, 1),
+        name="weights",
+    )(
+        jnp.concatenate([k.reshape(points, points * points) for k in kernels], axis=0),
+        jnp.asarray(select),
+        jnp.asarray(scale),
+    )
 
     def scratch(count):
         return [
@@ -670,17 +740,19 @@
         ]
 
     terms = pl.pallas_call(
-        functools.partial(collide_kernel, parts),
+        functools.partial(collide_kernel, (0,) * (2 * parts)),
         out_shape=jax.ShapeDtypeStruct((counts[0], local_vel), bf16),
         scratch_shapes=scratch(counts[0]),
-        compiler_params=params(36),
-        name="collide",
-    )(weights, table, *[chosen[0] for chosen in own], *early)
-
-    local = pl.BlockSpec(memory_space=pltpu.VMEM)
+        compiler_params=params(32),
+        cost_estimate=cost(1, 1),
+            name="collide",
+    )(weights, table, *firsts, *early)
+
+    lates = [early[1]] + [late] * (parts - 1)
+    late_firsts = (0,) * parts + (counts[0],) + tuple(counts[1] * g for g in range(parts - 1))
     anywhere = pl.BlockSpec(memory_space=pl.ANY)
     return pl.pallas_call(
-        functools.partial(finish_kernel, parts),
+        functools.partial(finish_kernel, late_firsts),
         in_specs=[local] * (4 + 2 * parts) + [anywhere] * parts,
         out_specs=anywhere,
         out_shape=jax.ShapeDtypeStruct(distribution.shape, jnp.float32),
@@ -695,7 +767,7 @@
         ],
         compiler_params=params(44),
         name="finish",
-    )(weights, table, spread, terms, *[chosen[1] for chosen in own], *lates, *reads)
+    )(weights, table, spread, terms, *lasts, *lates, *reads)
 
 
 def per_device(distribution, refine_level, gain_one, gain_two, loss_kernel):

time: 122 us -> 105 us (0.86)
  local copies, waits for them, and re-layouts: 31.6 us -> 22.9 us
  Pallas kernels: 43.4 us -> 39.7 us
  waiting for transfers between devices: 22.4 us -> 20.3 us
  starting transfers between devices: 19.7 us -> 18.2 us
    ppermute x6 -> x4, waiting for transfers between devices: 14.6 us -> 8.6 us  [swapped(): return lax.ppermute(value, 'vel', swap)]
    reshape x0 -> x3, local copies, waits for them, and re-layouts: none -> 4.53 us  [fast_device(): k.reshape(points, points * points)]
    ppermute x3, waiting for transfers between devices: 0.01 us -> 3.97 us  [fast_device(): lax.ppermute(across, ('vel', 'cx'), across_pairs)]
    pallas_call x8 -> x9, Pallas kernels: 43.4 us -> 39.7 us  [the longest x1 13.5 us: fast_device(): pl.pallas_call(functools.partial(finish_kernel, late_firsts), in_specs=[l...]
    rev x1 -> x0, local copies, waits for them, and re-layouts: 3.01 us -> none  [frequency_weights(): jnp.flip(stacked[:, 1:], 1)]
    slice x2 -> x0, local copies, waits for them, and re-layouts: 2.44 us -> none  [the longest x1 1.61 us: frequency_weights(): stacked[:, 1:]]
    another operation x4 -> x0, local copies, waits for them, and re-layouts: 2.01 us -> none  [frequency_weights(): stacked = jnp.stack(kernels).reshape(3, points, points * points)]
    ppermute x3, waiting for transfers between devices: 3.59 us -> 1.6 us  [fast_device(): lax.ppermute(down, 'cy', towards_lower)]
  transfers between devices with their start and end apart: 15 -> 13, of which waited for: 6 -> 6; matrix products, arithmetic and copies ran while one was open for 15% -> 8% of each run, Pallas kernels for 12% -> 22%
where the time goes in v3:
time: 105 us
  Pallas kernels  39.7 us (38%)
  local copies, waits for them, and re-layouts  22.9 us (22%)
  waiting for transfers between devices  20.3 us (19%)
  starting transfers between devices  18.2 us (17%)
  other arithmetic  3.05 us (3%)
    unnamed x64, local copies, waits for them, and re-layouts  17 us
    pallas_call x1, Pallas kernels, fast_device(): pl.pallas_call(functools.partial(finish_kernel, late_firsts), in_specs=[l...  13.5 us
    pallas_call x1, Pallas kernels, fast_device(): pl.pallas_call(functools.partial(collide_kernel, (0,) * (2 * parts)), out...  12.2 us
    pallas_call x3, Pallas kernels, upwind(): pl.pallas_call(functools.partial(upwind_kernel, g * group), in_specs=[sca...  9.09 us
    ppermute x3, starting transfers between devices, fast_device(): lax.ppermute(down, 'cy', towards_lower)  8.96 us
    ppermute x4, waiting for transfers between devices, swapped(): return lax.ppermute(value, 'vel', swap)  8.6 us
    ppermute x3, waiting for transfers between devices, fast_device(): lax.ppermute(up, 'cy', towards_upper)  6.17 us
    ppermute x4, starting transfers between devices, swapped(): return lax.ppermute(value, 'vel', swap)  5.39 us
  transfers between devices with their start and end apart: 13, of which 6 were waited for; matrix products, arithmetic and copies ran while one was open for 8% of the time, Pallas kernels for 22%

profile of v3, /device:TPU:0, one launch (start us, length us, event | category | flops | bytes accessed | tf_op | source)
XLA Modules:
  0.0 104.7 jit_solution(6518517740233605900)
XLA Ops:
  0.0 2.9 %edges.5 = (bf16[5,128,128]{2,1,0:T(8,128)(2,1)}, bf16[5,128,128]{2,1,0:T(8,128)(2,1)}, bf16[9,32,128]{2,1,0:T(8,128)(2,1)}) custom-call(s32[1]{0:T(128)} %bitcast.4.edge_ref, f32[72,128]{1,0:T(8,128)} %constant.81.clone.falls_ref, f32[16,4,4,6912]{3,2,1,0:T(4,128)} %field_ref.11), custom_call_target="tpu_custom_call" | custom-call | flops 1 | bytes 1 | tf_op jit(solution)/shard_map/edges/pallas_call | solution.py:650
  2.9 2.5 %collective-permute-start.2 = (bf16[9,32,128]{2,1,0:T(8,128)(2,1)}, bf16[9,32,128]{2,1,0:T(8,128)(2,1)S(1)}, u32[]{:S(2)}, u32[]{:S(2)}) collective-permute-start(bf16[9,32,128]{2,1,0:T(8,128)(2,1)} %get-tuple-element.50), channel_id=1, source_target_pairs={{0,12},{4,0},{8,4},{12,8},{16,20},{20,24},{24,28},{28,16},{1,13},{... | collective-permute-start | bytes 221192 | tf_op jit(solution)/shard_map/ppermute | solution.py:708
  5.4 3.6 %collective-permute-start = (bf16[5,128,128]{2,1,0:T(8,128)(2,1)}, bf16[5,128,128]{2,1,0:T(8,128)(2,1)S(1)}, u32[]{:S(2)}, u32[]{:S(2)}) collective-permute-start(bf16[5,128,128]{2,1,0:T(8,128)(2,1)} %get-tuple-element.48), channel_id=1, source_target_pairs={{0,3},{1,0},{2,1},{3,2},{4,7},{5,4},{6,5},{7,6},{8,11},{9,8},{10,9... | collective-permute-start | bytes 491528 | tf_op jit(solution)/shard_map/ppermute | solution.py:706
  10.4 3.0 %copy-done = f32[16,4,4,6912]{3,2,1,0:T(4,128)S(1)} copy-done((f32[16,4,4,6912]{3,2,1,0:T(4,128)S(1)}, f32[16,4,4,6912]{3,2,1,0:T(4,128)}, u32[]{:S(2)}) %copy-start) | copy-done | bytes 7077912
  13.4 1.0 edges.4
  14.6 2.2 %collective-permute-done.1.up_ref = bf16[5,128,128]{2,1,0:T(8,128)(2,1)S(1)} collective-permute-done((bf16[5,128,128]{2,1,0:T(8,128)(2,1)}, bf16[5,128,128]{2,1,0:T(8,128)(2,1)S(1)}, u32[]{:S(2)}, u32[]{:S(2)}) %collective-permute-start.1) | collective-permute-done | bytes 163872 | tf_op jit(solution)/shard_map/ppermute | solution.py:707
  16.8 1.7 %collective-permute-start.3 = (bf16[5,128,128]{2,1,0:T(8,128)(2,1)}, bf16[5,128,128]{2,1,0:T(8,128)(2,1)S(1)}, u32[]{:S(2)}, u32[]{:S(2)}) collective-permute-start(bf16[5,128,128]{2,1,0:T(8,128)(2,1)} %get-tuple-element.51), channel_id=1, source_target_pairs={{0,3},{1,0},{2,1},{3,2},{4,7},{5,4},{6,5},{7,6},{8,11},{9,8},{10,9... | collective-permute-start | bytes 491528 | tf_op jit(solution)/shard_map/ppermute | solution.py:706
  18.9 3.0 %copy-done.1 = f32[16,4,4,6912]{3,2,1,0:T(4,128)S(1)} copy-done((f32[16,4,4,6912]{3,2,1,0:T(4,128)S(1)}, f32[16,4,4,6912]{3,2,1,0:T(4,128)}, u32[]{:S(2)}) %copy-start.1) | copy-done | bytes 7077912
  21.9 3.0 %upwind.3 = (f32[64,72,128]{2,1,0:T(8,128)S(1)}, bf16[80,2304]{1,0:T(8,128)(2,1)S(1)}, bf16[48,2304]{1,0:T(8,128)(2,1)S(1)}) custom-call(s32[1]{0:T(128)} %bitcast.side_ref, f32[3,72,128]{2,1,0:T(8,128)S(1)} %get-tuple-element.81.speed_ref, bf16[256,512]{1,0:T(8,128)(2,1)S(1)} %fusion.picker_ref, f32[16,4,4,6912]{3,2,1,0:T(4,128)S(1)} %copy-done.1, ...), custom_call_target="tpu_custom_call" | custom-call | flops 1 | bytes 1 | tf_op jit(solution)/shard_map/upwind/pallas_call | solution.py:676
  24.9 1.9 %collective-permute-start.9 = (bf16[80,2304]{1,0:T(8,128)(2,1)S(1)}, bf16[80,2304]{1,0:T(8,128)(2,1)S(1)}, u32[]{:S(2)}, u32[]{:S(2)}) collective-permute-start(bf16[80,2304]{1,0:T(8,128)(2,1)S(1)} %get-tuple-element.57.refs_0_), channel_id=1, source_target_pairs={{0,16},{16,0},{1,17},{17,1},{2,18},{18,2},{3,19},{19,3},{4,20},{20... | collective-permute-start | bytes 1105928 | tf_op jit(solution)/shard_map/ppermute | solution.py:698
  26.8 2.0 %collective-permute-done.5.across_ref = bf16[9,32,128]{2,1,0:T(8,128)(2,1)S(1)} collective-permute-done((bf16[9,32,128]{2,1,0:T(8,128)(2,1)S(1)}, bf16[9,32,128]{2,1,0:T(8,128)(2,1)S(1)}, u32[]{:S(2)}, u32[]{:S(2)}) %collective-permute-start.5) | collective-permute-done | bytes 73760 | tf_op jit(solution)/shard_map/ppermute | solution.py:708
  28.8 3.0 %upwind.4 = (f32[64,72,128]{2,1,0:T(8,128)S(1)}, bf16[128,2304]{1,0:T(8,128)(2,1)S(1)}, bf16[48,2304]{1,0:T(8,128)(2,1)S(1)}) custom-call(s32[1]{0:T(128)} %bitcast.side_ref, f32[3,72,128]{2,1,0:T(8,128)S(1)} %get-tuple-element.82.speed_ref, bf16[256,512]{1,0:T(8,128)(2,1)S(1)} %fusion.picker_ref, f32[16,4,4,6912]{3,2,1,0:T(4,128)S(1)} %copy-done.1, ...), custom_call_target="tpu_custom_call" | custom-call | flops 1 | bytes 1 | tf_op jit(solution)/shard_map/upwind/pallas_call | solution.py:676
  31.9 2.1 %collective-permute-start.10 = (bf16[128,2304]{1,0:T(8,128)(2,1)S(1)}, bf16[128,2304]{1,0:T(8,128)(2,1)S(1)}, u32[]{:S(2)}, u32[]{:S(2)}) collective-permute-start(bf16[128,2304]{1,0:T(8,128)(2,1)S(1)} %get-tuple-element.62.refs_1_), channel_id=1, source_target_pairs={{0,16},{16,0},{1,17},{17,1},{2,18},{18,2},{3,19},{19,3},{4,20},{20... | collective-permute-start | bytes 1769480 | tf_op jit(solution)/shard_map/ppermute | solution.py:698
  34.3 3.6 %collective-permute-start.6 = (bf16[5,128,128]{2,1,0:T(8,128)(2,1)S(1)}, bf16[5,128,128]{2,1,0:T(8,128)(2,1)S(1)}, u32[]{:S(2)}, u32[]{:S(2)}) collective-permute-start(bf16[5,128,128]{2,1,0:T(8,128)(2,1)S(1)} %get-tuple-element.54), channel_id=1, source_target_pairs={{0,3},{1,0},{2,1},{3,2},{4,7},{5,4},{6,5},{7,6},{8,11},{9,8},{10,9... | collective-permute-start | bytes 491528 | tf_op jit(solution)/shard_map/ppermute | solution.py:706
  38.0 1.1 %collective-permute-start.8 = (bf16[9,32,128]{2,1,0:T(8,128)(2,1)S(1)}, bf16[9,32,128]{2,1,0:T(8,128)(2,1)S(1)}, u32[]{:S(2)}, u32[]{:S(2)}) collective-permute-start(bf16[9,32,128]{2,1,0:T(8,128)(2,1)S(1)} %get-tuple-element.56), channel_id=1, source_target_pairs={{0,12},{4,0},{8,4},{12,8},{16,20},{20,24},{24,28},{28,16},{1,13},{... | collective-permute-start | bytes 221192 | tf_op jit(solution)/shard_map/ppermute | solution.py:708
  39.0 2.0 %collective-permute-done.8.across_ref = bf16[9,32,128]{2,1,0:T(8,128)(2,1)S(1)} collective-permute-done((bf16[9,32,128]{2,1,0:T(8,128)(2,1)S(1)}, bf16[9,32,128]{2,1,0:T(8,128)(2,1)S(1)}, u32[]{:S(2)}, u32[]{:S(2)}) %collective-permute-start.8) | collective-permute-done | bytes 73760 | tf_op jit(solution)/shard_map/ppermute | solution.py:708
  41.0 1.6 %collective-permute-done.6.down_ref = bf16[5,128,128]{2,1,0:T(8,128)(2,1)S(1)} collective-permute-done((bf16[5,128,128]{2,1,0:T(8,128)(2,1)S(1)}, bf16[5,128,128]{2,1,0:T(8,128)(2,1)S(1)}, u32[]{:S(2)}, u32[]{:S(2)}) %collective-permute-start.6) | collective-permute-done | bytes 163872 | tf_op jit(solution)/shard_map/ppermute | solution.py:706
  42.6 3.9 %collective-permute-done.7.up_ref = bf16[5,128,128]{2,1,0:T(8,128)(2,1)S(1)} collective-permute-done((bf16[5,128,128]{2,1,0:T(8,128)(2,1)S(1)}, bf16[5,128,128]{2,1,0:T(8,128)(2,1)S(1)}, u32[]{:S(2)}, u32[]{:S(2)}) %collective-permute-start.7) | collective-permute-done | bytes 163872 | tf_op jit(solution)/shard_map/ppermute | solution.py:707
  47.3 3.0 %upwind.5 = (f32[64,72,128]{2,1,0:T(8,128)S(1)}, bf16[80,2304]{1,0:T(8,128)(2,1)S(1)}, bf16[48,2304]{1,0:T(8,128)(2,1)S(1)}) custom-call(s32[1]{0:T(128)} %bitcast.side_ref, f32[3,72,128]{2,1,0:T(8,128)S(1)} %get-tuple-element.83.speed_ref, bf16[256,512]{1,0:T(8,128)(2,1)S(1)} %fusion.picker_ref, f32[16,4,4,6912]{3,2,1,0:T(4,128)S(1)} %bitcast.21, ...), custom_call_target="tpu_custom_call" | custom-call | flops 1 | bytes 1 | tf_op jit(solution)/shard_map/upwind/pallas_call | solution.py:676
  50.3 1.4 %copy-done.5 = f32[64,72,128]{2,1,0:T(8,128)} copy-done((f32[64,72,128]{2,1,0:T(8,128)}, f32[64,72,128]{2,1,0:T(8,128)S(1)}, u32[]{:S(2)}) %copy-start.5) | copy-done | bytes 2359320
  53.4 8.6 %collective-permute-done.11.refs_5_ = bf16[80,2304]{1,0:T(8,128)(2,1)S(1)} collective-permute-done((bf16[80,2304]{1,0:T(8,128)(2,1)S(1)}, bf16[80,2304]{1,0:T(8,128)(2,1)S(1)}, u32[]{:S(2)}, u32[]{:S(2)}) %collective-permute-start.11) | collective-permute-done | bytes 368672 | tf_op jit(solution)/shard_map/ppermute | solution.py:698
  65.3 1.1 %reshape.245 = f32[24,576]{1,0:T(8,128)S(1)} reshape(f32[24,24,24]{2,1,0:T(8,128)} %param.11) | data formatting | bytes 110592 | tf_op jit(solution)/shard_map/reshape | solution.py:731
  66.5 1.7 %reshape.246 = f32[24,576]{1,0:T(8,128)} reshape(f32[24,24,24]{2,1,0:T(8,128)} %param.12) | data formatting | bytes 110592 | tf_op jit(solution)/shard_map/reshape | solution.py:731
  68.2 1.7 %reshape.247 = f32[24,576]{1,0:T(8,128)} reshape(f32[24,24,24]{2,1,0:T(8,128)} %param.13) | data formatting | bytes 110592 | tf_op jit(solution)/shard_map/reshape | solution.py:731
  70.8 1.2 %copy-done.16 = bf16[576,768]{1,0:T(8,128)(2,1)S(1)} copy-done((bf16[576,768]{1,0:T(8,128)(2,1)S(1)}, bf16[576,768]{1,0:T(8,128)(2,1)}, u32[]{:S(2)}) %copy-start.16) | copy-done | bytes 884760
  72.7 1.1 %copy-done.7 = bf16[128,2304]{1,0:T(8,128)(2,1)S(1)} copy-done((bf16[128,2304]{1,0:T(8,128)(2,1)S(1)}, bf16[128,2304]{1,0:T(8,128)(2,1)}, u32[]{:S(2)}) %copy-start.7) | copy-done | bytes 589848
  73.7 1.1 %copy-done.18 = bf16[128,2304]{1,0:T(8,128)(2,1)S(1)} copy-done((bf16[128,2304]{1,0:T(8,128)(2,1)S(1)}, bf16[128,2304]{1,0:T(8,128)(2,1)}, u32[]{:S(2)}) %copy-start.18) | copy-done | bytes 589848
  74.8 1.0 copy-done.20
  75.8 1.0 copy-done.22
  76.8 1.0 copy-done.24
  78.8 12.2 %collide.1.early_ref = bf16[80,6912]{1,0:T(8,128)(2,1)S(1)} custom-call(f32[3,24,384]{2,1,0:T(8,128)S(1)} %weights.1.weight_ref, bf16[704,768]{1,0:T(8,128)(2,1)S(1)} %copy-done.2, bf16[80,2304]{1,0:T(8,128)(2,1)S(1)} %copy-done.20, bf16[128,2304]{1,0:T(8,128)(2,1)S(1)} %copy-done.18, bf16[80,2304]{1,0:T(8,128)(2,1)S(1)} %copy-done.24, ...), custom_call_target="tpu_custom_call" | custom-call | flops 1 | bytes 1 | tf_op jit(solution)/shard_map/collide/pallas_call | solution.py:742
  91.1 13.5 %finish.1 = f32[16,4,4,6912]{3,2,1,0:T(4,128)} custom-call(f32[3,24,384]{2,1,0:T(8,128)S(1)} %weights.1.weight_ref, bf16[704,768]{1,0:T(8,128)(2,1)S(1)} %copy-done.2, bf16[512,256]{1,0:T(8,128)(2,1)S(1)} %copy-done.9, bf16[80,6912]{1,0:T(8,128)(2,1)S(1)} %collide.1.early_ref, bf16[48,2304]{1,0:T(8,128)(2,1)S(1)} %copy-done.15, ...), custom_call_target="tpu_custom_call" | custom-call | tf_op jit(solution)/shard_map/finish/pallas_call | solution.py:754
  (98 shorter events, 10.5 us)
Async XLA Ops:
  0.0 9.0 %copy-start.29 = (s32[16,4,4]{0,2,1:T(4,128)S(1)}, s32[16,4,4]{0,2,1:T(4,128)}, u32[]{:S(2)}) copy-start(s32[16,4,4]{0,2,1:T(4,128)} %param.10) | copy-start | bytes 3076
  0.0 10.4 %copy-start.27 = (f32[72,128]{1,0:T(8,128)S(1)}, f32[72,128]{1,0:T(8,128)}, u32[]{:S(2)}) copy-start(f32[72,128]{1,0:T(8,128)} %constant.81.clone.falls_ref) | copy-start | bytes 110596
  2.9 11.6 %collective-permute-start.2 = (bf16[9,32,128]{2,1,0:T(8,128)(2,1)}, bf16[9,32,128]{2,1,0:T(8,128)(2,1)S(1)}, u32[]{:S(2)}, u32[]{:S(2)}) collective-permute-start(bf16[9,32,128]{2,1,0:T(8,128)(2,1)} %get-tuple-element.50), channel_id=1, source_target_pairs={{0,12},{4,0},{8,4},{12,8},{16,20},{20,24},{24,28},{28,16},{1,13},{... | collective-permute-start | bytes 221192 | tf_op jit(solution)/shard_map/ppermute | solution.py:708
  5.4 9.2 %collective-permute-start = (bf16[5,128,128]{2,1,0:T(8,128)(2,1)}, bf16[5,128,128]{2,1,0:T(8,128)(2,1)S(1)}, u32[]{:S(2)}, u32[]{:S(2)}) collective-permute-start(bf16[5,128,128]{2,1,0:T(8,128)(2,1)} %get-tuple-element.48), channel_id=1, source_target_pairs={{0,3},{1,0},{2,1},{3,2},{4,7},{5,4},{6,5},{7,6},{8,11},{9,8},{10,9... | collective-permute-start | bytes 491528 | tf_op jit(solution)/shard_map/ppermute | solution.py:706
  9.0 7.8 %collective-permute-start.1 = (bf16[5,128,128]{2,1,0:T(8,128)(2,1)}, bf16[5,128,128]{2,1,0:T(8,128)(2,1)S(1)}, u32[]{:S(2)}, u32[]{:S(2)}) collective-permute-start(bf16[5,128,128]{2,1,0:T(8,128)(2,1)} %get-tuple-element.49), channel_id=1, source_target_pairs={{0,1},{1,2},{2,3},{3,0},{4,5},{5,6},{6,7},{7,4},{8,9},{9,10},{10,1... | collective-permute-start | bytes 491528 | tf_op jit(solution)/shard_map/ppermute | solution.py:707
  10.4 3.0 %copy-start = (f32[16,4,4,6912]{3,2,1,0:T(4,128)S(1)}, f32[16,4,4,6912]{3,2,1,0:T(4,128)}, u32[]{:S(2)}) copy-start(f32[16,4,4,6912]{3,2,1,0:T(4,128)} %field_ref.11) | copy-start | bytes 21233668
  16.8 12.0 %collective-permute-start.3 = (bf16[5,128,128]{2,1,0:T(8,128)(2,1)}, bf16[5,128,128]{2,1,0:T(8,128)(2,1)S(1)}, u32[]{:S(2)}, u32[]{:S(2)}) collective-permute-start(bf16[5,128,128]{2,1,0:T(8,128)(2,1)} %get-tuple-element.51), channel_id=1, source_target_pairs={{0,3},{1,0},{2,1},{3,2},{4,7},{5,4},{6,5},{7,6},{8,11},{9,8},{10,9... | collective-permute-start | bytes 491528 | tf_op jit(solution)/shard_map/ppermute | solution.py:706
  18.5 10.3 %collective-permute-start.4 = (bf16[5,128,128]{2,1,0:T(8,128)(2,1)}, bf16[5,128,128]{2,1,0:T(8,128)(2,1)S(1)}, u32[]{:S(2)}, u32[]{:S(2)}) collective-permute-start(bf16[5,128,128]{2,1,0:T(8,128)(2,1)} %get-tuple-element.52), channel_id=1, source_target_pairs={{0,1},{1,2},{2,3},{3,0},{4,5},{5,6},{6,7},{7,4},{8,9},{9,10},{10,1... | collective-permute-start | bytes 491528 | tf_op jit(solution)/shard_map/ppermute | solution.py:707
  18.9 3.0 %copy-start.1 = (f32[16,4,4,6912]{3,2,1,0:T(4,128)S(1)}, f32[16,4,4,6912]{3,2,1,0:T(4,128)}, u32[]{:S(2)}) copy-start(f32[16,4,4,6912]{3,2,1,0:T(4,128)} %field_ref.11) | copy-start | bytes 21233668
  21.9 12.1 %slice-start = ((s8[7077888]{0:T(1024)(128)(4,1)}), s8[4194304]{0:T(1024)(128)(4,1)S(1)}, s32[]{:S(2)}) async-start(s8[7077888]{0:T(1024)(128)(4,1)} %bitcast.20), calls=%async_computation | async-start | bytes 8388608
  24.9 7.0 %copy-start.14 = (bf16[48,2304]{1,0:T(8,128)(2,1)}, bf16[48,2304]{1,0:T(8,128)(2,1)S(1)}, u32[]{:S(2)}) copy-start(bf16[48,2304]{1,0:T(8,128)(2,1)S(1)} %get-tuple-element.61.refs_0_) | copy-start | bytes 663556
  24.9 7.0 %copy-start.19 = (bf16[80,2304]{1,0:T(8,128)(2,1)}, bf16[80,2304]{1,0:T(8,128)(2,1)S(1)}, u32[]{:S(2)}) copy-start(bf16[80,2304]{1,0:T(8,128)(2,1)S(1)} %get-tuple-element.57.refs_0_) | copy-start | bytes 1105924
  24.9 21.6 %collective-permute-start.9 = (bf16[80,2304]{1,0:T(8,128)(2,1)S(1)}, bf16[80,2304]{1,0:T(8,128)(2,1)S(1)}, u32[]{:S(2)}, u32[]{:S(2)}) collective-permute-start(bf16[80,2304]{1,0:T(8,128)(2,1)S(1)} %get-tuple-element.57.refs_0_), channel_id=1, source_target_pairs={{0,16},{16,0},{1,17},{17,1},{2,18},{18,2},{3,19},{19,3},{4,20},{20... | collective-permute-start | bytes 1105928 | tf_op jit(solution)/shard_map/ppermute | solution.py:698
  26.8 2.0 %collective-permute-start.5 = (bf16[9,32,128]{2,1,0:T(8,128)(2,1)S(1)}, bf16[9,32,128]{2,1,0:T(8,128)(2,1)S(1)}, u32[]{:S(2)}, u32[]{:S(2)}) collective-permute-start(bf16[9,32,128]{2,1,0:T(8,128)(2,1)S(1)} %get-tuple-element.53), channel_id=1, source_target_pairs={{0,12},{4,0},{8,4},{12,8},{16,20},{20,24},{24,28},{28,16},{1,13},{... | collective-permute-start | bytes 221192 | tf_op jit(solution)/shard_map/ppermute | solution.py:708
  28.8 5.2 %slice-start.1 = ((s8[7077888]{0:T(1024)(128)(4,1)}), s8[2883584]{0:T(1024)(128)(4,1)S(1)}, s32[]{:S(2)}) async-start(s8[7077888]{0:T(1024)(128)(4,1)} %bitcast.20), calls=%async_computation.1 | async-start | bytes 5767168
  31.9 20.7 %copy-start.10 = (bf16[48,2304]{1,0:T(8,128)(2,1)}, bf16[48,2304]{1,0:T(8,128)(2,1)S(1)}, u32[]{:S(2)}) copy-start(bf16[48,2304]{1,0:T(8,128)(2,1)S(1)} %get-tuple-element.73.refs_1_) | copy-start | bytes 663556
  31.9 30.8 %collective-permute-start.10 = (bf16[128,2304]{1,0:T(8,128)(2,1)S(1)}, bf16[128,2304]{1,0:T(8,128)(2,1)S(1)}, u32[]{:S(2)}, u32[]{:S(2)}) collective-permute-start(bf16[128,2304]{1,0:T(8,128)(2,1)S(1)} %get-tuple-element.62.refs_1_), channel_id=1, source_target_pairs={{0,16},{16,0},{1,17},{17,1},{2,18},{18,2},{3,19},{19,3},{4,20},{20... | collective-permute-start | bytes 1769480 | tf_op jit(solution)/shard_map/ppermute | solution.py:698
  34.3 8.2 %collective-permute-start.6 = (bf16[5,128,128]{2,1,0:T(8,128)(2,1)S(1)}, bf16[5,128,128]{2,1,0:T(8,128)(2,1)S(1)}, u32[]{:S(2)}, u32[]{:S(2)}) collective-permute-start(bf16[5,128,128]{2,1,0:T(8,128)(2,1)S(1)} %get-tuple-element.54), channel_id=1, source_target_pairs={{0,3},{1,0},{2,1},{3,2},{4,7},{5,4},{6,5},{7,6},{8,11},{9,8},{10,9... | collective-permute-start | bytes 491528 | tf_op jit(solution)/shard_map/ppermute | solution.py:706
  38.0 8.6 %collective-permute-start.7 = (bf16[5,128,128]{2,1,0:T(8,128)(2,1)S(1)}, bf16[5,128,128]{2,1,0:T(8,128)(2,1)S(1)}, u32[]{:S(2)}, u32[]{:S(2)}) collective-permute-start(bf16[5,128,128]{2,1,0:T(8,128)(2,1)S(1)} %get-tuple-element.55), channel_id=1, source_target_pairs={{0,1},{1,2},{2,3},{3,0},{4,5},{5,6},{6,7},{7,4},{8,9},{9,10},{10,1... | collective-permute-start | bytes 491528 | tf_op jit(solution)/shard_map/ppermute | solution.py:707
  38.0 3.0 %collective-permute-start.8 = (bf16[9,32,128]{2,1,0:T(8,128)(2,1)S(1)}, bf16[9,32,128]{2,1,0:T(8,128)(2,1)S(1)}, u32[]{:S(2)}, u32[]{:S(2)}) collective-permute-start(bf16[9,32,128]{2,1,0:T(8,128)(2,1)S(1)} %get-tuple-element.56), channel_id=1, source_target_pairs={{0,12},{4,0},{8,4},{12,8},{16,20},{20,24},{24,28},{28,16},{1,13},{... | collective-permute-start | bytes 221192 | tf_op jit(solution)/shard_map/ppermute | solution.py:708
  51.7 11.1 %copy-start.12 = (bf16[48,2304]{1,0:T(8,128)(2,1)}, bf16[48,2304]{1,0:T(8,128)(2,1)S(1)}, u32[]{:S(2)}) copy-start(bf16[48,2304]{1,0:T(8,128)(2,1)S(1)} %get-tuple-element.74.refs_2_) | copy-start | bytes 663556
  51.7 12.4 %copy-start.23 = (bf16[80,2304]{1,0:T(8,128)(2,1)}, bf16[80,2304]{1,0:T(8,128)(2,1)S(1)}, u32[]{:S(2)}) copy-start(bf16[80,2304]{1,0:T(8,128)(2,1)S(1)} %get-tuple-element.69.refs_2_) | copy-start | bytes 1105924
  51.7 19.0 %copy-start.28 = (f32[1,384]{1,0:T(1,128)S(1)}, f32[1,384]{1,0:T(1,128)}, u32[]{:S(2)}) copy-start(f32[1,384]{1,0:T(1,128)} %constant.84.clone.scale_ref) | copy-start | bytes 4612
  51.7 20.9 %copy-start.2 = (bf16[704,768]{1,0:T(8,128)(2,1)S(1)}, bf16[704,768]{1,0:T(8,128)(2,1)}, u32[]{:S(2)}) copy-start(bf16[704,768]{1,0:T(8,128)(2,1)} %constant.82.clone.table_ref) | copy-start | bytes 3244036
  51.7 10.3 %collective-permute-start.11 = (bf16[80,2304]{1,0:T(8,128)(2,1)S(1)}, bf16[80,2304]{1,0:T(8,128)(2,1)S(1)}, u32[]{:S(2)}, u32[]{:S(2)}) collective-permute-start(bf16[80,2304]{1,0:T(8,128)(2,1)S(1)} %get-tuple-element.69.refs_2_), channel_id=1, source_target_pairs={{0,16},{16,0},{1,17},{17,1},{2,18},{18,2},{3,19},{19,3},{4,20},{20... | collective-permute-start | bytes 1105928 | tf_op jit(solution)/shard_map/ppermute | solution.py:698
  63.6 27.4 %collective-permute-start.12 = (bf16[96,2304]{1,0:T(8,128)(2,1)}, bf16[96,2304]{1,0:T(8,128)(2,1)}, u32[]{:S(2)}, u32[]{:S(2)}) collective-permute-start(bf16[96,2304]{1,0:T(8,128)(2,1)} %pad_maximum_fusion), channel_id=1, source_target_pairs={{0,16},{16,0},{1,17},{17,1},{2,18},{18,2},{3,19},{19,3},{4,20},{20... | collective-permute-start | bytes 1327112 | tf_op jit(solution)/shard_map/ppermute | solution.py:698
  78.7 12.3 %copy-start.4 = (f32[64,72,128]{2,1,0:T(8,128)S(1)}, f32[64,72,128]{2,1,0:T(8,128)}, u32[]{:S(2)}) copy-start(f32[64,72,128]{2,1,0:T(8,128)} %copy-done.3) | copy-start | bytes 7077892
  78.7 12.3 %copy-start.8 = (bf16[128,2304]{1,0:T(8,128)(2,1)S(1)}, bf16[128,2304]{1,0:T(8,128)(2,1)}, u32[]{:S(2)}) copy-start(bf16[128,2304]{1,0:T(8,128)(2,1)} %copy-done.6) | copy-start | bytes 1769476
  78.7 12.3 %copy-start.9 = (bf16[512,256]{1,0:T(8,128)(2,1)S(1)}, bf16[512,256]{1,0:T(8,128)(2,1)}, u32[]{:S(2)}) copy-start(bf16[512,256]{1,0:T(8,128)(2,1)} %select_convert_fusion.spread_ref) | copy-start | bytes 786436
  78.7 12.3 %copy-start.11 = (bf16[48,2304]{1,0:T(8,128)(2,1)S(1)}, bf16[48,2304]{1,0:T(8,128)(2,1)}, u32[]{:S(2)}) copy-start(bf16[48,2304]{1,0:T(8,128)(2,1)} %copy-done.10) | copy-start | bytes 663556
  78.7 12.3 %copy-start.13 = (bf16[48,2304]{1,0:T(8,128)(2,1)S(1)}, bf16[48,2304]{1,0:T(8,128)(2,1)}, u32[]{:S(2)}) copy-start(bf16[48,2304]{1,0:T(8,128)(2,1)} %copy-done.12) | copy-start | bytes 663556
  78.8 12.3 %copy-start.15 = (bf16[48,2304]{1,0:T(8,128)(2,1)S(1)}, bf16[48,2304]{1,0:T(8,128)(2,1)}, u32[]{:S(2)}) copy-start(bf16[48,2304]{1,0:T(8,128)(2,1)} %copy-done.14) | copy-start | bytes 663556
  (13 other events, 15.8 us)

commit v4 on v3

--- a/solution.py
+++ b/solution.py
@@ -255,10 +255,12 @@
     return jnp.concatenate(parts, axis=1)
 
 
-def edges_kernel(
-    first, edge_ref, falls_ref, field_ref, down_ref, up_ref, across_ref, low_ref, high_ref, plane_ref, sems
-):
+def edges_kernel(first, edge_ref, falls_ref, field_ref, *refs):
+    down_ref, up_ref, across_ref, low_ref, high_ref, plane_ref, sems = refs
     steps = falls_ref.shape[0] // 8
+    width = low_ref.shape[0]
+    groups = across_ref.shape[0] // steps
+    half_steps = down_ref.shape[0] // groups
     here = pl.ds(first, low_ref.shape[3])
     last_y = field_ref.shape[1] - 1
     sources = [
@@ -272,29 +274,32 @@
     ]
     for load in loads:
         load.start()
-    width = low_ref.shape[0]
     below = [falls_ref[8 * s : 8 * s + 8, :][None] > 0.0 for s in range(steps)]
 
     def put(ref, at, value):
         ref[at] = value.reshape(-1, LANES).astype(jnp.bfloat16)
 
     loads[0].wait()
-    lowest = [tile_pair(low_ref, s, width) for s in range(steps)]
-    put(down_ref, 0, lowest[0])
-    for m in range(1, steps // 2 + 1):
-        put(down_ref, m, jnp.where(below[2 * m - 1], lowest[2 * m - 1], lowest[2 * m]))
+    for g in range(groups):
+        row = [tile_pair(low_ref, g * steps + s, width) for s in range(steps)]
+        put(down_ref, g * half_steps, row[0])
+        for m in range(1, steps // 2 + 1):
+            put(down_ref, g * half_steps + m, jnp.where(below[2 * m - 1], row[2 * m - 1], row[2 * m]))
     loads[1].wait()
-    last = [tile_pair(high_ref, s, width) for s in range(steps)]
-    for m in range(steps // 2):
-        put(up_ref, m, jnp.where(below[2 * m], last[2 * m + 1], last[2 * m]))
-    put(up_ref, steps // 2, last[steps - 1])
+    for g in range(groups):
+        row = [tile_pair(high_ref, g * steps + s, width) for s in range(steps)]
+        for m in range(steps // 2):
+            put(up_ref, g * half_steps + m, jnp.where(below[2 * m], row[2 * m + 1], row[2 * m]))
+        put(up_ref, g * half_steps + steps // 2, row[steps - 1])
     loads[2].wait()
-    for s in range(steps):
+    for s in range(groups * steps):
         put(across_ref, s, tile_pair(plane_ref, s, plane_ref.shape[1]))
 
 
 def upwind_kernel(
     base,
+    place_at,
+    into_late,
     side_ref,
     speed_ref,
     picker_ref,
@@ -316,10 +321,15 @@
     beside = jnp.where(side_ref[0] == 0, 2, 0)
     place = lax.broadcasted_iota(jnp.int32, (1, 8, LANES), 1) % width_z
     capacity = picker_ref.shape[0] // 2
-    late = late_ref.shape[0]
+    late = carried_refs[0].shape[0] if carried_refs else late_ref.shape[0]
     early = capacity - late
+    late_at = late_ref.shape[0] - late
     for ref in carried_refs:
-        early_ref[early:, :] = ref[...]
+        if into_late:
+            late_ref[:late, :] = ref[...]
+        else:
+            early_ref[early:, :] = ref[...]
+    half_steps = chunks * steps // 2 + 1
     for t in range(chunks):
         sizes, falls, sinks = [], [], []
         for u in range(steps):
@@ -328,12 +338,13 @@
             sizes.append([jnp.abs(c) for c in speed])
             falls.append(speed[1] < 0.0)
             sinks.append(speed[2] < 0.0)
-            outer = across_ref[step].astype(jnp.float32).reshape(width_y, 8, LANES)
+            outer = across_ref[place_at * chunks * steps + step].astype(jnp.float32).reshape(width_y, 8, LANES)
             wide[u, 0] = outer
             wide[u, width_x + 1] = outer
-            above = down_ref[(step + 1) // 2].astype(jnp.float32).reshape(width_x, 8, LANES)
-            under = up_ref[step // 2].astype(jnp.float32).reshape(width_x, 8, LANES)
-            border[u] = jnp.where(falls[u], above, under)
+            above = down_ref[place_at * half_steps + (step + 1) // 2].astype(jnp.float32)
+            under = up_ref[place_at * half_steps + step // 2].astype(jnp.float32)
+            shape = (width_x, 8, LANES)
+            border[u] = jnp.where(falls[u], above.reshape(shape), under.reshape(shape))
         loads[t].wait()
 
         def spread_out(x, carry):
@@ -384,31 +395,44 @@
                 here = slice(tile * LANES, (tile + 1) * LANES)
                 values = picked[first : first + capacity, u * LANES : (u + 1) * LANES]
                 early_ref[:early, here] = values[:early]
-                late_ref[:, here] = values[early:]
-
-
-def filter_parts(parts, weight_ref, table_ref, own_refs, other_refs, section, back):
-    slots = section.shape[1]
+                late_ref[late_at:, here] = values[early:]
+
+
+def window_loads(firsts, refs, cells, sems):
+    loads = []
+    for at, (ref, first) in enumerate(zip(refs, firsts)):
+        source = ref.at[pl.ds(first, cells.shape[1])]
+        loads.append(pltpu.make_async_copy(source, cells.at[at], sems.at[at]))
+        loads[-1].start()
+    return loads
+
+
+def filter_parts(weight_ref, table_ref, cells, loads, section, back):
+    count, slots, lanes = cells.shape
     padded = weight_ref.shape[2]
     height = table_ref.shape[0]
     window = height - 64
     pair_lanes = 2 * (height - 128)
-    pairs = own_refs[0][0].shape[1] // pair_lanes
-    half = 2 * pairs * parts
-    for parity in range(2):
-        rows = []
-        for ref, first in own_refs + other_refs:
-            for p in range(pairs):
-                at = p * pair_lanes + parity * (pair_lanes - window)
-                rows.append(ref[first : first + slots, at : at + window])
-        start = 64 * (1 - parity)
-        out = jnp.dot(
-            jnp.concatenate(rows, axis=0),
-            table_ref[start : start + window, :],
-            preferred_element_type=jnp.float32,
-        )
-        for at in range(half):
-            section[2 * at + parity] = out[at * slots : (at + 1) * slots]
+    pairs = lanes // pair_lanes
+    half = pairs * count
+    for side in range(2):
+        here = range(side * count // 2, (side + 1) * count // 2)
+        for at in here:
+            loads[at].wait()
+        for parity in range(2):
+            rows = []
+            for at in here:
+                for p in range(pairs):
+                    lane = p * pair_lanes + parity * (pair_lanes - window)
+                    rows.append(cells[at, :, lane : lane + window])
+            start = 64 * (1 - parity)
+            out = jnp.dot(
+                jnp.concatenate(rows, axis=0),
+                table_ref[start : start + window, :],
+                preferred_element_type=jnp.float32,
+            )
+            for at in range(half // 2):
+                section[side * half + 2 * at + parity] = out[at * slots : (at + 1) * slots]
 
     lane_tiles = padded // LANES
 
@@ -444,9 +468,8 @@
     lax.fori_loop(0, slots // 16 * lane_tiles, transform, 0)
 
 
-def terms_of(part, table_ref, own, back, put):
-    own_ref, first = own
-    slots, lanes = back.shape[3], own_ref.shape[1]
+def terms_of(part, table_ref, cells_ref, back, put):
+    _, slots, lanes = cells_ref.shape
     height = table_ref.shape[0]
     window = height - 64
     pair_lanes = 2 * (height - 128)
@@ -484,42 +507,44 @@
                     )
                 values.append(value)
             lane = at * pair_lanes + lane
-            cells = own_ref[first : first + slots, lane : lane + LANES].astype(jnp.float32)
+            cells = cells_ref[part, :, lane : lane + LANES].astype(jnp.float32)
             put(at * tiles + tile, (values[0] * values[1] - cells * values[2]).astype(jnp.bfloat16))
 
 
 def collide_kernel(firsts, weight_ref, table_ref, *refs):
     parts = len(firsts) // 2
-    windows = list(zip(refs, firsts))
-    own_refs, other_refs = windows[:parts], windows[parts:]
-    terms_ref, section, back = refs[2 * parts :]
-    filter_parts(parts, weight_ref, table_ref, own_refs, other_refs, section, back)
+    terms_ref, cells, section, back, sems = refs[2 * parts :]
+    lanes = cells.shape[2]
+    loads = window_loads(firsts, refs[: 2 * parts], cells, sems)
+    filter_parts(weight_ref, table_ref, cells, loads, section, back)
     for part in range(parts):
-        first = part * own_refs[0][0].shape[1]
 
         def put(tile, value):
-            terms_ref[:, first + tile * LANES : first + (tile + 1) * LANES] = value
-
-        terms_of(part, table_ref, own_refs[part], back, put)
+            first = part * lanes + tile * LANES
+            terms_ref[:, first : first + LANES] = value
+
+        terms_of(part, table_ref, cells, back, put)
 
 
 def finish_kernel(firsts, weight_ref, table_ref, spread_ref, early_ref, *refs):
     parts = len(firsts) // 2
-    windows = list(zip(refs, firsts))
-    own_refs, other_refs = windows[:parts], windows[parts:]
     read_refs = refs[2 * parts : 3 * parts]
-    out_ref, section, back, reads, spots, added, staged, read_sems, out_sems = refs[3 * parts :]
+    out_ref, cells, section, back, reads, spots, added, staged = refs[3 * parts : -3]
+    cell_sems, read_sems, out_sems = refs[-3:]
     width_x, width_y, width_z, lanes = staged.shape[1:]
     tiles = lanes // LANES
-    loads = [
+    loads = window_loads(firsts, refs[: 2 * parts], cells, cell_sems)
+    read_loads = [
         pltpu.make_async_copy(read_refs[part], reads.at[part], read_sems.at[part])
         for part in range(parts)
     ]
-    for load in loads:
+    for load in read_loads:
         load.start()
-    filter_parts(parts, weight_ref, table_ref, own_refs, other_refs, section, back)
+    filter_parts(weight_ref, table_ref, cells, loads, section, back)
     early = early_ref.shape[0]
     capacity = early + section.shape[1]
+    pieces = out_sems.shape[1]
+    piece_x = width_x // pieces
     stores = []
     for part in range(parts):
 
@@ -530,12 +555,13 @@
             spots[first : first + early, columns] = early_ref[:, lane : lane + LANES]
             spots[first + early : first + capacity, columns] = value
 
-        terms_of(part, table_ref, own_refs[part], back, put)
+        terms_of(part, table_ref, cells, back, put)
         added[...] = jnp.dot(spread_ref[...], spots[...], preferred_element_type=jnp.float32)
-        loads[part].wait()
+        read_loads[part].wait()
         slot = part % 2
         if part >= 2:
-            stores[part - 2].wait()
+            for store in stores[part - 2]:
+                store.wait()
 
         def add(x, carry):
             for y in range(width_y):
@@ -548,20 +574,24 @@
                     )
                     for parity in range(2):
                         lane = (2 * u + parity) * LANES
-                        piece = value[parity * width_z : (parity + 1) * width_z]
-                        staged[slot, x, y, :, lane : lane + LANES] = piece
+                        half = value[parity * width_z : (parity + 1) * width_z]
+                        staged[slot, x, y, :, lane : lane + LANES] = half
             return carry
 
-        lax.fori_loop(0, width_x, add, 0)
-        store = pltpu.make_async_copy(
-            staged.at[slot],
-            out_ref.at[:, :, :, part * lanes : (part + 1) * lanes],
-            out_sems.at[part],
-        )
-        store.start()
-        stores.append(store)
-    for store in stores[-2:]:
-        store.wait()
+        stores.append([])
+        for piece in range(pieces):
+            lax.fori_loop(piece * piece_x, (piece + 1) * piece_x, add, 0)
+            rows = pl.ds(piece * piece_x, piece_x)
+            store = pltpu.make_async_copy(
+                staged.at[slot, rows],
+                out_ref.at[rows, :, :, pl.ds(part * lanes, lanes)],
+                out_sems.at[part, piece],
+            )
+            store.start()
+            stores[part].append(store)
+    for part in range(max(parts - 2, 0), parts):
+        for store in stores[part]:
+            store.wait()
 
 
 def params(mib):
@@ -580,7 +610,7 @@
         and lax.axis_size("vel") == 2
         and width_z == 4
         and local_vel * 2 == points**3
-        and local_vel % group == 0
+        and local_vel == 3 * group
         and width_x * width_y * width_z % 128 == 0
     )
 
@@ -646,35 +676,39 @@
     scalar = pl.BlockSpec(memory_space=pltpu.SMEM)
     remote = pl.BlockSpec(memory_space=pltpu.HBM)
 
-    def edges_of(g):
+    def edges_of(first, groups):
         return pl.pallas_call(
-            functools.partial(edges_kernel, g * group),
+            functools.partial(edges_kernel, first * group),
             in_specs=[scalar, local, remote],
             out_specs=[local] * 3,
             out_shape=[
-                jax.ShapeDtypeStruct((half_steps, width_x * 8, LANES), bf16),
-                jax.ShapeDtypeStruct((half_steps, width_x * 8, LANES), bf16),
-                jax.ShapeDtypeStruct((steps, width_y * 8, LANES), bf16),
+                jax.ShapeDtypeStruct((groups * half_steps, width_x * 8, LANES), bf16),
+                jax.ShapeDtypeStruct((groups * half_steps, width_x * 8, LANES), bf16),
+                jax.ShapeDtypeStruct((groups * steps, width_y * 8, LANES), bf16),
             ],
             scratch_shapes=[
-                pltpu.VMEM((width_x, 1, width_z, group), jnp.float32),
-                pltpu.VMEM((width_x, 1, width_z, group), jnp.float32),
-                pltpu.VMEM((1, width_y, width_z, group), jnp.float32),
+                pltpu.VMEM((width_x, 1, width_z, groups * group), jnp.float32),
+                pltpu.VMEM((width_x, 1, width_z, groups * group), jnp.float32),
+                pltpu.VMEM((1, width_y, width_z, groups * group), jnp.float32),
                 pltpu.SemaphoreType.DMA((3,)),
             ],
-            compiler_params=params(58 if g == 0 else 16),
+            compiler_params=params(16),
             cost_estimate=cost(1, 1),
             name="edges",
         )(edge, falls, distribution)
 
-    edges = [edges_of(g) for g in range(parts)]
+    edges = [edges_of(0, 1), edges_of(1, parts - 1)]
     wide = 3
     chunks = steps // wide
 
     def upwind(g, halo, carried):
-        heights = (capacity if carried else counts[0], counts[1])
+        into_late = g > 1
+        heights = (
+            capacity if carried and not into_late else counts[0],
+            2 * counts[1] if carried and into_late else counts[1],
+        )
         return pl.pallas_call(
-            functools.partial(upwind_kernel, g * group),
+            functools.partial(upwind_kernel, g * group, max(g - 1, 0), into_late),
             in_specs=[scalar, local, local, remote] + [local] * (len(halo) + len(carried)),
             out_specs=[local] * 3,
             out_shape=[jax.ShapeDtypeStruct((block_rows, group_rows, LANES), jnp.float32)]
@@ -697,9 +731,9 @@
     def swapped(value):
         return lax.ppermute(value, "vel", swap)
 
-    reads, firsts, lasts, halos, early = [], [], [], [], []
-    for g in range(parts):
-        operands = edges[g] if g == 0 else turn(edges[g], halos[-1])
+    halos = []
+    for at in range(2):
+        operands = edges[at] if at == 0 else turn(edges[at], halos[0])
         down, up, across = operands
         halos.append(
             (
@@ -708,18 +742,14 @@
                 lax.ppermute(across, ("vel", "cx"), across_pairs),
             )
         )
+    reads, firsts, lasts, early = [], [], [], []
     for g in range(parts):
-        halo = halos[g] if g == 0 else turn(halos[g], firsts[-1])
-        if g > 1:
-            halo = turn(halo, early[g - 2])
-        read, first, last = upwind(g, halo, lasts[:1] if g == 1 else [])
+        halo = halos[0] if g == 0 else turn(halos[1], firsts[-1], *early[: g - 1])
+        read, first, last = upwind(g, halo, lasts[-1:])
         reads.append(read)
         firsts.append(first)
         lasts.append(last)
         early.append(swapped(first))
-    later = turn(jnp.concatenate(lasts[1:], axis=0), *early[1:])
-    late = swapped(later)
-
     kernels = turn((gain_one, gain_two, loss_kernel), firsts[-1])
     weights = pl.pallas_call(
         weights_kernel,
@@ -733,27 +763,35 @@
         jnp.asarray(scale),
     )
 
+    last, weights, spread = turn((lasts[-1], weights, spread), *early)
+    late = swapped(last)
+
     def scratch(count):
         return [
+            pltpu.VMEM((2 * parts, count, group), bf16),
             pltpu.VMEM((points, count, 2 * padded), jnp.float32),
             pltpu.VMEM((2, 3, points // 4, count, 2 * padded), bf16),
         ]
 
+    anywhere = pl.BlockSpec(memory_space=pl.ANY)
+    sems = pltpu.SemaphoreType.DMA((2 * parts,))
     terms = pl.pallas_call(
         functools.partial(collide_kernel, (0,) * (2 * parts)),
+        in_specs=[local] * 2 + [anywhere] * (2 * parts),
+        out_specs=local,
         out_shape=jax.ShapeDtypeStruct((counts[0], local_vel), bf16),
-        scratch_shapes=scratch(counts[0]),
-        compiler_params=params(32),
+        scratch_shapes=scratch(counts[0]) + [sems],
+        compiler_params=params(28),
         cost_estimate=cost(1, 1),
-            name="collide",
+        name="collide",
     )(weights, table, *firsts, *early)
 
-    lates = [early[1]] + [late] * (parts - 1)
-    late_firsts = (0,) * parts + (counts[0],) + tuple(counts[1] * g for g in range(parts - 1))
-    anywhere = pl.BlockSpec(memory_space=pl.ANY)
+    pieces = 4
+    own_late = (0, 0, counts[1])
+    other_late = (counts[0], 0, counts[1])
     return pl.pallas_call(
-        functools.partial(finish_kernel, late_firsts),
-        in_specs=[local] * (4 + 2 * parts) + [anywhere] * parts,
+        functools.partial(finish_kernel, own_late + other_late),
+        in_specs=[local] * 4 + [anywhere] * (3 * parts),
         out_specs=anywhere,
         out_shape=jax.ShapeDtypeStruct(distribution.shape, jnp.float32),
         scratch_shapes=scratch(counts[1])
@@ -762,12 +800,13 @@
             pltpu.VMEM((2 * capacity, group // 2), bf16),
             pltpu.VMEM((block_rows * 8, group // 2), jnp.float32),
             pltpu.VMEM((2, width_x, width_y, width_z, group), jnp.float32),
+            sems,
             pltpu.SemaphoreType.DMA((parts,)),
-            pltpu.SemaphoreType.DMA((parts,)),
+            pltpu.SemaphoreType.DMA((parts, pieces)),
         ],
-        compiler_params=params(44),
+        compiler_params=params(36),
         name="finish",
-    )(weights, table, spread, terms, *lasts, *lates, *reads)
+    )(weights, table, spread, terms, lasts[0], last, last, early[1], late, late, *reads)
 
 
 def per_device(distribution, refine_level, gain_one, gain_two, loss_kernel):

time: 105 us -> 105 us (level)
  waiting for transfers between devices: 20.3 us -> 29.4 us
  starting transfers between devices: 18.2 us -> 13.6 us
  local copies, waits for them, and re-layouts: 22.9 us -> 19.2 us
  other arithmetic: 3.05 us -> 1.5 us
    ppermute x3 -> x2, waiting for transfers between devices: 1.6 us -> 8.63 us  [fast_device(): lax.ppermute(down, 'cy', towards_lower)]
    unnamed x64 -> x38, local copies, waits for them, and re-layouts: 17 us -> 13.3 us
    ppermute x3 -> x2, waiting for transfers between devices: 6.17 us -> 9.61 us  [fast_device(): lax.ppermute(up, 'cy', towards_upper)]
    ppermute x3 -> x2, starting transfers between devices: 8.96 us -> 5.54 us  [fast_device(): lax.ppermute(down, 'cy', towards_lower)]
    ppermute x3 -> x2, waiting for transfers between devices: 3.97 us -> 2.68 us  [fast_device(): lax.ppermute(across, ('vel', 'cx'), across_pairs)]
    ppermute x3 -> x2, starting transfers between devices: 3.52 us -> 2.46 us  [fast_device(): lax.ppermute(across, ('vel', 'cx'), across_pairs)]
    pallas_call x8 -> x7, Pallas kernels: 39.1 us -> 39.4 us  [the longest x1 14.2 us: fast_device(): pl.pallas_call(functools.partial(finish_kernel, own_late + other_late), i...]
  transfers between devices with their start and end apart: 13 -> 10, of which waited for: 6 -> 6; matrix products, arithmetic and copies ran while one was open for 8% -> 7% of each run, Pallas kernels for 22% -> 22%
where the time goes in v4:
time: 105 us; the launch traced here: 104 us
  Pallas kernels  40.1 us (38%)
  waiting for transfers between devices  29.4 us (28%)
  local copies, waits for them, and re-layouts  19.2 us (18%)
  starting transfers between devices  13.6 us (13%)
  other arithmetic  1.5 us (1%)
    pallas_call x1, Pallas kernels, fast_device(): pl.pallas_call(functools.partial(finish_kernel, own_late + other_late), i...  14.2 us
    pallas_call x1, Pallas kernels, fast_device(): pl.pallas_call(functools.partial(collide_kernel, (0,) * (2 * parts)), in_...  13.7 us
    unnamed x38, local copies, waits for them, and re-layouts  13.3 us
    pallas_call x3, Pallas kernels, upwind(): pl.pallas_call(functools.partial(upwind_kernel, g * group, max(g - 1, 0),...  10.7 us
    ppermute x2, waiting for transfers between devices, fast_device(): lax.ppermute(up, 'cy', towards_upper)  9.61 us
    ppermute x2, waiting for transfers between devices, fast_device(): lax.ppermute(down, 'cy', towards_lower)  8.63 us
    ppermute x4, waiting for transfers between devices, swapped(): return lax.ppermute(value, 'vel', swap)  8.47 us
    ppermute x2, starting transfers between devices, fast_device(): lax.ppermute(down, 'cy', towards_lower)  5.54 us
  transfers between devices with their start and end apart: 10, of which 6 were waited for; matrix products, arithmetic and copies ran while one was open for 7% of the time, Pallas kernels for 22%

profile of v4, /device:TPU:0, one launch (start us, length us, event | category | flops | bytes accessed | tf_op | source)
XLA Modules:
  0.0 104.1 jit_solution(14730274223387563406)
XLA Ops:
  0.0 3.0 %copy-done = f32[16,4,4,6912]{3,2,1,0:T(4,128)S(1)} copy-done((f32[16,4,4,6912]{3,2,1,0:T(4,128)S(1)}, f32[16,4,4,6912]{3,2,1,0:T(4,128)}, u32[]{:S(2)}) %copy-start) | copy-done | bytes 7077912
  3.0 0.8 copy-done.15
  4.1 2.5 %collective-permute-start.2 = (bf16[9,32,128]{2,1,0:T(8,128)(2,1)S(1)}, bf16[9,32,128]{2,1,0:T(8,128)(2,1)S(1)}, u32[]{:S(2)}, u32[]{:S(2)}) collective-permute-start(bf16[9,32,128]{2,1,0:T(8,128)(2,1)S(1)} %get-tuple-element.40), channel_id=1, source_target_pairs={{0,12},{4,0},{8,4},{12,8},{16,20},{20,24},{24,28},{28,16},{1,13},{... | collective-permute-start | bytes 221192 | tf_op jit(solution)/shard_map/ppermute | solution.py:742
  6.5 3.6 %collective-permute-start = (bf16[5,128,128]{2,1,0:T(8,128)(2,1)S(1)}, bf16[5,128,128]{2,1,0:T(8,128)(2,1)S(1)}, u32[]{:S(2)}, u32[]{:S(2)}) collective-permute-start(bf16[5,128,128]{2,1,0:T(8,128)(2,1)S(1)} %get-tuple-element.38), channel_id=1, source_target_pairs={{0,3},{1,0},{2,1},{3,2},{4,7},{5,4},{6,5},{7,6},{8,11},{9,8},{10,9... | collective-permute-start | bytes 491528 | tf_op jit(solution)/shard_map/ppermute | solution.py:740
  11.7 3.1 %collective-permute-done.down_ref = bf16[5,128,128]{2,1,0:T(8,128)(2,1)S(1)} collective-permute-done((bf16[5,128,128]{2,1,0:T(8,128)(2,1)S(1)}, bf16[5,128,128]{2,1,0:T(8,128)(2,1)S(1)}, u32[]{:S(2)}, u32[]{:S(2)}) %collective-permute-start) | collective-permute-done | bytes 163872 | tf_op jit(solution)/shard_map/ppermute | solution.py:740
  14.8 2.9 %collective-permute-done.1.up_ref = bf16[5,128,128]{2,1,0:T(8,128)(2,1)S(1)} collective-permute-done((bf16[5,128,128]{2,1,0:T(8,128)(2,1)S(1)}, bf16[5,128,128]{2,1,0:T(8,128)(2,1)S(1)}, u32[]{:S(2)}, u32[]{:S(2)}) %collective-permute-start.1) | collective-permute-done | bytes 163872 | tf_op jit(solution)/shard_map/ppermute | solution.py:741
  17.7 3.0 %copy-done.1 = f32[16,4,4,6912]{3,2,1,0:T(4,128)S(1)} copy-done((f32[16,4,4,6912]{3,2,1,0:T(4,128)S(1)}, f32[16,4,4,6912]{3,2,1,0:T(4,128)}, u32[]{:S(2)}) %copy-start.1) | copy-done | bytes 7077912
  20.8 3.0 %upwind.3 = (f32[64,72,128]{2,1,0:T(8,128)S(1)}, bf16[80,2304]{1,0:T(8,128)(2,1)S(1)}, bf16[48,2304]{1,0:T(8,128)(2,1)S(1)}) custom-call(s32[1]{0:T(128)} %bitcast.side_ref, f32[3,72,128]{2,1,0:T(8,128)S(1)} %get-tuple-element.67.speed_ref, bf16[256,512]{1,0:T(8,128)(2,1)S(1)} %fusion.picker_ref, f32[16,4,4,6912]{3,2,1,0:T(4,128)S(1)} %copy-done.1, ...), custom_call_target="tpu_custom_call" | custom-call | flops 1 | bytes 1 | tf_op jit(solution)/shard_map/upwind/pallas_call | solution.py:710
  23.8 1.9 %collective-permute-start.6 = (bf16[80,2304]{1,0:T(8,128)(2,1)S(1)}, bf16[80,2304]{1,0:T(8,128)(2,1)S(1)}, u32[]{:S(2)}, u32[]{:S(2)}) collective-permute-start(bf16[80,2304]{1,0:T(8,128)(2,1)S(1)} %get-tuple-element.44.refs_0_), channel_id=1, source_target_pairs={{0,16},{16,0},{1,17},{17,1},{2,18},{18,2},{3,19},{19,3},{4,20},{20... | collective-permute-start | bytes 1105928 | tf_op jit(solution)/shard_map/ppermute | solution.py:732
  25.7 0.5 edges.2
  26.2 1.9 %collective-permute-start.3 = (bf16[10,128,128]{2,1,0:T(8,128)(2,1)S(1)}, bf16[10,128,128]{2,1,0:T(8,128)(2,1)S(1)}, u32[]{:S(2)}, u32[]{:S(2)}) collective-permute-start(bf16[10,128,128]{2,1,0:T(8,128)(2,1)S(1)} %get-tuple-element.41), channel_id=1, source_target_pairs={{0,3},{1,0},{2,1},{3,2},{4,7},{5,4},{6,5},{7,6},{8,11},{9,8},{10,9... | collective-permute-start | bytes 983048 | tf_op jit(solution)/shard_map/ppermute | solution.py:740
  28.3 2.7 %collective-permute-done.5.across_ref = bf16[18,32,128]{2,1,0:T(8,128)(2,1)S(1)} collective-permute-done((bf16[18,32,128]{2,1,0:T(8,128)(2,1)S(1)}, bf16[18,32,128]{2,1,0:T(8,128)(2,1)S(1)}, u32[]{:S(2)}, u32[]{:S(2)}) %collective-permute-start.5) | collective-permute-done | bytes 147488 | tf_op jit(solution)/shard_map/ppermute | solution.py:742
  31.0 5.5 %collective-permute-done.3.down_ref = bf16[10,128,128]{2,1,0:T(8,128)(2,1)S(1)} collective-permute-done((bf16[10,128,128]{2,1,0:T(8,128)(2,1)S(1)}, bf16[10,128,128]{2,1,0:T(8,128)(2,1)S(1)}, u32[]{:S(2)}, u32[]{:S(2)}) %collective-permute-start.3) | collective-permute-done | bytes 327712 | tf_op jit(solution)/shard_map/ppermute | solution.py:740
  36.5 6.7 %collective-permute-done.4.up_ref = bf16[10,128,128]{2,1,0:T(8,128)(2,1)S(1)} collective-permute-done((bf16[10,128,128]{2,1,0:T(8,128)(2,1)S(1)}, bf16[10,128,128]{2,1,0:T(8,128)(2,1)S(1)}, u32[]{:S(2)}, u32[]{:S(2)}) %collective-permute-start.4) | collective-permute-done | bytes 327712 | tf_op jit(solution)/shard_map/ppermute | solution.py:741
  43.2 3.9 %upwind.4 = (f32[64,72,128]{2,1,0:T(8,128)S(1)}, bf16[128,2304]{1,0:T(8,128)(2,1)}, bf16[48,2304]{1,0:T(8,128)(2,1)S(1)}) custom-call(s32[1]{0:T(128)} %bitcast.side_ref, f32[3,72,128]{2,1,0:T(8,128)S(1)} %get-tuple-element.68.speed_ref, bf16[256,512]{1,0:T(8,128)(2,1)S(1)} %fusion.picker_ref, f32[16,4,4,6912]{3,2,1,0:T(4,128)S(1)} %copy-done.2, ...), custom_call_target="tpu_custom_call" | custom-call | flops 1 | bytes 1 | tf_op jit(solution)/shard_map/upwind/pallas_call | solution.py:710
  47.1 1.4 %copy-done.6 = f32[64,72,128]{2,1,0:T(8,128)} copy-done((f32[64,72,128]{2,1,0:T(8,128)}, f32[64,72,128]{2,1,0:T(8,128)S(1)}, u32[]{:S(2)}) %copy-start.6) | copy-done | bytes 2359320
  48.5 1.1 %collective-permute-start.7 = (bf16[128,2304]{1,0:T(8,128)(2,1)}, bf16[128,2304]{1,0:T(8,128)(2,1)S(1)}, u32[]{:S(2)}, u32[]{:S(2)}) collective-permute-start(bf16[128,2304]{1,0:T(8,128)(2,1)} %get-tuple-element.49.refs_1_), channel_id=1, source_target_pairs={{0,16},{16,0},{1,17},{17,1},{2,18},{18,2},{3,19},{19,3},{4,20},{20... | collective-permute-start | bytes 1769480 | tf_op jit(solution)/shard_map/ppermute | solution.py:732
  49.7 3.8 %upwind.5 = (f32[64,72,128]{2,1,0:T(8,128)S(1)}, bf16[80,2304]{1,0:T(8,128)(2,1)}, bf16[96,2304]{1,0:T(8,128)(2,1)S(1)}) custom-call(s32[1]{0:T(128)} %bitcast.side_ref, f32[3,72,128]{2,1,0:T(8,128)S(1)} %get-tuple-element.69.speed_ref, bf16[256,512]{1,0:T(8,128)(2,1)S(1)} %fusion.picker_ref, f32[16,4,4,6912]{3,2,1,0:T(4,128)S(1)} %copy-done.2, ...), custom_call_target="tpu_custom_call" | custom-call | flops 1 | bytes 1 | tf_op jit(solution)/shard_map/upwind/pallas_call | solution.py:710
  53.5 1.4 %copy-done.8 = f32[64,72,128]{2,1,0:T(8,128)} copy-done((f32[64,72,128]{2,1,0:T(8,128)}, f32[64,72,128]{2,1,0:T(8,128)S(1)}, u32[]{:S(2)}) %copy-start.8) | copy-done | bytes 2359320
  54.9 0.9 collective-permute-start.8
  56.3 1.1 %reshape.245 = f32[24,576]{1,0:T(8,128)S(1)} reshape(f32[24,24,24]{2,1,0:T(8,128)} %param.11) | data formatting | bytes 110592 | tf_op jit(solution)/shard_map/reshape | solution.py:761
  57.4 1.7 %reshape.246 = f32[24,576]{1,0:T(8,128)} reshape(f32[24,24,24]{2,1,0:T(8,128)} %param.12) | data formatting | bytes 110592 | tf_op jit(solution)/shard_map/reshape | solution.py:761
  59.1 1.7 %reshape.247 = f32[24,576]{1,0:T(8,128)} reshape(f32[24,24,24]{2,1,0:T(8,128)} %param.13) | data formatting | bytes 110592 | tf_op jit(solution)/shard_map/reshape | solution.py:761
  60.8 0.9 pad_maximum_fusion.stacked_ref
  61.7 0.7 weights.1.weight_ref
  62.4 8.5 %collective-permute-done.8.refs_5_ = bf16[80,2304]{1,0:T(8,128)(2,1)} collective-permute-done((bf16[80,2304]{1,0:T(8,128)(2,1)}, bf16[80,2304]{1,0:T(8,128)(2,1)}, u32[]{:S(2)}, u32[]{:S(2)}) %collective-permute-start.8) | collective-permute-done | bytes 368672 | tf_op jit(solution)/shard_map/ppermute | solution.py:732
  70.9 1.5 %collective-permute-start.9 = (bf16[96,2304]{1,0:T(8,128)(2,1)S(1)}, bf16[96,2304]{1,0:T(8,128)(2,1)S(1)}, u32[]{:S(2)}, u32[]{:S(2)}) collective-permute-start(bf16[96,2304]{1,0:T(8,128)(2,1)S(1)} %get-tuple-element.61.refs_1_.refs_2_), channel_id=1, source_target_pairs={{0,16},{16,0},{1,17},{17,1},{2,18},{18,2},{3,19},{19,3},{4,20},{20... | collective-permute-start | bytes 1327112 | tf_op jit(solution)/shard_map/ppermute | solution.py:732
  72.4 1.0 copy-done.12
  73.4 1.0 copy-done.14
  74.4 13.7 %collide.1.early_ref = bf16[80,6912]{1,0:T(8,128)(2,1)S(1)} custom-call(f32[3,24,384]{2,1,0:T(8,128)S(1)} %weights.1.weight_ref, bf16[704,768]{1,0:T(8,128)(2,1)S(1)} %copy-done.3, bf16[80,2304]{1,0:T(8,128)(2,1)S(1)} %copy-done.12, bf16[128,2304]{1,0:T(8,128)(2,1)} %get-tuple-element.49.refs_1_, bf16[80,2304]{1,0:T(8,128)(2,1)} %get-tuple-element.55.refs_2_, ...), custom_call_target="tpu_custom_call" | custom-call | flops 1 | bytes 1 | tf_op jit(solution)/shard_map/collide/pallas_call | solution.py:778
  88.2 1.7 %copy-done.9 = f32[64,72,128]{2,1,0:T(8,128)S(1)} copy-done((f32[64,72,128]{2,1,0:T(8,128)S(1)}, f32[64,72,128]{2,1,0:T(8,128)}, u32[]{:S(2)}) %copy-start.9) | copy-done | bytes 2359320
  89.8 14.2 %finish.1 = f32[16,4,4,6912]{3,2,1,0:T(4,128)} custom-call(f32[3,24,384]{2,1,0:T(8,128)S(1)} %weights.1.weight_ref, bf16[704,768]{1,0:T(8,128)(2,1)S(1)} %copy-done.3, bf16[512,256]{1,0:T(8,128)(2,1)S(1)} %select_convert_fusion.spread_ref, bf16[80,6912]{1,0:T(8,128)(2,1)S(1)} %collide.1.early_ref, bf16[48,2304]{1,0:T(8,128)(2,1)S(1)} %get-tuple-element.48.refs_0_, ...), custom_call_target="tpu_custom_call" | custom-call | tf_op jit(solution)/shard_map/finish/pallas_call | solution.py:792
  (63 shorter events, 2.5 us)
Async XLA Ops:
  0.0 3.0 %copy-start = (f32[16,4,4,6912]{3,2,1,0:T(4,128)S(1)}, f32[16,4,4,6912]{3,2,1,0:T(4,128)}, u32[]{:S(2)}) copy-start(f32[16,4,4,6912]{3,2,1,0:T(4,128)} %field_ref.9) | copy-start | bytes 21233668
  3.0 0.8 copy-start.15
  3.8 6.4 %copy-start.18 = (s32[16,4,4]{0,2,1:T(4,128)S(1)}, s32[16,4,4]{0,2,1:T(4,128)}, u32[]{:S(2)}) copy-start(s32[16,4,4]{0,2,1:T(4,128)} %param.10) | copy-start | bytes 3076
  4.1 7.6 %collective-permute-start.2 = (bf16[9,32,128]{2,1,0:T(8,128)(2,1)S(1)}, bf16[9,32,128]{2,1,0:T(8,128)(2,1)S(1)}, u32[]{:S(2)}, u32[]{:S(2)}) collective-permute-start(bf16[9,32,128]{2,1,0:T(8,128)(2,1)S(1)} %get-tuple-element.40), channel_id=1, source_target_pairs={{0,12},{4,0},{8,4},{12,8},{16,20},{20,24},{24,28},{28,16},{1,13},{... | collective-permute-start | bytes 221192 | tf_op jit(solution)/shard_map/ppermute | solution.py:742
  6.5 8.3 %collective-permute-start = (bf16[5,128,128]{2,1,0:T(8,128)(2,1)S(1)}, bf16[5,128,128]{2,1,0:T(8,128)(2,1)S(1)}, u32[]{:S(2)}, u32[]{:S(2)}) collective-permute-start(bf16[5,128,128]{2,1,0:T(8,128)(2,1)S(1)} %get-tuple-element.38), channel_id=1, source_target_pairs={{0,3},{1,0},{2,1},{3,2},{4,7},{5,4},{6,5},{7,6},{8,11},{9,8},{10,9... | collective-permute-start | bytes 491528 | tf_op jit(solution)/shard_map/ppermute | solution.py:740
  10.2 7.6 %collective-permute-start.1 = (bf16[5,128,128]{2,1,0:T(8,128)(2,1)S(1)}, bf16[5,128,128]{2,1,0:T(8,128)(2,1)S(1)}, u32[]{:S(2)}, u32[]{:S(2)}) collective-permute-start(bf16[5,128,128]{2,1,0:T(8,128)(2,1)S(1)} %get-tuple-element.39), channel_id=1, source_target_pairs={{0,1},{1,2},{2,3},{3,0},{4,5},{5,6},{6,7},{7,4},{8,9},{9,10},{10,1... | collective-permute-start | bytes 491528 | tf_op jit(solution)/shard_map/ppermute | solution.py:741
  17.7 3.0 %copy-start.1 = (f32[16,4,4,6912]{3,2,1,0:T(4,128)S(1)}, f32[16,4,4,6912]{3,2,1,0:T(4,128)}, u32[]{:S(2)}) copy-start(f32[16,4,4,6912]{3,2,1,0:T(4,128)} %field_ref.9) | copy-start | bytes 21233668
  20.8 5.0 %copy-start.2 = (f32[16,4,4,6912]{3,2,1,0:T(4,128)S(1)}, f32[16,4,4,6912]{3,2,1,0:T(4,128)}, u32[]{:S(2)}) copy-start(f32[16,4,4,6912]{3,2,1,0:T(4,128)} %field_ref.9) | copy-start | bytes 21233668
  20.8 5.0 %copy-start.16 = (f32[72,128]{1,0:T(8,128)S(1)}, f32[72,128]{1,0:T(8,128)}, u32[]{:S(2)}) copy-start(f32[72,128]{1,0:T(8,128)} %constant.81.clone.falls_ref) | copy-start | bytes 110596
  23.8 2.4 %copy-start.4 = (f32[64,72,128]{2,1,0:T(8,128)}, f32[64,72,128]{2,1,0:T(8,128)S(1)}, u32[]{:S(2)}) copy-start(f32[64,72,128]{2,1,0:T(8,128)S(1)} %get-tuple-element.62.refs_6_) | copy-start | bytes 7077892
  23.8 2.4 %copy-start.11 = (bf16[80,2304]{1,0:T(8,128)(2,1)}, bf16[80,2304]{1,0:T(8,128)(2,1)S(1)}, u32[]{:S(2)}) copy-start(bf16[80,2304]{1,0:T(8,128)(2,1)S(1)} %get-tuple-element.44.refs_0_) | copy-start | bytes 1105924
  23.8 25.8 %collective-permute-start.6 = (bf16[80,2304]{1,0:T(8,128)(2,1)S(1)}, bf16[80,2304]{1,0:T(8,128)(2,1)S(1)}, u32[]{:S(2)}, u32[]{:S(2)}) collective-permute-start(bf16[80,2304]{1,0:T(8,128)(2,1)S(1)} %get-tuple-element.44.refs_0_), channel_id=1, source_target_pairs={{0,16},{16,0},{1,17},{17,1},{2,18},{18,2},{3,19},{19,3},{4,20},{20... | collective-permute-start | bytes 1105928 | tf_op jit(solution)/shard_map/ppermute | solution.py:732
  26.2 10.3 %collective-permute-start.3 = (bf16[10,128,128]{2,1,0:T(8,128)(2,1)S(1)}, bf16[10,128,128]{2,1,0:T(8,128)(2,1)S(1)}, u32[]{:S(2)}, u32[]{:S(2)}) collective-permute-start(bf16[10,128,128]{2,1,0:T(8,128)(2,1)S(1)} %get-tuple-element.41), channel_id=1, source_target_pairs={{0,3},{1,0},{2,1},{3,2},{4,7},{5,4},{6,5},{7,6},{8,11},{9,8},{10,9... | collective-permute-start | bytes 983048 | tf_op jit(solution)/shard_map/ppermute | solution.py:740
  28.2 15.0 %collective-permute-start.4 = (bf16[10,128,128]{2,1,0:T(8,128)(2,1)S(1)}, bf16[10,128,128]{2,1,0:T(8,128)(2,1)S(1)}, u32[]{:S(2)}, u32[]{:S(2)}) collective-permute-start(bf16[10,128,128]{2,1,0:T(8,128)(2,1)S(1)} %get-tuple-element.42), channel_id=1, source_target_pairs={{0,1},{1,2},{2,3},{3,0},{4,5},{5,6},{6,7},{7,4},{8,9},{9,10},{10,1... | collective-permute-start | bytes 983048 | tf_op jit(solution)/shard_map/ppermute | solution.py:741
  28.3 2.7 %collective-permute-start.5 = (bf16[18,32,128]{2,1,0:T(8,128)(2,1)S(1)}, bf16[18,32,128]{2,1,0:T(8,128)(2,1)S(1)}, u32[]{:S(2)}, u32[]{:S(2)}) collective-permute-start(bf16[18,32,128]{2,1,0:T(8,128)(2,1)S(1)} %get-tuple-element.43), channel_id=1, source_target_pairs={{0,12},{4,0},{8,4},{12,8},{16,20},{20,24},{24,28},{28,16},{1,13},{... | collective-permute-start | bytes 442376 | tf_op jit(solution)/shard_map/ppermute | solution.py:742
  47.1 1.4 %copy-start.6 = (f32[64,72,128]{2,1,0:T(8,128)}, f32[64,72,128]{2,1,0:T(8,128)S(1)}, u32[]{:S(2)}) copy-start(f32[64,72,128]{2,1,0:T(8,128)S(1)} %get-tuple-element.63.refs_7_) | copy-start | bytes 7077892
  48.5 22.4 %collective-permute-start.7 = (bf16[128,2304]{1,0:T(8,128)(2,1)}, bf16[128,2304]{1,0:T(8,128)(2,1)S(1)}, u32[]{:S(2)}, u32[]{:S(2)}) collective-permute-start(bf16[128,2304]{1,0:T(8,128)(2,1)} %get-tuple-element.49.refs_1_), channel_id=1, source_target_pairs={{0,16},{16,0},{1,17},{17,1},{2,18},{18,2},{3,19},{19,3},{4,20},{20... | collective-permute-start | bytes 1769480 | tf_op jit(solution)/shard_map/ppermute | solution.py:732
  49.6 3.8 %copy-start.13 = (bf16[80,2304]{1,0:T(8,128)(2,1)}, bf16[80,2304]{1,0:T(8,128)(2,1)S(1)}, u32[]{:S(2)}) copy-start(bf16[80,2304]{1,0:T(8,128)(2,1)S(1)} %collective-permute-done.6.refs_3_) | copy-start | bytes 1105924
  49.7 12.1 %copy-start.10 = (bf16[576,768]{1,0:T(8,128)(2,1)S(1)}, bf16[576,768]{1,0:T(8,128)(2,1)}, u32[]{:S(2)}) copy-start(bf16[576,768]{1,0:T(8,128)(2,1)} %constant.83.clone.select_ref) | copy-start | bytes 2654212
  49.7 12.1 %copy-start.17 = (f32[1,384]{1,0:T(1,128)S(1)}, f32[1,384]{1,0:T(1,128)}, u32[]{:S(2)}) copy-start(f32[1,384]{1,0:T(1,128)} %constant.84.clone.scale_ref) | copy-start | bytes 4612
  53.5 1.4 %copy-start.8 = (f32[64,72,128]{2,1,0:T(8,128)}, f32[64,72,128]{2,1,0:T(8,128)S(1)}, u32[]{:S(2)}) copy-start(f32[64,72,128]{2,1,0:T(8,128)S(1)} %get-tuple-element.64.refs_8_) | copy-start | bytes 7077892
  54.9 17.5 %copy-start.3 = (bf16[704,768]{1,0:T(8,128)(2,1)S(1)}, bf16[704,768]{1,0:T(8,128)(2,1)}, u32[]{:S(2)}) copy-start(bf16[704,768]{1,0:T(8,128)(2,1)} %constant.82.clone.table_ref) | copy-start | bytes 3244036
  54.9 16.0 %collective-permute-start.8 = (bf16[80,2304]{1,0:T(8,128)(2,1)}, bf16[80,2304]{1,0:T(8,128)(2,1)}, u32[]{:S(2)}, u32[]{:S(2)}) collective-permute-start(bf16[80,2304]{1,0:T(8,128)(2,1)} %get-tuple-element.55.refs_2_), channel_id=1, source_target_pairs={{0,16},{16,0},{1,17},{17,1},{2,18},{18,2},{3,19},{19,3},{4,20},{20... | collective-permute-start | bytes 1105928 | tf_op jit(solution)/shard_map/ppermute | solution.py:732
  70.9 17.2 %copy-start.5 = (f32[64,72,128]{2,1,0:T(8,128)S(1)}, f32[64,72,128]{2,1,0:T(8,128)}, u32[]{:S(2)}) copy-start(f32[64,72,128]{2,1,0:T(8,128)} %copy-done.4) | copy-start | bytes 7077892
  70.9 17.2 %copy-start.7 = (f32[64,72,128]{2,1,0:T(8,128)S(1)}, f32[64,72,128]{2,1,0:T(8,128)}, u32[]{:S(2)}) copy-start(f32[64,72,128]{2,1,0:T(8,128)} %copy-done.6) | copy-start | bytes 7077892
  70.9 17.2 %collective-permute-start.9 = (bf16[96,2304]{1,0:T(8,128)(2,1)S(1)}, bf16[96,2304]{1,0:T(8,128)(2,1)S(1)}, u32[]{:S(2)}, u32[]{:S(2)}) collective-permute-start(bf16[96,2304]{1,0:T(8,128)(2,1)S(1)} %get-tuple-element.61.refs_1_.refs_2_), channel_id=1, source_target_pairs={{0,16},{16,0},{1,17},{17,1},{2,18},{18,2},{3,19},{19,3},{4,20},{20... | collective-permute-start | bytes 1327112 | tf_op jit(solution)/shard_map/ppermute | solution.py:732
  72.4 1.0 copy-start.12
  73.4 1.0 copy-start.14
  88.2 1.7 %copy-start.9 = (f32[64,72,128]{2,1,0:T(8,128)S(1)}, f32[64,72,128]{2,1,0:T(8,128)}, u32[]{:S(2)}) copy-start(f32[64,72,128]{2,1,0:T(8,128)} %copy-done.8) | copy-start | bytes 7077892

commit v5 on v4

--- a/solution.py
+++ b/solution.py
@@ -125,6 +125,7 @@
 
 LANES = 128
 PLANES = 4
+LIMIT = 57
 
 
 def half_set(points):
@@ -298,8 +299,7 @@
 
 def upwind_kernel(
     base,
-    place_at,
-    into_late,
+    counts,
     side_ref,
     speed_ref,
     picker_ref,
@@ -307,42 +307,40 @@
     down_ref,
     up_ref,
     across_ref,
+    out_ref,
     *refs,
 ):
-    carried_refs, (read_ref, early_ref, late_ref), scratch = refs[:-8], refs[-8:-5], refs[-5:]
-    blocks, wide, border, cells, sems = scratch
+    chosen_refs, scratch = refs[:-7], refs[-7:]
+    blocks, reads, wide, border, cells, load_sems, store_sems = scratch
     chunks, width_x, width_y, width_z, lanes = blocks.shape
     steps = lanes // (2 * LANES)
+    group_lanes = chosen_refs[0].shape[1]
+    per_group = group_lanes // lanes
+    half_steps = per_group * steps // 2 + 1
     loads = []
     for t in range(chunks):
         source = field_ref.at[:, :, :, pl.ds(base + t * lanes, lanes)]
-        loads.append(pltpu.make_async_copy(source, blocks.at[t], sems.at[t]))
+        loads.append(pltpu.make_async_copy(source, blocks.at[t], load_sems.at[t]))
         loads[-1].start()
     beside = jnp.where(side_ref[0] == 0, 2, 0)
     place = lax.broadcasted_iota(jnp.int32, (1, 8, LANES), 1) % width_z
     capacity = picker_ref.shape[0] // 2
-    late = carried_refs[0].shape[0] if carried_refs else late_ref.shape[0]
-    early = capacity - late
-    late_at = late_ref.shape[0] - late
-    for ref in carried_refs:
-        if into_late:
-            late_ref[:late, :] = ref[...]
-        else:
-            early_ref[early:, :] = ref[...]
-    half_steps = chunks * steps // 2 + 1
+    stores = []
     for t in range(chunks):
+        group, chunk = t // per_group, t % per_group
         sizes, falls, sinks = [], [], []
         for u in range(steps):
-            step = t * steps + u
-            speed = [speed_ref[d, 8 * step : 8 * step + 8, :][None] for d in range(3)]
+            step = chunk * steps + u
+            row = 8 * (t * steps + u)
+            speed = [speed_ref[d, row : row + 8, :][None] for d in range(3)]
             sizes.append([jnp.abs(c) for c in speed])
             falls.append(speed[1] < 0.0)
             sinks.append(speed[2] < 0.0)
-            outer = across_ref[place_at * chunks * steps + step].astype(jnp.float32).reshape(width_y, 8, LANES)
+            outer = across_ref[t * steps + u].astype(jnp.float32).reshape(width_y, 8, LANES)
             wide[u, 0] = outer
             wide[u, width_x + 1] = outer
-            above = down_ref[place_at * half_steps + (step + 1) // 2].astype(jnp.float32)
-            under = up_ref[place_at * half_steps + step // 2].astype(jnp.float32)
+            above = down_ref[group * half_steps + (step + 1) // 2].astype(jnp.float32)
+            under = up_ref[group * half_steps + step // 2].astype(jnp.float32)
             shape = (width_x, 8, LANES)
             border[u] = jnp.where(falls[u], above.reshape(shape), under.reshape(shape))
         loads[t].wait()
@@ -375,8 +373,7 @@
                 lower = jnp.where(place == 0, pltpu.roll(field, 5, 1), pltpu.roll(field, 1, 1))
                 fluxes = fluxes + sizes[u][2] * (field - jnp.where(sinks[u], upper, lower))
                 read = field - fluxes
-                row = 8 * (t * steps + u)
-                read_ref[pl.ds(x * width_y, width_y), row : row + 8, :] = read
+                reads[t, pl.ds(x * width_y, width_y), 8 * u : 8 * u + 8, :] = read
                 rows = width_y * 8
                 at = pl.multiple_of(x * rows, rows)
                 cells[pl.ds(at, rows), u * LANES : (u + 1) * LANES] = read.reshape(
@@ -385,17 +382,23 @@
             return carry
 
         lax.fori_loop(0, width_x, advance, 0, unroll=2)
+        target = out_ref.at[:, pl.ds(8 * steps * t, 8 * steps), :]
+        stores.append(pltpu.make_async_copy(reads.at[t], target, store_sems.at[t]))
+        stores[-1].start()
         picked = jnp.dot(
             picker_ref[...], cells[...], preferred_element_type=jnp.float32
         ).astype(jnp.bfloat16)
         for parity in range(2):
             first = parity * capacity
-            for u in range(steps):
-                tile = 2 * (t * steps + u) + parity
-                here = slice(tile * LANES, (tile + 1) * LANES)
-                values = picked[first : first + capacity, u * LANES : (u + 1) * LANES]
-                early_ref[:early, here] = values[:early]
-                late_ref[late_at:, here] = values[early:]
+            for ref, count in zip(chosen_refs, counts):
+                rows = slice(group * count, (group + 1) * count)
+                for u in range(steps):
+                    tile = 2 * (chunk * steps + u) + parity
+                    here = slice(tile * LANES, (tile + 1) * LANES)
+                    ref[rows, here] = picked[first : first + count, u * LANES : (u + 1) * LANES]
+                first += count
+    for store in stores:
+        store.wait()
 
 
 def window_loads(firsts, refs, cells, sems):
@@ -526,21 +529,32 @@
         terms_of(part, table_ref, cells, back, put)
 
 
-def finish_kernel(firsts, weight_ref, table_ref, spread_ref, early_ref, *refs):
+def finish_kernel(firsts, sizes, weight_ref, table_ref, spread_any, *refs):
     parts = len(firsts) // 2
-    read_refs = refs[2 * parts : 3 * parts]
-    out_ref, cells, section, back, reads, spots, added, staged = refs[3 * parts : -3]
-    cell_sems, read_sems, out_sems = refs[-3:]
+    term_refs, refs = refs[: len(sizes) - 1], refs[len(sizes) - 1 :]
+    first_read, rest_read = refs[2 * parts : 2 * parts + 2]
+    out_ref, cells, section, back, reads, spots, added, staged = refs[2 * parts + 2 : -6]
+    spread_ref, early_ref, cell_sems, read_sems, out_sems, extra_sems = refs[-6:]
     width_x, width_y, width_z, lanes = staged.shape[1:]
     tiles = lanes // LANES
     loads = window_loads(firsts, refs[: 2 * parts], cells, cell_sems)
-    read_loads = [
-        pltpu.make_async_copy(read_refs[part], reads.at[part], read_sems.at[part])
-        for part in range(parts)
-    ]
-    for load in read_loads:
+    extra = [pltpu.make_async_copy(spread_any, spread_ref, extra_sems.at[0])]
+    at = 0
+    for ref, size in zip(term_refs, sizes):
+        target = early_ref.at[pl.ds(at, size)]
+        extra.append(pltpu.make_async_copy(ref, target, extra_sems.at[len(extra)]))
+        at += size
+    group_rows = reads.shape[2]
+    read_loads = []
+    for part in range(parts):
+        rows = pl.ds(max(part - 1, 0) * group_rows, group_rows)
+        source = (rest_read if part else first_read).at[:, rows, :]
+        read_loads.append(pltpu.make_async_copy(source, reads.at[part], read_sems.at[part]))
+    for load in extra + read_loads:
         load.start()
     filter_parts(weight_ref, table_ref, cells, loads, section, back)
+    for load in extra:
+        load.wait()
     early = early_ref.shape[0]
     capacity = early + section.shape[1]
     pieces = out_sems.shape[1]
@@ -625,8 +639,9 @@
     group_rows = group // LANES * width_z
     steps = group_rows // 8
     capacity = block_cells // 2
-    late = capacity * 3 // 8 // 16 * 16
-    counts = (capacity - late, late)
+    third = capacity * 3 // 8 // 16 * 16
+    counts = (third, third, capacity - 2 * third)
+    batches = len(counts)
     vel_at = lax.axis_index("vel")
     count_x, count_y = lax.axis_size("cx"), lax.axis_size("cy")
 
@@ -635,7 +650,7 @@
     speeds = jnp.broadcast_to(
         speeds.reshape(3, tiles, 1, LANES), (3, tiles, width_z, LANES)
     ).reshape(3, parts, tiles * width_z // parts, LANES)
-    speeds = [speeds[:, g] for g in range(parts)]
+    speeds = [speeds[:, 0], speeds[:, 1:].reshape(3, -1, LANES)]
     falls = np.arange(group) // points % points < points // 2
     falls = np.repeat(falls.reshape(-1, 1, LANES), width_z, axis=1).reshape(-1, LANES)
     falls = jnp.asarray(falls.astype(np.float32))
@@ -675,6 +690,7 @@
     local = pl.BlockSpec(memory_space=pltpu.VMEM)
     scalar = pl.BlockSpec(memory_space=pltpu.SMEM)
     remote = pl.BlockSpec(memory_space=pltpu.HBM)
+    anywhere = pl.BlockSpec(memory_space=pl.ANY)
 
     def edges_of(first, groups):
         return pl.pallas_call(
@@ -692,7 +708,7 @@
                 pltpu.VMEM((1, width_y, width_z, groups * group), jnp.float32),
                 pltpu.SemaphoreType.DMA((3,)),
             ],
-            compiler_params=params(16),
+            compiler_params=params(LIMIT),
             cost_estimate=cost(1, 1),
             name="edges",
         )(edge, falls, distribution)
@@ -701,29 +717,31 @@
     wide = 3
     chunks = steps // wide
 
-    def upwind(g, halo, carried):
-        into_late = g > 1
-        heights = (
-            capacity if carried and not into_late else counts[0],
-            2 * counts[1] if carried and into_late else counts[1],
-        )
+    def upwind(at, halo, sizes):
+        groups = parts - 1 if at else 1
         return pl.pallas_call(
-            functools.partial(upwind_kernel, g * group, max(g - 1, 0), into_late),
-            in_specs=[scalar, local, local, remote] + [local] * (len(halo) + len(carried)),
-            out_specs=[local] * 3,
-            out_shape=[jax.ShapeDtypeStruct((block_rows, group_rows, LANES), jnp.float32)]
-            + [jax.ShapeDtypeStruct((height, group), bf16) for height in heights],
+            functools.partial(upwind_kernel, at * group, sizes),
+            in_specs=[scalar, local, local, remote] + [local] * len(halo),
+            out_specs=[anywhere] + [local] * len(sizes),
+            out_shape=[
+                jax.ShapeDtypeStruct((block_rows, groups * group_rows, LANES), jnp.float32)
+            ]
+            + [jax.ShapeDtypeStruct((groups * size, group), bf16) for size in sizes],
             scratch_shapes=[
-                pltpu.VMEM((chunks, width_x, width_y, width_z, group // chunks), jnp.float32),
+                pltpu.VMEM(
+                    (groups * chunks, width_x, width_y, width_z, group // chunks), jnp.float32
+                ),
+                pltpu.VMEM((groups * chunks, block_rows, 8 * wide, LANES), jnp.float32),
                 pltpu.VMEM((wide, width_x + 2, width_y, 8, LANES), jnp.float32),
                 pltpu.VMEM((wide, width_x, 8, LANES), jnp.float32),
                 pltpu.VMEM((block_rows * 8, wide * LANES), bf16),
-                pltpu.SemaphoreType.DMA((chunks,)),
+                pltpu.SemaphoreType.DMA((groups * chunks,)),
+                pltpu.SemaphoreType.DMA((groups * chunks,)),
             ],
-            compiler_params=params(20),
+            compiler_params=params(LIMIT),
             cost_estimate=cost(1, 1),
             name="upwind",
-        )(side, speeds[g], picker, distribution, *halo, *carried)
+        )(side, speeds[at], picker, distribution, *halo)
 
     def turn(value, *earlier):
         return lax.optimization_barrier((value, *earlier))[0]
@@ -733,8 +751,7 @@
 
     halos = []
     for at in range(2):
-        operands = edges[at] if at == 0 else turn(edges[at], halos[0])
-        down, up, across = operands
+        down, up, across = edges[at]
         halos.append(
             (
                 lax.ppermute(down, "cy", towards_lower),
@@ -742,19 +759,14 @@
                 lax.ppermute(across, ("vel", "cx"), across_pairs),
             )
         )
-    reads, firsts, lasts, early = [], [], [], []
-    for g in range(parts):
-        halo = halos[0] if g == 0 else turn(halos[1], firsts[-1], *early[: g - 1])
-        read, first, last = upwind(g, halo, lasts[-1:])
-        reads.append(read)
-        firsts.append(first)
-        lasts.append(last)
-        early.append(swapped(first))
-    kernels = turn((gain_one, gain_two, loss_kernel), firsts[-1])
+    first_read, *first = upwind(0, turn(halos[0], edges[1]), counts)
+    first_other = [swapped(x) for x in first]
+    rest_read, *rest = upwind(1, turn(halos[1], first), counts)
+    kernels = turn((gain_one, gain_two, loss_kernel), halos[0])
     weights = pl.pallas_call(
         weights_kernel,
         out_shape=jax.ShapeDtypeStruct((3, points, padded), jnp.float32),
-        compiler_params=params(12),
+        compiler_params=params(LIMIT),
         cost_estimate=cost(1, 1),
         name="weights",
     )(
@@ -763,8 +775,8 @@
         jnp.asarray(scale),
     )
 
-    last, weights, spread = turn((lasts[-1], weights, spread), *early)
-    late = swapped(last)
+    operand, weights, spread = turn((rest[0], weights, spread), first_other)
+    others = [swapped(operand)]
 
     def scratch(count):
         return [
@@ -773,40 +785,68 @@
             pltpu.VMEM((2, 3, points // 4, count, 2 * padded), bf16),
         ]
 
-    anywhere = pl.BlockSpec(memory_space=pl.ANY)
     sems = pltpu.SemaphoreType.DMA((2 * parts,))
-    terms = pl.pallas_call(
-        functools.partial(collide_kernel, (0,) * (2 * parts)),
-        in_specs=[local] * 2 + [anywhere] * (2 * parts),
-        out_specs=local,
-        out_shape=jax.ShapeDtypeStruct((counts[0], local_vel), bf16),
-        scratch_shapes=scratch(counts[0]) + [sems],
-        compiler_params=params(28),
-        cost_estimate=cost(1, 1),
-        name="collide",
-    )(weights, table, *firsts, *early)
+    terms = []
+    for batch in range(batches - 1):
+        count = counts[batch]
+        starts = (0,) + tuple(g * count for g in range(parts - 1))
+        following = turn(rest[batch + 1], others[-1], *terms)
+        others.append(swapped(following))
+        terms.append(
+            pl.pallas_call(
+                functools.partial(collide_kernel, starts + starts),
+                in_specs=[local] * 2 + [anywhere] * (2 * parts),
+                out_specs=local,
+                out_shape=jax.ShapeDtypeStruct((count, local_vel), bf16),
+                scratch_shapes=scratch(count) + [sems],
+                compiler_params=params(LIMIT),
+                cost_estimate=cost(1, 1),
+                name="collide",
+            )(
+                weights,
+                table,
+                first[batch],
+                *[rest[batch]] * (parts - 1),
+                first_other[batch],
+                *[others[batch]] * (parts - 1),
+            )
+        )
 
     pieces = 4
-    own_late = (0, 0, counts[1])
-    other_late = (counts[0], 0, counts[1])
+    count = counts[-1]
+    starts = (0,) + tuple(g * count for g in range(parts - 1))
     return pl.pallas_call(
-        functools.partial(finish_kernel, own_late + other_late),
-        in_specs=[local] * 4 + [anywhere] * (3 * parts),
+        functools.partial(finish_kernel, starts + starts, counts),
+        in_specs=[local] * 2 + [anywhere] * (batches + 2 * parts + 2),
         out_specs=anywhere,
         out_shape=jax.ShapeDtypeStruct(distribution.shape, jnp.float32),
-        scratch_shapes=scratch(counts[1])
+        scratch_shapes=scratch(count)
         + [
             pltpu.VMEM((parts, block_rows, group_rows, LANES), jnp.float32),
             pltpu.VMEM((2 * capacity, group // 2), bf16),
             pltpu.VMEM((block_rows * 8, group // 2), jnp.float32),
             pltpu.VMEM((2, width_x, width_y, width_z, group), jnp.float32),
+            pltpu.VMEM(spread.shape, bf16),
+            pltpu.VMEM((capacity - count, local_vel), bf16),
             sems,
             pltpu.SemaphoreType.DMA((parts,)),
             pltpu.SemaphoreType.DMA((parts, pieces)),
+            pltpu.SemaphoreType.DMA((batches,)),
         ],
-        compiler_params=params(36),
+        compiler_params=params(LIMIT),
         name="finish",
-    )(weights, table, spread, terms, lasts[0], last, last, early[1], late, late, *reads)
+    )(
+        weights,
+        table,
+        spread,
+        *terms,
+        first[-1],
+        *[rest[-1]] * (parts - 1),
+        first_other[-1],
+        *[others[-1]] * (parts - 1),
+        first_read,
+        rest_read,
+    )
 
 
 def per_device(distribution, refine_level, gain_one, gain_two, loss_kernel):

time: 105 us -> 97.6 us (0.930)
  Pallas kernels: 40.1 us -> 60.9 us
  waiting for transfers between devices: 29.4 us -> 11.2 us
  local copies, waits for them, and re-layouts: 19.2 us -> 5.76 us
  starting transfers between devices: 13.6 us -> 16 us
  other arithmetic: 1.5 us -> 2.76 us
    pallas_call x5, Pallas kernels: 38.5 us -> 52.1 us  [the longest x2 22.2 us: fast_device(): pl.pallas_call(functools.partial(collide_kernel, starts + starts), in_spe...]
    unnamed x38 -> x32, local copies, waits for them, and re-layouts: 13.3 us -> 2.71 us
    ppermute x2, waiting for transfers between devices: 9.61 us -> 0.01 us  [fast_device(): lax.ppermute(up, 'cy', towards_upper)]
    ppermute x2, waiting for transfers between devices: 8.63 us -> 0.01 us  [fast_device(): lax.ppermute(down, 'cy', towards_lower)]
    pallas_call x2, Pallas kernels: 0.81 us -> 6.25 us  [edges_of(): pl.pallas_call(functools.partial(edges_kernel, first * group), in_specs=[...]
    reshape x3, local copies, waits for them, and re-layouts: 4.56 us -> 0.41 us  [fast_device(): k.reshape(points, points * points)]
    ppermute x4 -> x6, waiting for transfers between devices: 8.47 us -> 11.2 us  [swapped(): return lax.ppermute(value, 'vel', swap)]
    ppermute x2, waiting for transfers between devices: 2.68 us -> 0.01 us  [fast_device(): lax.ppermute(across, ('vel', 'cx'), across_pairs)]
  transfers between devices with their start and end apart: 10 -> 12, of which waited for: 6 -> 1; matrix products, arithmetic and copies ran while one was open for 7% -> 6% of each run, Pallas kernels for 22% -> 46%
where the time goes in v5:
time: 97.6 us; the launch traced here: 97.1 us
  Pallas kernels  60.9 us (62%)
  starting transfers between devices  16 us (16%)
  waiting for transfers between devices  11.2 us (11%)
  local copies, waits for them, and re-layouts  5.76 us (6%)
  other arithmetic  2.76 us (3%)
    pallas_call x2, Pallas kernels, fast_device(): pl.pallas_call(functools.partial(collide_kernel, starts + starts), in_spe...  22.2 us
    pallas_call x2, Pallas kernels, upwind(): pl.pallas_call(functools.partial(upwind_kernel, at * group, sizes), in_sp...  16.4 us
    pallas_call x1, Pallas kernels, fast_device(): pl.pallas_call(functools.partial(finish_kernel, starts + starts, counts),...  13.5 us
    ppermute x6, waiting for transfers between devices, swapped(): return lax.ppermute(value, 'vel', swap)  11.2 us
    ppermute x2, starting transfers between devices, fast_device(): lax.ppermute(down, 'cy', towards_lower)  7.18 us
    pallas_call x2, Pallas kernels, edges_of(): pl.pallas_call(functools.partial(edges_kernel, first * group), in_specs=[...  6.25 us
    ppermute x6, starting transfers between devices, swapped(): return lax.ppermute(value, 'vel', swap)  5.84 us
    ppermute x2, starting transfers between devices, fast_device(): lax.ppermute(across, ('vel', 'cx'), across_pairs)  2.91 us
  transfers between devices with their start and end apart: 12, of which 1 were waited for; matrix products, arithmetic and copies ran while one was open for 6% of the time, Pallas kernels for 46%

profile of v5, /device:TPU:0, one launch (start us, length us, event | category | flops | bytes accessed | tf_op | source)
XLA Modules:
  0.0 97.1 jit_solution(9048307981376071935)
XLA Ops:
  0.0 2.8 %edges.3 = (bf16[5,128,128]{2,1,0:T(8,128)(2,1)}, bf16[5,128,128]{2,1,0:T(8,128)(2,1)}, bf16[9,32,128]{2,1,0:T(8,128)(2,1)}) custom-call(s32[1]{0:T(128)} %bitcast.4.edge_ref, f32[72,128]{1,0:T(8,128)} %constant.81.clone.falls_ref, f32[16,4,4,6912]{3,2,1,0:T(4,128)} %field_ref.7), custom_call_target="tpu_custom_call" | custom-call | flops 1 | bytes 1 | tf_op jit(solution)/shard_map/edges/pallas_call | solution.py:696
  2.9 2.5 %collective-permute-start.5 = (bf16[9,32,128]{2,1,0:T(8,128)(2,1)}, bf16[9,32,128]{2,1,0:T(8,128)(2,1)S(1)}, u32[]{:S(2)}, u32[]{:S(2)}) collective-permute-start(bf16[9,32,128]{2,1,0:T(8,128)(2,1)} %get-tuple-element.38), channel_id=1, source_target_pairs={{0,12},{4,0},{8,4},{12,8},{16,20},{20,24},{24,28},{28,16},{1,13},{... | collective-permute-start | bytes 221192 | tf_op jit(solution)/shard_map/ppermute | solution.py:759
  5.3 3.6 %collective-permute-start.3 = (bf16[5,128,128]{2,1,0:T(8,128)(2,1)}, bf16[5,128,128]{2,1,0:T(8,128)(2,1)S(1)}, u32[]{:S(2)}, u32[]{:S(2)}) collective-permute-start(bf16[5,128,128]{2,1,0:T(8,128)(2,1)} %get-tuple-element.36), channel_id=1, source_target_pairs={{0,3},{1,0},{2,1},{3,2},{4,7},{5,4},{6,5},{7,6},{8,11},{9,8},{10,9... | collective-permute-start | bytes 491528 | tf_op jit(solution)/shard_map/ppermute | solution.py:757
  8.9 3.4 %edges.2 = (bf16[10,128,128]{2,1,0:T(8,128)(2,1)}, bf16[10,128,128]{2,1,0:T(8,128)(2,1)}, bf16[18,32,128]{2,1,0:T(8,128)(2,1)}) custom-call(s32[1]{0:T(128)} %bitcast.4.edge_ref, f32[72,128]{1,0:T(8,128)} %constant.81.clone.falls_ref, f32[16,4,4,6912]{3,2,1,0:T(4,128)} %field_ref.7), custom_call_target="tpu_custom_call" | custom-call | flops 1 | bytes 1 | tf_op jit(solution)/shard_map/edges/pallas_call | solution.py:696
  12.3 0.4 collective-permute-start.2
  12.8 3.6 %collective-permute-start = (bf16[10,128,128]{2,1,0:T(8,128)(2,1)}, bf16[10,128,128]{2,1,0:T(8,128)(2,1)S(1)}, u32[]{:S(2)}, u32[]{:S(2)}) collective-permute-start(bf16[10,128,128]{2,1,0:T(8,128)(2,1)} %get-tuple-element.33), channel_id=1, source_target_pairs={{0,3},{1,0},{2,1},{3,2},{4,7},{5,4},{6,5},{7,6},{8,11},{9,8},{10,9... | collective-permute-start | bytes 983048 | tf_op jit(solution)/shard_map/ppermute | solution.py:757
  17.8 0.6 slice_bitcast_fusion.speed_ref
  18.5 0.8 fusion.picker_ref
  19.7 0.5 copy-done.14
  20.2 0.1 copy-done.10
  20.4 6.6 %upwind.2 = (f32[64,72,128]{2,1,0:T(8,128)}, bf16[48,2304]{1,0:T(8,128)(2,1)}, bf16[48,2304]{1,0:T(8,128)(2,1)}, bf16[32,2304]{1,0:T(8,128)(2,1)}) custom-call(s32[1]{0:T(128)} %bitcast.side_ref, f32[3,72,128]{2,1,0:T(8,128)} %slice_bitcast_fusion.speed_ref, bf16[256,512]{1,0:T(8,128)(2,1)} %fusion.picker_ref, f32[16,4,4,6912]{3,2,1,0:T(4,128)} %field_ref.7, ...), custom_call_target="tpu_custom_call" | custom-call | flops 1 | bytes 1 | tf_op jit(solution)/shard_map/upwind/pallas_call | solution.py:722
  26.9 1.5 %collective-permute-start.8 = (bf16[32,2304]{1,0:T(8,128)(2,1)}, bf16[32,2304]{1,0:T(8,128)(2,1)S(1)}, u32[]{:S(2)}, u32[]{:S(2)}) collective-permute-start(bf16[32,2304]{1,0:T(8,128)(2,1)} %get-tuple-element.44.refs_2_), channel_id=1, source_target_pairs={{0,16},{16,0},{1,17},{17,1},{2,18},{18,2},{3,19},{19,3},{4,20},{20... | collective-permute-start | bytes 442376 | tf_op jit(solution)/shard_map/ppermute | solution.py:750
  28.5 0.6 collective-permute-start.6
  29.0 1.5 %collective-permute-start.7 = (bf16[48,2304]{1,0:T(8,128)(2,1)}, bf16[48,2304]{1,0:T(8,128)(2,1)S(1)}, u32[]{:S(2)}, u32[]{:S(2)}) collective-permute-start(bf16[48,2304]{1,0:T(8,128)(2,1)} %get-tuple-element.43.refs_0_), channel_id=1, source_target_pairs={{0,16},{16,0},{1,17},{17,1},{2,18},{18,2},{3,19},{19,3},{4,20},{20... | collective-permute-start | bytes 663560 | tf_op jit(solution)/shard_map/ppermute | solution.py:750
  30.5 0.9 select_convert_fusion.spread_any
  31.4 0.7 slice.8
  32.1 0.1 reshape.249
  32.3 0.1 reshape.250
  32.4 0.1 reshape.251
  32.6 0.7 pad_maximum_fusion.stacked_ref
  33.3 2.5 %weights.1.weight_ref = f32[3,24,384]{2,1,0:T(8,128)} custom-call(f32[72,576]{1,0:T(8,128)} %pad_maximum_fusion.stacked_ref, bf16[576,768]{1,0:T(8,128)(2,1)} %constant.83.clone.select_ref, f32[1,384]{1,0:T(1,128)} %constant.84.clone.scale_ref), custom_call_target="tpu_custom_call" | custom-call | flops 1 | bytes 1 | tf_op jit(solution)/shard_map/weights/pallas_call | solution.py:766
  35.8 0.7 copy-done.3
  36.6 9.8 %upwind.3 = (f32[64,144,128]{2,1,0:T(8,128)}, bf16[96,2304]{1,0:T(8,128)(2,1)}, bf16[96,2304]{1,0:T(8,128)(2,1)}, bf16[64,2304]{1,0:T(8,128)(2,1)}) custom-call(s32[1]{0:T(128)} %bitcast.side_ref, f32[3,144,128]{2,1,0:T(8,128)} %bitcast.15, bf16[256,512]{1,0:T(8,128)(2,1)} %fusion.picker_ref, f32[16,4,4,6912]{3,2,1,0:T(4,128)} %field_ref.7, ...), custom_call_target="tpu_custom_call" | custom-call | flops 1 | bytes 1 | tf_op jit(solution)/shard_map/upwind/pallas_call | solution.py:722
  46.5 0.6 collective-permute-start.9
  47.1 11.2 %collective-permute-done.9.refs_4_.refs_5_ = bf16[96,2304]{1,0:T(8,128)(2,1)S(1)} collective-permute-done((bf16[96,2304]{1,0:T(8,128)(2,1)}, bf16[96,2304]{1,0:T(8,128)(2,1)S(1)}, u32[]{:S(2)}, u32[]{:S(2)}) %collective-permute-start.9) | collective-permute-done | bytes 442400 | tf_op jit(solution)/shard_map/ppermute | solution.py:750
  58.3 0.4 collective-permute-start.10
  58.7 0.4 copy-done.1
  59.2 11.0 %collide.2.refs_0_ = bf16[48,6912]{1,0:T(8,128)(2,1)} custom-call(f32[3,24,384]{2,1,0:T(8,128)} %weights.1.weight_ref, bf16[704,768]{1,0:T(8,128)(2,1)} %constant.82.clone.table_ref, bf16[48,2304]{1,0:T(8,128)(2,1)} %get-tuple-element.42.refs_0_, bf16[96,2304]{1,0:T(8,128)(2,1)} %get-tuple-element.54.refs_1_.refs_2_, ...), custom_call_target="tpu_custom_call" | custom-call | flops 1 | bytes 1 | tf_op jit(solution)/shard_map/collide/pallas_call | solution.py:796
  70.2 1.3 %collective-permute-start.11 = (bf16[64,2304]{1,0:T(8,128)(2,1)}, bf16[64,2304]{1,0:T(8,128)(2,1)S(1)}, u32[]{:S(2)}, u32[]{:S(2)}) collective-permute-start(bf16[64,2304]{1,0:T(8,128)(2,1)} %get-tuple-element.58.refs_3_.refs_4_), channel_id=1, source_target_pairs={{0,16},{16,0},{1,17},{17,1},{2,18},{18,2},{3,19},{19,3},{4,20},{20... | collective-permute-start | bytes 884744 | tf_op jit(solution)/shard_map/ppermute | solution.py:750
  71.5 11.2 %collide.3.refs_1_ = bf16[48,6912]{1,0:T(8,128)(2,1)} custom-call(f32[3,24,384]{2,1,0:T(8,128)} %weights.1.weight_ref, bf16[704,768]{1,0:T(8,128)(2,1)} %constant.82.clone.table_ref, bf16[48,2304]{1,0:T(8,128)(2,1)} %get-tuple-element.43.refs_0_, bf16[96,2304]{1,0:T(8,128)(2,1)} %get-tuple-element.56.refs_1_.refs_2_, ...), custom_call_target="tpu_custom_call" | custom-call | flops 1 | bytes 1 | tf_op jit(solution)/shard_map/collide/pallas_call | solution.py:796
  82.7 0.7 copy-done.2
  83.5 13.5 %finish.1 = f32[16,4,4,6912]{3,2,1,0:T(4,128)} custom-call(f32[3,24,384]{2,1,0:T(8,128)} %weights.1.weight_ref, bf16[704,768]{1,0:T(8,128)(2,1)} %constant.82.clone.table_ref, bf16[512,256]{1,0:T(8,128)(2,1)} %select_convert_fusion.spread_any, bf16[48,6912]{1,0:T(8,128)(2,1)} %collide.2.refs_0_, bf16[48,6912]{1,0:T(8,128)(2,1)} %collide.3.refs_1_, ...), custom_call_target="tpu_custom_call" | custom-call | tf_op jit(solution)/shard_map/finish/pallas_call | solution.py:818
  (62 shorter events, 2.0 us)
Async XLA Ops:
  2.8 13.5 %copy-start.15 = (s32[16,4,4]{0,2,1:T(4,128)S(1)}, s32[16,4,4]{0,2,1:T(4,128)}, u32[]{:S(2)}) copy-start(s32[16,4,4]{0,2,1:T(4,128)} %param.10) | copy-start | bytes 3076
  2.9 16.7 %collective-permute-start.5 = (bf16[9,32,128]{2,1,0:T(8,128)(2,1)}, bf16[9,32,128]{2,1,0:T(8,128)(2,1)S(1)}, u32[]{:S(2)}, u32[]{:S(2)}) collective-permute-start(bf16[9,32,128]{2,1,0:T(8,128)(2,1)} %get-tuple-element.38), channel_id=1, source_target_pairs={{0,12},{4,0},{8,4},{12,8},{16,20},{20,24},{24,28},{28,16},{1,13},{... | collective-permute-start | bytes 221192 | tf_op jit(solution)/shard_map/ppermute | solution.py:759
  5.3 14.3 %collective-permute-start.3 = (bf16[5,128,128]{2,1,0:T(8,128)(2,1)}, bf16[5,128,128]{2,1,0:T(8,128)(2,1)S(1)}, u32[]{:S(2)}, u32[]{:S(2)}) collective-permute-start(bf16[5,128,128]{2,1,0:T(8,128)(2,1)} %get-tuple-element.36), channel_id=1, source_target_pairs={{0,3},{1,0},{2,1},{3,2},{4,7},{5,4},{6,5},{7,6},{8,11},{9,8},{10,9... | collective-permute-start | bytes 491528 | tf_op jit(solution)/shard_map/ppermute | solution.py:757
  8.9 10.7 %collective-permute-start.4 = (bf16[5,128,128]{2,1,0:T(8,128)(2,1)}, bf16[5,128,128]{2,1,0:T(8,128)(2,1)S(1)}, u32[]{:S(2)}, u32[]{:S(2)}) collective-permute-start(bf16[5,128,128]{2,1,0:T(8,128)(2,1)} %get-tuple-element.37), channel_id=1, source_target_pairs={{0,1},{1,2},{2,3},{3,0},{4,5},{5,6},{6,7},{7,4},{8,9},{9,10},{10,1... | collective-permute-start | bytes 491528 | tf_op jit(solution)/shard_map/ppermute | solution.py:758
  12.3 16.7 %collective-permute-start.2 = (bf16[18,32,128]{2,1,0:T(8,128)(2,1)}, bf16[18,32,128]{2,1,0:T(8,128)(2,1)S(1)}, u32[]{:S(2)}, u32[]{:S(2)}) collective-permute-start(bf16[18,32,128]{2,1,0:T(8,128)(2,1)} %get-tuple-element.35), channel_id=1, source_target_pairs={{0,12},{4,0},{8,4},{12,8},{16,20},{20,24},{24,28},{28,16},{1,13},{... | collective-permute-start | bytes 442376 | tf_op jit(solution)/shard_map/ppermute | solution.py:759
  12.8 23.0 %collective-permute-start = (bf16[10,128,128]{2,1,0:T(8,128)(2,1)}, bf16[10,128,128]{2,1,0:T(8,128)(2,1)S(1)}, u32[]{:S(2)}, u32[]{:S(2)}) collective-permute-start(bf16[10,128,128]{2,1,0:T(8,128)(2,1)} %get-tuple-element.33), channel_id=1, source_target_pairs={{0,3},{1,0},{2,1},{3,2},{4,7},{5,4},{6,5},{7,6},{8,11},{9,8},{10,9... | collective-permute-start | bytes 983048 | tf_op jit(solution)/shard_map/ppermute | solution.py:757
  17.7 14.4 %copy-start.5 = (f32[24,24,24]{2,1,0:T(8,128)S(1)}, f32[24,24,24]{2,1,0:T(8,128)}, u32[]{:S(2)}) copy-start(f32[24,24,24]{2,1,0:T(8,128)} %param.11) | copy-start | bytes 165892
  17.8 14.4 %copy-start.6 = (f32[24,24,24]{2,1,0:T(8,128)S(1)}, f32[24,24,24]{2,1,0:T(8,128)}, u32[]{:S(2)}) copy-start(f32[24,24,24]{2,1,0:T(8,128)} %param.12) | copy-start | bytes 165892
  19.3 13.1 %copy-start.7 = (f32[24,24,24]{2,1,0:T(8,128)S(1)}, f32[24,24,24]{2,1,0:T(8,128)}, u32[]{:S(2)}) copy-start(f32[24,24,24]{2,1,0:T(8,128)} %param.13) | copy-start | bytes 165892
  19.6 0.6 copy-start.14
  19.6 16.2 %collective-permute-start.1 = (bf16[10,128,128]{2,1,0:T(8,128)(2,1)}, bf16[10,128,128]{2,1,0:T(8,128)(2,1)S(1)}, u32[]{:S(2)}, u32[]{:S(2)}) collective-permute-start(bf16[10,128,128]{2,1,0:T(8,128)(2,1)} %get-tuple-element.34), channel_id=1, source_target_pairs={{0,1},{1,2},{2,3},{3,0},{4,5},{5,6},{6,7},{7,4},{8,9},{9,10},{10,1... | collective-permute-start | bytes 983048 | tf_op jit(solution)/shard_map/ppermute | solution.py:758
  19.7 0.7 copy-start.10
  19.7 0.7 copy-start.11
  26.9 19.5 %collective-permute-start.8 = (bf16[32,2304]{1,0:T(8,128)(2,1)}, bf16[32,2304]{1,0:T(8,128)(2,1)S(1)}, u32[]{:S(2)}, u32[]{:S(2)}) collective-permute-start(bf16[32,2304]{1,0:T(8,128)(2,1)} %get-tuple-element.44.refs_2_), channel_id=1, source_target_pairs={{0,16},{16,0},{1,17},{17,1},{2,18},{18,2},{3,19},{19,3},{4,20},{20... | collective-permute-start | bytes 442376 | tf_op jit(solution)/shard_map/ppermute | solution.py:750
  28.5 18.0 %collective-permute-start.6 = (bf16[48,2304]{1,0:T(8,128)(2,1)}, bf16[48,2304]{1,0:T(8,128)(2,1)S(1)}, u32[]{:S(2)}, u32[]{:S(2)}) collective-permute-start(bf16[48,2304]{1,0:T(8,128)(2,1)} %get-tuple-element.42.refs_0_), channel_id=1, source_target_pairs={{0,16},{16,0},{1,17},{17,1},{2,18},{18,2},{3,19},{19,3},{4,20},{20... | collective-permute-start | bytes 663560 | tf_op jit(solution)/shard_map/ppermute | solution.py:750
  29.0 6.8 %copy-start.12 = (bf16[18,32,128]{2,1,0:T(8,128)(2,1)}, bf16[18,32,128]{2,1,0:T(8,128)(2,1)S(1)}, u32[]{:S(2)}) copy-start(bf16[18,32,128]{2,1,0:T(8,128)(2,1)S(1)} %collective-permute-done.2.across_ref) | copy-start | bytes 442372
  29.0 17.4 %collective-permute-start.7 = (bf16[48,2304]{1,0:T(8,128)(2,1)}, bf16[48,2304]{1,0:T(8,128)(2,1)S(1)}, u32[]{:S(2)}, u32[]{:S(2)}) collective-permute-start(bf16[48,2304]{1,0:T(8,128)(2,1)} %get-tuple-element.43.refs_0_), channel_id=1, source_target_pairs={{0,16},{16,0},{1,17},{17,1},{2,18},{18,2},{3,19},{19,3},{4,20},{20... | collective-permute-start | bytes 663560 | tf_op jit(solution)/shard_map/ppermute | solution.py:750
  35.8 0.7 copy-start.3
  35.8 0.8 copy-start.4
  46.4 36.3 %copy-start.13 = (bf16[32,2304]{1,0:T(8,128)(2,1)}, bf16[32,2304]{1,0:T(8,128)(2,1)S(1)}, u32[]{:S(2)}) copy-start(bf16[32,2304]{1,0:T(8,128)(2,1)S(1)} %collective-permute-done.8.refs_5_) | copy-start | bytes 442372
  46.5 12.3 %copy-start.9 = (bf16[48,2304]{1,0:T(8,128)(2,1)}, bf16[48,2304]{1,0:T(8,128)(2,1)S(1)}, u32[]{:S(2)}) copy-start(bf16[48,2304]{1,0:T(8,128)(2,1)S(1)} %collective-permute-done.6.refs_3_) | copy-start | bytes 663556
  46.5 25.0 %copy-start.8 = (bf16[48,2304]{1,0:T(8,128)(2,1)}, bf16[48,2304]{1,0:T(8,128)(2,1)S(1)}, u32[]{:S(2)}) copy-start(bf16[48,2304]{1,0:T(8,128)(2,1)S(1)} %collective-permute-done.7.refs_3_) | copy-start | bytes 663556
  46.5 11.8 %collective-permute-start.9 = (bf16[96,2304]{1,0:T(8,128)(2,1)}, bf16[96,2304]{1,0:T(8,128)(2,1)S(1)}, u32[]{:S(2)}, u32[]{:S(2)}) collective-permute-start(bf16[96,2304]{1,0:T(8,128)(2,1)} %get-tuple-element.54.refs_1_.refs_2_), channel_id=1, source_target_pairs={{0,16},{16,0},{1,17},{17,1},{2,18},{18,2},{3,19},{19,3},{4,20},{20... | collective-permute-start | bytes 1327112 | tf_op jit(solution)/shard_map/ppermute | solution.py:750
  58.3 0.8 copy-start.1
  58.3 11.8 %collective-permute-start.10 = (bf16[96,2304]{1,0:T(8,128)(2,1)}, bf16[96,2304]{1,0:T(8,128)(2,1)S(1)}, u32[]{:S(2)}, u32[]{:S(2)}) collective-permute-start(bf16[96,2304]{1,0:T(8,128)(2,1)} %get-tuple-element.56.refs_1_.refs_2_), channel_id=1, source_target_pairs={{0,16},{16,0},{1,17},{17,1},{2,18},{18,2},{3,19},{19,3},{4,20},{20... | collective-permute-start | bytes 1327112 | tf_op jit(solution)/shard_map/ppermute | solution.py:750
  70.2 1.3 %copy-start = (bf16[96,2304]{1,0:T(8,128)(2,1)}, bf16[96,2304]{1,0:T(8,128)(2,1)S(1)}, u32[]{:S(2)}) copy-start(bf16[96,2304]{1,0:T(8,128)(2,1)S(1)} %collective-permute-done.10.refs_4_.refs_5_) | copy-start | bytes 1327108
  70.2 12.5 %collective-permute-start.11 = (bf16[64,2304]{1,0:T(8,128)(2,1)}, bf16[64,2304]{1,0:T(8,128)(2,1)S(1)}, u32[]{:S(2)}, u32[]{:S(2)}) collective-permute-start(bf16[64,2304]{1,0:T(8,128)(2,1)} %get-tuple-element.58.refs_3_.refs_4_), channel_id=1, source_target_pairs={{0,16},{16,0},{1,17},{17,1},{2,18},{18,2},{3,19},{19,3},{4,20},{20... | collective-permute-start | bytes 884744 | tf_op jit(solution)/shard_map/ppermute | solution.py:750
  82.7 0.7 copy-start.2

commit v6 on v5

--- a/solution.py
+++ b/solution.py
@@ -145,7 +145,9 @@
     rows = slice(margin, margin + points * points)
     table[rows, : len(pairs)] = np.cos(angles)
     table[rows, padded : padded + len(pairs)] = -np.sin(angles)
-    return table.astype(ml_dtypes.bfloat16)
+    window = points * points + margin
+    back = np.stack([table[margin : margin + window].T, table[:window].T])
+    return table.astype(ml_dtypes.bfloat16), back.astype(ml_dtypes.bfloat16)
 
 
 def frequency_select(points, padded):
@@ -297,26 +299,24 @@
         put(across_ref, s, tile_pair(plane_ref, s, plane_ref.shape[1]))
 
 
-def upwind_kernel(
-    base,
-    counts,
-    side_ref,
-    speed_ref,
-    picker_ref,
-    field_ref,
-    down_ref,
-    up_ref,
-    across_ref,
-    out_ref,
-    *refs,
-):
-    chosen_refs, scratch = refs[:-7], refs[-7:]
-    blocks, reads, wide, border, cells, load_sems, store_sems = scratch
+def upwind_kernel(base, counts, side_ref, *refs):
+    batches = len(counts)
+    outer_refs, field_ref = refs[:5], refs[5]
+    out_ref, target_refs, scratch = refs[6], refs[7 : 7 + batches], refs[7 + batches :]
+    inner_refs, chosen_refs, scratch = scratch[:5], scratch[5 : 5 + batches], scratch[5 + batches :]
+    speed_ref, picker_ref, down_ref, up_ref, across_ref = inner_refs
+    blocks, reads, wide, border, cells, load_sems, store_sems, side_sems = scratch
     chunks, width_x, width_y, width_z, lanes = blocks.shape
     steps = lanes // (2 * LANES)
     group_lanes = chosen_refs[0].shape[1]
     per_group = group_lanes // lanes
     half_steps = per_group * steps // 2 + 1
+    inputs = [
+        pltpu.make_async_copy(source, target, side_sems.at[at])
+        for at, (source, target) in enumerate(zip(outer_refs, inner_refs))
+    ]
+    for copy in inputs:
+        copy.start()
     loads = []
     for t in range(chunks):
         source = field_ref.at[:, :, :, pl.ds(base + t * lanes, lanes)]
@@ -326,6 +326,8 @@
     place = lax.broadcasted_iota(jnp.int32, (1, 8, LANES), 1) % width_z
     capacity = picker_ref.shape[0] // 2
     stores = []
+    for copy in inputs:
+        copy.wait()
     for t in range(chunks):
         group, chunk = t // per_group, t % per_group
         sizes, falls, sinks = [], [], []
@@ -397,6 +399,9 @@
                     here = slice(tile * LANES, (tile + 1) * LANES)
                     ref[rows, here] = picked[first : first + count, u * LANES : (u + 1) * LANES]
                 first += count
+    for at, (source, target) in enumerate(zip(chosen_refs, target_refs)):
+        stores.append(pltpu.make_async_copy(source, target, store_sems.at[chunks + at]))
+        stores[-1].start()
     for store in stores:
         store.wait()
 
@@ -471,28 +476,28 @@
     lax.fori_loop(0, slots // 16 * lane_tiles, transform, 0)
 
 
-def terms_of(part, table_ref, cells_ref, back, put):
+def inverse_parts(back_table, back):
+    _, kernels, pairs, slots, depth = back.shape
+    window = back_table.shape[2]
+    return [
+        jnp.dot(
+            back[parity].reshape(kernels * pairs * slots, depth),
+            back_table[parity],
+            preferred_element_type=jnp.float32,
+        ).reshape(kernels, pairs, slots, window)
+        for parity in range(2)
+    ]
+
+
+def terms_of(part, outs, cells_ref, put):
     _, slots, lanes = cells_ref.shape
-    height = table_ref.shape[0]
-    window = height - 64
-    pair_lanes = 2 * (height - 128)
+    window = outs[0].shape[3]
+    pair_lanes = 2 * (window - 64)
     pairs = lanes // pair_lanes
-    outs = []
-    for parity in range(2):
-        start = 64 * (1 - parity)
-        outs.append(
-            lax.dot_general(
-                back[parity, :, part * pairs : (part + 1) * pairs].reshape(
-                    3 * pairs * slots, back.shape[-1]
-                ),
-                table_ref[start : start + window, :],
-                (((1,), (1,)), ((), ())),
-                preferred_element_type=jnp.float32,
-            ).reshape(3, pairs, slots, window)
-        )
     tiles = pair_lanes // LANES
     near = lax.broadcasted_iota(jnp.int32, (slots, LANES), 1) < 64
-    for at in range(pairs):
+    for pair in range(pairs):
+        at = part * pairs + pair
         for tile in range(tiles):
             lane = tile * LANES
             odd_lane = lane - (pair_lanes - window)
@@ -509,31 +514,35 @@
                         outs[1][which, at, :, odd_lane : odd_lane + LANES],
                     )
                 values.append(value)
-            lane = at * pair_lanes + lane
+            lane = pair * pair_lanes + lane
             cells = cells_ref[part, :, lane : lane + LANES].astype(jnp.float32)
-            put(at * tiles + tile, (values[0] * values[1] - cells * values[2]).astype(jnp.bfloat16))
-
-
-def collide_kernel(firsts, weight_ref, table_ref, *refs):
+            put(pair * tiles + tile, (values[0] * values[1] - cells * values[2]).astype(jnp.bfloat16))
+
+
+def collide_kernel(firsts, weight_ref, table_ref, back_any, *refs):
     parts = len(firsts) // 2
-    terms_ref, cells, section, back, sems = refs[2 * parts :]
+    terms_ref, cells, section, back, back_table, sems = refs[2 * parts :]
     lanes = cells.shape[2]
     loads = window_loads(firsts, refs[: 2 * parts], cells, sems)
+    table_load = pltpu.make_async_copy(back_any, back_table, sems.at[2 * parts])
+    table_load.start()
     filter_parts(weight_ref, table_ref, cells, loads, section, back)
+    table_load.wait()
+    outs = inverse_parts(back_table, back)
     for part in range(parts):
 
         def put(tile, value):
             first = part * lanes + tile * LANES
             terms_ref[:, first : first + LANES] = value
 
-        terms_of(part, table_ref, cells, back, put)
-
-
-def finish_kernel(firsts, sizes, weight_ref, table_ref, spread_any, *refs):
+        terms_of(part, outs, cells, put)
+
+
+def finish_kernel(firsts, sizes, weight_ref, table_ref, back_any, spread_any, *refs):
     parts = len(firsts) // 2
     term_refs, refs = refs[: len(sizes) - 1], refs[len(sizes) - 1 :]
     first_read, rest_read = refs[2 * parts : 2 * parts + 2]
-    out_ref, cells, section, back, reads, spots, added, staged = refs[2 * parts + 2 : -6]
+    out_ref, cells, section, back, back_table, reads, spots, added, staged = refs[2 * parts + 2 : -6]
     spread_ref, early_ref, cell_sems, read_sems, out_sems, extra_sems = refs[-6:]
     width_x, width_y, width_z, lanes = staged.shape[1:]
     tiles = lanes // LANES
@@ -544,6 +553,7 @@
         target = early_ref.at[pl.ds(at, size)]
         extra.append(pltpu.make_async_copy(ref, target, extra_sems.at[len(extra)]))
         at += size
+    extra.append(pltpu.make_async_copy(back_any, back_table, cell_sems.at[2 * parts]))
     group_rows = reads.shape[2]
     read_loads = []
     for part in range(parts):
@@ -557,6 +567,7 @@
         load.wait()
     early = early_ref.shape[0]
     capacity = early + section.shape[1]
+    outs = inverse_parts(back_table, back)
     pieces = out_sems.shape[1]
     piece_x = width_x // pieces
     stores = []
@@ -569,7 +580,7 @@
             spots[first : first + early, columns] = early_ref[:, lane : lane + LANES]
             spots[first + early : first + capacity, columns] = value
 
-        terms_of(part, table_ref, cells, back, put)
+        terms_of(part, outs, cells, put)
         added[...] = jnp.dot(spread_ref[...], spots[...], preferred_element_type=jnp.float32)
         read_loads[part].wait()
         slot = part % 2
@@ -677,7 +688,7 @@
 
     padded = -(-len(half_set(points)[1]) // LANES) * LANES
     select, scale = frequency_select(points, padded)
-    table = jnp.asarray(plane_table(points, padded, 64))
+    table, back_table = [jnp.asarray(t) for t in plane_table(points, padded, 64)]
 
     towards_lower = [(j, (j - 1) % count_y) for j in range(count_y)]
     towards_upper = [(j, (j + 1) % count_y) for j in range(count_y)]
@@ -719,15 +730,19 @@
 
     def upwind(at, halo, sizes):
         groups = parts - 1 if at else 1
+        operands = (speeds[at], picker, *halo)
+        chosen = [(groups * size, group) for size in sizes]
         return pl.pallas_call(
             functools.partial(upwind_kernel, at * group, sizes),
-            in_specs=[scalar, local, local, remote] + [local] * len(halo),
-            out_specs=[anywhere] + [local] * len(sizes),
+            in_specs=[scalar] + [anywhere] * (len(operands) + 1),
+            out_specs=[anywhere] * (1 + len(sizes)),
             out_shape=[
                 jax.ShapeDtypeStruct((block_rows, groups * group_rows, LANES), jnp.float32)
             ]
-            + [jax.ShapeDtypeStruct((groups * size, group), bf16) for size in sizes],
-            scratch_shapes=[
+            + [jax.ShapeDtypeStruct(shape, bf16) for shape in chosen],
+            scratch_shapes=[pltpu.VMEM(x.shape, x.dtype) for x in operands]
+            + [pltpu.VMEM(shape, bf16) for shape in chosen]
+            + [
                 pltpu.VMEM(
                     (groups * chunks, width_x, width_y, width_z, group // chunks), jnp.float32
                 ),
@@ -736,12 +751,13 @@
                 pltpu.VMEM((wide, width_x, 8, LANES), jnp.float32),
                 pltpu.VMEM((block_rows * 8, wide * LANES), bf16),
                 pltpu.SemaphoreType.DMA((groups * chunks,)),
-                pltpu.SemaphoreType.DMA((groups * chunks,)),
+                pltpu.SemaphoreType.DMA((groups * chunks + len(sizes),)),
+                pltpu.SemaphoreType.DMA((len(operands),)),
             ],
             compiler_params=params(LIMIT),
             cost_estimate=cost(1, 1),
             name="upwind",
-        )(side, speeds[at], picker, distribution, *halo)
+        )(side, *operands, distribution)
 
     def turn(value, *earlier):
         return lax.optimization_barrier((value, *earlier))[0]
@@ -783,9 +799,10 @@
             pltpu.VMEM((2 * parts, count, group), bf16),
             pltpu.VMEM((points, count, 2 * padded), jnp.float32),
             pltpu.VMEM((2, 3, points // 4, count, 2 * padded), bf16),
+            pltpu.VMEM(back_table.shape, bf16),
         ]
 
-    sems = pltpu.SemaphoreType.DMA((2 * parts,))
+    sems = pltpu.SemaphoreType.DMA((2 * parts + 1,))
     terms = []
     for batch in range(batches - 1):
         count = counts[batch]
@@ -795,7 +812,7 @@
         terms.append(
             pl.pallas_call(
                 functools.partial(collide_kernel, starts + starts),
-                in_specs=[local] * 2 + [anywhere] * (2 * parts),
+                in_specs=[local] * 2 + [anywhere] * (1 + 2 * parts),
                 out_specs=local,
                 out_shape=jax.ShapeDtypeStruct((count, local_vel), bf16),
                 scratch_shapes=scratch(count) + [sems],
@@ -805,6 +822,7 @@
             )(
                 weights,
                 table,
+                back_table,
                 first[batch],
                 *[rest[batch]] * (parts - 1),
                 first_other[batch],
@@ -817,7 +835,7 @@
     starts = (0,) + tuple(g * count for g in range(parts - 1))
     return pl.pallas_call(
         functools.partial(finish_kernel, starts + starts, counts),
-        in_specs=[local] * 2 + [anywhere] * (batches + 2 * parts + 2),
+        in_specs=[local] * 2 + [anywhere] * (1 + batches + 2 * parts + 2),
         out_specs=anywhere,
         out_shape=jax.ShapeDtypeStruct(distribution.shape, jnp.float32),
         scratch_shapes=scratch(count)
@@ -838,6 +856,7 @@
     )(
         weights,
         table,
+        back_table,
         spread,
         *terms,
         first[-1],

time: 97.6 us -> 94.6 us (0.969)
  Pallas kernels: 60.9 us -> 57.9 us
    pallas_call x2, Pallas kernels: 16.4 us -> 14.7 us  [upwind(): pl.pallas_call(functools.partial(upwind_kernel, at * group, sizes), in_sp...]
    pallas_call x1, Pallas kernels: 13.5 us -> 12.3 us  [fast_device(): pl.pallas_call(functools.partial(finish_kernel, starts + starts, counts),...]
    unnamed x32 -> x34, local copies, waits for them, and re-layouts: 2.71 us -> 2.7 us
  transfers between devices with their start and end apart: 12 -> 12, of which waited for: 1 -> 1; matrix products, arithmetic and copies ran while one was open for 6% -> 6% of each run, Pallas kernels for 46% -> 45%
where the time goes in v6:
time: 94.6 us; the launch traced here: 94.2 us
  Pallas kernels  57.9 us (61%)
  starting transfers between devices  16 us (17%)
  waiting for transfers between devices  11.2 us (12%)
  local copies, waits for them, and re-layouts  5.77 us (6%)
  other arithmetic  2.81 us (3%)
    pallas_call x2, Pallas kernels, fast_device(): pl.pallas_call(functools.partial(collide_kernel, starts + starts), in_spe...  22 us
    pallas_call x2, Pallas kernels, upwind(): pl.pallas_call(functools.partial(upwind_kernel, at * group, sizes), in_sp...  14.7 us
    pallas_call x1, Pallas kernels, fast_device(): pl.pallas_call(functools.partial(finish_kernel, starts + starts, counts),...  12.3 us
    ppermute x6, waiting for transfers between devices, swapped(): return lax.ppermute(value, 'vel', swap)  11.2 us
    ppermute x2, starting transfers between devices, fast_device(): lax.ppermute(down, 'cy', towards_lower)  7.18 us
    pallas_call x2, Pallas kernels, edges_of(): pl.pallas_call(functools.partial(edges_kernel, first * group), in_specs=[...  6.26 us
    ppermute x6, starting transfers between devices, swapped(): return lax.ppermute(value, 'vel', swap)  5.86 us
    ppermute x2, starting transfers between devices, fast_device(): lax.ppermute(across, ('vel', 'cx'), across_pairs)  2.91 us
  transfers between devices with their start and end apart: 12, of which 1 were waited for; matrix products, arithmetic and copies ran while one was open for 6% of the time, Pallas kernels for 45%

profile of v6, /device:TPU:0, one launch (start us, length us, event | category | flops | bytes accessed | tf_op | source)
XLA Modules:
  0.0 94.2 jit_solution(507748811383207632)
XLA Ops:
  0.0 2.9 %edges.3 = (bf16[5,128,128]{2,1,0:T(8,128)(2,1)}, bf16[5,128,128]{2,1,0:T(8,128)(2,1)}, bf16[9,32,128]{2,1,0:T(8,128)(2,1)}) custom-call(s32[1]{0:T(128)} %bitcast.4.edge_ref, f32[72,128]{1,0:T(8,128)} %constant.83.clone.falls_ref, f32[16,4,4,6912]{3,2,1,0:T(4,128)} %refs_5_.3), custom_call_target="tpu_custom_call" | custom-call | flops 1 | bytes 1 | tf_op jit(solution)/shard_map/edges/pallas_call | solution.py:707
  2.9 2.5 %collective-permute-start.5 = (bf16[9,32,128]{2,1,0:T(8,128)(2,1)}, bf16[9,32,128]{2,1,0:T(8,128)(2,1)S(1)}, u32[]{:S(2)}, u32[]{:S(2)}) collective-permute-start(bf16[9,32,128]{2,1,0:T(8,128)(2,1)} %get-tuple-element.38), channel_id=1, source_target_pairs={{0,12},{4,0},{8,4},{12,8},{16,20},{20,24},{24,28},{28,16},{1,13},{... | collective-permute-start | bytes 221192 | tf_op jit(solution)/shard_map/ppermute | solution.py:775
  5.3 3.6 %collective-permute-start.3 = (bf16[5,128,128]{2,1,0:T(8,128)(2,1)}, bf16[5,128,128]{2,1,0:T(8,128)(2,1)S(1)}, u32[]{:S(2)}, u32[]{:S(2)}) collective-permute-start(bf16[5,128,128]{2,1,0:T(8,128)(2,1)} %get-tuple-element.36), channel_id=1, source_target_pairs={{0,3},{1,0},{2,1},{3,2},{4,7},{5,4},{6,5},{7,6},{8,11},{9,8},{10,9... | collective-permute-start | bytes 491528 | tf_op jit(solution)/shard_map/ppermute | solution.py:773
  8.9 3.4 %edges.2 = (bf16[10,128,128]{2,1,0:T(8,128)(2,1)}, bf16[10,128,128]{2,1,0:T(8,128)(2,1)}, bf16[18,32,128]{2,1,0:T(8,128)(2,1)}) custom-call(s32[1]{0:T(128)} %bitcast.4.edge_ref, f32[72,128]{1,0:T(8,128)} %constant.83.clone.falls_ref, f32[16,4,4,6912]{3,2,1,0:T(4,128)} %refs_5_.3), custom_call_target="tpu_custom_call" | custom-call | flops 1 | bytes 1 | tf_op jit(solution)/shard_map/edges/pallas_call | solution.py:707
  12.4 0.4 collective-permute-start.2
  12.8 3.6 %collective-permute-start = (bf16[10,128,128]{2,1,0:T(8,128)(2,1)}, bf16[10,128,128]{2,1,0:T(8,128)(2,1)S(1)}, u32[]{:S(2)}, u32[]{:S(2)}) collective-permute-start(bf16[10,128,128]{2,1,0:T(8,128)(2,1)} %get-tuple-element.33), channel_id=1, source_target_pairs={{0,3},{1,0},{2,1},{3,2},{4,7},{5,4},{6,5},{7,6},{8,11},{9,8},{10,9... | collective-permute-start | bytes 983048 | tf_op jit(solution)/shard_map/ppermute | solution.py:773
  17.8 0.6 slice_bitcast_fusion.refs_0_
  18.5 0.8 fusion.refs_1_
  19.7 0.5 copy-done.15
  20.2 0.1 copy-done.11
  20.4 5.5 %upwind.2 = (f32[64,72,128]{2,1,0:T(8,128)}, bf16[48,2304]{1,0:T(8,128)(2,1)}, bf16[48,2304]{1,0:T(8,128)(2,1)}, bf16[32,2304]{1,0:T(8,128)(2,1)}) custom-call(s32[1]{0:T(128)} %bitcast.side_ref, f32[3,72,128]{2,1,0:T(8,128)} %slice_bitcast_fusion.refs_0_, bf16[256,512]{1,0:T(8,128)(2,1)} %fusion.refs_1_, bf16[5,128,128]{2,1,0:T(8,128)(2,1)} %copy-done.11, ...), custom_call_target="tpu_custom_call" | custom-call | flops 1 | bytes 1 | tf_op jit(solution)/shard_map/upwind/pallas_call | solution.py:735
  25.9 1.5 %collective-permute-start.8 = (bf16[32,2304]{1,0:T(8,128)(2,1)}, bf16[32,2304]{1,0:T(8,128)(2,1)S(1)}, u32[]{:S(2)}, u32[]{:S(2)}) collective-permute-start(bf16[32,2304]{1,0:T(8,128)(2,1)} %get-tuple-element.44.refs_2_), channel_id=1, source_target_pairs={{0,16},{16,0},{1,17},{17,1},{2,18},{18,2},{3,19},{19,3},{4,20},{20... | collective-permute-start | bytes 442376 | tf_op jit(solution)/shard_map/ppermute | solution.py:766
  27.4 0.6 collective-permute-start.6
  28.0 1.5 %collective-permute-start.7 = (bf16[48,2304]{1,0:T(8,128)(2,1)}, bf16[48,2304]{1,0:T(8,128)(2,1)S(1)}, u32[]{:S(2)}, u32[]{:S(2)}) collective-permute-start(bf16[48,2304]{1,0:T(8,128)(2,1)} %get-tuple-element.43.refs_0_), channel_id=1, source_target_pairs={{0,16},{16,0},{1,17},{17,1},{2,18},{18,2},{3,19},{19,3},{4,20},{20... | collective-permute-start | bytes 663560 | tf_op jit(solution)/shard_map/ppermute | solution.py:766
  29.4 0.9 select_convert_fusion.spread_any
  30.4 0.7 slice.8
  31.1 0.1 reshape.249
  31.2 0.1 reshape.250
  31.4 0.1 reshape.251
  31.5 0.7 pad_maximum_fusion.stacked_ref
  32.2 2.5 %weights.1.weight_ref = f32[3,24,384]{2,1,0:T(8,128)} custom-call(f32[72,576]{1,0:T(8,128)} %pad_maximum_fusion.stacked_ref, bf16[576,768]{1,0:T(8,128)(2,1)} %constant.86.clone.select_ref, f32[1,384]{1,0:T(1,128)} %constant.87.clone.scale_ref), custom_call_target="tpu_custom_call" | custom-call | flops 1 | bytes 1 | tf_op jit(solution)/shard_map/weights/pallas_call | solution.py:782
  34.8 0.7 copy-done.4
  35.6 9.3 %upwind.3 = (f32[64,144,128]{2,1,0:T(8,128)}, bf16[96,2304]{1,0:T(8,128)(2,1)}, bf16[96,2304]{1,0:T(8,128)(2,1)}, bf16[64,2304]{1,0:T(8,128)(2,1)}) custom-call(s32[1]{0:T(128)} %bitcast.side_ref, f32[3,144,128]{2,1,0:T(8,128)} %bitcast.15, bf16[256,512]{1,0:T(8,128)(2,1)} %fusion.refs_1_, bf16[10,128,128]{2,1,0:T(8,128)(2,1)} %copy-done.4, ...), custom_call_target="tpu_custom_call" | custom-call | flops 1 | bytes 1 | tf_op jit(solution)/shard_map/upwind/pallas_call | solution.py:735
  44.9 0.6 collective-permute-start.9
  45.5 11.2 %collective-permute-done.9.refs_4_.refs_5_ = bf16[96,2304]{1,0:T(8,128)(2,1)S(1)} collective-permute-done((bf16[96,2304]{1,0:T(8,128)(2,1)}, bf16[96,2304]{1,0:T(8,128)(2,1)S(1)}, u32[]{:S(2)}, u32[]{:S(2)}) %collective-permute-start.9) | collective-permute-done | bytes 442400 | tf_op jit(solution)/shard_map/ppermute | solution.py:766
  56.8 0.4 collective-permute-start.10
  57.1 0.4 copy-done.1
  57.6 11.0 %collide.2.refs_0_ = bf16[48,6912]{1,0:T(8,128)(2,1)} custom-call(f32[3,24,384]{2,1,0:T(8,128)} %weights.1.weight_ref, bf16[704,768]{1,0:T(8,128)(2,1)} %constant.84.clone.table_ref, bf16[2,768,640]{2,1,0:T(8,128)(2,1)} %constant.85.clone.back_any, bf16[48,2304]{1,0:T(8,128)(2,1)} %get-tuple-element.42.refs_0_, ...), custom_call_target="tpu_custom_call" | custom-call | flops 1 | bytes 1 | tf_op jit(solution)/shard_map/collide/pallas_call | solution.py:813
  68.6 1.3 %collective-permute-start.11 = (bf16[64,2304]{1,0:T(8,128)(2,1)S(1)}, bf16[64,2304]{1,0:T(8,128)(2,1)S(1)}, u32[]{:S(2)}, u32[]{:S(2)}) collective-permute-start(bf16[64,2304]{1,0:T(8,128)(2,1)S(1)} %copy-done.2), channel_id=1, source_target_pairs={{0,16},{16,0},{1,17},{17,1},{2,18},{18,2},{3,19},{19,3},{4,20},{20... | collective-permute-start | bytes 884744 | tf_op jit(solution)/shard_map/ppermute | solution.py:766
  69.9 11.0 %collide.3.refs_1_ = bf16[48,6912]{1,0:T(8,128)(2,1)} custom-call(f32[3,24,384]{2,1,0:T(8,128)} %weights.1.weight_ref, bf16[704,768]{1,0:T(8,128)(2,1)} %constant.84.clone.table_ref, bf16[2,768,640]{2,1,0:T(8,128)(2,1)} %constant.85.clone.back_any, bf16[48,2304]{1,0:T(8,128)(2,1)} %get-tuple-element.43.refs_0_, ...), custom_call_target="tpu_custom_call" | custom-call | flops 1 | bytes 1 | tf_op jit(solution)/shard_map/collide/pallas_call | solution.py:813
  81.0 0.7 copy-done.3
  81.7 12.3 %finish.1 = f32[16,4,4,6912]{3,2,1,0:T(4,128)} custom-call(f32[3,24,384]{2,1,0:T(8,128)} %weights.1.weight_ref, bf16[704,768]{1,0:T(8,128)(2,1)} %constant.84.clone.table_ref, bf16[2,768,640]{2,1,0:T(8,128)(2,1)} %constant.85.clone.back_any, bf16[512,256]{1,0:T(8,128)(2,1)} %select_convert_fusion.spread_any, bf16[48,6912]{1,0:T(8,128)(2,1)} %collide.2.refs_0_, ...), custom_call_target="tpu_custom_call" | custom-call | tf_op jit(solution)/shard_map/finish/pallas_call | solution.py:836
  (64 shorter events, 2.0 us)
Async XLA Ops:
  2.9 13.5 %copy-start.16 = (s32[16,4,4]{0,2,1:T(4,128)S(1)}, s32[16,4,4]{0,2,1:T(4,128)}, u32[]{:S(2)}) copy-start(s32[16,4,4]{0,2,1:T(4,128)} %param.11) | copy-start | bytes 3076
  2.9 16.7 %collective-permute-start.5 = (bf16[9,32,128]{2,1,0:T(8,128)(2,1)}, bf16[9,32,128]{2,1,0:T(8,128)(2,1)S(1)}, u32[]{:S(2)}, u32[]{:S(2)}) collective-permute-start(bf16[9,32,128]{2,1,0:T(8,128)(2,1)} %get-tuple-element.38), channel_id=1, source_target_pairs={{0,12},{4,0},{8,4},{12,8},{16,20},{20,24},{24,28},{28,16},{1,13},{... | collective-permute-start | bytes 221192 | tf_op jit(solution)/shard_map/ppermute | solution.py:775
  5.3 14.3 %collective-permute-start.3 = (bf16[5,128,128]{2,1,0:T(8,128)(2,1)}, bf16[5,128,128]{2,1,0:T(8,128)(2,1)S(1)}, u32[]{:S(2)}, u32[]{:S(2)}) collective-permute-start(bf16[5,128,128]{2,1,0:T(8,128)(2,1)} %get-tuple-element.36), channel_id=1, source_target_pairs={{0,3},{1,0},{2,1},{3,2},{4,7},{5,4},{6,5},{7,6},{8,11},{9,8},{10,9... | collective-permute-start | bytes 491528 | tf_op jit(solution)/shard_map/ppermute | solution.py:773
  8.9 10.8 %collective-permute-start.4 = (bf16[5,128,128]{2,1,0:T(8,128)(2,1)}, bf16[5,128,128]{2,1,0:T(8,128)(2,1)S(1)}, u32[]{:S(2)}, u32[]{:S(2)}) collective-permute-start(bf16[5,128,128]{2,1,0:T(8,128)(2,1)} %get-tuple-element.37), channel_id=1, source_target_pairs={{0,1},{1,2},{2,3},{3,0},{4,5},{5,6},{6,7},{7,4},{8,9},{9,10},{10,1... | collective-permute-start | bytes 491528 | tf_op jit(solution)/shard_map/ppermute | solution.py:774
  12.4 15.6 %collective-permute-start.2 = (bf16[18,32,128]{2,1,0:T(8,128)(2,1)}, bf16[18,32,128]{2,1,0:T(8,128)(2,1)S(1)}, u32[]{:S(2)}, u32[]{:S(2)}) collective-permute-start(bf16[18,32,128]{2,1,0:T(8,128)(2,1)} %get-tuple-element.35), channel_id=1, source_target_pairs={{0,12},{4,0},{8,4},{12,8},{16,20},{20,24},{24,28},{28,16},{1,13},{... | collective-permute-start | bytes 442376 | tf_op jit(solution)/shard_map/ppermute | solution.py:775
  12.8 21.9 %collective-permute-start = (bf16[10,128,128]{2,1,0:T(8,128)(2,1)}, bf16[10,128,128]{2,1,0:T(8,128)(2,1)S(1)}, u32[]{:S(2)}, u32[]{:S(2)}) collective-permute-start(bf16[10,128,128]{2,1,0:T(8,128)(2,1)} %get-tuple-element.33), channel_id=1, source_target_pairs={{0,3},{1,0},{2,1},{3,2},{4,7},{5,4},{6,5},{7,6},{8,11},{9,8},{10,9... | collective-permute-start | bytes 983048 | tf_op jit(solution)/shard_map/ppermute | solution.py:773
  17.8 13.3 %copy-start.6 = (f32[24,24,24]{2,1,0:T(8,128)S(1)}, f32[24,24,24]{2,1,0:T(8,128)}, u32[]{:S(2)}) copy-start(f32[24,24,24]{2,1,0:T(8,128)} %param.12) | copy-start | bytes 165892
  17.8 13.4 %copy-start.7 = (f32[24,24,24]{2,1,0:T(8,128)S(1)}, f32[24,24,24]{2,1,0:T(8,128)}, u32[]{:S(2)}) copy-start(f32[24,24,24]{2,1,0:T(8,128)} %param.13) | copy-start | bytes 165892
  19.3 12.1 %copy-start.8 = (f32[24,24,24]{2,1,0:T(8,128)S(1)}, f32[24,24,24]{2,1,0:T(8,128)}, u32[]{:S(2)}) copy-start(f32[24,24,24]{2,1,0:T(8,128)} %param.14) | copy-start | bytes 165892
  19.6 0.6 copy-start.15
  19.6 15.1 %collective-permute-start.1 = (bf16[10,128,128]{2,1,0:T(8,128)(2,1)}, bf16[10,128,128]{2,1,0:T(8,128)(2,1)S(1)}, u32[]{:S(2)}, u32[]{:S(2)}) collective-permute-start(bf16[10,128,128]{2,1,0:T(8,128)(2,1)} %get-tuple-element.34), channel_id=1, source_target_pairs={{0,1},{1,2},{2,3},{3,0},{4,5},{5,6},{6,7},{7,4},{8,9},{9,10},{10,1... | collective-permute-start | bytes 983048 | tf_op jit(solution)/shard_map/ppermute | solution.py:774
  19.7 0.7 copy-start.11
  19.7 0.7 copy-start.12
  25.9 19.0 %collective-permute-start.8 = (bf16[32,2304]{1,0:T(8,128)(2,1)}, bf16[32,2304]{1,0:T(8,128)(2,1)S(1)}, u32[]{:S(2)}, u32[]{:S(2)}) collective-permute-start(bf16[32,2304]{1,0:T(8,128)(2,1)} %get-tuple-element.44.refs_2_), channel_id=1, source_target_pairs={{0,16},{16,0},{1,17},{17,1},{2,18},{18,2},{3,19},{19,3},{4,20},{20... | collective-permute-start | bytes 442376 | tf_op jit(solution)/shard_map/ppermute | solution.py:766
  27.4 17.5 %collective-permute-start.6 = (bf16[48,2304]{1,0:T(8,128)(2,1)}, bf16[48,2304]{1,0:T(8,128)(2,1)S(1)}, u32[]{:S(2)}, u32[]{:S(2)}) collective-permute-start(bf16[48,2304]{1,0:T(8,128)(2,1)} %get-tuple-element.42.refs_0_), channel_id=1, source_target_pairs={{0,16},{16,0},{1,17},{17,1},{2,18},{18,2},{3,19},{19,3},{4,20},{20... | collective-permute-start | bytes 663560 | tf_op jit(solution)/shard_map/ppermute | solution.py:766
  28.0 6.8 %copy-start.13 = (bf16[18,32,128]{2,1,0:T(8,128)(2,1)}, bf16[18,32,128]{2,1,0:T(8,128)(2,1)S(1)}, u32[]{:S(2)}) copy-start(bf16[18,32,128]{2,1,0:T(8,128)(2,1)S(1)} %collective-permute-done.2.refs_4_) | copy-start | bytes 442372
  28.0 16.9 %collective-permute-start.7 = (bf16[48,2304]{1,0:T(8,128)(2,1)}, bf16[48,2304]{1,0:T(8,128)(2,1)S(1)}, u32[]{:S(2)}, u32[]{:S(2)}) collective-permute-start(bf16[48,2304]{1,0:T(8,128)(2,1)} %get-tuple-element.43.refs_0_), channel_id=1, source_target_pairs={{0,16},{16,0},{1,17},{17,1},{2,18},{18,2},{3,19},{19,3},{4,20},{20... | collective-permute-start | bytes 663560 | tf_op jit(solution)/shard_map/ppermute | solution.py:766
  34.7 0.7 copy-start.4
  34.7 0.8 copy-start.5
  44.8 23.7 %copy-start.2 = (bf16[64,2304]{1,0:T(8,128)(2,1)S(1)}, bf16[64,2304]{1,0:T(8,128)(2,1)}, u32[]{:S(2)}) copy-start(bf16[64,2304]{1,0:T(8,128)(2,1)} %get-tuple-element.58.refs_3_.refs_4_) | copy-start | bytes 884740
  44.9 36.1 %copy-start.14 = (bf16[32,2304]{1,0:T(8,128)(2,1)}, bf16[32,2304]{1,0:T(8,128)(2,1)S(1)}, u32[]{:S(2)}) copy-start(bf16[32,2304]{1,0:T(8,128)(2,1)S(1)} %collective-permute-done.8.refs_5_) | copy-start | bytes 442372
  44.9 12.3 %copy-start.10 = (bf16[48,2304]{1,0:T(8,128)(2,1)}, bf16[48,2304]{1,0:T(8,128)(2,1)S(1)}, u32[]{:S(2)}) copy-start(bf16[48,2304]{1,0:T(8,128)(2,1)S(1)} %collective-permute-done.6.refs_3_) | copy-start | bytes 663556
  44.9 25.0 %copy-start.9 = (bf16[48,2304]{1,0:T(8,128)(2,1)}, bf16[48,2304]{1,0:T(8,128)(2,1)S(1)}, u32[]{:S(2)}) copy-start(bf16[48,2304]{1,0:T(8,128)(2,1)S(1)} %collective-permute-done.7.refs_3_) | copy-start | bytes 663556
  44.9 11.9 %collective-permute-start.9 = (bf16[96,2304]{1,0:T(8,128)(2,1)}, bf16[96,2304]{1,0:T(8,128)(2,1)S(1)}, u32[]{:S(2)}, u32[]{:S(2)}) collective-permute-start(bf16[96,2304]{1,0:T(8,128)(2,1)} %get-tuple-element.54.refs_1_.refs_2_), channel_id=1, source_target_pairs={{0,16},{16,0},{1,17},{17,1},{2,18},{18,2},{3,19},{19,3},{4,20},{20... | collective-permute-start | bytes 1327112 | tf_op jit(solution)/shard_map/ppermute | solution.py:766
  56.8 0.8 copy-start.1
  56.8 11.8 %collective-permute-start.10 = (bf16[96,2304]{1,0:T(8,128)(2,1)}, bf16[96,2304]{1,0:T(8,128)(2,1)S(1)}, u32[]{:S(2)}, u32[]{:S(2)}) collective-permute-start(bf16[96,2304]{1,0:T(8,128)(2,1)} %get-tuple-element.56.refs_1_.refs_2_), channel_id=1, source_target_pairs={{0,16},{16,0},{1,17},{17,1},{2,18},{18,2},{3,19},{19,3},{4,20},{20... | collective-permute-start | bytes 1327112 | tf_op jit(solution)/shard_map/ppermute | solution.py:766
  68.6 1.3 %copy-start = (bf16[96,2304]{1,0:T(8,128)(2,1)}, bf16[96,2304]{1,0:T(8,128)(2,1)S(1)}, u32[]{:S(2)}) copy-start(bf16[96,2304]{1,0:T(8,128)(2,1)S(1)} %collective-permute-done.10.refs_4_.refs_5_) | copy-start | bytes 1327108
  68.6 12.4 %collective-permute-start.11 = (bf16[64,2304]{1,0:T(8,128)(2,1)S(1)}, bf16[64,2304]{1,0:T(8,128)(2,1)S(1)}, u32[]{:S(2)}, u32[]{:S(2)}) collective-permute-start(bf16[64,2304]{1,0:T(8,128)(2,1)S(1)} %copy-done.2), channel_id=1, source_target_pairs={{0,16},{16,0},{1,17},{17,1},{2,18},{18,2},{3,19},{19,3},{4,20},{20... | collective-permute-start | bytes 884744 | tf_op jit(solution)/shard_map/ppermute | solution.py:766
  81.0 0.7 copy-start.3

commit v7 on v6

--- a/solution.py
+++ b/solution.py
@@ -139,14 +139,39 @@
 def plane_table(points, padded, margin):
     pairs, _ = half_set(points)
     first, second = np.divmod(np.arange(points * points), points)
-    products = (first[:, None] * pairs[None, :, 0] + second[:, None] * pairs[None, :, 1]) % points
-    angles = 2.0 * np.pi * products / points
+    index = np.arange(points)
+    angles = (index[:, None] * index[None, :] % points).astype(np.float32)
+    angles = angles * np.float32(2.0 * np.pi / points)
+    cosine, sine = [
+        t.astype(ml_dtypes.bfloat16).astype(np.float32) for t in (np.cos(angles), np.sin(angles))
+    ]
+    cos_y, sin_y = cosine[first][:, pairs[:, 0]], sine[first][:, pairs[:, 0]]
+    cos_z, sin_z = cosine[second][:, pairs[:, 1]], sine[second][:, pairs[:, 1]]
     table = np.zeros((points * points + 2 * margin, 2 * padded), np.float32)
     rows = slice(margin, margin + points * points)
-    table[rows, : len(pairs)] = np.cos(angles)
-    table[rows, padded : padded + len(pairs)] = -np.sin(angles)
+    table[rows, : len(pairs)] = cos_y * cos_z - sin_y * sin_z
+    table[rows, padded : padded + len(pairs)] = -(cos_y * sin_z + sin_y * cos_z)
     window = points * points + margin
-    back = np.stack([table[margin : margin + window].T, table[:window].T])
+    level = np.flatnonzero(pairs[:, 1] == 0)
+    rest = table.copy()
+    rest[:, np.concatenate([level, padded + level])] = 0.0
+    for start in (points * points + margin, 0):
+        rest[start : start + points, level] = cosine[:, pairs[level, 0]]
+        rest[start : start + points, padded + level] = -sine[:, pairs[level, 0]]
+    back = np.stack([rest[margin : margin + window].T, rest[:window].T])
+    copies = np.zeros((2, LANES, window), np.float32)
+    place = np.arange(points * points)
+    copies[0, (points * points + first) % LANES, place] = 1.0
+    copies[1, first, margin + place] = 1.0
+    back = np.concatenate([back, copies], axis=1)
+    spare = len(pairs)
+    lift = np.zeros((LANES, 2 * padded), np.float32)
+    for half in (0, padded):
+        columns = slice(spare % LANES, spare % LANES + points)
+        lift[columns, half + level] = table[margin : margin + points**2 : points, half + level]
+        table[:, half + level] = 0.0
+    table[margin + place, spare + first] = 1.0
+    table = np.concatenate([table, lift])
     return table.astype(ml_dtypes.bfloat16), back.astype(ml_dtypes.bfloat16)
 
 
@@ -256,6 +281,19 @@
         part = ref[:, :, :, at : at + LANES]
         parts.append(part.reshape(rows, part.shape[2], LANES))
     return jnp.concatenate(parts, axis=1)
+
+
+def plane_speeds(points, local_vel, width_z):
+    index = np.arange(points**3)
+    parts = (index // (points * points), index // points % points, index % points)
+    speeds = [
+        np.float32(0.3) * (np.float32(2.0) * part.astype(np.float32) - np.float32(points - 1))
+        / np.float32(points - 1)
+        for part in parts
+    ]
+    tiled = np.stack(speeds).reshape(3, -1, local_vel // LANES, 1, LANES).transpose(1, 0, 2, 3, 4)
+    repeated = np.repeat(tiled, width_z, axis=3)
+    return repeated.reshape(repeated.shape[0], 3, -1, LANES)
 
 
 def edges_kernel(first, edge_ref, falls_ref, field_ref, *refs):
@@ -304,16 +342,19 @@
     outer_refs, field_ref = refs[:5], refs[5]
     out_ref, target_refs, scratch = refs[6], refs[7 : 7 + batches], refs[7 + batches :]
     inner_refs, chosen_refs, scratch = scratch[:5], scratch[5 : 5 + batches], scratch[5 + batches :]
-    speed_ref, picker_ref, down_ref, up_ref, across_ref = inner_refs
-    blocks, reads, wide, border, cells, load_sems, store_sems, side_sems = scratch
+    speed_ref, wanted_ref, down_ref, up_ref, across_ref = inner_refs
+    picker_ref, blocks, reads, wide, border, cells, load_sems, store_sems, side_sems = scratch
     chunks, width_x, width_y, width_z, lanes = blocks.shape
     steps = lanes // (2 * LANES)
     group_lanes = chosen_refs[0].shape[1]
     per_group = group_lanes // lanes
     half_steps = per_group * steps // 2 + 1
+    first_row = base // LANES * width_z
+    rows = pl.ds(first_row, speed_ref.shape[1])
+    sources = (outer_refs[0].at[side_ref[0], :, rows, :],) + outer_refs[1:]
     inputs = [
         pltpu.make_async_copy(source, target, side_sems.at[at])
-        for at, (source, target) in enumerate(zip(outer_refs, inner_refs))
+        for at, (source, target) in enumerate(zip(sources, inner_refs))
     ]
     for copy in inputs:
         copy.start()
@@ -328,6 +369,9 @@
     stores = []
     for copy in inputs:
         copy.wait()
+    number = lax.broadcasted_iota(jnp.int32, picker_ref.shape, 0)
+    matches = number == wanted_ref[0:1, :]
+    picker_ref[...] = jnp.where(matches, 1.0, 0.0).astype(jnp.bfloat16)
     for t in range(chunks):
         group, chunk = t // per_group, t % per_group
         sizes, falls, sinks = [], [], []
@@ -369,10 +413,9 @@
                     jnp.concatenate([edge, field[:-1]], axis=0),
                 )
                 fluxes = fluxes + sizes[u][1] * (field - beside_y)
-                upper = jnp.where(
-                    place == width_z - 1, pltpu.roll(field, 3, 1), pltpu.roll(field, 7, 1)
-                )
-                lower = jnp.where(place == 0, pltpu.roll(field, 5, 1), pltpu.roll(field, 1, 1))
+                turned = pltpu.roll(field, 4, 1)
+                upper = pltpu.roll(jnp.where(place == 0, turned, field), 7, 1)
+                lower = pltpu.roll(jnp.where(place == width_z - 1, turned, field), 1, 1)
                 fluxes = fluxes + sizes[u][2] * (field - jnp.where(sinks[u], upper, lower))
                 read = field - fluxes
                 reads[t, pl.ds(x * width_y, width_y), 8 * u : 8 * u + 8, :] = read
@@ -383,7 +426,7 @@
                 ).astype(jnp.bfloat16)
             return carry
 
-        lax.fori_loop(0, width_x, advance, 0, unroll=2)
+        lax.fori_loop(0, width_x, advance, 0, unroll=4)
         target = out_ref.at[:, pl.ds(8 * steps * t, 8 * steps), :]
         stores.append(pltpu.make_async_copy(reads.at[t], target, store_sems.at[t]))
         stores[-1].start()
@@ -418,35 +461,41 @@
 def filter_parts(weight_ref, table_ref, cells, loads, section, back):
     count, slots, lanes = cells.shape
     padded = weight_ref.shape[2]
-    height = table_ref.shape[0]
+    height = table_ref.shape[0] - LANES
     window = height - 64
     pair_lanes = 2 * (height - 128)
     pairs = lanes // pair_lanes
     half = pairs * count
-    for side in range(2):
-        here = range(side * count // 2, (side + 1) * count // 2)
-        for at in here:
-            loads[at].wait()
-        for parity in range(2):
-            rows = []
-            for at in here:
-                for p in range(pairs):
-                    lane = p * pair_lanes + parity * (pair_lanes - window)
-                    rows.append(cells[at, :, lane : lane + window])
-            start = 64 * (1 - parity)
-            out = jnp.dot(
-                jnp.concatenate(rows, axis=0),
-                table_ref[start : start + window, :],
-                preferred_element_type=jnp.float32,
-            )
-            for at in range(half // 2):
-                section[side * half + 2 * at + parity] = out[at * slots : (at + 1) * slots]
+    sums_at = padded - LANES
+    for load in loads:
+        load.wait()
+    for parity in range(2):
+        rows = []
+        for at in range(count):
+            for p in range(pairs):
+                lane = p * pair_lanes + parity * (pair_lanes - window)
+                rows.append(cells[at, :, lane : lane + window])
+        start = 64 * (1 - parity)
+        out = jnp.dot(
+            jnp.concatenate(rows, axis=0),
+            table_ref[start : start + window, :],
+            preferred_element_type=jnp.float32,
+        )
+        sums = out[:, sums_at : sums_at + LANES].astype(jnp.bfloat16)
+        out = out + jnp.dot(sums, table_ref[height:, :], preferred_element_type=jnp.float32)
+        out = out.astype(jnp.bfloat16).astype(jnp.float32)
+        for at in range(half):
+            section[2 * at + parity] = out[at * slots : (at + 1) * slots]
 
     lane_tiles = padded // LANES
+    points = weight_ref.shape[1]
+    pairs_of, _ = half_set(points)
+    mean_at = int(np.flatnonzero((pairs_of == 0).all(axis=1))[0])
 
     def transform(index, carry):
         row = pl.multiple_of(index // lane_tiles * 16, 16)
         lane = pl.multiple_of(index % lane_tiles * LANES, LANES)
+        mean = lane + lax.broadcasted_iota(jnp.int32, (8, LANES), 1) == mean_at
         results = []
         for octet in range(2):
             here = pl.ds(row + 8 * octet, 8)
@@ -462,6 +511,9 @@
                 for a, (real, imag) in spectrum.items():
                     weight = weight_ref[which, pl.ds(a, 1), pl.ds(lane, LANES)]
                     weighted[a] = (real * weight, imag * weight)
+                real = weighted[0][0]
+                rounded = real.astype(jnp.bfloat16).astype(jnp.float32)
+                weighted[0] = (jnp.where(mean, rounded, real), weighted[0][1])
                 per_kernel.append(first_half_of(weighted))
             results.append(per_kernel)
         for which in range(3):
@@ -479,14 +531,18 @@
 def inverse_parts(back_table, back):
     _, kernels, pairs, slots, depth = back.shape
     window = back_table.shape[2]
-    return [
-        jnp.dot(
+    outs = []
+    for parity in range(2):
+        out = jnp.dot(
             back[parity].reshape(kernels * pairs * slots, depth),
-            back_table[parity],
+            back_table[parity, :depth],
             preferred_element_type=jnp.float32,
-        ).reshape(kernels, pairs, slots, window)
-        for parity in range(2)
-    ]
+        )
+        first = 0 if parity else window - LANES
+        level = out[:, first : first + LANES].astype(jnp.bfloat16)
+        out = out + jnp.dot(level, back_table[parity, depth:], preferred_element_type=jnp.float32)
+        outs.append(out.reshape(kernels, pairs, slots, window))
+    return outs
 
 
 def terms_of(part, outs, cells_ref, put):
@@ -657,11 +713,7 @@
     count_x, count_y = lax.axis_size("cx"), lax.axis_size("cy")
 
     tiles = local_vel // LANES
-    speeds = jnp.stack(courants(points, vel_at * local_vel, local_vel))
-    speeds = jnp.broadcast_to(
-        speeds.reshape(3, tiles, 1, LANES), (3, tiles, width_z, LANES)
-    ).reshape(3, parts, tiles * width_z // parts, LANES)
-    speeds = [speeds[:, 0], speeds[:, 1:].reshape(3, -1, LANES)]
+    speeds = jnp.asarray(plane_speeds(points, local_vel, width_z))
     falls = np.arange(group) // points % points < points // 2
     falls = np.repeat(falls.reshape(-1, 1, LANES), width_z, axis=1).reshape(-1, LANES)
     falls = jnp.asarray(falls.astype(np.float32))
@@ -679,7 +731,7 @@
     wanted = jnp.where(spot >= 0, spot + capacity * parity, -1)
     wanted = jnp.broadcast_to(wanted, shape).reshape(-1)
     numbers = jnp.arange(2 * capacity, dtype=jnp.int32)
-    picker = (numbers[:, None] == wanted[None, :]).astype(jnp.bfloat16)
+    wanted_rows = jnp.broadcast_to(wanted[None, :], (8, wanted.shape[0]))
     strength = jnp.broadcast_to(
         (0.25 * level.astype(jnp.float32)).reshape(block_rows, 1, width_z), shape
     ).reshape(-1)
@@ -730,7 +782,8 @@
 
     def upwind(at, halo, sizes):
         groups = parts - 1 if at else 1
-        operands = (speeds[at], picker, *halo)
+        operands = (speeds, wanted_rows, *halo)
+        local_speeds = jax.ShapeDtypeStruct((3, groups * group_rows, LANES), jnp.float32)
         chosen = [(groups * size, group) for size in sizes]
         return pl.pallas_call(
             functools.partial(upwind_kernel, at * group, sizes),
@@ -740,9 +793,10 @@
                 jax.ShapeDtypeStruct((block_rows, groups * group_rows, LANES), jnp.float32)
             ]
             + [jax.ShapeDtypeStruct(shape, bf16) for shape in chosen],
-            scratch_shapes=[pltpu.VMEM(x.shape, x.dtype) for x in operands]
+            scratch_shapes=[pltpu.VMEM(x.shape, x.dtype) for x in (local_speeds, *operands[1:])]
             + [pltpu.VMEM(shape, bf16) for shape in chosen]
             + [
+                pltpu.VMEM((2 * capacity, block_rows * 8), bf16),
                 pltpu.VMEM(
                     (groups * chunks, width_x, width_y, width_z, group // chunks), jnp.float32
                 ),
@@ -816,7 +870,7 @@
                 out_specs=local,
                 out_shape=jax.ShapeDtypeStruct((count, local_vel), bf16),
                 scratch_shapes=scratch(count) + [sems],
-                compiler_params=params(LIMIT),
+                compiler_params=params(24),
                 cost_estimate=cost(1, 1),
                 name="collide",
             )(

time: 94.6 us -> 96.5 us (1.020)
  Pallas kernels: 57.9 us -> 59.6 us
    pallas_call x1, Pallas kernels: 12.3 us -> 13.8 us  [fast_device(): pl.pallas_call(functools.partial(finish_kernel, starts + starts, counts),...]
    unnamed x34 -> x44, local copies, waits for them, and re-layouts: 2.7 us -> 4.15 us
  transfers between devices with their start and end apart: 12 -> 12, of which waited for: 1 -> 1; matrix products, arithmetic and copies ran while one was open for 6% -> 4% of each run, Pallas kernels for 45% -> 45%
where the time goes in v7:
time: 96.5 us; the launch traced here: 96.1 us
  Pallas kernels  59.6 us (62%)
  starting transfers between devices  16.4 us (17%)
  waiting for transfers between devices  11.3 us (12%)
  local copies, waits for them, and re-layouts  6.45 us (7%)
  other arithmetic  1.86 us (2%)
    pallas_call x2, Pallas kernels, fast_device(): pl.pallas_call(functools.partial(collide_kernel, starts + starts), in_spe...  22.7 us
    pallas_call x2, Pallas kernels, upwind(): pl.pallas_call(functools.partial(upwind_kernel, at * group, sizes), in_sp...  14.2 us
    pallas_call x1, Pallas kernels, fast_device(): pl.pallas_call(functools.partial(finish_kernel, starts + starts, counts),...  13.8 us
    ppermute x6, waiting for transfers between devices, swapped(): return lax.ppermute(value, 'vel', swap)  11.2 us
    ppermute x2, starting transfers between devices, fast_device(): lax.ppermute(down, 'cy', towards_lower)  7.18 us
    pallas_call x2, Pallas kernels, edges_of(): pl.pallas_call(functools.partial(edges_kernel, first * group), in_specs=[...  6.28 us
    ppermute x6, starting transfers between devices, swapped(): return lax.ppermute(value, 'vel', swap)  6.28 us
    unnamed x44, local copies, waits for them, and re-layouts  4.15 us
  transfers between devices with their start and end apart: 12, of which 1 were waited for; matrix products, arithmetic and copies ran while one was open for 4% of the time, Pallas kernels for 45%

profile of v7, /device:TPU:0, one launch (start us, length us, event | category | flops | bytes accessed | tf_op | source)
XLA Modules:
  0.0 96.1 jit_solution(2897973349737347234)
XLA Ops:
  0.0 2.9 %edges.3 = (bf16[5,128,128]{2,1,0:T(8,128)(2,1)}, bf16[5,128,128]{2,1,0:T(8,128)(2,1)}, bf16[9,32,128]{2,1,0:T(8,128)(2,1)}) custom-call(s32[1]{0:T(128)} %bitcast.1.edge_ref, f32[72,128]{1,0:T(8,128)} %constant.33.clone.falls_ref, f32[16,4,4,6912]{3,2,1,0:T(4,128)} %refs_5_.3), custom_call_target="tpu_custom_call" | custom-call | flops 1 | bytes 1 | tf_op jit(solution)/shard_map/edges/pallas_call | solution.py:759
  2.9 2.5 %collective-permute-start.5 = (bf16[9,32,128]{2,1,0:T(8,128)(2,1)}, bf16[9,32,128]{2,1,0:T(8,128)(2,1)S(1)}, u32[]{:S(2)}, u32[]{:S(2)}) collective-permute-start(bf16[9,32,128]{2,1,0:T(8,128)(2,1)} %get-tuple-element.38), channel_id=1, source_target_pairs={{0,12},{4,0},{8,4},{12,8},{16,20},{20,24},{24,28},{28,16},{1,13},{... | collective-permute-start | bytes 221192 | tf_op jit(solution)/shard_map/ppermute | solution.py:829
  5.4 3.6 %collective-permute-start.3 = (bf16[5,128,128]{2,1,0:T(8,128)(2,1)}, bf16[5,128,128]{2,1,0:T(8,128)(2,1)S(1)}, u32[]{:S(2)}, u32[]{:S(2)}) collective-permute-start(bf16[5,128,128]{2,1,0:T(8,128)(2,1)} %get-tuple-element.36), channel_id=1, source_target_pairs={{0,3},{1,0},{2,1},{3,2},{4,7},{5,4},{6,5},{7,6},{8,11},{9,8},{10,9... | collective-permute-start | bytes 491528 | tf_op jit(solution)/shard_map/ppermute | solution.py:827
  9.0 3.4 %edges.2 = (bf16[10,128,128]{2,1,0:T(8,128)(2,1)}, bf16[10,128,128]{2,1,0:T(8,128)(2,1)}, bf16[18,32,128]{2,1,0:T(8,128)(2,1)}) custom-call(s32[1]{0:T(128)} %bitcast.1.edge_ref, f32[72,128]{1,0:T(8,128)} %constant.33.clone.falls_ref, f32[16,4,4,6912]{3,2,1,0:T(4,128)} %refs_5_.3), custom_call_target="tpu_custom_call" | custom-call | flops 1 | bytes 1 | tf_op jit(solution)/shard_map/edges/pallas_call | solution.py:759
  12.4 0.4 collective-permute-start.2
  12.8 3.6 %collective-permute-start = (bf16[10,128,128]{2,1,0:T(8,128)(2,1)}, bf16[10,128,128]{2,1,0:T(8,128)(2,1)S(1)}, u32[]{:S(2)}, u32[]{:S(2)}) collective-permute-start(bf16[10,128,128]{2,1,0:T(8,128)(2,1)} %get-tuple-element.33), channel_id=1, source_target_pairs={{0,3},{1,0},{2,1},{3,2},{4,7},{5,4},{6,5},{7,6},{8,11},{9,8},{10,9... | collective-permute-start | bytes 983048 | tf_op jit(solution)/shard_map/ppermute | solution.py:827
  16.8 0.1 convert_reduce_fusion
  17.8 0.1 select_n.37
  18.1 0.7 broadcast_in_dim.48.refs_1_
  18.8 5.2 %upwind.2 = (f32[64,72,128]{2,1,0:T(8,128)}, bf16[48,2304]{1,0:T(8,128)(2,1)}, bf16[48,2304]{1,0:T(8,128)(2,1)}, bf16[32,2304]{1,0:T(8,128)(2,1)}) custom-call(s32[1]{0:T(128)} %bitcast.side_ref, f32[2,3,216,128]{3,2,1,0:T(8,128)} %constant.32.clone.refs_0_, s32[8,512]{1,0:T(8,128)} %broadcast_in_dim.48.refs_1_, bf16[5,128,128]{2,1,0:T(8,128)(2,1)} %copy-done.16, ...), custom_call_target="tpu_custom_call" | custom-call | flops 1 | bytes 1 | tf_op jit(solution)/shard_map/upwind/pallas_call | solution.py:788
  24.0 1.5 %collective-permute-start.8 = (bf16[32,2304]{1,0:T(8,128)(2,1)}, bf16[32,2304]{1,0:T(8,128)(2,1)S(1)}, u32[]{:S(2)}, u32[]{:S(2)}) collective-permute-start(bf16[32,2304]{1,0:T(8,128)(2,1)} %get-tuple-element.44.refs_2_), channel_id=1, source_target_pairs={{0,16},{16,0},{1,17},{17,1},{2,18},{18,2},{3,19},{19,3},{4,20},{20... | collective-permute-start | bytes 442376 | tf_op jit(solution)/shard_map/ppermute | solution.py:820
  25.6 0.6 collective-permute-start.6
  26.1 1.5 %collective-permute-start.7 = (bf16[48,2304]{1,0:T(8,128)(2,1)}, bf16[48,2304]{1,0:T(8,128)(2,1)S(1)}, u32[]{:S(2)}, u32[]{:S(2)}) collective-permute-start(bf16[48,2304]{1,0:T(8,128)(2,1)} %get-tuple-element.43.refs_0_), channel_id=1, source_target_pairs={{0,16},{16,0},{1,17},{17,1},{2,18},{18,2},{3,19},{19,3},{4,20},{20... | collective-permute-start | bytes 663560 | tf_op jit(solution)/shard_map/ppermute | solution.py:820
  27.6 0.9 select_convert_fusion.spread_any
  28.5 0.1 reshape.108
  28.6 0.1 reshape.109
  28.8 0.1 reshape.110
  29.0 0.7 pad_maximum_fusion.stacked_ref
  29.7 2.7 %weights.1.weight_ref = f32[3,24,384]{2,1,0:T(8,128)} custom-call(f32[72,576]{1,0:T(8,128)} %pad_maximum_fusion.stacked_ref, bf16[576,768]{1,0:T(8,128)(2,1)} %constant.36.clone.select_ref, f32[1,384]{1,0:T(1,128)} %constant.37.clone.scale_ref), custom_call_target="tpu_custom_call" | custom-call | flops 1 | bytes 1 | tf_op jit(solution)/shard_map/weights/pallas_call | solution.py:836
  32.4 0.7 copy-done.11
  33.1 0.7 copy-done.12
  33.8 8.9 %upwind.3 = (f32[64,144,128]{2,1,0:T(8,128)}, bf16[96,2304]{1,0:T(8,128)(2,1)}, bf16[96,2304]{1,0:T(8,128)(2,1)}, bf16[64,2304]{1,0:T(8,128)(2,1)}) custom-call(s32[1]{0:T(128)} %bitcast.side_ref, f32[2,3,216,128]{3,2,1,0:T(8,128)} %constant.32.clone.refs_0_, s32[8,512]{1,0:T(8,128)} %broadcast_in_dim.48.refs_1_, bf16[10,128,128]{2,1,0:T(8,128)(2,1)} %copy-done.11, ...), custom_call_target="tpu_custom_call" | custom-call | flops 1 | bytes 1 | tf_op jit(solution)/shard_map/upwind/pallas_call | solution.py:788
  42.8 0.6 collective-permute-start.9
  43.4 11.2 %collective-permute-done.9.refs_4_.refs_5_ = bf16[96,2304]{1,0:T(8,128)(2,1)S(1)} collective-permute-done((bf16[96,2304]{1,0:T(8,128)(2,1)}, bf16[96,2304]{1,0:T(8,128)(2,1)S(1)}, u32[]{:S(2)}, u32[]{:S(2)}) %collective-permute-start.9) | collective-permute-done | bytes 442400 | tf_op jit(solution)/shard_map/ppermute | solution.py:820
  54.6 1.1 %collective-permute-start.10 = (bf16[96,2304]{1,0:T(8,128)(2,1)}, bf16[96,2304]{1,0:T(8,128)(2,1)S(1)}, u32[]{:S(2)}, u32[]{:S(2)}) collective-permute-start(bf16[96,2304]{1,0:T(8,128)(2,1)} %get-tuple-element.56.refs_1_.refs_2_), channel_id=1, source_target_pairs={{0,16},{16,0},{1,17},{17,1},{2,18},{18,2},{3,19},{19,3},{4,20},{20... | collective-permute-start | bytes 1327112 | tf_op jit(solution)/shard_map/ppermute | solution.py:820
  55.8 1.0 %copy-done.6 = bf16[96,2304]{1,0:T(8,128)(2,1)S(1)} copy-done((bf16[96,2304]{1,0:T(8,128)(2,1)S(1)}, bf16[96,2304]{1,0:T(8,128)(2,1)}, u32[]{:S(2)}) %copy-start.6) | copy-done | bytes 442392
  56.8 11.2 %collide.2.refs_0_ = bf16[48,6912]{1,0:T(8,128)(2,1)S(1)} custom-call(f32[3,24,384]{2,1,0:T(8,128)S(1)} %copy-done.4, bf16[832,768]{1,0:T(8,128)(2,1)S(1)} %copy-done.1, bf16[2,896,640]{2,1,0:T(8,128)(2,1)S(1)} %copy-done, bf16[48,2304]{1,0:T(8,128)(2,1)S(1)} %copy-done.8, bf16[96,2304]{1,0:T(8,128)(2,1)S(1)} %copy-done.6, bf16[96,2304]{1,0:T(8,128)(2,1)S(1)} %copy-done.6, ...), custom_call_target="tpu_custom_call" | custom-call | flops 1 | bytes 1 | tf_op jit(solution)/shard_map/collide/pallas_call | solution.py:867
  68.1 1.0 %collective-permute-start.11 = (bf16[64,2304]{1,0:T(8,128)(2,1)S(1)}, bf16[64,2304]{1,0:T(8,128)(2,1)S(1)}, u32[]{:S(2)}, u32[]{:S(2)}) collective-permute-start(bf16[64,2304]{1,0:T(8,128)(2,1)S(1)} %copy-done.9), channel_id=1, source_target_pairs={{0,16},{16,0},{1,17},{17,1},{2,18},{18,2},{3,19},{19,3},{4,20},{20... | collective-permute-start | bytes 884744 | tf_op jit(solution)/shard_map/ppermute | solution.py:820
  69.1 11.4 %collide.3.refs_1_ = bf16[48,6912]{1,0:T(8,128)(2,1)S(1)} custom-call(f32[3,24,384]{2,1,0:T(8,128)S(1)} %copy-done.4, bf16[832,768]{1,0:T(8,128)(2,1)S(1)} %copy-done.1, bf16[2,896,640]{2,1,0:T(8,128)(2,1)S(1)} %copy-done, bf16[48,2304]{1,0:T(8,128)(2,1)S(1)} %copy-done.7, bf16[96,2304]{1,0:T(8,128)(2,1)S(1)} %copy-done.5, bf16[96,2304]{1,0:T(8,128)(2,1)S(1)} %copy-done.5, ...), custom_call_target="tpu_custom_call" | custom-call | flops 1 | bytes 1 | tf_op jit(solution)/shard_map/collide/pallas_call | solution.py:867
  80.5 0.9 copy-done.3
  81.4 0.7 copy-done.10
  82.1 13.8 %finish.1 = f32[16,4,4,6912]{3,2,1,0:T(4,128)} custom-call(f32[3,24,384]{2,1,0:T(8,128)} %weights.1.weight_ref, bf16[832,768]{1,0:T(8,128)(2,1)} %constant.34.clone.table_ref, bf16[2,896,640]{2,1,0:T(8,128)(2,1)} %constant.35.clone.back_any, bf16[512,256]{1,0:T(8,128)(2,1)} %select_convert_fusion.spread_any, bf16[48,6912]{1,0:T(8,128)(2,1)} %copy-done.2, ...), custom_call_target="tpu_custom_call" | custom-call | tf_op jit(solution)/shard_map/finish/pallas_call | solution.py:890
  (68 shorter events, 1.4 us)
Async XLA Ops:
  2.9 13.6 %copy-start.21 = (s32[16,4,4]{0,2,1:T(4,128)S(1)}, s32[16,4,4]{0,2,1:T(4,128)}, u32[]{:S(2)}) copy-start(s32[16,4,4]{0,2,1:T(4,128)} %param.12) | copy-start | bytes 3076
  2.9 15.1 %collective-permute-start.5 = (bf16[9,32,128]{2,1,0:T(8,128)(2,1)}, bf16[9,32,128]{2,1,0:T(8,128)(2,1)S(1)}, u32[]{:S(2)}, u32[]{:S(2)}) collective-permute-start(bf16[9,32,128]{2,1,0:T(8,128)(2,1)} %get-tuple-element.38), channel_id=1, source_target_pairs={{0,12},{4,0},{8,4},{12,8},{16,20},{20,24},{24,28},{28,16},{1,13},{... | collective-permute-start | bytes 221192 | tf_op jit(solution)/shard_map/ppermute | solution.py:829
  5.4 12.7 %collective-permute-start.3 = (bf16[5,128,128]{2,1,0:T(8,128)(2,1)}, bf16[5,128,128]{2,1,0:T(8,128)(2,1)S(1)}, u32[]{:S(2)}, u32[]{:S(2)}) collective-permute-start(bf16[5,128,128]{2,1,0:T(8,128)(2,1)} %get-tuple-element.36), channel_id=1, source_target_pairs={{0,3},{1,0},{2,1},{3,2},{4,7},{5,4},{6,5},{7,6},{8,11},{9,8},{10,9... | collective-permute-start | bytes 491528 | tf_op jit(solution)/shard_map/ppermute | solution.py:827
  9.0 9.1 %collective-permute-start.4 = (bf16[5,128,128]{2,1,0:T(8,128)(2,1)}, bf16[5,128,128]{2,1,0:T(8,128)(2,1)S(1)}, u32[]{:S(2)}, u32[]{:S(2)}) collective-permute-start(bf16[5,128,128]{2,1,0:T(8,128)(2,1)} %get-tuple-element.37), channel_id=1, source_target_pairs={{0,1},{1,2},{2,3},{3,0},{4,5},{5,6},{6,7},{7,4},{8,9},{9,10},{10,1... | collective-permute-start | bytes 491528 | tf_op jit(solution)/shard_map/ppermute | solution.py:828
  12.4 16.1 %copy-start.13 = (f32[24,24,24]{2,1,0:T(8,128)S(1)}, f32[24,24,24]{2,1,0:T(8,128)}, u32[]{:S(2)}) copy-start(f32[24,24,24]{2,1,0:T(8,128)} %param.13) | copy-start | bytes 165892
  12.4 16.3 %copy-start.14 = (f32[24,24,24]{2,1,0:T(8,128)S(1)}, f32[24,24,24]{2,1,0:T(8,128)}, u32[]{:S(2)}) copy-start(f32[24,24,24]{2,1,0:T(8,128)} %param.14) | copy-start | bytes 165892
  12.4 13.7 %collective-permute-start.2 = (bf16[18,32,128]{2,1,0:T(8,128)(2,1)}, bf16[18,32,128]{2,1,0:T(8,128)(2,1)S(1)}, u32[]{:S(2)}, u32[]{:S(2)}) collective-permute-start(bf16[18,32,128]{2,1,0:T(8,128)(2,1)} %get-tuple-element.35), channel_id=1, source_target_pairs={{0,12},{4,0},{8,4},{12,8},{16,20},{20,24},{24,28},{28,16},{1,13},{... | collective-permute-start | bytes 442376 | tf_op jit(solution)/shard_map/ppermute | solution.py:829
  12.8 19.5 %collective-permute-start = (bf16[10,128,128]{2,1,0:T(8,128)(2,1)}, bf16[10,128,128]{2,1,0:T(8,128)(2,1)S(1)}, u32[]{:S(2)}, u32[]{:S(2)}) collective-permute-start(bf16[10,128,128]{2,1,0:T(8,128)(2,1)} %get-tuple-element.33), channel_id=1, source_target_pairs={{0,3},{1,0},{2,1},{3,2},{4,7},{5,4},{6,5},{7,6},{8,11},{9,8},{10,9... | collective-permute-start | bytes 983048 | tf_op jit(solution)/shard_map/ppermute | solution.py:827
  17.4 11.4 %copy-start.15 = (f32[24,24,24]{2,1,0:T(8,128)S(1)}, f32[24,24,24]{2,1,0:T(8,128)}, u32[]{:S(2)}) copy-start(f32[24,24,24]{2,1,0:T(8,128)} %param.15) | copy-start | bytes 165892
  18.0 0.8 copy-start.20
  18.0 14.4 %collective-permute-start.1 = (bf16[10,128,128]{2,1,0:T(8,128)(2,1)}, bf16[10,128,128]{2,1,0:T(8,128)(2,1)S(1)}, u32[]{:S(2)}, u32[]{:S(2)}) collective-permute-start(bf16[10,128,128]{2,1,0:T(8,128)(2,1)} %get-tuple-element.34), channel_id=1, source_target_pairs={{0,1},{1,2},{2,3},{3,0},{4,5},{5,6},{6,7},{7,4},{8,9},{9,10},{10,1... | collective-permute-start | bytes 983048 | tf_op jit(solution)/shard_map/ppermute | solution.py:828
  24.0 18.7 %collective-permute-start.8 = (bf16[32,2304]{1,0:T(8,128)(2,1)}, bf16[32,2304]{1,0:T(8,128)(2,1)S(1)}, u32[]{:S(2)}, u32[]{:S(2)}) collective-permute-start(bf16[32,2304]{1,0:T(8,128)(2,1)} %get-tuple-element.44.refs_2_), channel_id=1, source_target_pairs={{0,16},{16,0},{1,17},{17,1},{2,18},{18,2},{3,19},{19,3},{4,20},{20... | collective-permute-start | bytes 442376 | tf_op jit(solution)/shard_map/ppermute | solution.py:820
  25.6 17.2 %collective-permute-start.6 = (bf16[48,2304]{1,0:T(8,128)(2,1)}, bf16[48,2304]{1,0:T(8,128)(2,1)S(1)}, u32[]{:S(2)}, u32[]{:S(2)}) collective-permute-start(bf16[48,2304]{1,0:T(8,128)(2,1)} %get-tuple-element.42.refs_0_), channel_id=1, source_target_pairs={{0,16},{16,0},{1,17},{17,1},{2,18},{18,2},{3,19},{19,3},{4,20},{20... | collective-permute-start | bytes 663560 | tf_op jit(solution)/shard_map/ppermute | solution.py:820
  26.1 6.2 %copy-start.19 = (bf16[18,32,128]{2,1,0:T(8,128)(2,1)}, bf16[18,32,128]{2,1,0:T(8,128)(2,1)S(1)}, u32[]{:S(2)}) copy-start(bf16[18,32,128]{2,1,0:T(8,128)(2,1)S(1)} %collective-permute-done.2.refs_4_) | copy-start | bytes 442372
  26.1 16.7 %collective-permute-start.7 = (bf16[48,2304]{1,0:T(8,128)(2,1)}, bf16[48,2304]{1,0:T(8,128)(2,1)S(1)}, u32[]{:S(2)}, u32[]{:S(2)}) collective-permute-start(bf16[48,2304]{1,0:T(8,128)(2,1)} %get-tuple-element.43.refs_0_), channel_id=1, source_target_pairs={{0,16},{16,0},{1,17},{17,1},{2,18},{18,2},{3,19},{19,3},{4,20},{20... | collective-permute-start | bytes 663560 | tf_op jit(solution)/shard_map/ppermute | solution.py:820
  29.6 26.1 %copy-start = (bf16[2,896,640]{2,1,0:T(8,128)(2,1)S(1)}, bf16[2,896,640]{2,1,0:T(8,128)(2,1)}, u32[]{:S(2)}) copy-start(bf16[2,896,640]{2,1,0:T(8,128)(2,1)} %constant.35.clone.back_any) | copy-start | bytes 6881284
  29.7 26.1 %copy-start.1 = (bf16[832,768]{1,0:T(8,128)(2,1)S(1)}, bf16[832,768]{1,0:T(8,128)(2,1)}, u32[]{:S(2)}) copy-start(bf16[832,768]{1,0:T(8,128)(2,1)} %constant.34.clone.table_ref) | copy-start | bytes 3833860
  29.7 26.1 %copy-start.8 = (bf16[48,2304]{1,0:T(8,128)(2,1)S(1)}, bf16[48,2304]{1,0:T(8,128)(2,1)}, u32[]{:S(2)}) copy-start(bf16[48,2304]{1,0:T(8,128)(2,1)} %get-tuple-element.42.refs_0_) | copy-start | bytes 663556
  32.3 23.4 %copy-start.4 = (f32[3,24,384]{2,1,0:T(8,128)S(1)}, f32[3,24,384]{2,1,0:T(8,128)}, u32[]{:S(2)}) copy-start(f32[3,24,384]{2,1,0:T(8,128)} %weights.1.weight_ref) | copy-start | bytes 331780
  32.3 0.7 copy-start.11
  33.1 0.7 copy-start.12
  33.8 35.3 %copy-start.7 = (bf16[48,2304]{1,0:T(8,128)(2,1)S(1)}, bf16[48,2304]{1,0:T(8,128)(2,1)}, u32[]{:S(2)}) copy-start(bf16[48,2304]{1,0:T(8,128)(2,1)} %get-tuple-element.43.refs_0_) | copy-start | bytes 663556
  42.7 26.3 %copy-start.5 = (bf16[96,2304]{1,0:T(8,128)(2,1)S(1)}, bf16[96,2304]{1,0:T(8,128)(2,1)}, u32[]{:S(2)}) copy-start(bf16[96,2304]{1,0:T(8,128)(2,1)} %get-tuple-element.56.refs_1_.refs_2_) | copy-start | bytes 1327108
  42.8 37.8 %copy-start.18 = (bf16[32,2304]{1,0:T(8,128)(2,1)}, bf16[32,2304]{1,0:T(8,128)(2,1)S(1)}, u32[]{:S(2)}) copy-start(bf16[32,2304]{1,0:T(8,128)(2,1)S(1)} %collective-permute-done.8.refs_5_) | copy-start | bytes 442372
  42.8 11.9 %collective-permute-start.9 = (bf16[96,2304]{1,0:T(8,128)(2,1)}, bf16[96,2304]{1,0:T(8,128)(2,1)S(1)}, u32[]{:S(2)}, u32[]{:S(2)}) collective-permute-start(bf16[96,2304]{1,0:T(8,128)(2,1)} %get-tuple-element.54.refs_1_.refs_2_), channel_id=1, source_target_pairs={{0,16},{16,0},{1,17},{17,1},{2,18},{18,2},{3,19},{19,3},{4,20},{20... | collective-permute-start | bytes 1327112 | tf_op jit(solution)/shard_map/ppermute | solution.py:820
  54.6 13.4 %collective-permute-start.10 = (bf16[96,2304]{1,0:T(8,128)(2,1)}, bf16[96,2304]{1,0:T(8,128)(2,1)S(1)}, u32[]{:S(2)}, u32[]{:S(2)}) collective-permute-start(bf16[96,2304]{1,0:T(8,128)(2,1)} %get-tuple-element.56.refs_1_.refs_2_), channel_id=1, source_target_pairs={{0,16},{16,0},{1,17},{17,1},{2,18},{18,2},{3,19},{19,3},{4,20},{20... | collective-permute-start | bytes 1327112 | tf_op jit(solution)/shard_map/ppermute | solution.py:820
  55.8 1.0 %copy-start.6 = (bf16[96,2304]{1,0:T(8,128)(2,1)S(1)}, bf16[96,2304]{1,0:T(8,128)(2,1)}, u32[]{:S(2)}) copy-start(bf16[96,2304]{1,0:T(8,128)(2,1)} %get-tuple-element.54.refs_1_.refs_2_) | copy-start | bytes 1327108
  56.8 11.3 %copy-start.9 = (bf16[64,2304]{1,0:T(8,128)(2,1)S(1)}, bf16[64,2304]{1,0:T(8,128)(2,1)}, u32[]{:S(2)}) copy-start(bf16[64,2304]{1,0:T(8,128)(2,1)} %get-tuple-element.58.refs_3_.refs_4_) | copy-start | bytes 884740
  68.0 12.5 %copy-start.2 = (bf16[48,6912]{1,0:T(8,128)(2,1)}, bf16[48,6912]{1,0:T(8,128)(2,1)S(1)}, u32[]{:S(2)}) copy-start(bf16[48,6912]{1,0:T(8,128)(2,1)S(1)} %collide.2.refs_0_) | copy-start | bytes 1990660
  68.1 13.4 %collective-permute-start.11 = (bf16[64,2304]{1,0:T(8,128)(2,1)S(1)}, bf16[64,2304]{1,0:T(8,128)(2,1)S(1)}, u32[]{:S(2)}, u32[]{:S(2)}) collective-permute-start(bf16[64,2304]{1,0:T(8,128)(2,1)S(1)} %copy-done.9), channel_id=1, source_target_pairs={{0,16},{16,0},{1,17},{17,1},{2,18},{18,2},{3,19},{19,3},{4,20},{20... | collective-permute-start | bytes 884744 | tf_op jit(solution)/shard_map/ppermute | solution.py:820
  80.5 0.9 copy-start.3
  81.4 0.7 copy-start.10
  (2 other events, 1.4 us)

commit v8 on v7

--- a/solution.py
+++ b/solution.py
@@ -706,8 +706,8 @@
     group_rows = group // LANES * width_z
     steps = group_rows // 8
     capacity = block_cells // 2
-    third = capacity * 3 // 8 // 16 * 16
-    counts = (third, third, capacity - 2 * third)
+    early_count = capacity // 2 // 16 * 16
+    counts = (early_count, capacity - early_count)
     batches = len(counts)
     vel_at = lax.axis_index("vel")
     count_x, count_y = lax.axis_size("cx"), lax.axis_size("cy")
@@ -870,7 +870,7 @@
                 out_specs=local,
                 out_shape=jax.ShapeDtypeStruct((count, local_vel), bf16),
                 scratch_shapes=scratch(count) + [sems],
-                compiler_params=params(24),
+                compiler_params=params(34),
                 cost_estimate=cost(1, 1),
                 name="collide",
             )(

time: 96.5 us -> 95 us (0.984)
  Pallas kernels: 59.6 us -> 55.8 us
  waiting for transfers between devices: 11.3 us -> 14.7 us
    pallas_call x2 -> x1, Pallas kernels: 22.7 us -> 13 us  [fast_device(): pl.pallas_call(functools.partial(collide_kernel, starts + starts), in_spe...]
    pallas_call x1, Pallas kernels: 13.8 us -> 19.7 us  [fast_device(): pl.pallas_call(functools.partial(finish_kernel, starts + starts, counts),...]
    ppermute x6 -> x4, waiting for transfers between devices: 11.2 us -> 13.8 us  [swapped(): return lax.ppermute(value, 'vel', swap)]
    ppermute x6 -> x4, starting transfers between devices: 6.28 us -> 5.61 us  [swapped(): return lax.ppermute(value, 'vel', swap)]
    unnamed x44 -> x36, local copies, waits for them, and re-layouts: 4.15 us -> 3.66 us
  transfers between devices with their start and end apart: 12 -> 10, of which waited for: 1 -> 2; matrix products, arithmetic and copies ran while one was open for 4% -> 4% of each run, Pallas kernels for 45% -> 35%
where the time goes in v8:
time: 95 us; the launch traced here: 94.6 us
  Pallas kernels  55.8 us (59%)
  starting transfers between devices  15.8 us (17%)
  waiting for transfers between devices  14.7 us (15%)
  local copies, waits for them, and re-layouts  5.98 us (6%)
  other arithmetic  1.87 us (2%)
    pallas_call x1, Pallas kernels, fast_device(): pl.pallas_call(functools.partial(finish_kernel, starts + starts, counts),...  19.7 us
    pallas_call x2, Pallas kernels, upwind(): pl.pallas_call(functools.partial(upwind_kernel, at * group, sizes), in_sp...  14.2 us
    ppermute x4, waiting for transfers between devices, swapped(): return lax.ppermute(value, 'vel', swap)  13.8 us
    pallas_call x1, Pallas kernels, fast_device(): pl.pallas_call(functools.partial(collide_kernel, starts + starts), in_spe...  13 us
    ppermute x2, starting transfers between devices, fast_device(): lax.ppermute(down, 'cy', towards_lower)  7.18 us
    pallas_call x2, Pallas kernels, edges_of(): pl.pallas_call(functools.partial(edges_kernel, first * group), in_specs=[...  6.25 us
    ppermute x4, starting transfers between devices, swapped(): return lax.ppermute(value, 'vel', swap)  5.61 us
    unnamed x36, local copies, waits for them, and re-layouts  3.66 us
  transfers between devices with their start and end apart: 10, of which 2 were waited for; matrix products, arithmetic and copies ran while one was open for 4% of the time, Pallas kernels for 35%

profile of v8, /device:TPU:0, one launch (start us, length us, event | category | flops | bytes accessed | tf_op | source)
XLA Modules:
  0.0 94.6 jit_solution(16406069802950983775)
XLA Ops:
  0.0 2.8 %edges.3 = (bf16[5,128,128]{2,1,0:T(8,128)(2,1)}, bf16[5,128,128]{2,1,0:T(8,128)(2,1)}, bf16[9,32,128]{2,1,0:T(8,128)(2,1)}) custom-call(s32[1]{0:T(128)} %bitcast.1.edge_ref, f32[72,128]{1,0:T(8,128)} %constant.33.clone.falls_ref, f32[16,4,4,6912]{3,2,1,0:T(4,128)} %refs_5_.3), custom_call_target="tpu_custom_call" | custom-call | flops 1 | bytes 1 | tf_op jit(solution)/shard_map/edges/pallas_call | solution.py:759
  2.9 2.5 %collective-permute-start.5 = (bf16[9,32,128]{2,1,0:T(8,128)(2,1)}, bf16[9,32,128]{2,1,0:T(8,128)(2,1)S(1)}, u32[]{:S(2)}, u32[]{:S(2)}) collective-permute-start(bf16[9,32,128]{2,1,0:T(8,128)(2,1)} %get-tuple-element.35), channel_id=1, source_target_pairs={{0,12},{4,0},{8,4},{12,8},{16,20},{20,24},{24,28},{28,16},{1,13},{... | collective-permute-start | bytes 221192 | tf_op jit(solution)/shard_map/ppermute | solution.py:829
  5.3 3.6 %collective-permute-start.3 = (bf16[5,128,128]{2,1,0:T(8,128)(2,1)}, bf16[5,128,128]{2,1,0:T(8,128)(2,1)S(1)}, u32[]{:S(2)}, u32[]{:S(2)}) collective-permute-start(bf16[5,128,128]{2,1,0:T(8,128)(2,1)} %get-tuple-element.33), channel_id=1, source_target_pairs={{0,3},{1,0},{2,1},{3,2},{4,7},{5,4},{6,5},{7,6},{8,11},{9,8},{10,9... | collective-permute-start | bytes 491528 | tf_op jit(solution)/shard_map/ppermute | solution.py:827
  8.9 3.4 %edges.2 = (bf16[10,128,128]{2,1,0:T(8,128)(2,1)}, bf16[10,128,128]{2,1,0:T(8,128)(2,1)}, bf16[18,32,128]{2,1,0:T(8,128)(2,1)}) custom-call(s32[1]{0:T(128)} %bitcast.1.edge_ref, f32[72,128]{1,0:T(8,128)} %constant.33.clone.falls_ref, f32[16,4,4,6912]{3,2,1,0:T(4,128)} %refs_5_.3), custom_call_target="tpu_custom_call" | custom-call | flops 1 | bytes 1 | tf_op jit(solution)/shard_map/edges/pallas_call | solution.py:759
  12.4 0.4 collective-permute-start.2
  12.8 3.6 %collective-permute-start = (bf16[10,128,128]{2,1,0:T(8,128)(2,1)}, bf16[10,128,128]{2,1,0:T(8,128)(2,1)S(1)}, u32[]{:S(2)}, u32[]{:S(2)}) collective-permute-start(bf16[10,128,128]{2,1,0:T(8,128)(2,1)} %get-tuple-element.30), channel_id=1, source_target_pairs={{0,3},{1,0},{2,1},{3,2},{4,7},{5,4},{6,5},{7,6},{8,11},{9,8},{10,9... | collective-permute-start | bytes 983048 | tf_op jit(solution)/shard_map/ppermute | solution.py:827
  16.4 0.1 copy.20
  16.8 0.1 convert_reduce_fusion
  17.2 0.1 copy.22
  17.5 0.1 copy.26
  17.8 0.1 select_n.37
  18.0 0.7 broadcast_in_dim.48.refs_1_
  18.8 5.3 %upwind.2 = (f32[64,72,128]{2,1,0:T(8,128)}, bf16[64,2304]{1,0:T(8,128)(2,1)}, bf16[64,2304]{1,0:T(8,128)(2,1)}) custom-call(s32[1]{0:T(128)} %bitcast.side_ref, f32[2,3,216,128]{3,2,1,0:T(8,128)} %constant.32.clone.refs_0_, s32[8,512]{1,0:T(8,128)} %broadcast_in_dim.48.refs_1_, bf16[5,128,128]{2,1,0:T(8,128)(2,1)} %copy-done.13, ...), custom_call_target="tpu_custom_call" | custom-call | flops 1 | bytes 1 | tf_op jit(solution)/shard_map/upwind/pallas_call | solution.py:788
  24.0 1.5 %collective-permute-start.6 = (bf16[64,2304]{1,0:T(8,128)(2,1)}, bf16[64,2304]{1,0:T(8,128)(2,1)S(1)}, u32[]{:S(2)}, u32[]{:S(2)}) collective-permute-start(bf16[64,2304]{1,0:T(8,128)(2,1)} %get-tuple-element.39.refs_0_), channel_id=1, source_target_pairs={{0,16},{16,0},{1,17},{17,1},{2,18},{18,2},{3,19},{19,3},{4,20},{20... | collective-permute-start | bytes 884744 | tf_op jit(solution)/shard_map/ppermute | solution.py:820
  25.6 0.6 collective-permute-start.7
  26.1 0.9 select_convert_fusion.spread_any
  27.0 0.1 reshape.108
  27.2 0.1 reshape.109
  27.4 0.1 reshape.110
  27.5 0.7 pad_maximum_fusion.stacked_ref
  28.2 2.7 %weights.1.weight_ref = f32[3,24,384]{2,1,0:T(8,128)} custom-call(f32[72,576]{1,0:T(8,128)} %pad_maximum_fusion.stacked_ref, bf16[576,768]{1,0:T(8,128)(2,1)} %constant.36.clone.select_ref, f32[1,384]{1,0:T(1,128)} %constant.37.clone.scale_ref), custom_call_target="tpu_custom_call" | custom-call | flops 1 | bytes 1 | tf_op jit(solution)/shard_map/weights/pallas_call | solution.py:836
  30.9 0.9 %collective-permute-done.1.refs_3_ = bf16[10,128,128]{2,1,0:T(8,128)(2,1)S(1)} collective-permute-done((bf16[10,128,128]{2,1,0:T(8,128)(2,1)}, bf16[10,128,128]{2,1,0:T(8,128)(2,1)S(1)}, u32[]{:S(2)}, u32[]{:S(2)}) %collective-permute-start.1) | collective-permute-done | bytes 327712 | tf_op jit(solution)/shard_map/ppermute | solution.py:828
  31.9 0.7 copy-done.8
  32.6 8.9 %upwind.3 = (f32[64,144,128]{2,1,0:T(8,128)}, bf16[128,2304]{1,0:T(8,128)(2,1)}, bf16[128,2304]{1,0:T(8,128)(2,1)}) custom-call(s32[1]{0:T(128)} %bitcast.side_ref, f32[2,3,216,128]{3,2,1,0:T(8,128)} %constant.32.clone.refs_0_, s32[8,512]{1,0:T(8,128)} %broadcast_in_dim.48.refs_1_, bf16[10,128,128]{2,1,0:T(8,128)(2,1)} %copy-done.7, ...), custom_call_target="tpu_custom_call" | custom-call | flops 1 | bytes 1 | tf_op jit(solution)/shard_map/upwind/pallas_call | solution.py:788
  41.5 1.8 %collective-permute-start.8 = (bf16[128,2304]{1,0:T(8,128)(2,1)}, bf16[128,2304]{1,0:T(8,128)(2,1)S(1)}, u32[]{:S(2)}, u32[]{:S(2)}) collective-permute-start(bf16[128,2304]{1,0:T(8,128)(2,1)} %get-tuple-element.50.refs_1_.refs_2_), channel_id=1, source_target_pairs={{0,16},{16,0},{1,17},{17,1},{2,18},{18,2},{3,19},{19,3},{4,20},{20... | collective-permute-start | bytes 1769480 | tf_op jit(solution)/shard_map/ppermute | solution.py:820
  43.3 13.8 %collective-permute-done.8.refs_4_.refs_5_ = bf16[128,2304]{1,0:T(8,128)(2,1)S(1)} collective-permute-done((bf16[128,2304]{1,0:T(8,128)(2,1)}, bf16[128,2304]{1,0:T(8,128)(2,1)S(1)}, u32[]{:S(2)}, u32[]{:S(2)}) %collective-permute-start.8) | collective-permute-done | bytes 589856 | tf_op jit(solution)/shard_map/ppermute | solution.py:820
  57.1 1.7 %collective-permute-start.9 = (bf16[128,2304]{1,0:T(8,128)(2,1)}, bf16[128,2304]{1,0:T(8,128)(2,1)S(1)}, u32[]{:S(2)}, u32[]{:S(2)}) collective-permute-start(bf16[128,2304]{1,0:T(8,128)(2,1)} %get-tuple-element.52.refs_2_.refs_3_), channel_id=1, source_target_pairs={{0,16},{16,0},{1,17},{17,1},{2,18},{18,2},{3,19},{19,3},{4,20},{20... | collective-permute-start | bytes 1769480 | tf_op jit(solution)/shard_map/ppermute | solution.py:820
  58.8 1.1 %copy-done.3 = bf16[128,2304]{1,0:T(8,128)(2,1)S(1)} copy-done((bf16[128,2304]{1,0:T(8,128)(2,1)S(1)}, bf16[128,2304]{1,0:T(8,128)(2,1)}, u32[]{:S(2)}) %copy-start.3) | copy-done | bytes 589848
  59.9 13.0 %collide.1.refs_0_ = bf16[64,6912]{1,0:T(8,128)(2,1)S(1)} custom-call(f32[3,24,384]{2,1,0:T(8,128)S(1)} %copy-done.4, bf16[832,768]{1,0:T(8,128)(2,1)S(1)} %copy-done.1, bf16[2,896,640]{2,1,0:T(8,128)(2,1)S(1)} %copy-done, bf16[64,2304]{1,0:T(8,128)(2,1)S(1)} %copy-done.5, bf16[128,2304]{1,0:T(8,128)(2,1)S(1)} %copy-done.3, bf16[128,2304]{1,0:T(8,128)(2,1)S(1)} %copy-done.3, ...), custom_call_target="tpu_custom_call" | custom-call | flops 1 | bytes 1 | tf_op jit(solution)/shard_map/collide/pallas_call | solution.py:867
  72.9 0.9 copy-done.2
  73.9 0.9 copy-done.6
  74.7 19.7 %finish.1 = f32[16,4,4,6912]{3,2,1,0:T(4,128)} custom-call(f32[3,24,384]{2,1,0:T(8,128)} %weights.1.weight_ref, bf16[832,768]{1,0:T(8,128)(2,1)} %constant.34.clone.table_ref, bf16[2,896,640]{2,1,0:T(8,128)(2,1)} %constant.35.clone.back_any, bf16[512,256]{1,0:T(8,128)(2,1)} %select_convert_fusion.spread_any, bf16[64,6912]{1,0:T(8,128)(2,1)} %copy-done.2, ...), custom_call_target="tpu_custom_call" | custom-call | tf_op jit(solution)/shard_map/finish/pallas_call | solution.py:890
  (55 shorter events, 1.0 us)
Async XLA Ops:
  2.9 13.5 %copy-start.17 = (s32[16,4,4]{0,2,1:T(4,128)S(1)}, s32[16,4,4]{0,2,1:T(4,128)}, u32[]{:S(2)}) copy-start(s32[16,4,4]{0,2,1:T(4,128)} %param.12) | copy-start | bytes 3076
  2.9 15.1 %collective-permute-start.5 = (bf16[9,32,128]{2,1,0:T(8,128)(2,1)}, bf16[9,32,128]{2,1,0:T(8,128)(2,1)S(1)}, u32[]{:S(2)}, u32[]{:S(2)}) collective-permute-start(bf16[9,32,128]{2,1,0:T(8,128)(2,1)} %get-tuple-element.35), channel_id=1, source_target_pairs={{0,12},{4,0},{8,4},{12,8},{16,20},{20,24},{24,28},{28,16},{1,13},{... | collective-permute-start | bytes 221192 | tf_op jit(solution)/shard_map/ppermute | solution.py:829
  5.3 12.7 %collective-permute-start.3 = (bf16[5,128,128]{2,1,0:T(8,128)(2,1)}, bf16[5,128,128]{2,1,0:T(8,128)(2,1)S(1)}, u32[]{:S(2)}, u32[]{:S(2)}) collective-permute-start(bf16[5,128,128]{2,1,0:T(8,128)(2,1)} %get-tuple-element.33), channel_id=1, source_target_pairs={{0,3},{1,0},{2,1},{3,2},{4,7},{5,4},{6,5},{7,6},{8,11},{9,8},{10,9... | collective-permute-start | bytes 491528 | tf_op jit(solution)/shard_map/ppermute | solution.py:827
  8.9 9.1 %collective-permute-start.4 = (bf16[5,128,128]{2,1,0:T(8,128)(2,1)}, bf16[5,128,128]{2,1,0:T(8,128)(2,1)S(1)}, u32[]{:S(2)}, u32[]{:S(2)}) collective-permute-start(bf16[5,128,128]{2,1,0:T(8,128)(2,1)} %get-tuple-element.34), channel_id=1, source_target_pairs={{0,1},{1,2},{2,3},{3,0},{4,5},{5,6},{6,7},{7,4},{8,9},{9,10},{10,1... | collective-permute-start | bytes 491528 | tf_op jit(solution)/shard_map/ppermute | solution.py:828
  12.3 14.7 %copy-start.9 = (f32[24,24,24]{2,1,0:T(8,128)S(1)}, f32[24,24,24]{2,1,0:T(8,128)}, u32[]{:S(2)}) copy-start(f32[24,24,24]{2,1,0:T(8,128)} %param.13) | copy-start | bytes 165892
  12.4 14.8 %copy-start.10 = (f32[24,24,24]{2,1,0:T(8,128)S(1)}, f32[24,24,24]{2,1,0:T(8,128)}, u32[]{:S(2)}) copy-start(f32[24,24,24]{2,1,0:T(8,128)} %param.14) | copy-start | bytes 165892
  12.4 18.5 %collective-permute-start.2 = (bf16[18,32,128]{2,1,0:T(8,128)(2,1)}, bf16[18,32,128]{2,1,0:T(8,128)(2,1)S(1)}, u32[]{:S(2)}, u32[]{:S(2)}) collective-permute-start(bf16[18,32,128]{2,1,0:T(8,128)(2,1)} %get-tuple-element.32), channel_id=1, source_target_pairs={{0,12},{4,0},{8,4},{12,8},{16,20},{20,24},{24,28},{28,16},{1,13},{... | collective-permute-start | bytes 442376 | tf_op jit(solution)/shard_map/ppermute | solution.py:829
  12.8 18.1 %collective-permute-start = (bf16[10,128,128]{2,1,0:T(8,128)(2,1)}, bf16[10,128,128]{2,1,0:T(8,128)(2,1)S(1)}, u32[]{:S(2)}, u32[]{:S(2)}) collective-permute-start(bf16[10,128,128]{2,1,0:T(8,128)(2,1)} %get-tuple-element.30), channel_id=1, source_target_pairs={{0,3},{1,0},{2,1},{3,2},{4,7},{5,4},{6,5},{7,6},{8,11},{9,8},{10,9... | collective-permute-start | bytes 983048 | tf_op jit(solution)/shard_map/ppermute | solution.py:827
  17.4 9.9 %copy-start.11 = (f32[24,24,24]{2,1,0:T(8,128)S(1)}, f32[24,24,24]{2,1,0:T(8,128)}, u32[]{:S(2)}) copy-start(f32[24,24,24]{2,1,0:T(8,128)} %param.15) | copy-start | bytes 165892
  17.9 0.8 copy-start.16
  17.9 13.9 %collective-permute-start.1 = (bf16[10,128,128]{2,1,0:T(8,128)(2,1)}, bf16[10,128,128]{2,1,0:T(8,128)(2,1)S(1)}, u32[]{:S(2)}, u32[]{:S(2)}) collective-permute-start(bf16[10,128,128]{2,1,0:T(8,128)(2,1)} %get-tuple-element.31), channel_id=1, source_target_pairs={{0,1},{1,2},{2,3},{3,0},{4,5},{5,6},{6,7},{7,4},{8,9},{9,10},{10,1... | collective-permute-start | bytes 983048 | tf_op jit(solution)/shard_map/ppermute | solution.py:828
  18.0 0.7 copy-start.13
  18.0 0.7 copy-start.14
  24.0 17.5 %collective-permute-start.6 = (bf16[64,2304]{1,0:T(8,128)(2,1)}, bf16[64,2304]{1,0:T(8,128)(2,1)S(1)}, u32[]{:S(2)}, u32[]{:S(2)}) collective-permute-start(bf16[64,2304]{1,0:T(8,128)(2,1)} %get-tuple-element.39.refs_0_), channel_id=1, source_target_pairs={{0,16},{16,0},{1,17},{17,1},{2,18},{18,2},{3,19},{19,3},{4,20},{20... | collective-permute-start | bytes 884744 | tf_op jit(solution)/shard_map/ppermute | solution.py:820
  25.6 16.0 %collective-permute-start.7 = (bf16[64,2304]{1,0:T(8,128)(2,1)}, bf16[64,2304]{1,0:T(8,128)(2,1)S(1)}, u32[]{:S(2)}, u32[]{:S(2)}) collective-permute-start(bf16[64,2304]{1,0:T(8,128)(2,1)} %get-tuple-element.40.refs_1_), channel_id=1, source_target_pairs={{0,16},{16,0},{1,17},{17,1},{2,18},{18,2},{3,19},{19,3},{4,20},{20... | collective-permute-start | bytes 884744 | tf_op jit(solution)/shard_map/ppermute | solution.py:820
  28.2 30.6 %copy-start = (bf16[2,896,640]{2,1,0:T(8,128)(2,1)S(1)}, bf16[2,896,640]{2,1,0:T(8,128)(2,1)}, u32[]{:S(2)}) copy-start(bf16[2,896,640]{2,1,0:T(8,128)(2,1)} %constant.35.clone.back_any) | copy-start | bytes 6881284
  28.2 30.6 %copy-start.1 = (bf16[832,768]{1,0:T(8,128)(2,1)S(1)}, bf16[832,768]{1,0:T(8,128)(2,1)}, u32[]{:S(2)}) copy-start(bf16[832,768]{1,0:T(8,128)(2,1)} %constant.34.clone.table_ref) | copy-start | bytes 3833860
  28.2 30.6 %copy-start.5 = (bf16[64,2304]{1,0:T(8,128)(2,1)S(1)}, bf16[64,2304]{1,0:T(8,128)(2,1)}, u32[]{:S(2)}) copy-start(bf16[64,2304]{1,0:T(8,128)(2,1)} %get-tuple-element.39.refs_0_) | copy-start | bytes 884740
  30.9 28.0 %copy-start.4 = (f32[3,24,384]{2,1,0:T(8,128)S(1)}, f32[3,24,384]{2,1,0:T(8,128)}, u32[]{:S(2)}) copy-start(f32[3,24,384]{2,1,0:T(8,128)} %weights.1.weight_ref) | copy-start | bytes 331780
  30.9 1.0 %copy-start.15 = (bf16[18,32,128]{2,1,0:T(8,128)(2,1)}, bf16[18,32,128]{2,1,0:T(8,128)(2,1)S(1)}, u32[]{:S(2)}) copy-start(bf16[18,32,128]{2,1,0:T(8,128)(2,1)S(1)} %collective-permute-done.2.refs_4_) | copy-start | bytes 442372
  30.9 1.0 %copy-start.7 = (bf16[10,128,128]{2,1,0:T(8,128)(2,1)}, bf16[10,128,128]{2,1,0:T(8,128)(2,1)S(1)}, u32[]{:S(2)}) copy-start(bf16[10,128,128]{2,1,0:T(8,128)(2,1)S(1)} %collective-permute-done.refs_2_) | copy-start | bytes 983044
  31.9 0.7 copy-start.8
  41.5 32.4 %copy-start.12 = (bf16[64,2304]{1,0:T(8,128)(2,1)}, bf16[64,2304]{1,0:T(8,128)(2,1)S(1)}, u32[]{:S(2)}) copy-start(bf16[64,2304]{1,0:T(8,128)(2,1)S(1)} %collective-permute-done.7.refs_4_) | copy-start | bytes 884740
  41.5 15.5 %collective-permute-start.8 = (bf16[128,2304]{1,0:T(8,128)(2,1)}, bf16[128,2304]{1,0:T(8,128)(2,1)S(1)}, u32[]{:S(2)}, u32[]{:S(2)}) collective-permute-start(bf16[128,2304]{1,0:T(8,128)(2,1)} %get-tuple-element.50.refs_1_.refs_2_), channel_id=1, source_target_pairs={{0,16},{16,0},{1,17},{17,1},{2,18},{18,2},{3,19},{19,3},{4,20},{20... | collective-permute-start | bytes 1769480 | tf_op jit(solution)/shard_map/ppermute | solution.py:820
  57.1 16.8 %collective-permute-start.9 = (bf16[128,2304]{1,0:T(8,128)(2,1)}, bf16[128,2304]{1,0:T(8,128)(2,1)S(1)}, u32[]{:S(2)}, u32[]{:S(2)}) collective-permute-start(bf16[128,2304]{1,0:T(8,128)(2,1)} %get-tuple-element.52.refs_2_.refs_3_), channel_id=1, source_target_pairs={{0,16},{16,0},{1,17},{17,1},{2,18},{18,2},{3,19},{19,3},{4,20},{20... | collective-permute-start | bytes 1769480 | tf_op jit(solution)/shard_map/ppermute | solution.py:820
  58.8 1.1 %copy-start.3 = (bf16[128,2304]{1,0:T(8,128)(2,1)S(1)}, bf16[128,2304]{1,0:T(8,128)(2,1)}, u32[]{:S(2)}) copy-start(bf16[128,2304]{1,0:T(8,128)(2,1)} %get-tuple-element.50.refs_1_.refs_2_) | copy-start | bytes 1769476
  72.9 0.9 %copy-start.2 = (bf16[64,6912]{1,0:T(8,128)(2,1)}, bf16[64,6912]{1,0:T(8,128)(2,1)S(1)}, u32[]{:S(2)}) copy-start(bf16[64,6912]{1,0:T(8,128)(2,1)S(1)} %collide.1.refs_0_) | copy-start | bytes 2654212
  73.9 0.9 copy-start.6

commit v9 on v8

--- a/solution.py
+++ b/solution.py
@@ -362,7 +362,8 @@
     for t in range(chunks):
         source = field_ref.at[:, :, :, pl.ds(base + t * lanes, lanes)]
         loads.append(pltpu.make_async_copy(source, blocks.at[t], load_sems.at[t]))
-        loads[-1].start()
+    for load in loads[:2]:
+        load.start()
     beside = jnp.where(side_ref[0] == 0, 2, 0)
     place = lax.broadcasted_iota(jnp.int32, (1, 8, LANES), 1) % width_z
     capacity = picker_ref.shape[0] // 2
@@ -390,6 +391,8 @@
             shape = (width_x, 8, LANES)
             border[u] = jnp.where(falls[u], above.reshape(shape), under.reshape(shape))
         loads[t].wait()
+        if t + 2 < chunks:
+            loads[t + 2].start()
 
         def spread_out(x, carry):
             for u in range(steps):
@@ -458,7 +461,7 @@
     return loads
 
 
-def filter_parts(weight_ref, table_ref, cells, loads, section, back):
+def filter_parts(weight_ref, table_ref, cells, loads, later, section, back):
     count, slots, lanes = cells.shape
     padded = weight_ref.shape[2]
     height = table_ref.shape[0] - LANES
@@ -469,6 +472,8 @@
     sums_at = padded - LANES
     for load in loads:
         load.wait()
+    for load in later:
+        load.start()
     for parity in range(2):
         rows = []
         for at in range(count):
@@ -482,10 +487,19 @@
             preferred_element_type=jnp.float32,
         )
         sums = out[:, sums_at : sums_at + LANES].astype(jnp.bfloat16)
-        out = out + jnp.dot(sums, table_ref[height:, :], preferred_element_type=jnp.float32)
-        out = out.astype(jnp.bfloat16).astype(jnp.float32)
-        for at in range(half):
-            section[2 * at + parity] = out[at * slots : (at + 1) * slots]
+        pieces = []
+        for first in (0, padded):
+            lift = table_ref[height:, first + sums_at : first + padded]
+            lifted = jnp.dot(sums, lift, preferred_element_type=jnp.float32)
+            pieces.append(out[:, first : first + sums_at])
+            pieces.append(out[:, first + sums_at : first + padded] + lifted)
+        lane = 0
+        for piece in pieces:
+            piece = piece.astype(jnp.bfloat16).astype(jnp.float32)
+            here = slice(lane, lane + piece.shape[1])
+            for at in range(half):
+                section[2 * at + parity, :, here] = piece[at * slots : (at + 1) * slots]
+            lane += piece.shape[1]
 
     lane_tiles = padded // LANES
     points = weight_ref.shape[1]
@@ -581,8 +595,7 @@
     lanes = cells.shape[2]
     loads = window_loads(firsts, refs[: 2 * parts], cells, sems)
     table_load = pltpu.make_async_copy(back_any, back_table, sems.at[2 * parts])
-    table_load.start()
-    filter_parts(weight_ref, table_ref, cells, loads, section, back)
+    filter_parts(weight_ref, table_ref, cells, loads, [table_load], section, back)
     table_load.wait()
     outs = inverse_parts(back_table, back)
     for part in range(parts):
@@ -616,9 +629,7 @@
         rows = pl.ds(max(part - 1, 0) * group_rows, group_rows)
         source = (rest_read if part else first_read).at[:, rows, :]
         read_loads.append(pltpu.make_async_copy(source, reads.at[part], read_sems.at[part]))
-    for load in extra + read_loads:
-        load.start()
-    filter_parts(weight_ref, table_ref, cells, loads, section, back)
+    filter_parts(weight_ref, table_ref, cells, loads, extra + read_loads, section, back)
     for load in extra:
         load.wait()
     early = early_ref.shape[0]

time: 95 us -> 92.7 us (0.976)
  Pallas kernels: 55.8 us -> 53.3 us
    pallas_call x2, Pallas kernels: 14.2 us -> 13.1 us  [upwind(): pl.pallas_call(functools.partial(upwind_kernel, at * group, sizes), in_sp...]
    pallas_call x1, Pallas kernels: 19.7 us -> 18.7 us  [fast_device(): pl.pallas_call(functools.partial(finish_kernel, starts + starts, counts),...]
  transfers between devices with their start and end apart: 10 -> 10, of which waited for: 2 -> 2; matrix products, arithmetic and copies ran while one was open for 4% -> 5% of each run, Pallas kernels for 35% -> 34%
where the time goes in v9:
time: 92.7 us; the launch traced here: 92.3 us
  Pallas kernels  53.3 us (57%)
  starting transfers between devices  15.8 us (17%)
  waiting for transfers between devices  14.9 us (16%)
  local copies, waits for them, and re-layouts  5.98 us (6%)
  other arithmetic  1.87 us (2%)
    pallas_call x1, Pallas kernels, fast_device(): pl.pallas_call(functools.partial(finish_kernel, starts + starts, counts),...  18.7 us
    ppermute x4, waiting for transfers between devices, swapped(): return lax.ppermute(value, 'vel', swap)  13.8 us
    pallas_call x2, Pallas kernels, upwind(): pl.pallas_call(functools.partial(upwind_kernel, at * group, sizes), in_sp...  13.1 us
    pallas_call x1, Pallas kernels, fast_device(): pl.pallas_call(functools.partial(collide_kernel, starts + starts), in_spe...  12.6 us
    ppermute x2, starting transfers between devices, fast_device(): lax.ppermute(down, 'cy', towards_lower)  7.18 us
    pallas_call x2, Pallas kernels, edges_of(): pl.pallas_call(functools.partial(edges_kernel, first * group), in_specs=[...  6.25 us
    ppermute x4, starting transfers between devices, swapped(): return lax.ppermute(value, 'vel', swap)  5.61 us
    unnamed x36, local copies, waits for them, and re-layouts  3.66 us
  transfers between devices with their start and end apart: 10, of which 2 were waited for; matrix products, arithmetic and copies ran while one was open for 5% of the time, Pallas kernels for 34%

profile of v9, /device:TPU:0, one launch (start us, length us, event | category | flops | bytes accessed | tf_op | source)
XLA Modules:
  0.0 92.3 jit_solution(17973856972339371947)
XLA Ops:
  0.0 2.8 %edges.3 = (bf16[5,128,128]{2,1,0:T(8,128)(2,1)}, bf16[5,128,128]{2,1,0:T(8,128)(2,1)}, bf16[9,32,128]{2,1,0:T(8,128)(2,1)}) custom-call(s32[1]{0:T(128)} %bitcast.1.edge_ref, f32[72,128]{1,0:T(8,128)} %constant.33.clone.falls_ref, f32[16,4,4,6912]{3,2,1,0:T(4,128)} %refs_5_.3), custom_call_target="tpu_custom_call" | custom-call | flops 1 | bytes 1 | tf_op jit(solution)/shard_map/edges/pallas_call | solution.py:770
  2.9 2.5 %collective-permute-start.5 = (bf16[9,32,128]{2,1,0:T(8,128)(2,1)}, bf16[9,32,128]{2,1,0:T(8,128)(2,1)S(1)}, u32[]{:S(2)}, u32[]{:S(2)}) collective-permute-start(bf16[9,32,128]{2,1,0:T(8,128)(2,1)} %get-tuple-element.35), channel_id=1, source_target_pairs={{0,12},{4,0},{8,4},{12,8},{16,20},{20,24},{24,28},{28,16},{1,13},{... | collective-permute-start | bytes 221192 | tf_op jit(solution)/shard_map/ppermute | solution.py:840
  5.3 3.6 %collective-permute-start.3 = (bf16[5,128,128]{2,1,0:T(8,128)(2,1)}, bf16[5,128,128]{2,1,0:T(8,128)(2,1)S(1)}, u32[]{:S(2)}, u32[]{:S(2)}) collective-permute-start(bf16[5,128,128]{2,1,0:T(8,128)(2,1)} %get-tuple-element.33), channel_id=1, source_target_pairs={{0,3},{1,0},{2,1},{3,2},{4,7},{5,4},{6,5},{7,6},{8,11},{9,8},{10,9... | collective-permute-start | bytes 491528 | tf_op jit(solution)/shard_map/ppermute | solution.py:838
  8.9 3.4 %edges.2 = (bf16[10,128,128]{2,1,0:T(8,128)(2,1)}, bf16[10,128,128]{2,1,0:T(8,128)(2,1)}, bf16[18,32,128]{2,1,0:T(8,128)(2,1)}) custom-call(s32[1]{0:T(128)} %bitcast.1.edge_ref, f32[72,128]{1,0:T(8,128)} %constant.33.clone.falls_ref, f32[16,4,4,6912]{3,2,1,0:T(4,128)} %refs_5_.3), custom_call_target="tpu_custom_call" | custom-call | flops 1 | bytes 1 | tf_op jit(solution)/shard_map/edges/pallas_call | solution.py:770
  12.4 0.4 collective-permute-start.2
  12.8 3.6 %collective-permute-start = (bf16[10,128,128]{2,1,0:T(8,128)(2,1)}, bf16[10,128,128]{2,1,0:T(8,128)(2,1)S(1)}, u32[]{:S(2)}, u32[]{:S(2)}) collective-permute-start(bf16[10,128,128]{2,1,0:T(8,128)(2,1)} %get-tuple-element.30), channel_id=1, source_target_pairs={{0,3},{1,0},{2,1},{3,2},{4,7},{5,4},{6,5},{7,6},{8,11},{9,8},{10,9... | collective-permute-start | bytes 983048 | tf_op jit(solution)/shard_map/ppermute | solution.py:838
  16.4 0.1 copy.20
  16.8 0.1 convert_reduce_fusion
  17.2 0.1 copy.22
  17.5 0.1 copy.26
  17.8 0.1 select_n.37
  18.0 0.7 broadcast_in_dim.48.refs_1_
  18.8 5.1 %upwind.2 = (f32[64,72,128]{2,1,0:T(8,128)}, bf16[64,2304]{1,0:T(8,128)(2,1)}, bf16[64,2304]{1,0:T(8,128)(2,1)}) custom-call(s32[1]{0:T(128)} %bitcast.side_ref, f32[2,3,216,128]{3,2,1,0:T(8,128)} %constant.32.clone.refs_0_, s32[8,512]{1,0:T(8,128)} %broadcast_in_dim.48.refs_1_, bf16[5,128,128]{2,1,0:T(8,128)(2,1)} %copy-done.13, ...), custom_call_target="tpu_custom_call" | custom-call | flops 1 | bytes 1 | tf_op jit(solution)/shard_map/upwind/pallas_call | solution.py:799
  23.8 1.5 %collective-permute-start.6 = (bf16[64,2304]{1,0:T(8,128)(2,1)}, bf16[64,2304]{1,0:T(8,128)(2,1)S(1)}, u32[]{:S(2)}, u32[]{:S(2)}) collective-permute-start(bf16[64,2304]{1,0:T(8,128)(2,1)} %get-tuple-element.39.refs_0_), channel_id=1, source_target_pairs={{0,16},{16,0},{1,17},{17,1},{2,18},{18,2},{3,19},{19,3},{4,20},{20... | collective-permute-start | bytes 884744 | tf_op jit(solution)/shard_map/ppermute | solution.py:831
  25.4 0.6 collective-permute-start.7
  25.9 0.9 select_convert_fusion.spread_any
  26.8 0.1 reshape.108
  27.0 0.1 reshape.109
  27.1 0.1 reshape.110
  27.3 0.7 pad_maximum_fusion.stacked_ref
  28.0 2.7 %weights.1.weight_ref = f32[3,24,384]{2,1,0:T(8,128)} custom-call(f32[72,576]{1,0:T(8,128)} %pad_maximum_fusion.stacked_ref, bf16[576,768]{1,0:T(8,128)(2,1)} %constant.36.clone.select_ref, f32[1,384]{1,0:T(1,128)} %constant.37.clone.scale_ref), custom_call_target="tpu_custom_call" | custom-call | flops 1 | bytes 1 | tf_op jit(solution)/shard_map/weights/pallas_call | solution.py:847
  30.7 1.2 %collective-permute-done.1.refs_3_ = bf16[10,128,128]{2,1,0:T(8,128)(2,1)S(1)} collective-permute-done((bf16[10,128,128]{2,1,0:T(8,128)(2,1)}, bf16[10,128,128]{2,1,0:T(8,128)(2,1)S(1)}, u32[]{:S(2)}, u32[]{:S(2)}) %collective-permute-start.1) | collective-permute-done | bytes 327712 | tf_op jit(solution)/shard_map/ppermute | solution.py:839
  31.9 0.7 copy-done.8
  32.6 8.0 %upwind.3 = (f32[64,144,128]{2,1,0:T(8,128)}, bf16[128,2304]{1,0:T(8,128)(2,1)}, bf16[128,2304]{1,0:T(8,128)(2,1)}) custom-call(s32[1]{0:T(128)} %bitcast.side_ref, f32[2,3,216,128]{3,2,1,0:T(8,128)} %constant.32.clone.refs_0_, s32[8,512]{1,0:T(8,128)} %broadcast_in_dim.48.refs_1_, bf16[10,128,128]{2,1,0:T(8,128)(2,1)} %copy-done.7, ...), custom_call_target="tpu_custom_call" | custom-call | flops 1 | bytes 1 | tf_op jit(solution)/shard_map/upwind/pallas_call | solution.py:799
  40.6 1.8 %collective-permute-start.8 = (bf16[128,2304]{1,0:T(8,128)(2,1)}, bf16[128,2304]{1,0:T(8,128)(2,1)S(1)}, u32[]{:S(2)}, u32[]{:S(2)}) collective-permute-start(bf16[128,2304]{1,0:T(8,128)(2,1)} %get-tuple-element.50.refs_1_.refs_2_), channel_id=1, source_target_pairs={{0,16},{16,0},{1,17},{17,1},{2,18},{18,2},{3,19},{19,3},{4,20},{20... | collective-permute-start | bytes 1769480 | tf_op jit(solution)/shard_map/ppermute | solution.py:831
  42.4 13.8 %collective-permute-done.8.refs_4_.refs_5_ = bf16[128,2304]{1,0:T(8,128)(2,1)S(1)} collective-permute-done((bf16[128,2304]{1,0:T(8,128)(2,1)}, bf16[128,2304]{1,0:T(8,128)(2,1)S(1)}, u32[]{:S(2)}, u32[]{:S(2)}) %collective-permute-start.8) | collective-permute-done | bytes 589856 | tf_op jit(solution)/shard_map/ppermute | solution.py:831
  56.2 1.7 %collective-permute-start.9 = (bf16[128,2304]{1,0:T(8,128)(2,1)}, bf16[128,2304]{1,0:T(8,128)(2,1)S(1)}, u32[]{:S(2)}, u32[]{:S(2)}) collective-permute-start(bf16[128,2304]{1,0:T(8,128)(2,1)} %get-tuple-element.52.refs_2_.refs_3_), channel_id=1, source_target_pairs={{0,16},{16,0},{1,17},{17,1},{2,18},{18,2},{3,19},{19,3},{4,20},{20... | collective-permute-start | bytes 1769480 | tf_op jit(solution)/shard_map/ppermute | solution.py:831
  57.9 1.1 %copy-done.3 = bf16[128,2304]{1,0:T(8,128)(2,1)S(1)} copy-done((bf16[128,2304]{1,0:T(8,128)(2,1)S(1)}, bf16[128,2304]{1,0:T(8,128)(2,1)}, u32[]{:S(2)}) %copy-start.3) | copy-done | bytes 589848
  59.0 12.6 %collide.1.refs_0_ = bf16[64,6912]{1,0:T(8,128)(2,1)S(1)} custom-call(f32[3,24,384]{2,1,0:T(8,128)S(1)} %copy-done.4, bf16[832,768]{1,0:T(8,128)(2,1)S(1)} %copy-done.1, bf16[2,896,640]{2,1,0:T(8,128)(2,1)S(1)} %copy-done, bf16[64,2304]{1,0:T(8,128)(2,1)S(1)} %copy-done.5, bf16[128,2304]{1,0:T(8,128)(2,1)S(1)} %copy-done.3, bf16[128,2304]{1,0:T(8,128)(2,1)S(1)} %copy-done.3, ...), custom_call_target="tpu_custom_call" | custom-call | flops 1 | bytes 1 | tf_op jit(solution)/shard_map/collide/pallas_call | solution.py:878
  71.6 0.9 %copy-done.2 = bf16[64,6912]{1,0:T(8,128)(2,1)} copy-done((bf16[64,6912]{1,0:T(8,128)(2,1)}, bf16[64,6912]{1,0:T(8,128)(2,1)S(1)}, u32[]{:S(2)}) %copy-start.2) | copy-done | bytes 884760
  72.6 0.9 copy-done.6
  73.4 18.7 %finish.1 = f32[16,4,4,6912]{3,2,1,0:T(4,128)} custom-call(f32[3,24,384]{2,1,0:T(8,128)} %weights.1.weight_ref, bf16[832,768]{1,0:T(8,128)(2,1)} %constant.34.clone.table_ref, bf16[2,896,640]{2,1,0:T(8,128)(2,1)} %constant.35.clone.back_any, bf16[512,256]{1,0:T(8,128)(2,1)} %select_convert_fusion.spread_any, bf16[64,6912]{1,0:T(8,128)(2,1)} %copy-done.2, ...), custom_call_target="tpu_custom_call" | custom-call | tf_op jit(solution)/shard_map/finish/pallas_call | solution.py:901
  (55 shorter events, 1.0 us)
Async XLA Ops:
  2.9 13.5 %copy-start.17 = (s32[16,4,4]{0,2,1:T(4,128)S(1)}, s32[16,4,4]{0,2,1:T(4,128)}, u32[]{:S(2)}) copy-start(s32[16,4,4]{0,2,1:T(4,128)} %param.12) | copy-start | bytes 3076
  2.9 15.1 %collective-permute-start.5 = (bf16[9,32,128]{2,1,0:T(8,128)(2,1)}, bf16[9,32,128]{2,1,0:T(8,128)(2,1)S(1)}, u32[]{:S(2)}, u32[]{:S(2)}) collective-permute-start(bf16[9,32,128]{2,1,0:T(8,128)(2,1)} %get-tuple-element.35), channel_id=1, source_target_pairs={{0,12},{4,0},{8,4},{12,8},{16,20},{20,24},{24,28},{28,16},{1,13},{... | collective-permute-start | bytes 221192 | tf_op jit(solution)/shard_map/ppermute | solution.py:840
  5.3 12.7 %collective-permute-start.3 = (bf16[5,128,128]{2,1,0:T(8,128)(2,1)}, bf16[5,128,128]{2,1,0:T(8,128)(2,1)S(1)}, u32[]{:S(2)}, u32[]{:S(2)}) collective-permute-start(bf16[5,128,128]{2,1,0:T(8,128)(2,1)} %get-tuple-element.33), channel_id=1, source_target_pairs={{0,3},{1,0},{2,1},{3,2},{4,7},{5,4},{6,5},{7,6},{8,11},{9,8},{10,9... | collective-permute-start | bytes 491528 | tf_op jit(solution)/shard_map/ppermute | solution.py:838
  8.9 9.1 %collective-permute-start.4 = (bf16[5,128,128]{2,1,0:T(8,128)(2,1)}, bf16[5,128,128]{2,1,0:T(8,128)(2,1)S(1)}, u32[]{:S(2)}, u32[]{:S(2)}) collective-permute-start(bf16[5,128,128]{2,1,0:T(8,128)(2,1)} %get-tuple-element.34), channel_id=1, source_target_pairs={{0,1},{1,2},{2,3},{3,0},{4,5},{5,6},{6,7},{7,4},{8,9},{9,10},{10,1... | collective-permute-start | bytes 491528 | tf_op jit(solution)/shard_map/ppermute | solution.py:839
  12.3 14.5 %copy-start.9 = (f32[24,24,24]{2,1,0:T(8,128)S(1)}, f32[24,24,24]{2,1,0:T(8,128)}, u32[]{:S(2)}) copy-start(f32[24,24,24]{2,1,0:T(8,128)} %param.13) | copy-start | bytes 165892
  12.4 14.6 %copy-start.10 = (f32[24,24,24]{2,1,0:T(8,128)S(1)}, f32[24,24,24]{2,1,0:T(8,128)}, u32[]{:S(2)}) copy-start(f32[24,24,24]{2,1,0:T(8,128)} %param.14) | copy-start | bytes 165892
  12.4 18.3 %collective-permute-start.2 = (bf16[18,32,128]{2,1,0:T(8,128)(2,1)}, bf16[18,32,128]{2,1,0:T(8,128)(2,1)S(1)}, u32[]{:S(2)}, u32[]{:S(2)}) collective-permute-start(bf16[18,32,128]{2,1,0:T(8,128)(2,1)} %get-tuple-element.32), channel_id=1, source_target_pairs={{0,12},{4,0},{8,4},{12,8},{16,20},{20,24},{24,28},{28,16},{1,13},{... | collective-permute-start | bytes 442376 | tf_op jit(solution)/shard_map/ppermute | solution.py:840
  12.8 17.9 %collective-permute-start = (bf16[10,128,128]{2,1,0:T(8,128)(2,1)}, bf16[10,128,128]{2,1,0:T(8,128)(2,1)S(1)}, u32[]{:S(2)}, u32[]{:S(2)}) collective-permute-start(bf16[10,128,128]{2,1,0:T(8,128)(2,1)} %get-tuple-element.30), channel_id=1, source_target_pairs={{0,3},{1,0},{2,1},{3,2},{4,7},{5,4},{6,5},{7,6},{8,11},{9,8},{10,9... | collective-permute-start | bytes 983048 | tf_op jit(solution)/shard_map/ppermute | solution.py:838
  17.4 9.7 %copy-start.11 = (f32[24,24,24]{2,1,0:T(8,128)S(1)}, f32[24,24,24]{2,1,0:T(8,128)}, u32[]{:S(2)}) copy-start(f32[24,24,24]{2,1,0:T(8,128)} %param.15) | copy-start | bytes 165892
  17.9 0.8 copy-start.16
  17.9 13.9 %collective-permute-start.1 = (bf16[10,128,128]{2,1,0:T(8,128)(2,1)}, bf16[10,128,128]{2,1,0:T(8,128)(2,1)S(1)}, u32[]{:S(2)}, u32[]{:S(2)}) collective-permute-start(bf16[10,128,128]{2,1,0:T(8,128)(2,1)} %get-tuple-element.31), channel_id=1, source_target_pairs={{0,1},{1,2},{2,3},{3,0},{4,5},{5,6},{6,7},{7,4},{8,9},{9,10},{10,1... | collective-permute-start | bytes 983048 | tf_op jit(solution)/shard_map/ppermute | solution.py:839
  18.0 0.7 copy-start.13
  18.0 0.7 copy-start.14
  23.8 16.8 %collective-permute-start.6 = (bf16[64,2304]{1,0:T(8,128)(2,1)}, bf16[64,2304]{1,0:T(8,128)(2,1)S(1)}, u32[]{:S(2)}, u32[]{:S(2)}) collective-permute-start(bf16[64,2304]{1,0:T(8,128)(2,1)} %get-tuple-element.39.refs_0_), channel_id=1, source_target_pairs={{0,16},{16,0},{1,17},{17,1},{2,18},{18,2},{3,19},{19,3},{4,20},{20... | collective-permute-start | bytes 884744 | tf_op jit(solution)/shard_map/ppermute | solution.py:831
  25.4 15.3 %collective-permute-start.7 = (bf16[64,2304]{1,0:T(8,128)(2,1)}, bf16[64,2304]{1,0:T(8,128)(2,1)S(1)}, u32[]{:S(2)}, u32[]{:S(2)}) collective-permute-start(bf16[64,2304]{1,0:T(8,128)(2,1)} %get-tuple-element.40.refs_1_), channel_id=1, source_target_pairs={{0,16},{16,0},{1,17},{17,1},{2,18},{18,2},{3,19},{19,3},{4,20},{20... | collective-permute-start | bytes 884744 | tf_op jit(solution)/shard_map/ppermute | solution.py:831
  28.0 29.9 %copy-start = (bf16[2,896,640]{2,1,0:T(8,128)(2,1)S(1)}, bf16[2,896,640]{2,1,0:T(8,128)(2,1)}, u32[]{:S(2)}) copy-start(bf16[2,896,640]{2,1,0:T(8,128)(2,1)} %constant.35.clone.back_any) | copy-start | bytes 6881284
  28.0 29.9 %copy-start.1 = (bf16[832,768]{1,0:T(8,128)(2,1)S(1)}, bf16[832,768]{1,0:T(8,128)(2,1)}, u32[]{:S(2)}) copy-start(bf16[832,768]{1,0:T(8,128)(2,1)} %constant.34.clone.table_ref) | copy-start | bytes 3833860
  28.0 29.9 %copy-start.5 = (bf16[64,2304]{1,0:T(8,128)(2,1)S(1)}, bf16[64,2304]{1,0:T(8,128)(2,1)}, u32[]{:S(2)}) copy-start(bf16[64,2304]{1,0:T(8,128)(2,1)} %get-tuple-element.39.refs_0_) | copy-start | bytes 884740
  30.7 27.3 %copy-start.4 = (f32[3,24,384]{2,1,0:T(8,128)S(1)}, f32[3,24,384]{2,1,0:T(8,128)}, u32[]{:S(2)}) copy-start(f32[3,24,384]{2,1,0:T(8,128)} %weights.1.weight_ref) | copy-start | bytes 331780
  30.7 1.2 %copy-start.15 = (bf16[18,32,128]{2,1,0:T(8,128)(2,1)}, bf16[18,32,128]{2,1,0:T(8,128)(2,1)S(1)}, u32[]{:S(2)}) copy-start(bf16[18,32,128]{2,1,0:T(8,128)(2,1)S(1)} %collective-permute-done.2.refs_4_) | copy-start | bytes 442372
  30.7 1.2 %copy-start.7 = (bf16[10,128,128]{2,1,0:T(8,128)(2,1)}, bf16[10,128,128]{2,1,0:T(8,128)(2,1)S(1)}, u32[]{:S(2)}) copy-start(bf16[10,128,128]{2,1,0:T(8,128)(2,1)S(1)} %collective-permute-done.refs_2_) | copy-start | bytes 983044
  31.9 0.7 copy-start.8
  40.6 31.9 %copy-start.12 = (bf16[64,2304]{1,0:T(8,128)(2,1)}, bf16[64,2304]{1,0:T(8,128)(2,1)S(1)}, u32[]{:S(2)}) copy-start(bf16[64,2304]{1,0:T(8,128)(2,1)S(1)} %collective-permute-done.7.refs_4_) | copy-start | bytes 884740
  40.6 15.5 %collective-permute-start.8 = (bf16[128,2304]{1,0:T(8,128)(2,1)}, bf16[128,2304]{1,0:T(8,128)(2,1)S(1)}, u32[]{:S(2)}, u32[]{:S(2)}) collective-permute-start(bf16[128,2304]{1,0:T(8,128)(2,1)} %get-tuple-element.50.refs_1_.refs_2_), channel_id=1, source_target_pairs={{0,16},{16,0},{1,17},{17,1},{2,18},{18,2},{3,19},{19,3},{4,20},{20... | collective-permute-start | bytes 1769480 | tf_op jit(solution)/shard_map/ppermute | solution.py:831
  56.2 16.4 %collective-permute-start.9 = (bf16[128,2304]{1,0:T(8,128)(2,1)}, bf16[128,2304]{1,0:T(8,128)(2,1)S(1)}, u32[]{:S(2)}, u32[]{:S(2)}) collective-permute-start(bf16[128,2304]{1,0:T(8,128)(2,1)} %get-tuple-element.52.refs_2_.refs_3_), channel_id=1, source_target_pairs={{0,16},{16,0},{1,17},{17,1},{2,18},{18,2},{3,19},{19,3},{4,20},{20... | collective-permute-start | bytes 1769480 | tf_op jit(solution)/shard_map/ppermute | solution.py:831
  57.9 1.1 %copy-start.3 = (bf16[128,2304]{1,0:T(8,128)(2,1)S(1)}, bf16[128,2304]{1,0:T(8,128)(2,1)}, u32[]{:S(2)}) copy-start(bf16[128,2304]{1,0:T(8,128)(2,1)} %get-tuple-element.50.refs_1_.refs_2_) | copy-start | bytes 1769476
  71.6 0.9 %copy-start.2 = (bf16[64,6912]{1,0:T(8,128)(2,1)}, bf16[64,6912]{1,0:T(8,128)(2,1)S(1)}, u32[]{:S(2)}) copy-start(bf16[64,6912]{1,0:T(8,128)(2,1)S(1)} %collide.1.refs_0_) | copy-start | bytes 2654212
  72.6 0.9 copy-start.6

commit v10 on v9

--- a/solution.py
+++ b/solution.py
@@ -916,7 +916,7 @@
             pltpu.SemaphoreType.DMA((parts, pieces)),
             pltpu.SemaphoreType.DMA((batches,)),
         ],
-        compiler_params=params(LIMIT),
+        compiler_params=params(47),
         name="finish",
     )(
         weights,

time: 92.7 us -> 89.1 us (0.961)
  Pallas kernels: 53.3 us -> 51.4 us
  local copies, waits for them, and re-layouts: 5.98 us -> 4.23 us
    unnamed x36 -> x34, local copies, waits for them, and re-layouts: 3.66 us -> 1.92 us
    pallas_call x1, Pallas kernels: 18.7 us -> 17 us  [fast_device(): pl.pallas_call(functools.partial(finish_kernel, starts + starts, counts),...]
  transfers between devices with their start and end apart: 10 -> 10, of which waited for: 2 -> 2; matrix products, arithmetic and copies ran while one was open for 5% -> 4% of each run, Pallas kernels for 34% -> 36%
where the time goes in v10:
time: 89.1 us; the launch traced here: 88.7 us
  Pallas kernels  51.4 us (58%)
  starting transfers between devices  15.8 us (18%)
  waiting for transfers between devices  15.7 us (18%)
  local copies, waits for them, and re-layouts  4.23 us (5%)
  other arithmetic  1.14 us (1%)
    pallas_call x1, Pallas kernels, fast_device(): pl.pallas_call(functools.partial(finish_kernel, starts + starts, counts),...  17 us
    ppermute x4, waiting for transfers between devices, swapped(): return lax.ppermute(value, 'vel', swap)  13.8 us
    pallas_call x2, Pallas kernels, upwind(): pl.pallas_call(functools.partial(upwind_kernel, at * group, sizes), in_sp...  13 us
    pallas_call x1, Pallas kernels, fast_device(): pl.pallas_call(functools.partial(collide_kernel, starts + starts), in_spe...  12.4 us
    ppermute x2, starting transfers between devices, fast_device(): lax.ppermute(down, 'cy', towards_lower)  7.18 us
    pallas_call x2, Pallas kernels, edges_of(): pl.pallas_call(functools.partial(edges_kernel, first * group), in_specs=[...  6.25 us
    ppermute x4, starting transfers between devices, swapped(): return lax.ppermute(value, 'vel', swap)  5.61 us
    ppermute x2, starting transfers between devices, fast_device(): lax.ppermute(across, ('vel', 'cx'), across_pairs)  2.91 us
  transfers between devices with their start and end apart: 10, of which 2 were waited for; matrix products, arithmetic and copies ran while one was open for 4% of the time, Pallas kernels for 36%

profile of v10, /device:TPU:0, one launch (start us, length us, event | category | flops | bytes accessed | tf_op | source)
XLA Modules:
  0.0 88.7 jit_solution(2091261917619804993)
XLA Ops:
  0.0 2.8 %edges.3 = (bf16[5,128,128]{2,1,0:T(8,128)(2,1)}, bf16[5,128,128]{2,1,0:T(8,128)(2,1)}, bf16[9,32,128]{2,1,0:T(8,128)(2,1)}) custom-call(s32[1]{0:T(128)} %bitcast.1.edge_ref, f32[72,128]{1,0:T(8,128)} %constant.33.clone.falls_ref, f32[16,4,4,6912]{3,2,1,0:T(4,128)} %refs_5_.3), custom_call_target="tpu_custom_call" | custom-call | flops 1 | bytes 1 | tf_op jit(solution)/shard_map/edges/pallas_call | solution.py:770
  2.9 2.5 %collective-permute-start.5 = (bf16[9,32,128]{2,1,0:T(8,128)(2,1)}, bf16[9,32,128]{2,1,0:T(8,128)(2,1)S(1)}, u32[]{:S(2)}, u32[]{:S(2)}) collective-permute-start(bf16[9,32,128]{2,1,0:T(8,128)(2,1)} %get-tuple-element.35), channel_id=1, source_target_pairs={{0,12},{4,0},{8,4},{12,8},{16,20},{20,24},{24,28},{28,16},{1,13},{... | collective-permute-start | bytes 221192 | tf_op jit(solution)/shard_map/ppermute | solution.py:840
  5.3 3.6 %collective-permute-start.3 = (bf16[5,128,128]{2,1,0:T(8,128)(2,1)}, bf16[5,128,128]{2,1,0:T(8,128)(2,1)S(1)}, u32[]{:S(2)}, u32[]{:S(2)}) collective-permute-start(bf16[5,128,128]{2,1,0:T(8,128)(2,1)} %get-tuple-element.33), channel_id=1, source_target_pairs={{0,3},{1,0},{2,1},{3,2},{4,7},{5,4},{6,5},{7,6},{8,11},{9,8},{10,9... | collective-permute-start | bytes 491528 | tf_op jit(solution)/shard_map/ppermute | solution.py:838
  8.9 3.4 %edges.2 = (bf16[10,128,128]{2,1,0:T(8,128)(2,1)}, bf16[10,128,128]{2,1,0:T(8,128)(2,1)}, bf16[18,32,128]{2,1,0:T(8,128)(2,1)}) custom-call(s32[1]{0:T(128)} %bitcast.1.edge_ref, f32[72,128]{1,0:T(8,128)} %constant.33.clone.falls_ref, f32[16,4,4,6912]{3,2,1,0:T(4,128)} %refs_5_.3), custom_call_target="tpu_custom_call" | custom-call | flops 1 | bytes 1 | tf_op jit(solution)/shard_map/edges/pallas_call | solution.py:770
  12.4 0.4 collective-permute-start.2
  12.8 3.6 %collective-permute-start = (bf16[10,128,128]{2,1,0:T(8,128)(2,1)}, bf16[10,128,128]{2,1,0:T(8,128)(2,1)S(1)}, u32[]{:S(2)}, u32[]{:S(2)}) collective-permute-start(bf16[10,128,128]{2,1,0:T(8,128)(2,1)} %get-tuple-element.30), channel_id=1, source_target_pairs={{0,3},{1,0},{2,1},{3,2},{4,7},{5,4},{6,5},{7,6},{8,11},{9,8},{10,9... | collective-permute-start | bytes 983048 | tf_op jit(solution)/shard_map/ppermute | solution.py:838
  16.4 0.1 copy.20
  16.5 0.1 copy.19
  16.8 0.1 convert_reduce_fusion
  17.2 0.1 copy.22
  17.5 0.1 copy.26
  17.7 0.1 broadcast_in_dim.50
  17.8 0.1 select_n.37
  18.0 0.7 broadcast_in_dim.48.refs_1_
  18.8 5.0 %upwind.2 = (f32[64,72,128]{2,1,0:T(8,128)}, bf16[64,2304]{1,0:T(8,128)(2,1)}, bf16[64,2304]{1,0:T(8,128)(2,1)}) custom-call(s32[1]{0:T(128)} %bitcast.side_ref, f32[2,3,216,128]{3,2,1,0:T(8,128)} %constant.32.clone.refs_0_, s32[8,512]{1,0:T(8,128)} %broadcast_in_dim.48.refs_1_, bf16[5,128,128]{2,1,0:T(8,128)(2,1)} %copy-done.12, ...), custom_call_target="tpu_custom_call" | custom-call | flops 1 | bytes 1 | tf_op jit(solution)/shard_map/upwind/pallas_call | solution.py:799
  23.8 1.5 %collective-permute-start.6 = (bf16[64,2304]{1,0:T(8,128)(2,1)}, bf16[64,2304]{1,0:T(8,128)(2,1)S(1)}, u32[]{:S(2)}, u32[]{:S(2)}) collective-permute-start(bf16[64,2304]{1,0:T(8,128)(2,1)} %get-tuple-element.39.refs_0_), channel_id=1, source_target_pairs={{0,16},{16,0},{1,17},{17,1},{2,18},{18,2},{3,19},{19,3},{4,20},{20... | collective-permute-start | bytes 884744 | tf_op jit(solution)/shard_map/ppermute | solution.py:831
  25.3 0.6 collective-permute-start.7
  25.9 0.2 select_convert_fusion.spread_any
  26.1 0.1 reshape.108
  26.3 0.1 reshape.109
  26.4 0.1 reshape.110
  26.6 0.7 pad_maximum_fusion.stacked_ref
  27.3 2.7 %weights.1.weight_ref = f32[3,24,384]{2,1,0:T(8,128)} custom-call(f32[72,576]{1,0:T(8,128)} %pad_maximum_fusion.stacked_ref, bf16[576,768]{1,0:T(8,128)(2,1)} %constant.36.clone.select_ref, f32[1,384]{1,0:T(1,128)} %constant.37.clone.scale_ref), custom_call_target="tpu_custom_call" | custom-call | flops 1 | bytes 1 | tf_op jit(solution)/shard_map/weights/pallas_call | solution.py:847
  30.0 1.9 %collective-permute-done.1.refs_3_ = bf16[10,128,128]{2,1,0:T(8,128)(2,1)S(1)} collective-permute-done((bf16[10,128,128]{2,1,0:T(8,128)(2,1)}, bf16[10,128,128]{2,1,0:T(8,128)(2,1)S(1)}, u32[]{:S(2)}, u32[]{:S(2)}) %collective-permute-start.1) | collective-permute-done | bytes 327712 | tf_op jit(solution)/shard_map/ppermute | solution.py:839
  31.9 0.8 copy-done.8
  32.6 8.0 %upwind.3 = (f32[64,144,128]{2,1,0:T(8,128)}, bf16[128,2304]{1,0:T(8,128)(2,1)}, bf16[128,2304]{1,0:T(8,128)(2,1)}) custom-call(s32[1]{0:T(128)} %bitcast.side_ref, f32[2,3,216,128]{3,2,1,0:T(8,128)} %constant.32.clone.refs_0_, s32[8,512]{1,0:T(8,128)} %broadcast_in_dim.48.refs_1_, bf16[10,128,128]{2,1,0:T(8,128)(2,1)} %copy-done.7, ...), custom_call_target="tpu_custom_call" | custom-call | flops 1 | bytes 1 | tf_op jit(solution)/shard_map/upwind/pallas_call | solution.py:799
  40.7 1.8 %collective-permute-start.8 = (bf16[128,2304]{1,0:T(8,128)(2,1)}, bf16[128,2304]{1,0:T(8,128)(2,1)S(1)}, u32[]{:S(2)}, u32[]{:S(2)}) collective-permute-start(bf16[128,2304]{1,0:T(8,128)(2,1)} %get-tuple-element.50.refs_1_.refs_2_), channel_id=1, source_target_pairs={{0,16},{16,0},{1,17},{17,1},{2,18},{18,2},{3,19},{19,3},{4,20},{20... | collective-permute-start | bytes 1769480 | tf_op jit(solution)/shard_map/ppermute | solution.py:831
  42.4 13.8 %collective-permute-done.8.refs_4_.refs_5_ = bf16[128,2304]{1,0:T(8,128)(2,1)S(1)} collective-permute-done((bf16[128,2304]{1,0:T(8,128)(2,1)}, bf16[128,2304]{1,0:T(8,128)(2,1)S(1)}, u32[]{:S(2)}, u32[]{:S(2)}) %collective-permute-start.8) | collective-permute-done | bytes 589856 | tf_op jit(solution)/shard_map/ppermute | solution.py:831
  56.2 1.7 %collective-permute-start.9 = (bf16[128,2304]{1,0:T(8,128)(2,1)}, bf16[128,2304]{1,0:T(8,128)(2,1)S(1)}, u32[]{:S(2)}, u32[]{:S(2)}) collective-permute-start(bf16[128,2304]{1,0:T(8,128)(2,1)} %get-tuple-element.52.refs_2_.refs_3_), channel_id=1, source_target_pairs={{0,16},{16,0},{1,17},{17,1},{2,18},{18,2},{3,19},{19,3},{4,20},{20... | collective-permute-start | bytes 1769480 | tf_op jit(solution)/shard_map/ppermute | solution.py:831
  58.0 1.1 %copy-done.3 = bf16[128,2304]{1,0:T(8,128)(2,1)S(1)} copy-done((bf16[128,2304]{1,0:T(8,128)(2,1)S(1)}, bf16[128,2304]{1,0:T(8,128)(2,1)}, u32[]{:S(2)}) %copy-start.3) | copy-done | bytes 589848
  59.0 12.4 %collide.1.refs_0_ = bf16[64,6912]{1,0:T(8,128)(2,1)S(1)} custom-call(f32[3,24,384]{2,1,0:T(8,128)S(1)} %copy-done.4, bf16[832,768]{1,0:T(8,128)(2,1)S(1)} %copy-done.1, bf16[2,896,640]{2,1,0:T(8,128)(2,1)S(1)} %copy-done, bf16[64,2304]{1,0:T(8,128)(2,1)S(1)} %copy-done.5, bf16[128,2304]{1,0:T(8,128)(2,1)S(1)} %copy-done.3, bf16[128,2304]{1,0:T(8,128)(2,1)S(1)} %copy-done.3, ...), custom_call_target="tpu_custom_call" | custom-call | flops 1 | bytes 1 | tf_op jit(solution)/shard_map/collide/pallas_call | solution.py:878
  71.5 17.0 %finish.1 = f32[16,4,4,6912]{3,2,1,0:T(4,128)} custom-call(f32[3,24,384]{2,1,0:T(8,128)S(1)} %copy-done.4, bf16[832,768]{1,0:T(8,128)(2,1)S(1)} %copy-done.1, bf16[2,896,640]{2,1,0:T(8,128)(2,1)S(1)} %copy-done, bf16[512,256]{1,0:T(8,128)(2,1)S(1)} %select_convert_fusion.spread_any, bf16[64,6912]{1,0:T(8,128)(2,1)S(1)} %collide.1.refs_0_, ...), custom_call_target="tpu_custom_call" | custom-call | tf_op jit(solution)/shard_map/finish/pallas_call | solution.py:901
  (53 shorter events, 0.8 us)
Async XLA Ops:
  2.8 13.6 %copy-start.16 = (s32[16,4,4]{0,2,1:T(4,128)S(1)}, s32[16,4,4]{0,2,1:T(4,128)}, u32[]{:S(2)}) copy-start(s32[16,4,4]{0,2,1:T(4,128)} %param.12) | copy-start | bytes 3076
  2.9 15.1 %collective-permute-start.5 = (bf16[9,32,128]{2,1,0:T(8,128)(2,1)}, bf16[9,32,128]{2,1,0:T(8,128)(2,1)S(1)}, u32[]{:S(2)}, u32[]{:S(2)}) collective-permute-start(bf16[9,32,128]{2,1,0:T(8,128)(2,1)} %get-tuple-element.35), channel_id=1, source_target_pairs={{0,12},{4,0},{8,4},{12,8},{16,20},{20,24},{24,28},{28,16},{1,13},{... | collective-permute-start | bytes 221192 | tf_op jit(solution)/shard_map/ppermute | solution.py:840
  5.3 12.7 %collective-permute-start.3 = (bf16[5,128,128]{2,1,0:T(8,128)(2,1)}, bf16[5,128,128]{2,1,0:T(8,128)(2,1)S(1)}, u32[]{:S(2)}, u32[]{:S(2)}) collective-permute-start(bf16[5,128,128]{2,1,0:T(8,128)(2,1)} %get-tuple-element.33), channel_id=1, source_target_pairs={{0,3},{1,0},{2,1},{3,2},{4,7},{5,4},{6,5},{7,6},{8,11},{9,8},{10,9... | collective-permute-start | bytes 491528 | tf_op jit(solution)/shard_map/ppermute | solution.py:838
  8.9 9.1 %collective-permute-start.4 = (bf16[5,128,128]{2,1,0:T(8,128)(2,1)}, bf16[5,128,128]{2,1,0:T(8,128)(2,1)S(1)}, u32[]{:S(2)}, u32[]{:S(2)}) collective-permute-start(bf16[5,128,128]{2,1,0:T(8,128)(2,1)} %get-tuple-element.34), channel_id=1, source_target_pairs={{0,1},{1,2},{2,3},{3,0},{4,5},{5,6},{6,7},{7,4},{8,9},{9,10},{10,1... | collective-permute-start | bytes 491528 | tf_op jit(solution)/shard_map/ppermute | solution.py:839
  12.3 13.8 %copy-start.9 = (f32[24,24,24]{2,1,0:T(8,128)S(1)}, f32[24,24,24]{2,1,0:T(8,128)}, u32[]{:S(2)}) copy-start(f32[24,24,24]{2,1,0:T(8,128)} %param.13) | copy-start | bytes 165892
  12.4 13.9 %copy-start.10 = (f32[24,24,24]{2,1,0:T(8,128)S(1)}, f32[24,24,24]{2,1,0:T(8,128)}, u32[]{:S(2)}) copy-start(f32[24,24,24]{2,1,0:T(8,128)} %param.14) | copy-start | bytes 165892
  12.4 17.6 %collective-permute-start.2 = (bf16[18,32,128]{2,1,0:T(8,128)(2,1)}, bf16[18,32,128]{2,1,0:T(8,128)(2,1)S(1)}, u32[]{:S(2)}, u32[]{:S(2)}) collective-permute-start(bf16[18,32,128]{2,1,0:T(8,128)(2,1)} %get-tuple-element.32), channel_id=1, source_target_pairs={{0,12},{4,0},{8,4},{12,8},{16,20},{20,24},{24,28},{28,16},{1,13},{... | collective-permute-start | bytes 442376 | tf_op jit(solution)/shard_map/ppermute | solution.py:840
  12.8 17.1 %collective-permute-start = (bf16[10,128,128]{2,1,0:T(8,128)(2,1)}, bf16[10,128,128]{2,1,0:T(8,128)(2,1)S(1)}, u32[]{:S(2)}, u32[]{:S(2)}) collective-permute-start(bf16[10,128,128]{2,1,0:T(8,128)(2,1)} %get-tuple-element.30), channel_id=1, source_target_pairs={{0,3},{1,0},{2,1},{3,2},{4,7},{5,4},{6,5},{7,6},{8,11},{9,8},{10,9... | collective-permute-start | bytes 983048 | tf_op jit(solution)/shard_map/ppermute | solution.py:838
  17.4 9.0 %copy-start.11 = (f32[24,24,24]{2,1,0:T(8,128)S(1)}, f32[24,24,24]{2,1,0:T(8,128)}, u32[]{:S(2)}) copy-start(f32[24,24,24]{2,1,0:T(8,128)} %param.15) | copy-start | bytes 165892
  17.9 0.8 copy-start.15
  17.9 13.9 %collective-permute-start.1 = (bf16[10,128,128]{2,1,0:T(8,128)(2,1)}, bf16[10,128,128]{2,1,0:T(8,128)(2,1)S(1)}, u32[]{:S(2)}, u32[]{:S(2)}) collective-permute-start(bf16[10,128,128]{2,1,0:T(8,128)(2,1)} %get-tuple-element.31), channel_id=1, source_target_pairs={{0,1},{1,2},{2,3},{3,0},{4,5},{5,6},{6,7},{7,4},{8,9},{9,10},{10,1... | collective-permute-start | bytes 983048 | tf_op jit(solution)/shard_map/ppermute | solution.py:839
  18.0 0.7 copy-start.12
  18.0 0.7 copy-start.13
  23.8 16.8 %collective-permute-start.6 = (bf16[64,2304]{1,0:T(8,128)(2,1)}, bf16[64,2304]{1,0:T(8,128)(2,1)S(1)}, u32[]{:S(2)}, u32[]{:S(2)}) collective-permute-start(bf16[64,2304]{1,0:T(8,128)(2,1)} %get-tuple-element.39.refs_0_), channel_id=1, source_target_pairs={{0,16},{16,0},{1,17},{17,1},{2,18},{18,2},{3,19},{19,3},{4,20},{20... | collective-permute-start | bytes 884744 | tf_op jit(solution)/shard_map/ppermute | solution.py:831
  25.3 15.3 %collective-permute-start.7 = (bf16[64,2304]{1,0:T(8,128)(2,1)}, bf16[64,2304]{1,0:T(8,128)(2,1)S(1)}, u32[]{:S(2)}, u32[]{:S(2)}) collective-permute-start(bf16[64,2304]{1,0:T(8,128)(2,1)} %get-tuple-element.40.refs_1_), channel_id=1, source_target_pairs={{0,16},{16,0},{1,17},{17,1},{2,18},{18,2},{3,19},{19,3},{4,20},{20... | collective-permute-start | bytes 884744 | tf_op jit(solution)/shard_map/ppermute | solution.py:831
  27.3 30.7 %copy-start = (bf16[2,896,640]{2,1,0:T(8,128)(2,1)S(1)}, bf16[2,896,640]{2,1,0:T(8,128)(2,1)}, u32[]{:S(2)}) copy-start(bf16[2,896,640]{2,1,0:T(8,128)(2,1)} %constant.35.clone.back_any) | copy-start | bytes 6881284
  27.3 30.7 %copy-start.1 = (bf16[832,768]{1,0:T(8,128)(2,1)S(1)}, bf16[832,768]{1,0:T(8,128)(2,1)}, u32[]{:S(2)}) copy-start(bf16[832,768]{1,0:T(8,128)(2,1)} %constant.34.clone.table_ref) | copy-start | bytes 3833860
  27.3 30.7 %copy-start.5 = (bf16[64,2304]{1,0:T(8,128)(2,1)S(1)}, bf16[64,2304]{1,0:T(8,128)(2,1)}, u32[]{:S(2)}) copy-start(bf16[64,2304]{1,0:T(8,128)(2,1)} %get-tuple-element.39.refs_0_) | copy-start | bytes 884740
  29.9 28.0 %copy-start.4 = (f32[3,24,384]{2,1,0:T(8,128)S(1)}, f32[3,24,384]{2,1,0:T(8,128)}, u32[]{:S(2)}) copy-start(f32[3,24,384]{2,1,0:T(8,128)} %weights.1.weight_ref) | copy-start | bytes 331780
  29.9 1.9 %copy-start.14 = (bf16[18,32,128]{2,1,0:T(8,128)(2,1)}, bf16[18,32,128]{2,1,0:T(8,128)(2,1)S(1)}, u32[]{:S(2)}) copy-start(bf16[18,32,128]{2,1,0:T(8,128)(2,1)S(1)} %collective-permute-done.2.refs_4_) | copy-start | bytes 442372
  29.9 1.9 %copy-start.7 = (bf16[10,128,128]{2,1,0:T(8,128)(2,1)}, bf16[10,128,128]{2,1,0:T(8,128)(2,1)S(1)}, u32[]{:S(2)}) copy-start(bf16[10,128,128]{2,1,0:T(8,128)(2,1)S(1)} %collective-permute-done.refs_2_) | copy-start | bytes 983044
  31.9 0.8 copy-start.8
  32.6 38.9 %copy-start.6 = (bf16[64,2304]{1,0:T(8,128)(2,1)S(1)}, bf16[64,2304]{1,0:T(8,128)(2,1)}, u32[]{:S(2)}) copy-start(bf16[64,2304]{1,0:T(8,128)(2,1)} %get-tuple-element.40.refs_1_) | copy-start | bytes 884740
  40.6 30.9 %copy-start.2 = (bf16[128,2304]{1,0:T(8,128)(2,1)S(1)}, bf16[128,2304]{1,0:T(8,128)(2,1)}, u32[]{:S(2)}) copy-start(bf16[128,2304]{1,0:T(8,128)(2,1)} %get-tuple-element.52.refs_2_.refs_3_) | copy-start | bytes 1769476
  40.7 15.5 %collective-permute-start.8 = (bf16[128,2304]{1,0:T(8,128)(2,1)}, bf16[128,2304]{1,0:T(8,128)(2,1)S(1)}, u32[]{:S(2)}, u32[]{:S(2)}) collective-permute-start(bf16[128,2304]{1,0:T(8,128)(2,1)} %get-tuple-element.50.refs_1_.refs_2_), channel_id=1, source_target_pairs={{0,16},{16,0},{1,17},{17,1},{2,18},{18,2},{3,19},{19,3},{4,20},{20... | collective-permute-start | bytes 1769480 | tf_op jit(solution)/shard_map/ppermute | solution.py:831
  56.2 15.3 %collective-permute-start.9 = (bf16[128,2304]{1,0:T(8,128)(2,1)}, bf16[128,2304]{1,0:T(8,128)(2,1)S(1)}, u32[]{:S(2)}, u32[]{:S(2)}) collective-permute-start(bf16[128,2304]{1,0:T(8,128)(2,1)} %get-tuple-element.52.refs_2_.refs_3_), channel_id=1, source_target_pairs={{0,16},{16,0},{1,17},{17,1},{2,18},{18,2},{3,19},{19,3},{4,20},{20... | collective-permute-start | bytes 1769480 | tf_op jit(solution)/shard_map/ppermute | solution.py:831
  58.0 1.1 %copy-start.3 = (bf16[128,2304]{1,0:T(8,128)(2,1)S(1)}, bf16[128,2304]{1,0:T(8,128)(2,1)}, u32[]{:S(2)}) copy-start(bf16[128,2304]{1,0:T(8,128)(2,1)} %get-tuple-element.50.refs_1_.refs_2_) | copy-start | bytes 1769476

commit v11 on v10

--- a/solution.py
+++ b/solution.py
@@ -672,7 +672,7 @@
 
         stores.append([])
         for piece in range(pieces):
-            lax.fori_loop(piece * piece_x, (piece + 1) * piece_x, add, 0)
+            lax.fori_loop(piece * piece_x, (piece + 1) * piece_x, add, 0, unroll=2)
             rows = pl.ds(piece * piece_x, piece_x)
             store = pltpu.make_async_copy(
                 staged.at[slot, rows],

time: 89.1 us -> 89.2 us (level)
  no operation moved by 1% of the time
where the time goes in v11:
time: 89.2 us; the launch traced here: 88.8 us
  Pallas kernels  51.5 us (58%)
  starting transfers between devices  15.8 us (18%)
  waiting for transfers between devices  15.7 us (18%)
  local copies, waits for them, and re-layouts  4.23 us (5%)
  other arithmetic  1.14 us (1%)
    pallas_call x1, Pallas kernels, fast_device(): pl.pallas_call(functools.partial(finish_kernel, starts + starts, counts),...  17.1 us
    ppermute x4, waiting for transfers between devices, swapped(): return lax.ppermute(value, 'vel', swap)  13.8 us
    pallas_call x2, Pallas kernels, upwind(): pl.pallas_call(functools.partial(upwind_kernel, at * group, sizes), in_sp...  13 us
    pallas_call x1, Pallas kernels, fast_device(): pl.pallas_call(functools.partial(collide_kernel, starts + starts), in_spe...  12.4 us
    ppermute x2, starting transfers between devices, fast_device(): lax.ppermute(down, 'cy', towards_lower)  7.18 us
    pallas_call x2, Pallas kernels, edges_of(): pl.pallas_call(functools.partial(edges_kernel, first * group), in_specs=[...  6.25 us
    ppermute x4, starting transfers between devices, swapped(): return lax.ppermute(value, 'vel', swap)  5.61 us
    ppermute x2, starting transfers between devices, fast_device(): lax.ppermute(across, ('vel', 'cx'), across_pairs)  2.91 us
  transfers between devices with their start and end apart: 10, of which 2 were waited for; matrix products, arithmetic and copies ran while one was open for 4% of the time, Pallas kernels for 36%

profile of v11, /device:TPU:0, one launch (start us, length us, event | category | flops | bytes accessed | tf_op | source)
XLA Modules:
  0.0 88.8 jit_solution(14218943343916732837)
XLA Ops:
  0.0 2.8 %edges.3 = (bf16[5,128,128]{2,1,0:T(8,128)(2,1)}, bf16[5,128,128]{2,1,0:T(8,128)(2,1)}, bf16[9,32,128]{2,1,0:T(8,128)(2,1)}) custom-call(s32[1]{0:T(128)} %bitcast.1.edge_ref, f32[72,128]{1,0:T(8,128)} %constant.33.clone.falls_ref, f32[16,4,4,6912]{3,2,1,0:T(4,128)} %refs_5_.3), custom_call_target="tpu_custom_call" | custom-call | flops 1 | bytes 1 | tf_op jit(solution)/shard_map/edges/pallas_call | solution.py:770
  2.9 2.5 %collective-permute-start.5 = (bf16[9,32,128]{2,1,0:T(8,128)(2,1)}, bf16[9,32,128]{2,1,0:T(8,128)(2,1)S(1)}, u32[]{:S(2)}, u32[]{:S(2)}) collective-permute-start(bf16[9,32,128]{2,1,0:T(8,128)(2,1)} %get-tuple-element.35), channel_id=1, source_target_pairs={{0,12},{4,0},{8,4},{12,8},{16,20},{20,24},{24,28},{28,16},{1,13},{... | collective-permute-start | bytes 221192 | tf_op jit(solution)/shard_map/ppermute | solution.py:840
  5.3 3.6 %collective-permute-start.3 = (bf16[5,128,128]{2,1,0:T(8,128)(2,1)}, bf16[5,128,128]{2,1,0:T(8,128)(2,1)S(1)}, u32[]{:S(2)}, u32[]{:S(2)}) collective-permute-start(bf16[5,128,128]{2,1,0:T(8,128)(2,1)} %get-tuple-element.33), channel_id=1, source_target_pairs={{0,3},{1,0},{2,1},{3,2},{4,7},{5,4},{6,5},{7,6},{8,11},{9,8},{10,9... | collective-permute-start | bytes 491528 | tf_op jit(solution)/shard_map/ppermute | solution.py:838
  8.9 3.4 %edges.2 = (bf16[10,128,128]{2,1,0:T(8,128)(2,1)}, bf16[10,128,128]{2,1,0:T(8,128)(2,1)}, bf16[18,32,128]{2,1,0:T(8,128)(2,1)}) custom-call(s32[1]{0:T(128)} %bitcast.1.edge_ref, f32[72,128]{1,0:T(8,128)} %constant.33.clone.falls_ref, f32[16,4,4,6912]{3,2,1,0:T(4,128)} %refs_5_.3), custom_call_target="tpu_custom_call" | custom-call | flops 1 | bytes 1 | tf_op jit(solution)/shard_map/edges/pallas_call | solution.py:770
  12.4 0.4 collective-permute-start.2
  12.8 3.6 %collective-permute-start = (bf16[10,128,128]{2,1,0:T(8,128)(2,1)}, bf16[10,128,128]{2,1,0:T(8,128)(2,1)S(1)}, u32[]{:S(2)}, u32[]{:S(2)}) collective-permute-start(bf16[10,128,128]{2,1,0:T(8,128)(2,1)} %get-tuple-element.30), channel_id=1, source_target_pairs={{0,3},{1,0},{2,1},{3,2},{4,7},{5,4},{6,5},{7,6},{8,11},{9,8},{10,9... | collective-permute-start | bytes 983048 | tf_op jit(solution)/shard_map/ppermute | solution.py:838
  16.4 0.1 copy.20
  16.5 0.1 copy.19
  16.8 0.1 convert_reduce_fusion
  17.2 0.1 copy.22
  17.5 0.1 copy.26
  17.7 0.1 broadcast_in_dim.50
  17.8 0.1 select_n.37
  18.0 0.7 broadcast_in_dim.48.refs_1_
  18.8 5.0 %upwind.2 = (f32[64,72,128]{2,1,0:T(8,128)}, bf16[64,2304]{1,0:T(8,128)(2,1)}, bf16[64,2304]{1,0:T(8,128)(2,1)}) custom-call(s32[1]{0:T(128)} %bitcast.side_ref, f32[2,3,216,128]{3,2,1,0:T(8,128)} %constant.32.clone.refs_0_, s32[8,512]{1,0:T(8,128)} %broadcast_in_dim.48.refs_1_, bf16[5,128,128]{2,1,0:T(8,128)(2,1)} %copy-done.12, ...), custom_call_target="tpu_custom_call" | custom-call | flops 1 | bytes 1 | tf_op jit(solution)/shard_map/upwind/pallas_call | solution.py:799
  23.8 1.5 %collective-permute-start.6 = (bf16[64,2304]{1,0:T(8,128)(2,1)}, bf16[64,2304]{1,0:T(8,128)(2,1)S(1)}, u32[]{:S(2)}, u32[]{:S(2)}) collective-permute-start(bf16[64,2304]{1,0:T(8,128)(2,1)} %get-tuple-element.39.refs_0_), channel_id=1, source_target_pairs={{0,16},{16,0},{1,17},{17,1},{2,18},{18,2},{3,19},{19,3},{4,20},{20... | collective-permute-start | bytes 884744 | tf_op jit(solution)/shard_map/ppermute | solution.py:831
  25.3 0.6 collective-permute-start.7
  25.9 0.2 select_convert_fusion.spread_any
  26.1 0.1 reshape.108
  26.3 0.1 reshape.109
  26.4 0.1 reshape.110
  26.6 0.7 pad_maximum_fusion.stacked_ref
  27.3 2.7 %weights.1.weight_ref = f32[3,24,384]{2,1,0:T(8,128)} custom-call(f32[72,576]{1,0:T(8,128)} %pad_maximum_fusion.stacked_ref, bf16[576,768]{1,0:T(8,128)(2,1)} %constant.36.clone.select_ref, f32[1,384]{1,0:T(1,128)} %constant.37.clone.scale_ref), custom_call_target="tpu_custom_call" | custom-call | flops 1 | bytes 1 | tf_op jit(solution)/shard_map/weights/pallas_call | solution.py:847
  30.0 1.9 %collective-permute-done.1.refs_3_ = bf16[10,128,128]{2,1,0:T(8,128)(2,1)S(1)} collective-permute-done((bf16[10,128,128]{2,1,0:T(8,128)(2,1)}, bf16[10,128,128]{2,1,0:T(8,128)(2,1)S(1)}, u32[]{:S(2)}, u32[]{:S(2)}) %collective-permute-start.1) | collective-permute-done | bytes 327712 | tf_op jit(solution)/shard_map/ppermute | solution.py:839
  31.9 0.8 copy-done.8
  32.6 8.0 %upwind.3 = (f32[64,144,128]{2,1,0:T(8,128)}, bf16[128,2304]{1,0:T(8,128)(2,1)}, bf16[128,2304]{1,0:T(8,128)(2,1)}) custom-call(s32[1]{0:T(128)} %bitcast.side_ref, f32[2,3,216,128]{3,2,1,0:T(8,128)} %constant.32.clone.refs_0_, s32[8,512]{1,0:T(8,128)} %broadcast_in_dim.48.refs_1_, bf16[10,128,128]{2,1,0:T(8,128)(2,1)} %copy-done.7, ...), custom_call_target="tpu_custom_call" | custom-call | flops 1 | bytes 1 | tf_op jit(solution)/shard_map/upwind/pallas_call | solution.py:799
  40.7 1.8 %collective-permute-start.8 = (bf16[128,2304]{1,0:T(8,128)(2,1)}, bf16[128,2304]{1,0:T(8,128)(2,1)S(1)}, u32[]{:S(2)}, u32[]{:S(2)}) collective-permute-start(bf16[128,2304]{1,0:T(8,128)(2,1)} %get-tuple-element.50.refs_1_.refs_2_), channel_id=1, source_target_pairs={{0,16},{16,0},{1,17},{17,1},{2,18},{18,2},{3,19},{19,3},{4,20},{20... | collective-permute-start | bytes 1769480 | tf_op jit(solution)/shard_map/ppermute | solution.py:831
  42.4 13.8 %collective-permute-done.8.refs_4_.refs_5_ = bf16[128,2304]{1,0:T(8,128)(2,1)S(1)} collective-permute-done((bf16[128,2304]{1,0:T(8,128)(2,1)}, bf16[128,2304]{1,0:T(8,128)(2,1)S(1)}, u32[]{:S(2)}, u32[]{:S(2)}) %collective-permute-start.8) | collective-permute-done | bytes 589856 | tf_op jit(solution)/shard_map/ppermute | solution.py:831
  56.2 1.7 %collective-permute-start.9 = (bf16[128,2304]{1,0:T(8,128)(2,1)}, bf16[128,2304]{1,0:T(8,128)(2,1)S(1)}, u32[]{:S(2)}, u32[]{:S(2)}) collective-permute-start(bf16[128,2304]{1,0:T(8,128)(2,1)} %get-tuple-element.52.refs_2_.refs_3_), channel_id=1, source_target_pairs={{0,16},{16,0},{1,17},{17,1},{2,18},{18,2},{3,19},{19,3},{4,20},{20... | collective-permute-start | bytes 1769480 | tf_op jit(solution)/shard_map/ppermute | solution.py:831
  58.0 1.1 %copy-done.3 = bf16[128,2304]{1,0:T(8,128)(2,1)S(1)} copy-done((bf16[128,2304]{1,0:T(8,128)(2,1)S(1)}, bf16[128,2304]{1,0:T(8,128)(2,1)}, u32[]{:S(2)}) %copy-start.3) | copy-done | bytes 589848
  59.0 12.4 %collide.1.refs_0_ = bf16[64,6912]{1,0:T(8,128)(2,1)S(1)} custom-call(f32[3,24,384]{2,1,0:T(8,128)S(1)} %copy-done.4, bf16[832,768]{1,0:T(8,128)(2,1)S(1)} %copy-done.1, bf16[2,896,640]{2,1,0:T(8,128)(2,1)S(1)} %copy-done, bf16[64,2304]{1,0:T(8,128)(2,1)S(1)} %copy-done.5, bf16[128,2304]{1,0:T(8,128)(2,1)S(1)} %copy-done.3, bf16[128,2304]{1,0:T(8,128)(2,1)S(1)} %copy-done.3, ...), custom_call_target="tpu_custom_call" | custom-call | flops 1 | bytes 1 | tf_op jit(solution)/shard_map/collide/pallas_call | solution.py:878
  71.5 17.1 %finish.1 = f32[16,4,4,6912]{3,2,1,0:T(4,128)} custom-call(f32[3,24,384]{2,1,0:T(8,128)S(1)} %copy-done.4, bf16[832,768]{1,0:T(8,128)(2,1)S(1)} %copy-done.1, bf16[2,896,640]{2,1,0:T(8,128)(2,1)S(1)} %copy-done, bf16[512,256]{1,0:T(8,128)(2,1)S(1)} %select_convert_fusion.spread_any, bf16[64,6912]{1,0:T(8,128)(2,1)S(1)} %collide.1.refs_0_, ...), custom_call_target="tpu_custom_call" | custom-call | tf_op jit(solution)/shard_map/finish/pallas_call | solution.py:901
  (53 shorter events, 0.8 us)
Async XLA Ops:
  2.8 13.6 %copy-start.16 = (s32[16,4,4]{0,2,1:T(4,128)S(1)}, s32[16,4,4]{0,2,1:T(4,128)}, u32[]{:S(2)}) copy-start(s32[16,4,4]{0,2,1:T(4,128)} %param.12) | copy-start | bytes 3076
  2.9 15.1 %collective-permute-start.5 = (bf16[9,32,128]{2,1,0:T(8,128)(2,1)}, bf16[9,32,128]{2,1,0:T(8,128)(2,1)S(1)}, u32[]{:S(2)}, u32[]{:S(2)}) collective-permute-start(bf16[9,32,128]{2,1,0:T(8,128)(2,1)} %get-tuple-element.35), channel_id=1, source_target_pairs={{0,12},{4,0},{8,4},{12,8},{16,20},{20,24},{24,28},{28,16},{1,13},{... | collective-permute-start | bytes 221192 | tf_op jit(solution)/shard_map/ppermute | solution.py:840
  5.3 12.7 %collective-permute-start.3 = (bf16[5,128,128]{2,1,0:T(8,128)(2,1)}, bf16[5,128,128]{2,1,0:T(8,128)(2,1)S(1)}, u32[]{:S(2)}, u32[]{:S(2)}) collective-permute-start(bf16[5,128,128]{2,1,0:T(8,128)(2,1)} %get-tuple-element.33), channel_id=1, source_target_pairs={{0,3},{1,0},{2,1},{3,2},{4,7},{5,4},{6,5},{7,6},{8,11},{9,8},{10,9... | collective-permute-start | bytes 491528 | tf_op jit(solution)/shard_map/ppermute | solution.py:838
  8.9 9.1 %collective-permute-start.4 = (bf16[5,128,128]{2,1,0:T(8,128)(2,1)}, bf16[5,128,128]{2,1,0:T(8,128)(2,1)S(1)}, u32[]{:S(2)}, u32[]{:S(2)}) collective-permute-start(bf16[5,128,128]{2,1,0:T(8,128)(2,1)} %get-tuple-element.34), channel_id=1, source_target_pairs={{0,1},{1,2},{2,3},{3,0},{4,5},{5,6},{6,7},{7,4},{8,9},{9,10},{10,1... | collective-permute-start | bytes 491528 | tf_op jit(solution)/shard_map/ppermute | solution.py:839
  12.3 13.8 %copy-start.9 = (f32[24,24,24]{2,1,0:T(8,128)S(1)}, f32[24,24,24]{2,1,0:T(8,128)}, u32[]{:S(2)}) copy-start(f32[24,24,24]{2,1,0:T(8,128)} %param.13) | copy-start | bytes 165892
  12.4 13.9 %copy-start.10 = (f32[24,24,24]{2,1,0:T(8,128)S(1)}, f32[24,24,24]{2,1,0:T(8,128)}, u32[]{:S(2)}) copy-start(f32[24,24,24]{2,1,0:T(8,128)} %param.14) | copy-start | bytes 165892
  12.4 17.6 %collective-permute-start.2 = (bf16[18,32,128]{2,1,0:T(8,128)(2,1)}, bf16[18,32,128]{2,1,0:T(8,128)(2,1)S(1)}, u32[]{:S(2)}, u32[]{:S(2)}) collective-permute-start(bf16[18,32,128]{2,1,0:T(8,128)(2,1)} %get-tuple-element.32), channel_id=1, source_target_pairs={{0,12},{4,0},{8,4},{12,8},{16,20},{20,24},{24,28},{28,16},{1,13},{... | collective-permute-start | bytes 442376 | tf_op jit(solution)/shard_map/ppermute | solution.py:840
  12.8 17.1 %collective-permute-start = (bf16[10,128,128]{2,1,0:T(8,128)(2,1)}, bf16[10,128,128]{2,1,0:T(8,128)(2,1)S(1)}, u32[]{:S(2)}, u32[]{:S(2)}) collective-permute-start(bf16[10,128,128]{2,1,0:T(8,128)(2,1)} %get-tuple-element.30), channel_id=1, source_target_pairs={{0,3},{1,0},{2,1},{3,2},{4,7},{5,4},{6,5},{7,6},{8,11},{9,8},{10,9... | collective-permute-start | bytes 983048 | tf_op jit(solution)/shard_map/ppermute | solution.py:838
  17.4 9.0 %copy-start.11 = (f32[24,24,24]{2,1,0:T(8,128)S(1)}, f32[24,24,24]{2,1,0:T(8,128)}, u32[]{:S(2)}) copy-start(f32[24,24,24]{2,1,0:T(8,128)} %param.15) | copy-start | bytes 165892
  17.9 0.8 copy-start.15
  17.9 13.9 %collective-permute-start.1 = (bf16[10,128,128]{2,1,0:T(8,128)(2,1)}, bf16[10,128,128]{2,1,0:T(8,128)(2,1)S(1)}, u32[]{:S(2)}, u32[]{:S(2)}) collective-permute-start(bf16[10,128,128]{2,1,0:T(8,128)(2,1)} %get-tuple-element.31), channel_id=1, source_target_pairs={{0,1},{1,2},{2,3},{3,0},{4,5},{5,6},{6,7},{7,4},{8,9},{9,10},{10,1... | collective-permute-start | bytes 983048 | tf_op jit(solution)/shard_map/ppermute | solution.py:839
  18.0 0.7 copy-start.12
  18.0 0.7 copy-start.13
  23.8 16.8 %collective-permute-start.6 = (bf16[64,2304]{1,0:T(8,128)(2,1)}, bf16[64,2304]{1,0:T(8,128)(2,1)S(1)}, u32[]{:S(2)}, u32[]{:S(2)}) collective-permute-start(bf16[64,2304]{1,0:T(8,128)(2,1)} %get-tuple-element.39.refs_0_), channel_id=1, source_target_pairs={{0,16},{16,0},{1,17},{17,1},{2,18},{18,2},{3,19},{19,3},{4,20},{20... | collective-permute-start | bytes 884744 | tf_op jit(solution)/shard_map/ppermute | solution.py:831
  25.3 15.3 %collective-permute-start.7 = (bf16[64,2304]{1,0:T(8,128)(2,1)}, bf16[64,2304]{1,0:T(8,128)(2,1)S(1)}, u32[]{:S(2)}, u32[]{:S(2)}) collective-permute-start(bf16[64,2304]{1,0:T(8,128)(2,1)} %get-tuple-element.40.refs_1_), channel_id=1, source_target_pairs={{0,16},{16,0},{1,17},{17,1},{2,18},{18,2},{3,19},{19,3},{4,20},{20... | collective-permute-start | bytes 884744 | tf_op jit(solution)/shard_map/ppermute | solution.py:831
  27.3 30.7 %copy-start = (bf16[2,896,640]{2,1,0:T(8,128)(2,1)S(1)}, bf16[2,896,640]{2,1,0:T(8,128)(2,1)}, u32[]{:S(2)}) copy-start(bf16[2,896,640]{2,1,0:T(8,128)(2,1)} %constant.35.clone.back_any) | copy-start | bytes 6881284
  27.3 30.7 %copy-start.1 = (bf16[832,768]{1,0:T(8,128)(2,1)S(1)}, bf16[832,768]{1,0:T(8,128)(2,1)}, u32[]{:S(2)}) copy-start(bf16[832,768]{1,0:T(8,128)(2,1)} %constant.34.clone.table_ref) | copy-start | bytes 3833860
  27.3 30.7 %copy-start.5 = (bf16[64,2304]{1,0:T(8,128)(2,1)S(1)}, bf16[64,2304]{1,0:T(8,128)(2,1)}, u32[]{:S(2)}) copy-start(bf16[64,2304]{1,0:T(8,128)(2,1)} %get-tuple-element.39.refs_0_) | copy-start | bytes 884740
  29.9 28.0 %copy-start.4 = (f32[3,24,384]{2,1,0:T(8,128)S(1)}, f32[3,24,384]{2,1,0:T(8,128)}, u32[]{:S(2)}) copy-start(f32[3,24,384]{2,1,0:T(8,128)} %weights.1.weight_ref) | copy-start | bytes 331780
  29.9 1.9 %copy-start.14 = (bf16[18,32,128]{2,1,0:T(8,128)(2,1)}, bf16[18,32,128]{2,1,0:T(8,128)(2,1)S(1)}, u32[]{:S(2)}) copy-start(bf16[18,32,128]{2,1,0:T(8,128)(2,1)S(1)} %collective-permute-done.2.refs_4_) | copy-start | bytes 442372
  29.9 1.9 %copy-start.7 = (bf16[10,128,128]{2,1,0:T(8,128)(2,1)}, bf16[10,128,128]{2,1,0:T(8,128)(2,1)S(1)}, u32[]{:S(2)}) copy-start(bf16[10,128,128]{2,1,0:T(8,128)(2,1)S(1)} %collective-permute-done.refs_2_) | copy-start | bytes 983044
  31.9 0.8 copy-start.8
  32.6 38.9 %copy-start.6 = (bf16[64,2304]{1,0:T(8,128)(2,1)S(1)}, bf16[64,2304]{1,0:T(8,128)(2,1)}, u32[]{:S(2)}) copy-start(bf16[64,2304]{1,0:T(8,128)(2,1)} %get-tuple-element.40.refs_1_) | copy-start | bytes 884740
  40.6 30.9 %copy-start.2 = (bf16[128,2304]{1,0:T(8,128)(2,1)S(1)}, bf16[128,2304]{1,0:T(8,128)(2,1)}, u32[]{:S(2)}) copy-start(bf16[128,2304]{1,0:T(8,128)(2,1)} %get-tuple-element.52.refs_2_.refs_3_) | copy-start | bytes 1769476
  40.7 15.5 %collective-permute-start.8 = (bf16[128,2304]{1,0:T(8,128)(2,1)}, bf16[128,2304]{1,0:T(8,128)(2,1)S(1)}, u32[]{:S(2)}, u32[]{:S(2)}) collective-permute-start(bf16[128,2304]{1,0:T(8,128)(2,1)} %get-tuple-element.50.refs_1_.refs_2_), channel_id=1, source_target_pairs={{0,16},{16,0},{1,17},{17,1},{2,18},{18,2},{3,19},{19,3},{4,20},{20... | collective-permute-start | bytes 1769480 | tf_op jit(solution)/shard_map/ppermute | solution.py:831
  56.2 15.3 %collective-permute-start.9 = (bf16[128,2304]{1,0:T(8,128)(2,1)}, bf16[128,2304]{1,0:T(8,128)(2,1)S(1)}, u32[]{:S(2)}, u32[]{:S(2)}) collective-permute-start(bf16[128,2304]{1,0:T(8,128)(2,1)} %get-tuple-element.52.refs_2_.refs_3_), channel_id=1, source_target_pairs={{0,16},{16,0},{1,17},{17,1},{2,18},{18,2},{3,19},{19,3},{4,20},{20... | collective-permute-start | bytes 1769480 | tf_op jit(solution)/shard_map/ppermute | solution.py:831
  58.0 1.1 %copy-start.3 = (bf16[128,2304]{1,0:T(8,128)(2,1)S(1)}, bf16[128,2304]{1,0:T(8,128)(2,1)}, u32[]{:S(2)}) copy-start(bf16[128,2304]{1,0:T(8,128)(2,1)} %get-tuple-element.50.refs_1_.refs_2_) | copy-start | bytes 1769476
